TPU v7x, 32 devices: a whole 2x2x4 slice. The times are simulated.
32 devices in a mesh: groups: 2 (over y), dp: 4 (over z), mp: 4 (over x, core).
Axes of the slice: x: 2, y: 2, z: 4, core: 2. Of those that a mesh axis runs over, the one named last changes fastest.
Arguments:
- tokens: bfloat16 [16384, 2048], P(('groups', 'dp'), 'mp'), parts along dimension 0, may hold values from -6 to 6
- x_weight: bfloat16 [2048, 2048], P(None, 'mp'), may hold values from -0.125 to 0.125
- z_weight: bfloat16 [2048, 2048], P(None, 'mp'), may hold values from -0.125 to 0.125
- bc_weight: bfloat16 [2048, 512], P(None, 'mp'), may hold values from -0.125 to 0.125
- dt_weight: bfloat16 [2048, 32], P(None, 'mp'), may hold values from -0.125 to 0.125
- dt_bias: float32 [32], P('mp'), may hold values from -3 to 1
- decay_rate: float32 [32], P('mp'), may hold values from 0.003 to 0.03
- norm_gain: float32 [2048], P('mp'), may hold values from 0.1 to 1.9
- out_weight: bfloat16 [2048, 2048], P('mp'), may hold values from -0.125 to 0.125
- store_states: bfloat16 [128, 131072], P(('groups', 'dp'), 'mp'), parts along dimension 0, may hold values from -6 to 6
- home_rows: int32 [128], P('groups'), parts along dimension 0, may hold values from 0 to 63, as said below
- event_counts: int32 [128], P(('groups', 'dp')), parts along dimension 0, may hold values from 1 to 128, as said below
Outputs:
- out_tokens: bfloat16 [16384, 2048], P(('groups', 'dp', 'mp')), parts along dimension 0
- new_store: bfloat16 [128, 131072], P(('groups', 'dp'), 'mp'), parts along dimension 0
There are 2 independent parts, one for each index of `groups`. A program takes and returns all parts, laid end to end along the dimension named above; an argument that names none is the same for every part. Nothing has to cross between parts.
Inputs may be any that keep to these rules, and one draw needn't show every extreme that they name: A permutation: session r's state is row home_rows[r] of the store. The 16 sessions of one aligned block keep at most 4 states in one aligned block of 16 store rows, and every block of sessions reaches 4 in some block of rows. `event_counts`: event slots at or after a session's count are padding.
All inputs are finite; a program needn't handle non-finite values.
Results may differ from a plain program's by a relative error of at most 0.02.
Values may be sent and summed in bfloat16 or wider, within the bound.
No kernel may reach another device: no remote copies, remote signals or barrier semaphores. Data moves between devices by JAX's collectives and lax.ppermute only.
A program may use at most 128 MiB of HBM per device.

v0:
```python
import jax
import jax.numpy as jnp
from jax import lax
from jax.sharding import PartitionSpec as P


def pack_rows(values, wanted, slot_count):
    slots = jnp.arange(slot_count, dtype=jnp.int32)
    chosen = wanted[None, :] == slots[:, None]
    filled = jnp.any(chosen, axis=1)
    places = jnp.arange(wanted.shape[0], dtype=jnp.int32)
    source = jnp.sum(chosen.astype(jnp.int32) * places[None, :], axis=1)
    picked = jnp.take(values, source, axis=0)
    return jnp.where(filled[:, None], picked, jnp.zeros((), values.dtype))


def rank_within(keys, order):
    earlier = (keys[None, :] == keys[:, None]) & (order[None, :] < order[:, None])
    return jnp.sum(earlier.astype(jnp.int32), axis=1)


def body(
    tokens,
    x_weight,
    z_weight,
    bc_weight,
    dt_weight,
    dt_bias,
    decay_rate,
    norm_gain,
    out_weight,
    store_states,
    home_rows,
    event_counts,
):
    shard_count = lax.axis_size("dp")
    store_index = lax.axis_index("dp")
    sessions_here = store_states.shape[0]
    state_width = store_states.shape[1]
    capacity = max(2, (sessions_here + shard_count - 1) // shard_count)
    slot_count = shard_count * capacity
    local_heads = dt_bias.shape[0]
    head_size = x_weight.shape[1] // local_heads
    state_size = bc_weight.shape[1] // 2
    total_rows = tokens.shape[0]
    event_slots = total_rows // sessions_here
    positions = jnp.arange(sessions_here, dtype=jnp.int32)
    store_rows = store_index * sessions_here + positions
    everyone = jnp.arange(home_rows.shape[0], dtype=jnp.int32)
    owner = jnp.sum(
        (home_rows[None, :] == store_rows[:, None]).astype(jnp.int32) * everyone[None, :], axis=1
    )
    server = owner // sessions_here
    row_slot = server * capacity + rank_within(server, positions)
    outbound = pack_rows(store_states, row_slot, slot_count).reshape(
        shard_count, capacity, state_width
    )
    inbound = lax.all_to_all(outbound, "dp", split_axis=0, concat_axis=0, tiled=True).reshape(
        slot_count, state_width
    )
    wanted = lax.dynamic_slice_in_dim(home_rows, store_index * sessions_here, sessions_here)
    home_shard = wanted // sessions_here
    session_slot = home_shard * capacity + rank_within(home_shard, wanted % sessions_here)
    weights = (x_weight, z_weight, bc_weight, dt_weight)
    shard_cols = lax.all_gather(tokens, "mp", axis=1, tiled=True)
    x_sum, z_sum, bc_sum, dt_sum = tuple(
        (jnp.dot(shard_cols, weight, preferred_element_type=jnp.float32) for weight in weights)
    )
    initial_state = jnp.take(inbound, session_slot, axis=0).reshape(
        sessions_here, local_heads, head_size, state_size
    )
    inputs = x_sum.astype(jnp.bfloat16).reshape(sessions_here, event_slots, local_heads, head_size)
    gate_values = z_sum.astype(jnp.bfloat16)
    bc_values = bc_sum.astype(jnp.bfloat16).reshape(sessions_here, event_slots, 2 * state_size)
    b_matrix = bc_values[:, :, :state_size]
    c_matrix = bc_values[:, :, state_size:]
    valid_mask = (jnp.arange(event_slots, dtype=jnp.int32)[None, :] < event_counts[:, None]).astype(
        jnp.float32
    )
    step_sizes = (
        jax.nn.softplus(
            dt_sum.reshape(sessions_here, event_slots, local_heads) + dt_bias[None, None, :]
        )
        * valid_mask[:, :, None]
    )
    decay_sum = jnp.cumsum(step_sizes * decay_rate[None, None, :], axis=1)
    lagged = jnp.transpose(decay_sum, (0, 2, 1))
    causal_mask = jnp.arange(event_slots)[:, None] >= jnp.arange(event_slots)[None, :]
    decay_gaps = jnp.where(causal_mask, lagged[:, :, :, None] - lagged[:, :, None, :], 0.0)
    kernel = jnp.einsum("stn,sun->stu", c_matrix, b_matrix, preferred_element_type=jnp.float32)
    step_rows = jnp.transpose(step_sizes, (0, 2, 1))
    mixing = (
        jnp.where(causal_mask, jnp.exp(-decay_gaps), 0.0)
        * step_rows[:, :, None, :]
        * kernel[:, None, :, :]
    ).astype(jnp.bfloat16)
    diagonal_part = jnp.einsum(
        "shtu,suhp->sthp", mixing, inputs, preferred_element_type=jnp.float32
    )
    carried = (
        jnp.einsum("stn,shpn->sthp", c_matrix, initial_state, preferred_element_type=jnp.float32)
        * jnp.exp(-decay_sum)[:, :, :, None]
    )
    outputs = diagonal_part + carried
    final_decay = decay_sum[:, -1:, :]
    weighted = (
        b_matrix[:, :, None, :] * (jnp.exp(-(final_decay - decay_sum)) * step_sizes)[:, :, :, None]
    ).astype(jnp.bfloat16)
    new_state = (
        jnp.exp(-final_decay[:, 0, :])[:, :, None, None] * initial_state
        + jnp.einsum("suhp,suhn->shpn", inputs, weighted, preferred_element_type=jnp.float32)
    ).astype(jnp.bfloat16)
    flat_outputs = outputs.reshape(total_rows, local_heads * head_size)
    gated_values = flat_outputs * jax.nn.silu(gate_values.astype(jnp.float32))
    inverse_rms = lax.rsqrt(jnp.mean(gated_values * gated_values, axis=1, keepdims=True) + 1e-05)
    normed = (
        gated_values * inverse_rms * norm_gain[None, :] * valid_mask.reshape(total_rows, 1)
    ).astype(jnp.bfloat16)
    out_sum = lax.psum_scatter(
        jnp.dot(normed, out_weight, preferred_element_type=jnp.float32).astype(jnp.bfloat16),
        "mp",
        scatter_dimension=0,
        tiled=True,
    )
    outgoing = pack_rows(
        new_state.reshape(sessions_here, state_width), session_slot, slot_count
    ).reshape(shard_count, capacity, state_width)
    returned = lax.all_to_all(outgoing, "dp", split_axis=0, concat_axis=0, tiled=True).reshape(
        slot_count, state_width
    )
    new_store = jnp.take(returned, row_slot, axis=0)
    return (out_sum, new_store)


def solution(mesh):
    return jax.shard_map(
        body,
        mesh=mesh,
        in_specs=(
            P(("groups", "dp"), "mp"),
            P(None, "mp"),
            P(None, "mp"),
            P(None, "mp"),
            P(None, "mp"),
            P("mp"),
            P("mp"),
            P("mp"),
            P("mp", None),
            P(("groups", "dp"), "mp"),
            P("groups"),
            P(("groups", "dp")),
        ),
        out_specs=(P(("groups", "dp", "mp"), None), P(("groups", "dp"), "mp")),
        check_vma=False,
    )
```

profile of v0, /device:TPU:0, one launch (start us, length us, event | category | flops | bytes accessed | tf_op | source)
XLA Modules:
  0.0 219.1 jit_solution(15264939764608752194)
XLA Ops:
  7.2 0.0 copy-start
  7.2 0.0 all-gather.2.cloned.1.call-start
  7.2 0.7 all-gather.2.cloned.1.call-update
  7.9 0.8 select_reduce_fusion.2
  8.8 0.2 convert_reduce_fusion.1
  9.0 0.6 compare_and_fusion
  9.6 0.1 select_reduce_fusion.1
  9.7 0.4 copy-done.15
  10.1 0.1 fusion.23
  10.2 2.2 %gather_fusion = bf16[16,32768]{1,0:T(8,128)(2,1)} fusion(bf16[16,32768]{1,0:T(8,128)(2,1)S(1)} %copy-done.1, s32[1024]{0:T(1024)S(1)} %pad_clamp_fusion.3), kind=kCustom, calls=%fused_computation.clone | custom fusion | bytes 2097216 | tf_op jit(solution)/shard_map/jit(_take)/gather | solution.py:13
  12.5 1.4 select_select_fusion.1
  13.9 1.2 reshape.181
  15.1 6.3 %all-to-all-start = ((bf16[4,4,32768]{2,1,0:T(4,128)(2,1)}), bf16[4,4,32768]{2,1,0:T(4,128)(2,1)}, u32[]{:S(2)}, u32[]{:S(2)}) async-start(bf16[4,4,32768]{2,1,0:T(4,128)(2,1)} %reshape.181), calls=%async_computation | async-start | bytes 2097152 | tf_op jit(solution)/shard_map/all_to_all | solution.py:58
  21.4 0.1 and_select_fusion.1
  21.5 0.2 convert_reduce_fusion
  21.7 0.1 select_reduce_fusion
  21.9 0.6 pad_clamp_fusion.1
  22.5 0.7 fusion.22
  23.2 0.6 iota_compare_fusion
  23.8 0.5 compare_and_fusion.1
  24.3 0.7 fusion.27
  25.0 22.3 %all-to-all-done = bf16[4,4,32768]{2,1,0:T(4,128)(2,1)} async-done(((bf16[4,4,32768]{2,1,0:T(4,128)(2,1)}), bf16[4,4,32768]{2,1,0:T(4,128)(2,1)}, u32[]{:S(2)}, u32[]{:S(2)}) %all-to-all-start) | async-done | bytes 1048608 | tf_op jit(solution)/shard_map/all_to_all | solution.py:58
  47.2 1.4 reshape.182
  48.6 2.2 %gather_fusion.1 = bf16[16,32768]{1,0:T(8,128)(2,1)} fusion(bf16[16,32768]{1,0:T(8,128)(2,1)S(1)} %reshape.182, s32[1024]{0:T(1024)S(1)} %pad_clamp_fusion.2), kind=kCustom, calls=%fused_computation.1.clone | custom fusion | bytes 2097216 | tf_op jit(solution)/shard_map/jit(_take)/gather | solution.py:69
  50.8 1.4 broadcast_select_fusion.1
  52.2 3.3 %reshape.183 = bf16[16,8,64,64]{3,2,1,0:T(8,128)(2,1)} reshape(bf16[16,32768]{1,0:T(8,128)(2,1)S(1)} %broadcast_select_fusion.1) | data formatting | bytes 2097152 | tf_op jit(solution)/shard_map/reshape | solution.py:69
  55.5 15.1 %all-gather.2.cloned.1.call-done = bf16[2048,2048]{1,0:T(8,128)(2,1)} async-done(((bf16[2048,512]{1,0:T(8,128)(2,1)}), bf16[2048,2048]{1,0:T(8,128)(2,1)}) %all-gather.2.cloned.1.call-update) | async-done | bytes 8388624 | tf_op jit(solution)/shard_map/all_gather | solution.py:65
  70.6 5.7 %broadcast_multiply_fusion = (f32[16,128,8]{1,2,0:T(8,128)S(1)}, f32[16,128,8]{1,2,0:T(8,128)S(1)}) fusion(f32[8]{0:T(128)S(1)} %copy-done.10, f32[16,128]{1,0:T(8,128)S(1)} %get-tuple-element.12, f32[8]{0:T(128)S(1)} %copy-done.11, bf16[2048,2048]{1,0:T(8,128)(2,1)} %all-gather.2.cloned.1.call-done, bf16[2048,8]{0,1:T(8,128)(2,1)S(1)} %copy-done.7), kind=kOutput, calls=%fused_computation.47 | convolution fusion | flops 67256320 | bytes 8560704 | tf_op jit(solution)/shard_map/dot_general | solution.py:67
  76.3 1.4 copy.60
  77.7 1.4 fusion.31
  79.0 0.4 copy.71
  79.4 1.1 negate_exponential_fusion
  80.5 5.8 %convolution_convert_fusion.3 = bf16[2048,128]{1,0:T(8,128)(2,1)S(1)} fusion(bf16[2048,2048]{1,0:T(8,128)(2,1)} %all-gather.2.cloned.1.call-done, bf16[2048,128]{1,0:T(8,128)(2,1)} %param.17), kind=kOutput, calls=%fused_computation.26 | convolution fusion | flops 1074003968 | bytes 9437184 | tf_op jit(solution)/shard_map/dot_general | solution.py:67
  86.3 0.8 copy-done.3
  87.1 1.5 fusion.18
  88.6 1.2 copy.78
  89.9 0.9 convert_element_type.72
  90.7 0.1 copy.68
  90.8 0.4 copy.61
  91.2 1.6 copy.66
  92.8 9.8 %convolution_convert_fusion.2 = bf16[2048,512]{1,0:T(8,128)(2,1)} fusion(bf16[2048,2048]{1,0:T(8,128)(2,1)} %all-gather.2.cloned.1.call-done, bf16[2048,512]{1,0:T(8,128)(2,1)} %param.15), kind=kOutput, calls=%fused_computation.25 | convolution fusion | flops 4296015872 | bytes 12582912 | tf_op jit(solution)/shard_map/dot_general | solution.py:67
  102.6 6.2 %reshape.234 = bf16[16,128,8,64]{3,2,1,0:T(8,128)(2,1)} reshape(bf16[2048,512]{1,0:T(8,128)(2,1)} %convolution_convert_fusion.2) | data formatting | bytes 4194304 | tf_op jit(solution)/shard_map/reshape | solution.py:72
  108.8 5.2 %copy.65 = bf16[16,128,8,64]{1,3,2,0:T(8,128)(2,1)} copy(bf16[16,128,8,64]{3,2,1,0:T(8,128)(2,1)} %reshape.234) | data formatting | bytes 4194304 | tf_op jit(solution)/shard_map/reshape | solution.py:72
  114.0 6.8 %fusion = f32[16,8,64,128]{3,2,1,0:T(8,128)S(1)} fusion(bf16[16,128,8,64]{1,3,2,0:T(8,128)(2,1)} %copy.65, f32[16,128,128]{2,1,0:T(8,128)S(1)} %copy-done.5, f32[16,8,128]{2,1,0:T(8,128)S(1)} %bitcast.52, f32[16,8,128]{2,1,0:T(8,128)S(1)} %copy.61, pred[128,128]{1,0:T(8,128)(4,1)S(1)} %copy-done.8), kind=kOutput, calls=%fused_computation.8 | convolution fusion | flops 283115520 | bytes 7487488 | tf_op jit(solution)/shard_map/shtu,suhp->sthp/dot_general | solution.py:97
  120.8 0.9 bitcast_add_fusion
  121.7 0.0 copy-start.19
  121.7 2.4 %copy.67 = f32[16,128,8,64]{1,0,3,2:T(8,128)S(1)} copy(f32[16,128,8,64]{1,3,2,0:T(8,128)S(1)} %bitcast_add_fusion) | data formatting | bytes 8388608 | tf_op jit(solution)/shard_map/add | solution.py:104
  124.1 9.1 %multiply_reduce_fusion = (f32[2048]{0:T(1024)S(1)}, f32[2048,512]{0,1:T(8,128)S(1)}) fusion(bf16[2048,2048]{1,0:T(8,128)(2,1)} %all-gather.2.cloned.1.call-done, bf16[2048,512]{1,0:T(8,128)(2,1)S(1)} %copy-done.19, f32[64,8,16,128]{3,2,1,0:T(8,128)S(1)} %bitcast.51), kind=kOutput, calls=%fused_computation.17 | convolution fusion | flops 4304402432 | bytes 18882560 | tf_op jit(solution)/shard_map/dot_general | solution.py:67
  133.3 7.1 %convolution_convert_fusion = bf16[2048,2048]{1,0:T(8,128)(2,1)} fusion(bf16[512,2048]{1,0:T(8,128)(2,1)S(1)} %copy-done, f32[2048,512]{0,1:T(8,128)S(1)} %get-tuple-element.16, f32[2048]{0:T(1024)S(1)} %copy-done.9, f32[512]{0:T(512)S(1)} %copy-done.20, f32[2048]{0:T(1024)S(1)} %add_rsqrt_fusion), kind=kOutput, calls=%fused_computation.5 | convolution fusion | flops 4303355904 | bytes 14698496 | tf_op jit(solution)/shard_map/dot_general | solution.py:120
  140.3 0.0 reduce-scatter.2.cloned.1.call-update
  140.4 0.1 copy.69
  140.4 0.1 exponential_multiply_fusion
  140.5 0.8 copy-done.6
  141.4 4.8 %add_convert_fusion = bf16[16,8,64,64]{3,2,1,0:T(8,128)(2,1)} fusion(bf16[16,8,64,64]{3,2,1,0:T(8,128)(2,1)} %reshape.183, bf16[16,128,8,64]{1,3,2,0:T(8,128)(2,1)} %copy.65, f32[16,128,8]{1,2,0:T(8,128)S(1)} %exponential_multiply_fusion, f32[16,128,64]{1,2,0:T(8,128)S(1)} %copy-done.6, f32[16,8]{1,0:T(8,128)S(1)} %copy.69), kind=kOutput, calls=%fused_computation.14 | convolution fusion | flops 138412032 | bytes 4784640 | tf_op jit(solution)/shard_map/suhp,suhn->shpn/dot_general | solution.py:111
  146.1 2.9 %reshape.185 = bf16[16,32768]{1,0:T(8,128)(2,1)S(1)} reshape(bf16[16,8,64,64]{3,2,1,0:T(8,128)(2,1)} %add_convert_fusion) | data formatting | bytes 2097152 | tf_op jit(solution)/shard_map/reshape | solution.py:126
  149.1 2.3 %gather_fusion.2 = bf16[16,32768]{1,0:T(8,128)(2,1)} fusion(bf16[16,32768]{1,0:T(8,128)(2,1)S(1)} %reshape.185, s32[1024]{0:T(1024)} %pad_clamp_fusion.1), kind=kCustom, calls=%fused_computation.2.clone | custom fusion | bytes 2097216 | tf_op jit(solution)/shard_map/jit(_take)/gather | solution.py:13
  151.4 1.6 select_select_fusion
  153.1 1.2 reshape.186
  154.3 4.8 %all-to-all-start.1 = ((bf16[4,4,32768]{2,1,0:T(4,128)(2,1)}), bf16[4,4,32768]{2,1,0:T(4,128)(2,1)}, u32[]{:S(2)}, u32[]{:S(2)}) async-start(bf16[4,4,32768]{2,1,0:T(4,128)(2,1)} %reshape.186), calls=%async_computation.2 | async-start | bytes 2097152 | tf_op jit(solution)/shard_map/all_to_all | solution.py:128
  159.1 26.1 %all-to-all-done.1 = bf16[4,4,32768]{2,1,0:T(4,128)(2,1)} async-done(((bf16[4,4,32768]{2,1,0:T(4,128)(2,1)}), bf16[4,4,32768]{2,1,0:T(4,128)(2,1)}, u32[]{:S(2)}, u32[]{:S(2)}) %all-to-all-start.1) | async-done | bytes 1048608 | tf_op jit(solution)/shard_map/all_to_all | solution.py:128
  185.2 1.4 reshape.187
  186.6 2.2 %gather_fusion.3 = bf16[16,32768]{1,0:T(8,128)(2,1)} fusion(bf16[16,32768]{1,0:T(8,128)(2,1)S(1)} %reshape.187, s32[1024]{0:T(1024)S(1)} %pad_clamp_fusion), kind=kCustom, calls=%fused_computation.3.clone | custom fusion | bytes 2097216 | tf_op jit(solution)/shard_map/jit(_take)/gather | solution.py:131
  188.8 2.4 %broadcast_select_fusion = bf16[16,32768]{1,0:T(8,128)(2,1)} fusion(bf16[16,32768]{1,0:T(8,128)(2,1)} %gather_fusion.3, pred[16]{0:T(512)(128)(4,1)S(1)} %copy-done.12), kind=kLoop, calls=%fused_computation.37 | loop fusion | flops 524288 | bytes 2097168 | tf_op jit(solution)/shard_map/jit(_take)/select_n | solution.py:131
  191.2 21.1 %reduce-scatter.2.cloned.1.call-done = bf16[512,2048]{1,0:T(8,128)(2,1)} async-done(((bf16[2048,2048]{1,0:T(8,128)(2,1)}), bf16[512,2048]{1,0:T(8,128)(2,1)}) %reduce-scatter.2.cloned.1.call-update) | async-done | bytes 2097168 | tf_op jit(solution)/shard_map/reduce_scatter | solution.py:119
  (53 shorter events, 0.2 us)
Async XLA Ops:
  7.2 126.1 %copy-start = (bf16[512,2048]{1,0:T(8,128)(2,1)S(1)}, bf16[512,2048]{1,0:T(8,128)(2,1)}, u32[]{:S(2)}) copy-start(bf16[512,2048]{1,0:T(8,128)(2,1)} %param.22) | copy-start | bytes 6291460
  7.2 3.1 %copy-start.1 = (bf16[16,32768]{1,0:T(8,128)(2,1)S(1)}, bf16[16,32768]{1,0:T(8,128)(2,1)}, u32[]{:S(2)}) copy-start(bf16[16,32768]{1,0:T(8,128)(2,1)} %param.23) | copy-start | bytes 3145732
  7.2 63.4 %all-gather.2.cloned.1.call-start = ((), (), s32[]{:S(2)}) async-start(), calls=%async_computation.3 | async-start | bytes 10485760 | tf_op jit(solution)/shard_map/all_gather | solution.py:65
  9.6 0.5 copy-start.15
  12.5 9.0 %copy-start.14 = (s32[64]{0:T(128)S(1)}, s32[64]{0:T(128)}, u32[]{:S(2)}) copy-start(s32[64]{0:T(128)} %param.24) | copy-start | bytes 772
  12.5 11.8 %copy-start.13 = (s32[16]{0:T(128)S(1)}, s32[16]{0:T(128)}, u32[]{:S(2)}) copy-start(s32[16]{0:T(128)} %param.25) | copy-start | bytes 196
  15.1 32.1 %all-to-all-start = ((bf16[4,4,32768]{2,1,0:T(4,128)(2,1)}), bf16[4,4,32768]{2,1,0:T(4,128)(2,1)}, u32[]{:S(2)}, u32[]{:S(2)}) async-start(bf16[4,4,32768]{2,1,0:T(4,128)(2,1)} %reshape.181), calls=%async_computation | async-start | bytes 2097152 | tf_op jit(solution)/shard_map/all_to_all | solution.py:58
  21.4 190.9 %reduce-scatter.2.cloned.1.call-start = ((), (), s32[]{:S(2)}) async-start(), calls=%async_computation.4 | async-start | bytes 10485760 | tf_op jit(solution)/shard_map/reduce_scatter | solution.py:119
  50.8 19.8 %copy-start.7 = (bf16[2048,8]{0,1:T(8,128)(2,1)S(1)}, bf16[2048,8]{0,1:T(8,128)(2,1)}, u32[]{:S(2)}) copy-start(bf16[2048,8]{0,1:T(8,128)(2,1)} %param.18) | copy-start | bytes 98308
  50.8 19.8 %copy-start.10 = (f32[8]{0:T(128)S(1)}, f32[8]{0:T(128)}, u32[]{:S(2)}) copy-start(f32[8]{0:T(128)} %param.20) | copy-start | bytes 100
  50.8 19.8 %copy-start.11 = (f32[8]{0:T(128)S(1)}, f32[8]{0:T(128)}, u32[]{:S(2)}) copy-start(f32[8]{0:T(128)} %param.19) | copy-start | bytes 100
  86.3 0.8 copy-start.3
  108.8 5.2 %copy-start.5 = (f32[16,128,128]{2,1,0:T(8,128)S(1)}, f32[16,128,128]{2,1,0:T(8,128)}, u32[]{:S(2)}) copy-start(f32[16,128,128]{2,1,0:T(8,128)} %fusion.18) | copy-start | bytes 3145732
  108.8 5.2 %copy-start.8 = (pred[128,128]{1,0:T(8,128)(4,1)S(1)}, pred[128,128]{1,0:T(8,128)(4,1)}, u32[]{:S(2)}) copy-start(pred[128,128]{1,0:T(8,128)(4,1)} %iota_compare_fusion) | copy-start | bytes 49156
  114.0 6.8 %copy-start.2 = (bf16[16,8,64,64]{3,2,1,0:T(8,128)(2,1)S(1)}, bf16[16,8,64,64]{3,2,1,0:T(8,128)(2,1)}, u32[]{:S(2)}) copy-start(bf16[16,8,64,64]{3,2,1,0:T(8,128)(2,1)} %reshape.183) | copy-start | bytes 3145732
  114.0 6.8 %copy-start.4 = (bf16[2048,128]{1,0:T(8,128)(2,1)S(1)}, bf16[2048,128]{1,0:T(8,128)(2,1)}, u32[]{:S(2)}) copy-start(bf16[2048,128]{1,0:T(8,128)(2,1)} %copy-done.3) | copy-start | bytes 1572868
  121.7 2.4 %copy-start.19 = (bf16[2048,512]{1,0:T(8,128)(2,1)S(1)}, bf16[2048,512]{1,0:T(8,128)(2,1)}, u32[]{:S(2)}) copy-start(bf16[2048,512]{1,0:T(8,128)(2,1)} %param.16) | copy-start | bytes 6291460
  124.1 9.2 %copy-start.9 = (f32[2048]{0:T(1024)S(1)}, f32[2048]{0:T(1024)}, u32[]{:S(2)}) copy-start(f32[2048]{0:T(1024)} %get-tuple-element.11) | copy-start | bytes 24580
  124.1 9.2 %copy-start.20 = (f32[512]{0:T(512)S(1)}, f32[512]{0:T(512)}, u32[]{:S(2)}) copy-start(f32[512]{0:T(512)} %param.21) | copy-start | bytes 6148
  140.3 1.0 copy-start.6
  149.1 2.4 %copy-start.17 = (pred[16]{0:T(512)(128)(4,1)S(1)}, pred[16]{0:T(512)(128)(4,1)}, u32[]{:S(2)}) copy-start(pred[16]{0:T(512)(128)(4,1)} %fusion.22) | copy-start | bytes 52
  149.1 2.3 %copy-start.18 = (pred[16]{0:T(512)(128)(4,1)S(1)}, pred[16]{0:T(512)(128)(4,1)}, u32[]{:S(2)}) copy-start(pred[16]{0:T(512)(128)(4,1)} %compare_and_fusion.1) | copy-start | bytes 52
  151.4 7.6 %copy-start.16 = (s32[16]{0:T(128)S(1)}, s32[16]{0:T(128)}, u32[]{:S(2)}) copy-start(s32[16]{0:T(128)} %copy-done.15) | copy-start | bytes 196
  154.3 30.9 %all-to-all-start.1 = ((bf16[4,4,32768]{2,1,0:T(4,128)(2,1)}), bf16[4,4,32768]{2,1,0:T(4,128)(2,1)}, u32[]{:S(2)}, u32[]{:S(2)}) async-start(bf16[4,4,32768]{2,1,0:T(4,128)(2,1)} %reshape.186), calls=%async_computation.2 | async-start | bytes 2097152 | tf_op jit(solution)/shard_map/all_to_all | solution.py:128
  186.6 2.2 %copy-start.12 = (pred[16]{0:T(512)(128)(4,1)S(1)}, pred[16]{0:T(512)(128)(4,1)}, u32[]{:S(2)}) copy-start(pred[16]{0:T(512)(128)(4,1)} %get-tuple-element.3) | copy-start | bytes 52
Sparse Core Ops, SparseCore 0:
  9.6 60.9 all-gather.1
  140.5 71.7 reduce-scatter.1
where the time goes:
time: 220 us; the launch traced here: 219 us
  waiting for transfers between devices  85.3 us (39%)
  matrix products  51.3 us (23%)
  local copies, waits for them, and re-layouts  41.3 us (19%)
  other arithmetic  15.7 us (7%)
  between operations  14.3 us (6%)
  starting transfers between devices  11.1 us (5%)
    dot_general x4, matrix products, body(): jnp.dot(shard_cols, weight, preferred_element_type=jnp.float32)  30.4 us
    all_to_all x1, waiting for transfers between devices, body(): lax.all_to_all(outgoing, 'dp', split_axis=0, concat_axis=0, tiled=True)  26.1 us
    all_to_all x1, waiting for transfers between devices, body(): lax.all_to_all(outbound, 'dp', split_axis=0, concat_axis=0, tiled=True)  22.3 us
    reduce_scatter x1, waiting for transfers between devices, body(): lax.psum_scatter(jnp.dot(normed, out_weight, preferred_element_type=jnp.f...  21.1 us
    all_gather x1, waiting for transfers between devices, body(): shard_cols = lax.all_gather(tokens, 'mp', axis=1, tiled=True)  15.1 us
    reshape x2, local copies, waits for them, and re-layouts, body(): x_sum.astype(jnp.bfloat16)  11.4 us
    dot_general x1, matrix products, body(): jnp.dot(normed, out_weight, preferred_element_type=jnp.float32)  7.07 us
    dot_general x1, matrix products, body(): jnp.einsum('shtu,suhp->sthp', mixing, inputs, preferred_element_type=jnp....  6.77 us
  transfers between devices with their start and end apart: 4, of which 4 were waited for; matrix products, arithmetic and copies ran while one was open for 17% of the time, Pallas kernels for 0%

commit v1 on v0

v1 whole, which is shorter than its diff:
```python
import functools

import jax
import jax.numpy as jnp
from jax import lax
from jax.experimental import pallas as pl
from jax.experimental.pallas import tpu as pltpu
from jax.sharding import PartitionSpec as P

BF = jnp.bfloat16
F32 = jnp.float32


def pack_rows(values, wanted, slot_count):
    slots = jnp.arange(slot_count, dtype=jnp.int32)
    chosen = wanted[None, :] == slots[:, None]
    places = jnp.arange(wanted.shape[0], dtype=jnp.int32)
    source = jnp.sum(chosen.astype(jnp.int32) * places[None, :], axis=1)
    return jnp.take(values, source, axis=0)


def rank_within(keys, order):
    earlier = (keys[None, :] == keys[:, None]) & (order[None, :] < order[:, None])
    return jnp.sum(earlier.astype(jnp.int32), axis=1)


def layer_kernel(
    heads, span, me_ref, slot_ref, count_ref, t0, t1, t2, t3, xw, zw, bw, bias, rate, gain, states,
    n0, n1, n2, n3, new_states, xs, zs, bcs,
):
    me = me_ref[0]
    pieces = (t0, t1, t2, t3)
    normed_out = (n0, n1, n2, n3)
    depth = t0.shape[1]
    quads = heads // 4

    def project(weight, columns):
        total = None
        for distance in range(4):
            first = pl.multiple_of((me ^ distance) * depth, depth)
            part = jnp.dot(
                pieces[distance][...],
                weight[pl.ds(first, depth), columns],
                preferred_element_type=F32,
            )
            total = part if total is None else total + part
        return total

    bcs[...] = project(bw, slice(None))
    for quad in range(quads):
        columns = slice(quad * 256, quad * 256 + 256)
        xs[:, columns] = project(xw, columns).astype(BF)
        zs[:, columns] = project(zw, columns).astype(BF)

    lane = lax.broadcasted_iota(jnp.int32, (span, 128), 1)
    row = lax.broadcasted_iota(jnp.int32, (span, 128), 0)
    low = lane < 64
    causal = row >= lane
    lane8 = lax.broadcasted_iota(jnp.int32, (heads, span), 1)
    head_mask = [((lane // 32) == k).astype(F32).astype(BF) for k in range(4)]
    head_masks = [jnp.concatenate([m, m], axis=1) for m in head_mask]

    for distance in range(4):
        place = me ^ distance
        first = pl.multiple_of(place * span, span)
        rows = pl.ds(first, span)
        count = count_ref[place]
        bc = bcs[rows, 0:128]
        turned = pltpu.roll(bc, 64, 1)
        bc_low = jnp.where(low, bc, 0.0).astype(BF)
        bc_high = jnp.where(low, 0.0, turned).astype(BF)
        c_low = jnp.where(low, turned, 0.0).astype(BF)
        c_high = jnp.where(low, 0.0, bc).astype(BF)
        scores = lax.dot_general(
            c_low, bc_low, (((1,), (1,)), ((), ())), preferred_element_type=F32
        )
        scores = jnp.where(causal, scores, 0.0)
        raw = jnp.transpose(bcs[rows, 128:256])[:heads] + bias[...]
        soft = jnp.maximum(raw, 0.0) + jnp.log1p(jnp.exp(-jnp.abs(raw)))
        step = jnp.where(lane8 < count, soft, 0.0)
        total = step * rate[...]
        shift = 1
        while shift < span:
            total = total + jnp.where(lane8 >= shift, pltpu.roll(total, shift, 1), 0.0)
            shift *= 2
        last = total[:, span - 1 : span]
        weights = jnp.exp(jnp.minimum(total - last, 0.0)) * step
        kept = jnp.exp(-last)
        cum = jnp.transpose(jnp.concatenate([total, jnp.zeros((128 - heads, span), F32)], axis=0))
        state = states[slot_ref[place]]
        carried = lax.dot_general(
            jnp.concatenate([c_low, c_high], axis=0),
            state,
            (((1,), (1,)), ((), ())),
            preferred_element_type=F32,
        )
        b_both = jnp.concatenate([bc_low, bc_high], axis=0)
        gated = []
        squares = None
        for quad in range(quads):
            columns = slice(quad * 256, quad * 256 + 256)
            x = xs[rows, columns]
            mixes = []
            blocks = []
            spread = None
            for k in range(4):
                head = quad * 4 + k
                level = jnp.broadcast_to(cum[:, head : head + 1], (span, 128))
                gap = jnp.minimum(total[head : head + 1, :] - level, 0.0)
                mixes.append((jnp.exp(gap) * step[head : head + 1, :] * scores).astype(BF))
                blocks.append(x * head_masks[k])
                spread = level if spread is None else jnp.where(lane >= 32 * k, level, spread)
            diagonal = jnp.dot(
                jnp.concatenate(mixes, axis=1),
                jnp.concatenate(blocks, axis=0),
                preferred_element_type=F32,
            )
            fade = jnp.exp(-spread)
            part = slice(quad * 128, quad * 128 + 128)
            before = jnp.concatenate(
                [carried[:span, part] * fade, carried[span:, part] * fade], axis=1
            )
            gate = zs[rows, columns].astype(F32)
            value = (diagonal + before) * (gate / (1.0 + jnp.exp(-gate)))
            gated.append(value)
            own = jnp.sum(value * value, axis=1, keepdims=True)
            squares = own if squares is None else squares + own
            weight_rows = jnp.concatenate(
                [
                    jnp.broadcast_to(weights[quad * 4 + k : quad * 4 + k + 1, :], (32, span))
                    for k in range(4)
                ],
                axis=0,
            )
            xf = x.astype(F32)
            even = (jnp.transpose(xf[:, :128]) * weight_rows).astype(BF)
            odd = (jnp.transpose(xf[:, 128:]) * weight_rows).astype(BF)
            added = jnp.dot(
                jnp.concatenate([even, odd], axis=1), b_both, preferred_element_type=F32
            )
            keep_rows = jnp.concatenate(
                [
                    jnp.broadcast_to(kept[quad * 4 + k : quad * 4 + k + 1, :], (32, 128))
                    for k in range(4)
                ],
                axis=0,
            )
            new_states[place, quad * 128 : quad * 128 + 128, :] = (
                keep_rows * state[quad * 128 : quad * 128 + 128].astype(F32) + added
            ).astype(BF)
        inverse = lax.rsqrt(squares * (1.0 / (heads * 64)) + 1e-05)
        inverse = jnp.where(row[:, :1] < count, inverse, 0.0)
        for quad in range(quads):
            columns = slice(quad * 256, quad * 256 + 256)
            normed_out[distance][:, columns] = (
                gated[quad] * inverse * gain[:, columns]
            ).astype(BF)


def layer_call(me, slots, counts, pieces, weights, small, states):
    rows, depth = pieces[0].shape
    heads = small[0].shape[0]
    width = weights[0].shape[1]
    span = rows // 4
    vmem = pl.BlockSpec(memory_space=pltpu.VMEM)
    smem = pl.BlockSpec(memory_space=pltpu.SMEM)
    return pl.pallas_call(
        functools.partial(layer_kernel, heads, span),
        out_shape=[jax.ShapeDtypeStruct((span, width), BF)] * 4
        + [jax.ShapeDtypeStruct((4,) + states.shape[1:], BF)],
        in_specs=[smem] * 3 + [vmem] * 11,
        out_specs=[vmem] * 5,
        scratch_shapes=[
            pltpu.VMEM((rows, width), BF),
            pltpu.VMEM((rows, width), BF),
            pltpu.VMEM((rows, weights[2].shape[1]), F32),
        ],
        compiler_params=pltpu.CompilerParams(vmem_limit_bytes=40 * 2**20),
        cost_estimate=pl.CostEstimate(
            flops=2 * rows * depth * 4 * 1280, bytes_accessed=9 * 2**20, transcendentals=0
        ),
        name="layer",
    )(me, slots, counts, *pieces, *weights, *small, states)


def out_kernel(chunks, *refs):
    weights = refs[chunks * 4 : chunks * 4 + 4]
    out = refs[-1]
    span = refs[0].shape[0]
    for chunk in range(chunks):
        total = None
        for distance in range(4):
            part = jnp.dot(
                refs[chunk * 4 + distance][...],
                weights[distance][...],
                preferred_element_type=F32,
            )
            total = part if total is None else total + part
        out[chunk * span : (chunk + 1) * span, :] = total.astype(BF)


def out_call(normed, weights):
    chunks = len(normed)
    span, depth = normed[0][0].shape
    columns = weights[0].shape[1]
    block = 512
    return pl.pallas_call(
        functools.partial(out_kernel, chunks),
        grid=(columns // block,),
        out_shape=jax.ShapeDtypeStruct((chunks * span, columns), BF),
        in_specs=[pl.BlockSpec((span, depth), lambda j: (0, 0))] * (chunks * 4)
        + [pl.BlockSpec((depth, block), lambda j: (0, j))] * 4,
        out_specs=pl.BlockSpec((chunks * span, block), lambda j: (0, j)),
        compiler_params=pltpu.CompilerParams(vmem_limit_bytes=32 * 2**20),
        cost_estimate=pl.CostEstimate(
            flops=2 * chunks * span * depth * 4 * columns,
            bytes_accessed=12 * 2**20,
            transcendentals=0,
        ),
        name="project_out",
    )(*[piece for chunk in normed for piece in chunk], *weights)


def body(
    tokens,
    x_weight,
    z_weight,
    bc_weight,
    dt_weight,
    dt_bias,
    decay_rate,
    norm_gain,
    out_weight,
    store_states,
    home_rows,
    event_counts,
):
    shard_count = lax.axis_size("dp")
    model_shards = lax.axis_size("mp")
    store_index = lax.axis_index("dp")
    me = lax.axis_index("mp")
    sessions_here, state_width = store_states.shape
    capacity = max(2, (sessions_here + shard_count - 1) // shard_count)
    slot_count = shard_count * capacity
    heads = dt_bias.shape[0]
    width = x_weight.shape[1]
    depth = tokens.shape[1]
    span = tokens.shape[0] // sessions_here
    chunks = sessions_here // model_shards

    def exchange(value, distance):
        pairs = [(j, j ^ distance) for j in range(model_shards)]
        return lax.ppermute(value, "mp", pairs)

    by_chunk = tokens.reshape(model_shards, chunks, span, depth)
    own = [by_chunk[:, c].reshape(model_shards * span, depth) for c in range(chunks)]
    across = [exchange(own[c], 2) for c in range(chunks)]
    sibling = [exchange(own[c], 1) for c in range(chunks)]
    far = [exchange(across[c], 1) for c in range(chunks)]

    positions = jnp.arange(sessions_here, dtype=jnp.int32)
    store_rows = store_index * sessions_here + positions
    everyone = jnp.arange(home_rows.shape[0], dtype=jnp.int32)
    owner = jnp.sum(
        (home_rows[None, :] == store_rows[:, None]).astype(jnp.int32) * everyone[None, :], axis=1
    )
    server = owner // sessions_here
    row_slot = server * capacity + rank_within(server, positions)
    outbound = pack_rows(store_states, row_slot, slot_count).reshape(
        shard_count, capacity, state_width // 128, 128
    )
    inbound = lax.all_to_all(outbound, "dp", split_axis=0, concat_axis=0, tiled=True).reshape(
        slot_count, state_width // 128, 128
    )
    wanted = lax.dynamic_slice_in_dim(home_rows, store_index * sessions_here, sessions_here)
    home_shard = wanted // sessions_here
    session_slot = home_shard * capacity + rank_within(home_shard, wanted % sessions_here)

    new_column = jnp.arange(width, dtype=jnp.int32)
    quad, parity, k, pair = (
        new_column // 256,
        (new_column // 128) % 2,
        (new_column // 32) % 4,
        new_column % 32,
    )
    old_column = (quad * 4 + k) * 64 + pair * 2 + parity
    order = (old_column[None, :] == jnp.arange(width, dtype=jnp.int32)[:, None]).astype(BF)
    xw = jnp.dot(x_weight, order, preferred_element_type=F32).astype(BF)
    zw = jnp.dot(z_weight, order, preferred_element_type=F32).astype(BF)
    ow = jnp.dot(order.T, out_weight, preferred_element_type=F32).astype(BF)
    bw = jnp.concatenate(
        [bc_weight, dt_weight, jnp.zeros((bc_weight.shape[0], 128 - heads), BF)], axis=1
    )
    gain = (
        norm_gain.reshape(heads // 4, 4, 32, 2).transpose(0, 3, 1, 2).reshape(1, width)
    )

    replicas = lax.axis_size("groups") * shard_count
    replica = lax.axis_index("groups") * shard_count + store_index
    share = width // replicas
    ow_part = exchange(lax.dynamic_slice_in_dim(ow, replica * share, share), 2)
    ow_across = lax.all_gather(ow_part, ("groups", "dp"), axis=0, tiled=True)
    ow_sibling = exchange(ow, 1)
    ow_far = exchange(ow_across, 1)

    small = (dt_bias.reshape(heads, 1), decay_rate.reshape(heads, 1), gain)
    slots = session_slot.reshape(model_shards, chunks)
    counts = event_counts.reshape(model_shards, chunks)
    mine = me.reshape(1).astype(jnp.int32)
    normed = []
    states = []
    for c in range(chunks):
        *parts, new_states = layer_call(
            mine,
            slots[:, c],
            counts[:, c],
            (own[c], sibling[c], across[c], far[c]),
            (xw, zw, bw),
            small,
            inbound,
        )
        normed.append([parts[0]] + [exchange(parts[d], d) for d in range(1, 4)])
        states.append(new_states)
    new_state = jnp.stack(states, axis=1).reshape(sessions_here, state_width // 128, 128)
    outgoing = pack_rows(new_state, session_slot, slot_count).reshape(
        shard_count, capacity, state_width // 128, 128
    )
    returned = lax.all_to_all(outgoing, "dp", split_axis=0, concat_axis=0, tiled=True).reshape(
        slot_count, state_width // 128, 128
    )
    new_store = jnp.take(returned, row_slot, axis=0).reshape(sessions_here, state_width)
    out_tokens = out_call(normed, (ow, ow_sibling, ow_across, ow_far))
    return (out_tokens, new_store)


def solution(mesh):
    return jax.shard_map(
        body,
        mesh=mesh,
        in_specs=(
            P(("groups", "dp"), "mp"),
            P(None, "mp"),
            P(None, "mp"),
            P(None, "mp"),
            P(None, "mp"),
            P("mp"),
            P("mp"),
            P("mp"),
            P("mp", None),
            P(("groups", "dp"), "mp"),
            P("groups"),
            P(("groups", "dp")),
        ),
        out_specs=(P(("groups", "dp", "mp"), None), P(("groups", "dp"), "mp")),
        check_vma=False,
    )
```

time: 220 us -> 170 us (0.77)
  matrix products: 51.3 us -> 7.97 us
  waiting for transfers between devices: 85.3 us -> 45.4 us
  Pallas kernels: 0 us -> 37.4 us
  starting transfers between devices: 11.1 us -> 28.1 us
  local copies, waits for them, and re-layouts: 41.3 us -> 28.2 us
  other arithmetic: 15.7 us -> 7.7 us
    dot_general x9 -> x3, matrix products: 51.3 us -> 7.97 us  [the longest x1 2.69 us: body(): zw = jnp.dot(z_weight, order, preferred_element_type=F32).astype(BF)]
    pallas_call x0 -> x5, Pallas kernels: none -> 37.4 us  [the longest x4 29.7 us: layer_call(): pl.pallas_call(functools.partial(layer_kernel, heads, span), out_shape=[j...]
    ppermute x0 -> x27, waiting for transfers between devices: none -> 35.1 us  [exchange(): return lax.ppermute(value, 'mp', pairs)]
    all_to_all x1, waiting for transfers between devices: 22.3 us -> 0.01 us  [body(): lax.all_to_all(outbound, 'dp', split_axis=0, concat_axis=0, tiled=True)]
    reshape x8 -> x6, local copies, waits for them, and re-layouts: 22.7 us -> 0.55 us  [the longest x2 0.22 us: body(): norm_gain.reshape(heads // 4, 4, 32, 2).transpose(0, 3, 1, 2)]
    reduce_scatter x1 -> x0, waiting for transfers between devices: 21.1 us -> none  [body(): lax.psum_scatter(jnp.dot(normed, out_weight, preferred_element_type=jnp.f...]
    ppermute x0 -> x27, starting transfers between devices: none -> 18.2 us  [exchange(): return lax.ppermute(value, 'mp', pairs)]
    all_to_all x1, waiting for transfers between devices: 26.1 us -> 10.3 us  [body(): lax.all_to_all(outgoing, 'dp', split_axis=0, concat_axis=0, tiled=True)]
  transfers between devices with their start and end apart: 4 -> 30, of which waited for: 4 -> 9; matrix products, arithmetic and copies ran while one was open for 17% -> 17% of each run, Pallas kernels for 0% -> 18%
where the time goes in v1:
time: 170 us; the launch traced here: 169 us
  waiting for transfers between devices  45.4 us (27%)
  Pallas kernels  37.4 us (22%)
  local copies, waits for them, and re-layouts  28.2 us (17%)
  starting transfers between devices  28.1 us (17%)
  between operations  14.4 us (8%)
  matrix products  7.97 us (5%)
  other arithmetic  7.7 us (5%)
    ppermute x27, waiting for transfers between devices, exchange(): return lax.ppermute(value, 'mp', pairs)  35.1 us
    pallas_call x4, Pallas kernels, layer_call(): pl.pallas_call(functools.partial(layer_kernel, heads, span), out_shape=[j...  29.7 us
    ppermute x27, starting transfers between devices, exchange(): return lax.ppermute(value, 'mp', pairs)  18.2 us
    unnamed x91, local copies, waits for them, and re-layouts  16.3 us
    all_to_all x1, waiting for transfers between devices, body(): lax.all_to_all(outgoing, 'dp', split_axis=0, concat_axis=0, tiled=True)  10.3 us
    pallas_call x1, Pallas kernels, out_call(): pl.pallas_call(functools.partial(out_kernel, chunks), grid=(columns // bl...  7.7 us
    all_to_all x1, starting transfers between devices, body(): lax.all_to_all(outgoing, 'dp', split_axis=0, concat_axis=0, tiled=True)  5.04 us
    all_to_all x1, starting transfers between devices, body(): lax.all_to_all(outbound, 'dp', split_axis=0, concat_axis=0, tiled=True)  4.87 us
  transfers between devices with their start and end apart: 30, of which 9 were waited for; matrix products, arithmetic and copies ran while one was open for 17% of the time, Pallas kernels for 18%

profile of v1, /device:TPU:0, one launch (start us, length us, event | category | flops | bytes accessed | tf_op | source)
XLA Modules:
  0.0 169.2 jit_solution(10531680472437112438)
XLA Ops:
  7.2 3.1 %fusion.25 = (bf16[4,1,128,512]{3,2,1,0:T(8,128)(2,1)}, bf16[4,1,128,512]{3,2,1,0:T(8,128)(2,1)}, bf16[4,1,128,512]{3,2,1,0:T(8,128)(2,1)}, bf16[4,1,128,512]{3,2,1,0:T(8,128)(2,1)}) fusion(bf16[4,4,128,512]{3,2,1,0:T(8,128)(2,1)} %bitcast.52), kind=kLoop, calls=%fused_computation.93 | loop fusion | bytes 4194304 | tf_op jit(solution)/shard_map/slice | solution.py:256
  10.2 2.9 %collective-permute-start.19 = (bf16[512,512]{1,0:T(8,128)(2,1)}, bf16[512,512]{1,0:T(8,128)(2,1)}, u32[]{:S(2)}, u32[]{:S(2)}) collective-permute-start(bf16[512,512]{1,0:T(8,128)(2,1)} %bitcast.13.t0), channel_id=1, source_target_pairs={{0,2},{1,3},{2,0},{3,1},{4,6},{5,7},{6,4},{7,5},{8,10},{9,11},{10,... | collective-permute-start | bytes 1572872 | tf_op jit(solution)/shard_map/ppermute | solution.py:253
  13.3 0.4 collective-permute-start.12
  13.7 2.6 %convolution_convert_fusion.refs_16_ = bf16[512,2048]{1,0:T(8,128)(2,1)} fusion(bf16[512,2048]{1,0:T(8,128)(2,1)S(1)} %copy-done, s32[512]{0:T(512)S(1)} %fusion.14), kind=kOutput, calls=%fused_computation.3 | convolution fusion | flops 1075052544 | bytes 4196352 | tf_op jit(solution)/shard_map/dot_general | solution.py:290
  16.4 1.0 constant_dynamic-slice_fusion
  17.3 1.8 %collective-permute-start.25 = (bf16[64,2048]{1,0:T(8,128)(2,1)S(1)}, bf16[64,2048]{1,0:T(8,128)(2,1)}, u32[]{:S(2)}, u32[]{:S(2)}) collective-permute-start(bf16[64,2048]{1,0:T(8,128)(2,1)S(1)} %constant_dynamic-slice_fusion), channel_id=1, source_target_pairs={{0,2},{1,3},{2,0},{3,1},{4,6},{5,7},{6,4},{7,5},{8,10},{9,11},{10,... | collective-permute-start | bytes 786440 | tf_op jit(solution)/shard_map/ppermute | solution.py:253
  19.8 2.2 %gather_fusion = bf16[16,32768]{1,0:T(8,128)(2,1)} fusion(bf16[16,32768]{1,0:T(8,128)(2,1)S(1)} %copy-done.35, s32[1024]{0:T(1024)S(1)} %pad_clamp_fusion.2), kind=kCustom, calls=%fused_computation.2 | custom fusion | bytes 2097216 | tf_op jit(solution)/shard_map/jit(_take)/gather | solution.py:19
  22.0 1.4 copy.69
  23.4 1.1 broadcast_select_fusion.2
  24.6 4.9 %all-to-all-start = ((bf16[4,4,256,128]{3,2,1,0:T(8,128)(2,1)}), bf16[4,4,256,128]{3,2,1,0:T(8,128)(2,1)}, u32[]{:S(2)}, u32[]{:S(2)}) async-start(bf16[4,4,256,128]{3,2,1,0:T(8,128)(2,1)} %broadcast_select_fusion.2), calls=%async_computation | async-start | bytes 2097152 | tf_op jit(solution)/shard_map/all_to_all | solution.py:272
  29.4 12.8 %collective-permute-done.25 = bf16[64,2048]{1,0:T(8,128)(2,1)} collective-permute-done((bf16[64,2048]{1,0:T(8,128)(2,1)S(1)}, bf16[64,2048]{1,0:T(8,128)(2,1)}, u32[]{:S(2)}, u32[]{:S(2)}) %collective-permute-start.25) | collective-permute-done | bytes 262176 | tf_op jit(solution)/shard_map/ppermute | solution.py:253
  42.3 1.7 %collective-permute-start.7 = (bf16[512,512]{1,0:T(8,128)(2,1)}, bf16[512,512]{1,0:T(8,128)(2,1)}, u32[]{:S(2)}, u32[]{:S(2)}) collective-permute-start(bf16[512,512]{1,0:T(8,128)(2,1)} %bitcast.11.t0), channel_id=1, source_target_pairs={{0,2},{1,3},{2,0},{3,1},{4,6},{5,7},{6,4},{7,5},{8,10},{9,11},{10,... | collective-permute-start | bytes 1572872 | tf_op jit(solution)/shard_map/ppermute | solution.py:253
  44.1 1.0 copy.49
  45.4 1.6 maximum_maximum_fusion.bw
  47.0 2.6 %fusion.xw = bf16[2048,512]{1,0:T(8,128)(2,1)} fusion(bf16[2048,512]{1,0:T(8,128)(2,1)S(1)} %copy-done.42, s32[512]{0:T(512)S(1)} %fusion.14), kind=kOutput, calls=%fused_computation.6 | convolution fusion | flops 1075052544 | bytes 4196352 | tf_op jit(solution)/shard_map/dot_general | solution.py:288
  49.9 2.7 %fusion.1.zw = bf16[2048,512]{1,0:T(8,128)(2,1)} fusion(bf16[2048,512]{1,0:T(8,128)(2,1)S(1)} %copy-done.43, s32[512]{0:T(512)S(1)} %fusion.14), kind=kOutput, calls=%fused_computation.7 | convolution fusion | flops 1075052544 | bytes 4196352 | tf_op jit(solution)/shard_map/dot_general | solution.py:289
  52.9 0.5 collective-permute-start.14
  53.5 0.3 slice_reduce_fusion
  54.0 3.2 %collective-permute-done.7.t2 = bf16[512,512]{1,0:T(8,128)(2,1)} collective-permute-done((bf16[512,512]{1,0:T(8,128)(2,1)}, bf16[512,512]{1,0:T(8,128)(2,1)}, u32[]{:S(2)}, u32[]{:S(2)}) %collective-permute-start.7) | collective-permute-done | bytes 524320 | tf_op jit(solution)/shard_map/ppermute | solution.py:253
  57.7 9.2 %collective-permute-done.1.t2 = bf16[512,512]{1,0:T(8,128)(2,1)} collective-permute-done((bf16[512,512]{1,0:T(8,128)(2,1)}, bf16[512,512]{1,0:T(8,128)(2,1)}, u32[]{:S(2)}, u32[]{:S(2)}) %collective-permute-start.1) | collective-permute-done | bytes 524320 | tf_op jit(solution)/shard_map/ppermute | solution.py:253
  66.9 0.5 collective-permute-start.2
  67.5 1.6 copy-done.24
  69.0 1.6 copy-done.26
  70.6 7.9 %layer.7 = (bf16[128,512]{1,0:T(8,128)(2,1)S(1)}, bf16[128,512]{1,0:T(8,128)(2,1)}, bf16[128,512]{1,0:T(8,128)(2,1)S(1)}, bf16[128,512]{1,0:T(8,128)(2,1)S(1)}, bf16[4,256,128]{2,1,0:T(8,128)(2,1)S(1)}) custom-call(s32[1]{0:T(128)} %bitcast.me_ref, s32[4]{0:T(128)S(1)} %get-tuple-element.62.slot_ref, s32[4]{0:T(128)S(1)} %get-tuple-element.43.count_ref, ...), custom_call_target="tpu_custom_call" | custom-call | flops 2684354560 | bytes 9437184 | tf_op jit(solution)/shard_map/layer/pallas_call | solution.py:167
  78.6 0.6 copy-done.12
  79.2 0.6 copy-done.18
  79.9 0.7 copy-done.27
  80.7 7.4 %layer.6 = (bf16[128,512]{1,0:T(8,128)(2,1)S(1)}, bf16[128,512]{1,0:T(8,128)(2,1)S(1)}, bf16[128,512]{1,0:T(8,128)(2,1)S(1)}, bf16[128,512]{1,0:T(8,128)(2,1)S(1)}, bf16[4,256,128]{2,1,0:T(8,128)(2,1)S(1)}) custom-call(s32[1]{0:T(128)} %bitcast.me_ref, s32[4]{0:T(128)S(1)} %get-tuple-element.61.slot_ref, s32[4]{0:T(128)S(1)} %get-tuple-element.44.count_ref, ...), custom_call_target="tpu_custom_call" | custom-call | flops 2684354560 | bytes 9437184 | tf_op jit(solution)/shard_map/layer/pallas_call | solution.py:167
  88.1 0.6 copy-done.10
  88.7 0.6 copy-done.14
  89.4 0.6 copy-done.19
  90.0 0.6 copy-done.29
  90.7 7.2 %layer.5 = (bf16[128,512]{1,0:T(8,128)(2,1)S(1)}, bf16[128,512]{1,0:T(8,128)(2,1)S(1)}, bf16[128,512]{1,0:T(8,128)(2,1)S(1)}, bf16[128,512]{1,0:T(8,128)(2,1)S(1)}, bf16[4,256,128]{2,1,0:T(8,128)(2,1)S(1)}) custom-call(s32[1]{0:T(128)} %bitcast.me_ref, s32[4]{0:T(128)S(1)} %get-tuple-element.60.slot_ref, s32[4]{0:T(128)S(1)} %get-tuple-element.45.count_ref, ...), custom_call_target="tpu_custom_call" | custom-call | flops 2684354560 | bytes 9437184 | tf_op jit(solution)/shard_map/layer/pallas_call | solution.py:167
  97.9 0.6 copy-done.6
  98.5 0.6 copy-done.8
  99.1 0.6 copy-done.31
  99.8 7.2 %layer.4 = (bf16[128,512]{1,0:T(8,128)(2,1)S(1)}, bf16[128,512]{1,0:T(8,128)(2,1)S(1)}, bf16[128,512]{1,0:T(8,128)(2,1)S(1)}, bf16[128,512]{1,0:T(8,128)(2,1)S(1)}, bf16[4,256,128]{2,1,0:T(8,128)(2,1)S(1)}) custom-call(s32[1]{0:T(128)} %bitcast.me_ref, s32[4]{0:T(128)S(1)} %get-tuple-element.59.slot_ref, s32[4]{0:T(128)S(1)} %get-tuple-element.46.count_ref, ...), custom_call_target="tpu_custom_call" | custom-call | flops 2684354560 | bytes 9437184 | tf_op jit(solution)/shard_map/layer/pallas_call | solution.py:167
  107.2 0.4 copy-done.2
  107.7 1.6 gather_fusion.1
  109.4 0.4 collective-permute-start.26
  109.8 2.4 %broadcast_select_fusion.1 = bf16[16,256,128]{2,1,0:T(8,128)(2,1)} fusion(bf16[16,256,128]{2,1,0:T(8,128)(2,1)} %gather_fusion.1, pred[16]{0:T(512)(128)(4,1)S(1)} %compare_and_fusion.1), kind=kLoop, calls=%fused_computation.13 | loop fusion | flops 524288 | bytes 2097168 | tf_op jit(solution)/shard_map/jit(_take)/select_n | solution.py:19
  112.2 5.0 %all-to-all-start.1 = ((bf16[4,4,256,128]{3,2,1,0:T(8,128)(2,1)}), bf16[4,4,256,128]{3,2,1,0:T(8,128)(2,1)}, u32[]{:S(2)}, u32[]{:S(2)}) async-start(bf16[4,4,256,128]{3,2,1,0:T(8,128)(2,1)} %bitcast.48), calls=%async_computation.1 | async-start | bytes 2097152 | tf_op jit(solution)/shard_map/all_to_all | solution.py:328
  117.2 1.5 collective-permute-start.22
  118.7 0.4 collective-permute-start.23
  119.4 4.4 %collective-permute-done.22.refs_14_ = bf16[128,512]{1,0:T(8,128)(2,1)S(1)} collective-permute-done((bf16[128,512]{1,0:T(8,128)(2,1)}, bf16[128,512]{1,0:T(8,128)(2,1)S(1)}, u32[]{:S(2)}, u32[]{:S(2)}) %collective-permute-start.22) | collective-permute-done | bytes 131104 | tf_op jit(solution)/shard_map/ppermute | solution.py:253
  123.7 1.5 collective-permute-start.16
  125.2 0.5 collective-permute-done.23.refs_15_
  125.8 0.6 copy-done.16
  126.4 2.0 %collective-permute-start.17 = (bf16[128,512]{1,0:T(8,128)(2,1)S(1)}, bf16[128,512]{1,0:T(8,128)(2,1)S(1)}, u32[]{:S(2)}, u32[]{:S(2)}) collective-permute-start(bf16[128,512]{1,0:T(8,128)(2,1)S(1)} %copy-done.11), channel_id=1, source_target_pairs={{0,3},{1,2},{2,1},{3,0},{4,7},{5,6},{6,5},{7,4},{8,11},{9,10},{10,... | collective-permute-start | bytes 393224 | tf_op jit(solution)/shard_map/ppermute | solution.py:253
  128.4 0.7 copy-done.20
  129.1 0.5 collective-permute-start.10
  129.6 0.6 copy-done.22
  130.3 0.3 collective-permute-start.11
  130.6 1.7 %collective-permute-done.17.refs_11_ = bf16[128,512]{1,0:T(8,128)(2,1)S(1)} collective-permute-done((bf16[128,512]{1,0:T(8,128)(2,1)S(1)}, bf16[128,512]{1,0:T(8,128)(2,1)S(1)}, u32[]{:S(2)}, u32[]{:S(2)}) %collective-permute-start.17) | collective-permute-done | bytes 131104 | tf_op jit(solution)/shard_map/ppermute | solution.py:253
  132.3 0.8 collective-permute-start.9
  133.1 10.3 %all-to-all-done.1 = bf16[4,4,256,128]{3,2,1,0:T(8,128)(2,1)} async-done(((bf16[4,4,256,128]{3,2,1,0:T(8,128)(2,1)}), bf16[4,4,256,128]{3,2,1,0:T(8,128)(2,1)}, u32[]{:S(2)}, u32[]{:S(2)}) %all-to-all-start.1) | async-done | bytes 1048608 | tf_op jit(solution)/shard_map/all_to_all | solution.py:328
  143.4 2.9 %gather_fusion.2 = bf16[16,256,128]{2,1,0:T(8,128)(2,1)} fusion(bf16[16,256,128]{2,1,0:T(8,128)(2,1)} %bitcast.20, s32[1024]{0:T(1024)S(1)} %pad_clamp_fusion), kind=kCustom, calls=%fused_computation.1.clone | custom fusion | bytes 2097216 | tf_op jit(solution)/shard_map/jit(_take)/gather | solution.py:331
  146.3 1.5 collective-permute-start.4
  147.8 0.3 collective-permute-start.5
  148.2 1.5 broadcast_select_fusion
  149.7 1.6 copy.72
  151.4 1.3 collective-permute-done.4.refs_2_
  152.7 1.9 %collective-permute-done.5.refs_3_ = bf16[128,512]{1,0:T(8,128)(2,1)S(1)} collective-permute-done((bf16[128,512]{1,0:T(8,128)(2,1)S(1)}, bf16[128,512]{1,0:T(8,128)(2,1)S(1)}, u32[]{:S(2)}, u32[]{:S(2)}) %collective-permute-start.5) | collective-permute-done | bytes 131104 | tf_op jit(solution)/shard_map/ppermute | solution.py:253
  154.6 7.7 %project_out.1 = bf16[512,2048]{1,0:T(8,128)(2,1)} custom-call(bf16[128,512]{1,0:T(8,128)(2,1)S(1)} %copy-done.34, bf16[128,512]{1,0:T(8,128)(2,1)S(1)} %collective-permute-done.3.refs_1_, bf16[128,512]{1,0:T(8,128)(2,1)S(1)} %collective-permute-done.4.refs_2_, bf16[128,512]{1,0:T(8,128)(2,1)S(1)} %collective-permute-done.5.refs_3_, ...), custom_call_target="tpu_custom_call" | custom-call | flops 4294967296 | bytes 12582912 | tf_op jit(solution)/shard_map/project_out/pallas_call | solution.py:207
  (138 shorter events, 3.3 us)
Async XLA Ops:
  7.2 6.5 %copy-start = (bf16[512,2048]{1,0:T(8,128)(2,1)S(1)}, bf16[512,2048]{1,0:T(8,128)(2,1)}, u32[]{:S(2)}) copy-start(bf16[512,2048]{1,0:T(8,128)(2,1)} %param.22) | copy-start | bytes 6291460
  10.2 42.3 %collective-permute-start.19 = (bf16[512,512]{1,0:T(8,128)(2,1)}, bf16[512,512]{1,0:T(8,128)(2,1)}, u32[]{:S(2)}, u32[]{:S(2)}) collective-permute-start(bf16[512,512]{1,0:T(8,128)(2,1)} %bitcast.13.t0), channel_id=1, source_target_pairs={{0,2},{1,3},{2,0},{3,1},{4,6},{5,7},{6,4},{7,5},{8,10},{9,11},{10,... | collective-permute-start | bytes 1572872 | tf_op jit(solution)/shard_map/ppermute | solution.py:253
  13.2 39.6 %collective-permute-start.18 = (bf16[512,512]{1,0:T(8,128)(2,1)}, bf16[512,512]{1,0:T(8,128)(2,1)}, u32[]{:S(2)}, u32[]{:S(2)}) collective-permute-start(bf16[512,512]{1,0:T(8,128)(2,1)} %bitcast.13.t0), channel_id=1, source_target_pairs={{0,1},{1,0},{2,3},{3,2},{4,5},{5,4},{6,7},{7,6},{8,9},{9,8},{10,11... | collective-permute-start | bytes 1572872 | tf_op jit(solution)/shard_map/ppermute | solution.py:253
  13.2 39.7 %collective-permute-start.13 = (bf16[512,512]{1,0:T(8,128)(2,1)}, bf16[512,512]{1,0:T(8,128)(2,1)}, u32[]{:S(2)}, u32[]{:S(2)}) collective-permute-start(bf16[512,512]{1,0:T(8,128)(2,1)} %bitcast.12.t0), channel_id=1, source_target_pairs={{0,2},{1,3},{2,0},{3,1},{4,6},{5,7},{6,4},{7,5},{8,10},{9,11},{10,... | collective-permute-start | bytes 1572872 | tf_op jit(solution)/shard_map/ppermute | solution.py:253
  13.3 40.6 %collective-permute-start.12 = (bf16[512,512]{1,0:T(8,128)(2,1)}, bf16[512,512]{1,0:T(8,128)(2,1)}, u32[]{:S(2)}, u32[]{:S(2)}) collective-permute-start(bf16[512,512]{1,0:T(8,128)(2,1)} %bitcast.12.t0), channel_id=1, source_target_pairs={{0,1},{1,0},{2,3},{3,2},{4,5},{5,4},{6,7},{7,6},{8,9},{9,8},{10,11... | collective-permute-start | bytes 1572872 | tf_op jit(solution)/shard_map/ppermute | solution.py:253
  13.7 5.5 %copy-start.41 = (s32[64]{0:T(128)S(1)}, s32[64]{0:T(128)}, u32[]{:S(2)}) copy-start(s32[64]{0:T(128)} %param.24) | copy-start | bytes 772
  13.7 6.1 %copy-start.35 = (bf16[16,32768]{1,0:T(8,128)(2,1)S(1)}, bf16[16,32768]{1,0:T(8,128)(2,1)}, u32[]{:S(2)}) copy-start(bf16[16,32768]{1,0:T(8,128)(2,1)} %param.23) | copy-start | bytes 3145732
  17.3 24.9 %collective-permute-start.25 = (bf16[64,2048]{1,0:T(8,128)(2,1)S(1)}, bf16[64,2048]{1,0:T(8,128)(2,1)}, u32[]{:S(2)}, u32[]{:S(2)}) collective-permute-start(bf16[64,2048]{1,0:T(8,128)(2,1)S(1)} %constant_dynamic-slice_fusion), channel_id=1, source_target_pairs={{0,2},{1,3},{2,0},{3,1},{4,6},{5,7},{6,4},{7,5},{8,10},{9,11},{10,... | collective-permute-start | bytes 786440 | tf_op jit(solution)/shard_map/ppermute | solution.py:253
  23.4 20.7 %copy-start.36 = (bf16[2048,8]{0,1:T(8,128)(2,1)S(1)}, bf16[2048,8]{0,1:T(8,128)(2,1)}, u32[]{:S(2)}) copy-start(bf16[2048,8]{0,1:T(8,128)(2,1)} %param.18) | copy-start | bytes 98308
  24.6 42.9 %all-to-all-start = ((bf16[4,4,256,128]{3,2,1,0:T(8,128)(2,1)}), bf16[4,4,256,128]{3,2,1,0:T(8,128)(2,1)}, u32[]{:S(2)}, u32[]{:S(2)}) async-start(bf16[4,4,256,128]{3,2,1,0:T(8,128)(2,1)} %broadcast_select_fusion.2), calls=%async_computation | async-start | bytes 2097152 | tf_op jit(solution)/shard_map/all_to_all | solution.py:272
  29.4 79.9 %all-gather.2.cloned.1.call-start = ((), (), s32[]{:S(2)}) async-start(), calls=%async_computation.2 | async-start | bytes 2359296 | tf_op jit(solution)/shard_map/all_gather | solution.py:302
  42.3 14.9 %collective-permute-start.7 = (bf16[512,512]{1,0:T(8,128)(2,1)}, bf16[512,512]{1,0:T(8,128)(2,1)}, u32[]{:S(2)}, u32[]{:S(2)}) collective-permute-start(bf16[512,512]{1,0:T(8,128)(2,1)} %bitcast.11.t0), channel_id=1, source_target_pairs={{0,2},{1,3},{2,0},{3,1},{4,6},{5,7},{6,4},{7,5},{8,10},{9,11},{10,... | collective-permute-start | bytes 1572872 | tf_op jit(solution)/shard_map/ppermute | solution.py:253
  45.1 1.9 %copy-start.42 = (bf16[2048,512]{1,0:T(8,128)(2,1)S(1)}, bf16[2048,512]{1,0:T(8,128)(2,1)}, u32[]{:S(2)}) copy-start(bf16[2048,512]{1,0:T(8,128)(2,1)} %param.15) | copy-start | bytes 6291460
  47.0 2.8 %copy-start.43 = (bf16[2048,512]{1,0:T(8,128)(2,1)S(1)}, bf16[2048,512]{1,0:T(8,128)(2,1)}, u32[]{:S(2)}) copy-start(bf16[2048,512]{1,0:T(8,128)(2,1)} %param.16) | copy-start | bytes 6291460
  49.8 3.6 %copy-start.38 = (s32[16]{0:T(128)S(1)}, s32[16]{0:T(128)}, u32[]{:S(2)}) copy-start(s32[16]{0:T(128)} %param.25) | copy-start | bytes 196
  49.8 7.4 %copy-start.37 = (f32[512]{0:T(512)S(1)}, f32[512]{0:T(512)}, u32[]{:S(2)}) copy-start(f32[512]{0:T(512)} %param.21) | copy-start | bytes 6148
  49.8 7.7 %copy-start.39 = (f32[8]{0:T(128)S(1)}, f32[8]{0:T(128)}, u32[]{:S(2)}) copy-start(f32[8]{0:T(128)} %param.19) | copy-start | bytes 100
  49.8 7.8 %copy-start.40 = (f32[8]{0:T(128)S(1)}, f32[8]{0:T(128)}, u32[]{:S(2)}) copy-start(f32[8]{0:T(128)} %param.20) | copy-start | bytes 100
  52.5 14.4 %collective-permute-start.1 = (bf16[512,512]{1,0:T(8,128)(2,1)}, bf16[512,512]{1,0:T(8,128)(2,1)}, u32[]{:S(2)}, u32[]{:S(2)}) collective-permute-start(bf16[512,512]{1,0:T(8,128)(2,1)} %bitcast.2.t0), channel_id=1, source_target_pairs={{0,2},{1,3},{2,0},{3,1},{4,6},{5,7},{6,4},{7,5},{8,10},{9,11},{10,... | collective-permute-start | bytes 1572872 | tf_op jit(solution)/shard_map/ppermute | solution.py:253
  52.8 14.1 %collective-permute-start.20 = (bf16[512,512]{1,0:T(8,128)(2,1)}, bf16[512,512]{1,0:T(8,128)(2,1)}, u32[]{:S(2)}, u32[]{:S(2)}) collective-permute-start(bf16[512,512]{1,0:T(8,128)(2,1)} %collective-permute-done.19.t2), channel_id=1, source_target_pairs={{0,1},{1,0},{2,3},{3,2},{4,5},{5,4},{6,7},{7,6},{8,9},{9,8},{10,11... | collective-permute-start | bytes 1572872 | tf_op jit(solution)/shard_map/ppermute | solution.py:253
  52.9 27.7 %collective-permute-start.14 = (bf16[512,512]{1,0:T(8,128)(2,1)}, bf16[512,512]{1,0:T(8,128)(2,1)}, u32[]{:S(2)}, u32[]{:S(2)}) collective-permute-start(bf16[512,512]{1,0:T(8,128)(2,1)} %collective-permute-done.13.t2), channel_id=1, source_target_pairs={{0,1},{1,0},{2,3},{3,2},{4,5},{5,4},{6,7},{7,6},{8,9},{9,8},{10,11... | collective-permute-start | bytes 1572872 | tf_op jit(solution)/shard_map/ppermute | solution.py:253
  53.8 36.8 %collective-permute-start.6 = (bf16[512,512]{1,0:T(8,128)(2,1)}, bf16[512,512]{1,0:T(8,128)(2,1)}, u32[]{:S(2)}, u32[]{:S(2)}) collective-permute-start(bf16[512,512]{1,0:T(8,128)(2,1)} %bitcast.11.t0), channel_id=1, source_target_pairs={{0,1},{1,0},{2,3},{3,2},{4,5},{5,4},{6,7},{7,6},{8,9},{9,8},{10,11... | collective-permute-start | bytes 1572872 | tf_op jit(solution)/shard_map/ppermute | solution.py:253
  57.2 33.5 %collective-permute-start.8 = (bf16[512,512]{1,0:T(8,128)(2,1)}, bf16[512,512]{1,0:T(8,128)(2,1)}, u32[]{:S(2)}, u32[]{:S(2)}) collective-permute-start(bf16[512,512]{1,0:T(8,128)(2,1)} %collective-permute-done.7.t2), channel_id=1, source_target_pairs={{0,1},{1,0},{2,3},{3,2},{4,5},{5,4},{6,7},{7,6},{8,9},{9,8},{10,11... | collective-permute-start | bytes 1572872 | tf_op jit(solution)/shard_map/ppermute | solution.py:253
  66.9 32.8 %collective-permute-start = (bf16[512,512]{1,0:T(8,128)(2,1)}, bf16[512,512]{1,0:T(8,128)(2,1)}, u32[]{:S(2)}, u32[]{:S(2)}) collective-permute-start(bf16[512,512]{1,0:T(8,128)(2,1)} %bitcast.2.t0), channel_id=1, source_target_pairs={{0,1},{1,0},{2,3},{3,2},{4,5},{5,4},{6,7},{7,6},{8,9},{9,8},{10,11... | collective-permute-start | bytes 1572872 | tf_op jit(solution)/shard_map/ppermute | solution.py:253
  66.9 32.8 %collective-permute-start.2 = (bf16[512,512]{1,0:T(8,128)(2,1)}, bf16[512,512]{1,0:T(8,128)(2,1)}, u32[]{:S(2)}, u32[]{:S(2)}) collective-permute-start(bf16[512,512]{1,0:T(8,128)(2,1)} %collective-permute-done.1.t2), channel_id=1, source_target_pairs={{0,1},{1,0},{2,3},{3,2},{4,5},{5,4},{6,7},{7,6},{8,9},{9,8},{10,11... | collective-permute-start | bytes 1572872 | tf_op jit(solution)/shard_map/ppermute | solution.py:253
  67.5 1.6 copy-start.24
  69.0 1.6 copy-start.26
  70.6 10.0 %copy-start.25 = (bf16[2048,512]{1,0:T(8,128)(2,1)S(1)}, bf16[2048,512]{1,0:T(8,128)(2,1)}, u32[]{:S(2)}) copy-start(bf16[2048,512]{1,0:T(8,128)(2,1)} %fusion.xw) | copy-start | bytes 6291460
  79.2 0.7 copy-start.18
  79.9 0.7 copy-start.27
  80.5 74.0 %collective-permute-start.24 = (bf16[512,2048]{1,0:T(8,128)(2,1)}, bf16[512,2048]{1,0:T(8,128)(2,1)}, u32[]{:S(2)}, u32[]{:S(2)}) collective-permute-start(bf16[512,2048]{1,0:T(8,128)(2,1)} %convolution_convert_fusion.refs_16_), channel_id=1, source_target_pairs={{0,1},{1,0},{2,3},{3,2},{4,5},{5,4},{6,7},{7,6},{8,9},{9,8},{10,11... | collective-permute-start | bytes 6291464 | tf_op jit(solution)/shard_map/ppermute | solution.py:253
  107.0 0.7 copy-start.4
  107.0 0.7 copy-start.33
  109.3 9.4 %copy-start.13 = (bf16[128,512]{1,0:T(8,128)(2,1)S(1)}, bf16[128,512]{1,0:T(8,128)(2,1)}, u32[]{:S(2)}) copy-start(bf16[128,512]{1,0:T(8,128)(2,1)} %copy-done.12) | copy-start | bytes 393220
  109.3 14.4 %copy-start.15 = (bf16[128,512]{1,0:T(8,128)(2,1)S(1)}, bf16[128,512]{1,0:T(8,128)(2,1)}, u32[]{:S(2)}) copy-start(bf16[128,512]{1,0:T(8,128)(2,1)} %copy-done.14) | copy-start | bytes 393220
  109.3 17.1 %copy-start.11 = (bf16[128,512]{1,0:T(8,128)(2,1)S(1)}, bf16[128,512]{1,0:T(8,128)(2,1)}, u32[]{:S(2)}) copy-start(bf16[128,512]{1,0:T(8,128)(2,1)} %copy-done.10) | copy-start | bytes 393220
  109.3 19.7 %copy-start.9 = (bf16[128,512]{1,0:T(8,128)(2,1)S(1)}, bf16[128,512]{1,0:T(8,128)(2,1)}, u32[]{:S(2)}) copy-start(bf16[128,512]{1,0:T(8,128)(2,1)} %copy-done.8) | copy-start | bytes 393220
  109.3 20.9 %copy-start.7 = (bf16[128,512]{1,0:T(8,128)(2,1)S(1)}, bf16[128,512]{1,0:T(8,128)(2,1)}, u32[]{:S(2)}) copy-start(bf16[128,512]{1,0:T(8,128)(2,1)} %copy-done.6) | copy-start | bytes 393220
  109.4 45.2 %collective-permute-start.26 = (bf16[512,2048]{1,0:T(8,128)(2,1)}, bf16[512,2048]{1,0:T(8,128)(2,1)}, u32[]{:S(2)}, u32[]{:S(2)}) collective-permute-start(bf16[512,2048]{1,0:T(8,128)(2,1)} %all-gather.2.cloned.1.call-done.refs_18_), channel_id=1, source_target_pairs={{0,1},{1,0},{2,3},{3,2},{4,5},{5,4},{6,7},{7,6},{8,9},{9,8},{10,11... | collective-permute-start | bytes 6291464 | tf_op jit(solution)/shard_map/ppermute | solution.py:253
  112.2 34.1 %copy-start.5 = (bf16[128,512]{1,0:T(8,128)(2,1)S(1)}, bf16[128,512]{1,0:T(8,128)(2,1)}, u32[]{:S(2)}) copy-start(bf16[128,512]{1,0:T(8,128)(2,1)} %copy-done.4) | copy-start | bytes 393220
  112.2 34.1 %copy-start.3 = (bf16[128,512]{1,0:T(8,128)(2,1)S(1)}, bf16[128,512]{1,0:T(8,128)(2,1)}, u32[]{:S(2)}) copy-start(bf16[128,512]{1,0:T(8,128)(2,1)} %copy-done.2) | copy-start | bytes 393220
  112.2 31.2 %all-to-all-start.1 = ((bf16[4,4,256,128]{3,2,1,0:T(8,128)(2,1)}), bf16[4,4,256,128]{3,2,1,0:T(8,128)(2,1)}, u32[]{:S(2)}, u32[]{:S(2)}) async-start(bf16[4,4,256,128]{3,2,1,0:T(8,128)(2,1)} %bitcast.48), calls=%async_computation.1 | async-start | bytes 2097152 | tf_op jit(solution)/shard_map/all_to_all | solution.py:328
  117.2 1.9 %collective-permute-start.21 = (bf16[128,512]{1,0:T(8,128)(2,1)}, bf16[128,512]{1,0:T(8,128)(2,1)S(1)}, u32[]{:S(2)}, u32[]{:S(2)}) collective-permute-start(bf16[128,512]{1,0:T(8,128)(2,1)} %get-tuple-element.36), channel_id=1, source_target_pairs={{0,1},{1,0},{2,3},{3,2},{4,5},{5,4},{6,7},{7,6},{8,9},{9,8},{10,11... | collective-permute-start | bytes 393224 | tf_op jit(solution)/shard_map/ppermute | solution.py:253
  117.2 6.5 %collective-permute-start.22 = (bf16[128,512]{1,0:T(8,128)(2,1)}, bf16[128,512]{1,0:T(8,128)(2,1)S(1)}, u32[]{:S(2)}, u32[]{:S(2)}) collective-permute-start(bf16[128,512]{1,0:T(8,128)(2,1)} %copy-done.18), channel_id=1, source_target_pairs={{0,2},{1,3},{2,0},{3,1},{4,6},{5,7},{6,4},{7,5},{8,10},{9,11},{10,... | collective-permute-start | bytes 393224 | tf_op jit(solution)/shard_map/ppermute | solution.py:253
  118.7 7.0 %collective-permute-start.23 = (bf16[128,512]{1,0:T(8,128)(2,1)S(1)}, bf16[128,512]{1,0:T(8,128)(2,1)S(1)}, u32[]{:S(2)}, u32[]{:S(2)}) collective-permute-start(bf16[128,512]{1,0:T(8,128)(2,1)S(1)} %copy-done.13), channel_id=1, source_target_pairs={{0,3},{1,2},{2,1},{3,0},{4,7},{5,6},{6,5},{7,4},{8,11},{9,10},{10,... | collective-permute-start | bytes 393224 | tf_op jit(solution)/shard_map/ppermute | solution.py:253
  119.1 9.4 %collective-permute-start.15 = (bf16[128,512]{1,0:T(8,128)(2,1)}, bf16[128,512]{1,0:T(8,128)(2,1)S(1)}, u32[]{:S(2)}, u32[]{:S(2)}) collective-permute-start(bf16[128,512]{1,0:T(8,128)(2,1)} %copy-done.19), channel_id=1, source_target_pairs={{0,1},{1,0},{2,3},{3,2},{4,5},{5,4},{6,7},{7,6},{8,9},{9,8},{10,11... | collective-permute-start | bytes 393224 | tf_op jit(solution)/shard_map/ppermute | solution.py:253
  123.7 5.9 %collective-permute-start.16 = (bf16[128,512]{1,0:T(8,128)(2,1)S(1)}, bf16[128,512]{1,0:T(8,128)(2,1)S(1)}, u32[]{:S(2)}, u32[]{:S(2)}) collective-permute-start(bf16[128,512]{1,0:T(8,128)(2,1)S(1)} %copy-done.15), channel_id=1, source_target_pairs={{0,2},{1,3},{2,0},{3,1},{4,6},{5,7},{6,4},{7,5},{8,10},{9,11},{10,... | collective-permute-start | bytes 393224 | tf_op jit(solution)/shard_map/ppermute | solution.py:253
  125.7 0.7 copy-start.16
  126.4 5.9 %collective-permute-start.17 = (bf16[128,512]{1,0:T(8,128)(2,1)S(1)}, bf16[128,512]{1,0:T(8,128)(2,1)S(1)}, u32[]{:S(2)}, u32[]{:S(2)}) collective-permute-start(bf16[128,512]{1,0:T(8,128)(2,1)S(1)} %copy-done.11), channel_id=1, source_target_pairs={{0,3},{1,2},{2,1},{3,0},{4,7},{5,6},{6,5},{7,4},{8,11},{9,10},{10,... | collective-permute-start | bytes 393224 | tf_op jit(solution)/shard_map/ppermute | solution.py:253
  128.4 0.7 copy-start.20
  129.1 17.2 %collective-permute-start.10 = (bf16[128,512]{1,0:T(8,128)(2,1)S(1)}, bf16[128,512]{1,0:T(8,128)(2,1)}, u32[]{:S(2)}, u32[]{:S(2)}) collective-permute-start(bf16[128,512]{1,0:T(8,128)(2,1)S(1)} %copy-done.9), channel_id=1, source_target_pairs={{0,2},{1,3},{2,0},{3,1},{4,6},{5,7},{6,4},{7,5},{8,10},{9,11},{10,... | collective-permute-start | bytes 393224 | tf_op jit(solution)/shard_map/ppermute | solution.py:253
  130.3 16.0 %collective-permute-start.11 = (bf16[128,512]{1,0:T(8,128)(2,1)S(1)}, bf16[128,512]{1,0:T(8,128)(2,1)S(1)}, u32[]{:S(2)}, u32[]{:S(2)}) collective-permute-start(bf16[128,512]{1,0:T(8,128)(2,1)S(1)} %copy-done.7), channel_id=1, source_target_pairs={{0,3},{1,2},{2,1},{3,0},{4,7},{5,6},{6,5},{7,4},{8,11},{9,10},{10,... | collective-permute-start | bytes 393224 | tf_op jit(solution)/shard_map/ppermute | solution.py:253
  132.3 15.5 %collective-permute-start.9 = (bf16[128,512]{1,0:T(8,128)(2,1)S(1)}, bf16[128,512]{1,0:T(8,128)(2,1)S(1)}, u32[]{:S(2)}, u32[]{:S(2)}) collective-permute-start(bf16[128,512]{1,0:T(8,128)(2,1)S(1)} %get-tuple-element.28), channel_id=1, source_target_pairs={{0,1},{1,0},{2,3},{3,2},{4,5},{5,4},{6,7},{7,6},{8,9},{9,8},{10,11... | collective-permute-start | bytes 393224 | tf_op jit(solution)/shard_map/ppermute | solution.py:253
  146.3 5.1 %collective-permute-start.3 = (bf16[128,512]{1,0:T(8,128)(2,1)S(1)}, bf16[128,512]{1,0:T(8,128)(2,1)S(1)}, u32[]{:S(2)}, u32[]{:S(2)}) collective-permute-start(bf16[128,512]{1,0:T(8,128)(2,1)S(1)} %copy-done.5), channel_id=1, source_target_pairs={{0,1},{1,0},{2,3},{3,2},{4,5},{5,4},{6,7},{7,6},{8,9},{9,8},{10,11... | collective-permute-start | bytes 393224 | tf_op jit(solution)/shard_map/ppermute | solution.py:253
  146.3 6.4 %collective-permute-start.4 = (bf16[128,512]{1,0:T(8,128)(2,1)S(1)}, bf16[128,512]{1,0:T(8,128)(2,1)S(1)}, u32[]{:S(2)}, u32[]{:S(2)}) collective-permute-start(bf16[128,512]{1,0:T(8,128)(2,1)S(1)} %copy-done.3), channel_id=1, source_target_pairs={{0,2},{1,3},{2,0},{3,1},{4,6},{5,7},{6,4},{7,5},{8,10},{9,11},{10,... | collective-permute-start | bytes 393224 | tf_op jit(solution)/shard_map/ppermute | solution.py:253
  147.8 6.7 %collective-permute-start.5 = (bf16[128,512]{1,0:T(8,128)(2,1)S(1)}, bf16[128,512]{1,0:T(8,128)(2,1)S(1)}, u32[]{:S(2)}, u32[]{:S(2)}) collective-permute-start(bf16[128,512]{1,0:T(8,128)(2,1)S(1)} %get-tuple-element.26), channel_id=1, source_target_pairs={{0,3},{1,2},{2,1},{3,0},{4,7},{5,6},{6,5},{7,4},{8,11},{9,10},{10,... | collective-permute-start | bytes 393224 | tf_op jit(solution)/shard_map/ppermute | solution.py:253
  148.1 6.4 %copy-start.1 = (bf16[512,2048]{1,0:T(8,128)(2,1)S(1)}, bf16[512,2048]{1,0:T(8,128)(2,1)}, u32[]{:S(2)}) copy-start(bf16[512,2048]{1,0:T(8,128)(2,1)} %all-gather.2.cloned.1.call-done.refs_18_) | copy-start | bytes 6291460
  148.1 6.4 %copy-start.17 = (bf16[128,512]{1,0:T(8,128)(2,1)S(1)}, bf16[128,512]{1,0:T(8,128)(2,1)}, u32[]{:S(2)}) copy-start(bf16[128,512]{1,0:T(8,128)(2,1)} %copy-done.16) | copy-start | bytes 393220
  148.1 6.4 %copy-start.21 = (bf16[128,512]{1,0:T(8,128)(2,1)S(1)}, bf16[128,512]{1,0:T(8,128)(2,1)}, u32[]{:S(2)}) copy-start(bf16[128,512]{1,0:T(8,128)(2,1)} %copy-done.20) | copy-start | bytes 393220
  148.1 6.4 %copy-start.23 = (bf16[128,512]{1,0:T(8,128)(2,1)S(1)}, bf16[128,512]{1,0:T(8,128)(2,1)}, u32[]{:S(2)}) copy-start(bf16[128,512]{1,0:T(8,128)(2,1)} %copy-done.22) | copy-start | bytes 393220
  148.2 6.4 %copy-start.28 = (bf16[128,512]{1,0:T(8,128)(2,1)S(1)}, bf16[128,512]{1,0:T(8,128)(2,1)}, u32[]{:S(2)}) copy-start(bf16[128,512]{1,0:T(8,128)(2,1)} %copy-done.27) | copy-start | bytes 393220
  148.2 6.4 %copy-start.30 = (bf16[128,512]{1,0:T(8,128)(2,1)S(1)}, bf16[128,512]{1,0:T(8,128)(2,1)}, u32[]{:S(2)}) copy-start(bf16[128,512]{1,0:T(8,128)(2,1)} %copy-done.29) | copy-start | bytes 393220
  148.2 6.4 %copy-start.32 = (bf16[128,512]{1,0:T(8,128)(2,1)S(1)}, bf16[128,512]{1,0:T(8,128)(2,1)}, u32[]{:S(2)}) copy-start(bf16[128,512]{1,0:T(8,128)(2,1)} %copy-done.31) | copy-start | bytes 393220
  148.2 6.4 %copy-start.34 = (bf16[128,512]{1,0:T(8,128)(2,1)S(1)}, bf16[128,512]{1,0:T(8,128)(2,1)}, u32[]{:S(2)}) copy-start(bf16[128,512]{1,0:T(8,128)(2,1)} %copy-done.33) | copy-start | bytes 393220
  (10 other events, 6.4 us)
Sparse Core Ops, SparseCore 0:
  44.2 49.5 all-gather.1

commit v2 on v1

v2 whole, which is shorter than its diff:
```python
import functools

import jax
import jax.numpy as jnp
import numpy as np
from jax import lax
from jax.experimental import pallas as pl
from jax.experimental.pallas import tpu as pltpu
from jax.sharding import PartitionSpec as P

BF = jnp.bfloat16
F32 = jnp.float32


def pick(values, index):
    chosen = index[..., None] == jnp.arange(values.shape[0], dtype=jnp.int32)
    return jnp.sum(jnp.where(chosen, values, 0), axis=-1, dtype=jnp.int32)


def count_before(same, order):
    earlier = order[None, :] < order[:, None]
    return jnp.sum((same & earlier).astype(jnp.int32), axis=1)


def split_sessions(home_rows, block, per_target):
    total = home_rows.shape[0]
    session = jnp.arange(total, dtype=jnp.int32)
    server = session // block
    shard = home_rows // block
    same_server = server[:, None] == server[None, :]
    same_pair = same_server & (shard[:, None] == shard[None, :])
    rank = count_before(same_pair, session)
    size = jnp.sum(same_pair.astype(jnp.int32), axis=1)
    single = (rank ^ 1) >= size
    both_single = same_server & single[:, None] & single[None, :]
    single_rank = count_before(both_single, session)
    partners = (same_pair & (rank[None, :] == (rank ^ 1)[:, None])) | (
        both_single & (single_rank[None, :] == (single_rank ^ 1)[:, None])
    )
    partner = jnp.sum(jnp.where(partners, session[None, :], 0), axis=1, dtype=jnp.int32)
    step = partner ^ 1
    lowest = session
    reach = 1
    while reach < block // 2:
        lowest = jnp.minimum(lowest, pick(lowest, step))
        step = pick(step, step)
        reach *= 2
    half = (lowest > pick(lowest, partner)).astype(jnp.int32)
    same_half = half[:, None] == half[None, :]
    target = session // per_target
    turn = count_before(same_half & (target[:, None] == target[None, :]), session)
    chunk = half * (per_target // 2) + turn
    place = count_before(same_half & same_pair, session)
    return server, shard, half, chunk, place


def layer_kernel(
    heads, span, meta, a0, a1, a2, a3, b0, b1, b2, b3, t2, t3, xw, zw, bw, bias, rate, gain, order,
    s0, s1, s2, s3, earlier, n0, n1, n2, n3, outgoing, xs, zs, bcs, fresh, sems,
):
    del earlier
    me = meta[12]
    states = (s0, s1, s2, s3)
    pieces = (
        jnp.concatenate([a0[...], a1[...], a2[...], a3[...]], axis=0),
        jnp.concatenate([b0[...], b1[...], b2[...], b3[...]], axis=0),
        t2[...],
        t3[...],
    )
    normed_out = (n0, n1, n2, n3)
    depth = t2.shape[1]
    quads = heads // 4

    def project(weight, columns):
        total = None
        for distance in range(4):
            first = pl.multiple_of((me ^ distance) * depth, depth)
            part = jnp.dot(
                pieces[distance],
                weight[pl.ds(first, depth), columns],
                preferred_element_type=F32,
            )
            total = part if total is None else total + part
        return total

    bcs[...] = project(bw, slice(None))
    for weight, rounded in ((xw, xs), (zw, zs)):
        natural = jnp.concatenate(
            [
                project(weight, slice(quad * 256, quad * 256 + 256)).astype(BF)
                for quad in range(quads)
            ],
            axis=1,
        )
        rounded[...] = jnp.dot(natural, order[...], preferred_element_type=F32).astype(BF)

    lane = lax.broadcasted_iota(jnp.int32, (span, 128), 1)
    row = lax.broadcasted_iota(jnp.int32, (span, 128), 0)
    low = lane < 64
    causal = row >= lane
    lane8 = lax.broadcasted_iota(jnp.int32, (heads, span), 1)
    head_mask = [((lane // 32) == k).astype(F32).astype(BF) for k in range(4)]
    head_masks = [jnp.concatenate([m, m], axis=1) for m in head_mask]

    sends = []
    for distance in range(4):
        place = me ^ distance
        first = pl.multiple_of(place * span, span)
        rows = pl.ds(first, span)
        count = meta[8 + place]
        bc = bcs[rows, 0:128]
        turned = pltpu.roll(bc, 64, 1)
        bc_low = jnp.where(low, bc, 0.0).astype(BF)
        bc_high = jnp.where(low, 0.0, turned).astype(BF)
        c_low = jnp.where(low, turned, 0.0).astype(BF)
        c_high = jnp.where(low, 0.0, bc).astype(BF)
        scores = lax.dot_general(
            c_low, bc_low, (((1,), (1,)), ((), ())), preferred_element_type=F32
        )
        scores = jnp.where(causal, scores, 0.0)
        raw = jnp.transpose(bcs[rows, 128:256])[:heads] + bias[...]
        soft = jnp.maximum(raw, 0.0) + jnp.log1p(jnp.exp(-jnp.abs(raw)))
        step = jnp.where(lane8 < count, soft, 0.0)
        total = step * rate[...]
        shift = 1
        while shift < span:
            total = total + jnp.where(lane8 >= shift, pltpu.roll(total, shift, 1), 0.0)
            shift *= 2
        last = total[:, span - 1 : span]
        weights = jnp.exp(jnp.minimum(total - last, 0.0)) * step
        kept = jnp.exp(-last)
        cum = jnp.transpose(jnp.concatenate([total, jnp.zeros((128 - heads, span), F32)], axis=0))
        state = states[distance][...]
        carried = lax.dot_general(
            jnp.concatenate([c_low, c_high], axis=0),
            state,
            (((1,), (1,)), ((), ())),
            preferred_element_type=F32,
        )
        b_both = jnp.concatenate([bc_low, bc_high], axis=0)
        gated = []
        squares = None
        for quad in range(quads):
            columns = slice(quad * 256, quad * 256 + 256)
            x = xs[rows, columns]
            mixes = []
            blocks = []
            spread = None
            for k in range(4):
                head = quad * 4 + k
                level = jnp.broadcast_to(cum[:, head : head + 1], (span, 128))
                gap = jnp.minimum(total[head : head + 1, :] - level, 0.0)
                mixes.append((jnp.exp(gap) * step[head : head + 1, :] * scores).astype(BF))
                blocks.append(x * head_masks[k])
                spread = level if spread is None else jnp.where(lane >= 32 * k, level, spread)
            diagonal = jnp.dot(
                jnp.concatenate(mixes, axis=1),
                jnp.concatenate(blocks, axis=0),
                preferred_element_type=F32,
            )
            fade = jnp.exp(-spread)
            part = slice(quad * 128, quad * 128 + 128)
            before = jnp.concatenate(
                [carried[:span, part] * fade, carried[span:, part] * fade], axis=1
            )
            gate = zs[rows, columns].astype(F32)
            value = (diagonal + before) * (gate / (1.0 + jnp.exp(-gate)))
            gated.append(value)
            own = jnp.sum(value * value, axis=1, keepdims=True)
            squares = own if squares is None else squares + own
            weight_rows = jnp.concatenate(
                [
                    jnp.broadcast_to(weights[quad * 4 + k : quad * 4 + k + 1, :], (32, span))
                    for k in range(4)
                ],
                axis=0,
            )
            xf = x.astype(F32)
            even = (jnp.transpose(xf[:, :128]) * weight_rows).astype(BF)
            odd = (jnp.transpose(xf[:, 128:]) * weight_rows).astype(BF)
            added = jnp.dot(
                jnp.concatenate([even, odd], axis=1), b_both, preferred_element_type=F32
            )
            keep_rows = jnp.concatenate(
                [
                    jnp.broadcast_to(kept[quad * 4 + k : quad * 4 + k + 1, :], (32, 128))
                    for k in range(4)
                ],
                axis=0,
            )
            fresh[distance, quad * 128 : quad * 128 + 128, :] = (
                keep_rows * state[quad * 128 : quad * 128 + 128].astype(F32) + added
            ).astype(BF)
        sends.append(
            pltpu.make_async_copy(
                fresh.at[distance], outgoing.at[meta[4 + place]], sems.at[distance]
            )
        )
        sends[-1].start()
        inverse = lax.rsqrt(squares * (1.0 / (heads * 64)) + 1e-05)
        inverse = jnp.where(row[:, :1] < count, inverse, 0.0)
        normed = jnp.concatenate(
            [
                (gated[quad] * inverse * gain[:, quad * 256 : quad * 256 + 256]).astype(BF)
                for quad in range(quads)
            ],
            axis=1,
        )
        normed_out[distance][...] = lax.dot_general(
            normed, order[...], (((1,), (1,)), ((), ())), preferred_element_type=F32
        ).astype(BF)
    for send in sends:
        send.wait()


def layer_call(meta, tokens, sibling, across, far, weights, small, inbound, earlier):
    rows, depth = across.shape
    heads = small[0].shape[0]
    width = weights[0].shape[1]
    span = rows // 4
    vmem = pl.BlockSpec(memory_space=pltpu.VMEM)

    def session_block(k):
        return pl.BlockSpec((None, span, depth), lambda i, meta: (meta[k], 0, 0))

    def state_block(distance):
        return pl.BlockSpec(
            (None,) + inbound.shape[1:], lambda i, meta: (meta[4 + (meta[12] ^ distance)], 0, 0)
        )

    sessions = [session_block(k) for k in range(4)]
    operands = [*[tokens] * 4, *[sibling] * 4, across, far, *weights, *small, *[inbound] * 4]
    aliases = {}
    if earlier is None:
        earlier = jnp.zeros((8, 128), BF)
    else:
        aliases = {len(operands) + 1: 4}
    return pl.pallas_call(
        functools.partial(layer_kernel, heads, span),
        out_shape=[jax.ShapeDtypeStruct((span, width), BF)] * 4
        + [jax.ShapeDtypeStruct(inbound.shape, BF)],
        grid_spec=pltpu.PrefetchScalarGridSpec(
            num_scalar_prefetch=1,
            grid=(1,),
            in_specs=sessions
            + sessions
            + [vmem] * 9
            + [state_block(k) for k in range(4)]
            + [pl.BlockSpec(memory_space=pl.ANY)],
            out_specs=[vmem] * 4 + [pl.BlockSpec(memory_space=pl.ANY)],
            scratch_shapes=[
                pltpu.VMEM((rows, width), BF),
                pltpu.VMEM((rows, width), BF),
                pltpu.VMEM((rows, weights[2].shape[1]), F32),
                pltpu.VMEM((4,) + inbound.shape[1:], BF),
                pltpu.SemaphoreType.DMA((4,)),
            ],
        ),
        input_output_aliases=aliases,
        compiler_params=pltpu.CompilerParams(vmem_limit_bytes=40 * 2**20),
        cost_estimate=pl.CostEstimate(
            flops=8 * 10**9, bytes_accessed=9 * 2**20, transcendentals=0
        ),
        name="layer",
    )(meta, *operands, earlier)


def out_kernel(chunks, at_ref, *refs):
    weights = refs[chunks * 4 : chunks * 4 + 4]
    out = refs[-1]
    span = refs[0].shape[0]
    for chunk in range(chunks):
        total = None
        for distance in range(4):
            part = jnp.dot(
                refs[chunk * 4 + distance][...],
                weights[distance][...],
                preferred_element_type=F32,
            )
            total = part if total is None else total + part
        out[pl.ds(pl.multiple_of(at_ref[chunk] * span, span), span), :] = total.astype(BF)


def out_call(at, normed, weights):
    chunks = len(normed)
    span, depth = normed[0][0].shape
    columns = weights[0].shape[1]
    block = 512
    return pl.pallas_call(
        functools.partial(out_kernel, chunks),
        grid=(columns // block,),
        out_shape=jax.ShapeDtypeStruct((chunks * span, columns), BF),
        in_specs=[pl.BlockSpec(memory_space=pltpu.SMEM)]
        + [pl.BlockSpec((span, depth), lambda j: (0, 0))] * (chunks * 4)
        + [pl.BlockSpec((depth, block), lambda j: (0, j))] * 4,
        out_specs=pl.BlockSpec((chunks * span, block), lambda j: (0, j)),
        compiler_params=pltpu.CompilerParams(vmem_limit_bytes=32 * 2**20),
        cost_estimate=pl.CostEstimate(
            flops=2 * chunks * span * depth * 4 * columns,
            bytes_accessed=12 * 2**20,
            transcendentals=0,
        ),
        name="project_out",
    )(at, *[piece for chunk in normed for piece in chunk], *weights)


def body(
    tokens,
    x_weight,
    z_weight,
    bc_weight,
    dt_weight,
    dt_bias,
    decay_rate,
    norm_gain,
    out_weight,
    store_states,
    home_rows,
    event_counts,
):
    shard_count = lax.axis_size("dp")
    model_shards = lax.axis_size("mp")
    shard_index = lax.axis_index("dp")
    me = lax.axis_index("mp")
    sessions_here, state_width = store_states.shape
    heads = dt_bias.shape[0]
    width = x_weight.shape[1]
    depth = tokens.shape[1]
    span = tokens.shape[0] // sessions_here
    chunks = sessions_here // model_shards
    capacity = max(2, (sessions_here + shard_count - 1) // shard_count)
    places = (capacity + 1) // 2
    slot_count = shard_count * places
    row_shape = (state_width // 128, 128)

    def exchange(value, distance):
        pairs = [(j, j ^ distance) for j in range(model_shards)]
        return lax.ppermute(value, "mp", pairs)

    def trade(value):
        return lax.all_to_all(
            value.reshape((shard_count, places) + row_shape),
            "dp",
            split_axis=0,
            concat_axis=0,
            tiled=True,
        ).reshape((slot_count,) + row_shape)

    replicas = lax.axis_size("groups") * shard_count
    replica = lax.axis_index("groups") * shard_count + shard_index
    share = width // replicas
    ow_part = exchange(lax.dynamic_slice_in_dim(out_weight, replica * share, share), 2)
    sibling = exchange(tokens, 1)

    server, shard, half, chunk, place = split_sessions(home_rows, sessions_here, chunks)
    local = jnp.arange(sessions_here, dtype=jnp.int32)
    mine = shard_index * sessions_here + local
    by_turn = (jnp.arange(chunks)[:, None, None] == pick(chunk, mine)) & (
        jnp.arange(model_shards)[None, :, None] == local // chunks
    )

    def arranged(values):
        return jnp.sum(jnp.where(by_turn, values, 0), axis=2, dtype=jnp.int32)

    turns = arranged(local)
    slots = arranged(pick(shard * places + place, mine))
    counts = arranged(event_counts)
    meta = jnp.concatenate(
        [turns, slots, counts, jnp.full((chunks, 4), me, jnp.int32)], axis=1
    )
    at = jnp.sum(
        jnp.where(jnp.arange(model_shards)[None, :] == me, turns - me * chunks, 0), axis=1
    )

    by_session = tokens.reshape(sessions_here, span, depth)
    own = [
        jnp.concatenate(
            [lax.dynamic_slice_in_dim(by_session, turns[c, j], 1) for j in range(model_shards)]
        ).reshape(model_shards * span, depth)
        for c in range(chunks)
    ]
    across = [exchange(own[c], 2) for c in range(chunks)]

    store_row = home_rows - shard_index * sessions_here
    here = shard == shard_index
    there = server * places + place
    wanted = jnp.arange(slot_count, dtype=jnp.int32)
    kept = store_states.reshape((sessions_here,) + row_shape)
    inbound = []
    for k in range(2):
        chosen = (wanted[:, None] == there[None, :]) & (here & (half == k))[None, :]
        source = jnp.sum(jnp.where(chosen, store_row[None, :], 0), axis=1)
        inbound.append(trade(jnp.take(kept, source, axis=0, mode="clip")))
    owned = here[None, :] & (store_row[None, :] == local[:, None])
    came_back = jnp.sum(jnp.where(owned, half * slot_count + there, 0), axis=1)

    new_column = np.arange(width)
    old_column = (
        (new_column // 256 * 4 + new_column // 32 % 4) * 64
        + new_column % 32 * 2
        + new_column // 128 % 2
    )
    order = jnp.asarray(old_column[None, :] == np.arange(width)[:, None], BF)
    bw = jnp.concatenate(
        [bc_weight, dt_weight, jnp.zeros((bc_weight.shape[0], 128 - heads), BF)], axis=1
    )
    gain = norm_gain.reshape(heads // 4, 4, 32, 2).transpose(0, 3, 1, 2).reshape(1, width)

    ow_across = lax.all_gather(ow_part, ("groups", "dp"), axis=0, tiled=True)
    ow_sibling = exchange(out_weight, 1)
    ow_far = exchange(ow_across, 1)

    small = (dt_bias.reshape(heads, 1), decay_rate.reshape(heads, 1), gain, order)
    normed = []
    returned = []
    earlier = None
    sibling = sibling.reshape(sessions_here, span, depth)
    for c in range(chunks):
        turn = meta[c]
        arrived = across[c]
        if c >= 2:
            arrived, _ = lax.optimization_barrier((arrived, normed[c - 2][0]))
            turn, _ = lax.optimization_barrier((turn, normed[c - 2]))
        if c >= 1:
            turn, _ = lax.optimization_barrier((turn, normed[c - 1][0]))
        far = exchange(arrived, 1)
        *parts, outgoing = layer_call(
            turn,
            by_session,
            sibling,
            arrived,
            far,
            (x_weight, z_weight, bw),
            small,
            inbound[c * 2 // chunks],
            earlier,
        )
        earlier = outgoing
        if (c + 1) % (chunks // 2) == 0:
            returned.append(trade(outgoing))
            earlier = None
        normed.append([parts[0]] + [exchange(parts[d], d) for d in range(1, 4)])
    new_store = jnp.take(jnp.concatenate(returned), came_back, axis=0, mode="clip").reshape(
        sessions_here, state_width
    )
    out_tokens = out_call(at, normed, (out_weight, ow_sibling, ow_across, ow_far))
    return (out_tokens, new_store)


def solution(mesh):
    return jax.shard_map(
        body,
        mesh=mesh,
        in_specs=(
            P(("groups", "dp"), "mp"),
            P(None, "mp"),
            P(None, "mp"),
            P(None, "mp"),
            P(None, "mp"),
            P("mp"),
            P("mp"),
            P("mp"),
            P("mp", None),
            P(("groups", "dp"), "mp"),
            P("groups"),
            P(("groups", "dp")),
        ),
        out_specs=(P(("groups", "dp", "mp"), None), P(("groups", "dp"), "mp")),
        check_vma=False,
    )
```

time: 170 us -> 221 us (1.30)
  between operations: 14.4 us -> 45.4 us
  Pallas kernels: 37.4 us -> 51.1 us
  matrix products: 7.97 us -> 0 us
  starting transfers between devices: 28.1 us -> 35.9 us
  local copies, waits for them, and re-layouts: 28.2 us -> 34.1 us
  other arithmetic: 7.7 us -> 10.1 us
    pallas_call x4, Pallas kernels: 29.7 us -> 43.4 us  [layer_call(): pl.pallas_call(functools.partial(layer_kernel, heads, span), out_shape=[j...]
    all_to_all x2 -> x4, starting transfers between devices: 9.91 us -> 20.4 us  [trade(): lax.all_to_all(value.reshape((shard_count, places) + row_shape), 'dp', sp...]
    dot_general x3 -> x0, matrix products: 7.97 us -> none  [the longest x1 2.69 us: body(): zw = jnp.dot(z_weight, order, preferred_element_type=F32).astype(BF)]
    unnamed x91 -> x81, local copies, waits for them, and re-layouts: 16.3 us -> 24.1 us
    select_n x9 -> x2, other arithmetic: 5.14 us -> 0.01 us  [the longest x1 0.01 us: split_sessions(): target = session // per_target]
    concatenate x0 -> x6, other arithmetic: none -> 4.88 us  [the longest x4 2.7 us: body(): jnp.concatenate([lax.dynamic_slice_in_dim(by_session, turns[c, j], 1) for...]
    ppermute x27 -> x24, starting transfers between devices: 18.2 us -> 15.4 us  [exchange(): return lax.ppermute(value, 'mp', pairs)]
    slice x2 -> x1, local copies, waits for them, and re-layouts: 3.36 us -> 0.71 us  [body(): turns[c, j]]
  transfers between devices with their start and end apart: 30 -> 29, of which waited for: 9 -> 7; matrix products, arithmetic and copies ran while one was open for 17% -> 11% of each run, Pallas kernels for 18% -> 20%
where the time goes in v2:
time: 221 us; the launch traced here: 220 us
  Pallas kernels  51.1 us (23%)
  between operations  45.4 us (21%)
  waiting for transfers between devices  43.4 us (20%)
  starting transfers between devices  35.9 us (16%)
  local copies, waits for them, and re-layouts  34.1 us (15%)
  other arithmetic  10.1 us (5%)
    pallas_call x4, Pallas kernels, layer_call(): pl.pallas_call(functools.partial(layer_kernel, heads, span), out_shape=[j...  43.4 us
    ppermute x24, waiting for transfers between devices, exchange(): return lax.ppermute(value, 'mp', pairs)  35.6 us
    unnamed x81, local copies, waits for them, and re-layouts  24.1 us
    all_to_all x4, starting transfers between devices, trade(): lax.all_to_all(value.reshape((shard_count, places) + row_shape), 'dp', sp...  20.4 us
    ppermute x24, starting transfers between devices, exchange(): return lax.ppermute(value, 'mp', pairs)  15.4 us
    all_to_all x4, waiting for transfers between devices, trade(): lax.all_to_all(value.reshape((shard_count, places) + row_shape), 'dp', sp...  7.78 us
    pallas_call x1, Pallas kernels, out_call(): pl.pallas_call(functools.partial(out_kernel, chunks), grid=(columns // bl...  7.73 us
  transfers between devices with their start and end apart: 29, of which 7 were waited for; matrix products, arithmetic and copies ran while one was open for 11% of the time, Pallas kernels for 20%

profile of v2, /device:TPU:0, one launch (start us, length us, event | category | flops | bytes accessed | tf_op | source)
XLA Modules:
  0.0 220.0 jit_solution(10182464120556001654)
XLA Ops:
  7.7 1.0 constant_dynamic-slice_fusion
  8.7 2.6 %collective-permute-start.22 = (bf16[64,2048]{1,0:T(8,128)(2,1)S(1)}, bf16[64,2048]{1,0:T(8,128)(2,1)S(1)}, u32[]{:S(2)}, u32[]{:S(2)}) collective-permute-start(bf16[64,2048]{1,0:T(8,128)(2,1)S(1)} %constant_dynamic-slice_fusion), channel_id=1, source_target_pairs={{0,2},{1,3},{2,0},{3,1},{4,6},{5,7},{6,4},{7,5},{8,10},{9,11},{10,... | collective-permute-start | bytes 786440 | tf_op jit(solution)/shard_map/ppermute | solution.py:338
  11.3 0.7 broadcast_subtract_fusion
  13.8 0.9 fusion.6
  14.7 0.7 fusion.13
  46.4 0.7 copy-done.34
  47.1 1.8 constant_dynamic-slice_fusion.4
  49.0 0.9 pad_maximum_fusion.4
  49.9 0.9 pad_maximum_fusion.2
  50.8 2.0 collective-permute-start.6
  53.3 1.4 gather_fusion
  54.7 5.4 %all-to-all-start = ((bf16[4,2,256,128]{3,2,1,0:T(8,128)(2,1)}), bf16[4,2,256,128]{3,2,1,0:T(8,128)(2,1)}, u32[]{:S(2)}, u32[]{:S(2)}) async-start(bf16[4,2,256,128]{3,2,1,0:T(8,128)(2,1)} %bitcast.11), calls=%async_computation | async-start | bytes 1048576 | tf_op jit(solution)/shard_map/all_to_all | solution.py:341
  60.1 0.9 pad_maximum_fusion.3
  61.0 1.5 collective-permute-start.11
  62.6 24.8 %collective-permute-done.1.t2 = bf16[512,512]{1,0:T(8,128)(2,1)} collective-permute-done((bf16[512,512]{1,0:T(8,128)(2,1)S(1)}, bf16[512,512]{1,0:T(8,128)(2,1)}, u32[]{:S(2)}, u32[]{:S(2)}) %collective-permute-start.1) | collective-permute-done | bytes 524320 | tf_op jit(solution)/shard_map/ppermute | solution.py:338
  87.4 1.0 copy.36
  88.9 1.5 gather_fusion.1
  90.5 1.5 maximum_maximum_fusion.bw
  92.0 0.5 collective-permute-start.7
  92.5 4.9 %all-to-all-start.1 = ((bf16[4,2,256,128]{3,2,1,0:T(8,128)(2,1)}), bf16[4,2,256,128]{3,2,1,0:T(8,128)(2,1)}, u32[]{:S(2)}, u32[]{:S(2)}) async-start(bf16[4,2,256,128]{3,2,1,0:T(8,128)(2,1)} %bitcast.69), calls=%async_computation.1 | async-start | bytes 1048576 | tf_op jit(solution)/shard_map/all_to_all | solution.py:341
  97.4 1.6 copy-done.3
  99.0 1.6 copy-done.5
  100.6 1.0 copy-done.22
  101.6 10.8 %layer.4 = (bf16[128,512]{1,0:T(8,128)(2,1)S(1)}, bf16[128,512]{1,0:T(8,128)(2,1)S(1)}, bf16[128,512]{1,0:T(8,128)(2,1)S(1)}, bf16[128,512]{1,0:T(8,128)(2,1)S(1)}, bf16[8,256,128]{2,1,0:T(8,128)(2,1)S(1)}) custom-call(s32[16]{0:T(128)S(1)} %get-tuple-element.109.meta, bf16[16,128,512]{2,1,0:T(8,128)(2,1)S(1)} %bitcast.48, ...), custom_call_target="tpu_custom_call" | custom-call | flops 8000000000 | bytes 9437184 | tf_op jit(solution)/shard_map/layer/pallas_call | solution.py:238
  112.5 0.6 copy-done.25
  113.2 10.9 %layer.5 = (bf16[128,512]{1,0:T(8,128)(2,1)S(1)}, bf16[128,512]{1,0:T(8,128)(2,1)S(1)}, bf16[128,512]{1,0:T(8,128)(2,1)S(1)}, bf16[128,512]{1,0:T(8,128)(2,1)S(1)}, bf16[8,256,128]{2,1,0:T(8,128)(2,1)S(1)}) custom-call(s32[16]{0:T(128)S(1)} %get-tuple-element.33.meta, bf16[16,128,512]{2,1,0:T(8,128)(2,1)S(1)} %bitcast.52, ...), custom_call_target="tpu_custom_call", output_to_operand_aliasing={{4}: (22, {})} | custom-call | flops 8000000000 | bytes 9437184 | tf_op jit(solution)/shard_map/layer/pallas_call | solution.py:238
  124.0 0.8 copy-done.1
  124.8 0.6 copy-done.27
  125.5 0.6 collective-permute-start.10
  126.1 1.5 collective-permute-start.9
  127.8 2.8 %collective-permute-done.10.refs_7_ = bf16[128,512]{1,0:T(8,128)(2,1)S(1)} collective-permute-done((bf16[128,512]{1,0:T(8,128)(2,1)S(1)}, bf16[128,512]{1,0:T(8,128)(2,1)S(1)}, u32[]{:S(2)}, u32[]{:S(2)}) %collective-permute-start.10) | collective-permute-done | bytes 131104 | tf_op jit(solution)/shard_map/ppermute | solution.py:338
  130.7 0.8 collective-permute-start.4
  131.4 1.6 collective-permute-start.5
  133.0 1.0 collective-permute-done.9.refs_6_
  134.1 0.7 copy-done.8
  134.7 0.7 copy-done.10
  135.9 1.0 collective-permute-done.4.refs_2_
  137.0 0.7 copy-done.12
  137.6 2.2 %collective-permute-done.5.refs_3_ = bf16[128,512]{1,0:T(8,128)(2,1)S(1)} collective-permute-done((bf16[128,512]{1,0:T(8,128)(2,1)S(1)}, bf16[128,512]{1,0:T(8,128)(2,1)S(1)}, u32[]{:S(2)}, u32[]{:S(2)}) %collective-permute-start.5) | collective-permute-done | bytes 131104 | tf_op jit(solution)/shard_map/ppermute | solution.py:338
  139.8 0.6 copy-done.14
  140.5 5.1 %all-to-all-start.2 = ((bf16[4,2,256,128]{3,2,1,0:T(8,128)(2,1)}), bf16[4,2,256,128]{3,2,1,0:T(8,128)(2,1)}, u32[]{:S(2)}, u32[]{:S(2)}) async-start(bf16[4,2,256,128]{3,2,1,0:T(8,128)(2,1)} %bitcast.64), calls=%async_computation.2 | async-start | bytes 1048576 | tf_op jit(solution)/shard_map/all_to_all | solution.py:341
  145.6 1.6 copy-done.4
  147.2 1.6 copy-done.6
  148.8 1.0 copy-done.24
  149.9 10.8 %layer.6 = (bf16[128,512]{1,0:T(8,128)(2,1)S(1)}, bf16[128,512]{1,0:T(8,128)(2,1)S(1)}, bf16[128,512]{1,0:T(8,128)(2,1)S(1)}, bf16[128,512]{1,0:T(8,128)(2,1)S(1)}, bf16[8,256,128]{2,1,0:T(8,128)(2,1)S(1)}) custom-call(s32[16]{0:T(128)S(1)} %get-tuple-element.40.meta, bf16[16,128,512]{2,1,0:T(8,128)(2,1)S(1)} %bitcast.56, ...), custom_call_target="tpu_custom_call" | custom-call | flops 8000000000 | bytes 9437184 | tf_op jit(solution)/shard_map/layer/pallas_call | solution.py:238
  160.7 0.6 copy-done.16
  161.3 0.6 copy-done.17
  162.0 0.6 copy-done.18
  162.7 0.6 copy-done.29
  163.3 10.8 %layer.7 = (bf16[128,512]{1,0:T(8,128)(2,1)S(1)}, bf16[128,512]{1,0:T(8,128)(2,1)S(1)}, bf16[128,512]{1,0:T(8,128)(2,1)S(1)}, bf16[128,512]{1,0:T(8,128)(2,1)S(1)}, bf16[8,256,128]{2,1,0:T(8,128)(2,1)S(1)}) custom-call(s32[16]{0:T(128)S(1)} %get-tuple-element.47.meta, bf16[16,128,512]{2,1,0:T(8,128)(2,1)S(1)} %bitcast.60, ...), custom_call_target="tpu_custom_call", output_to_operand_aliasing={{4}: (22, {})} | custom-call | flops 8000000000 | bytes 9437184 | tf_op jit(solution)/shard_map/layer/pallas_call | solution.py:238
  174.2 0.8 copy-done.2
  174.9 0.7 copy-done.19
  175.6 0.7 copy-done.20
  176.3 0.7 copy-done.21
  176.9 0.7 copy-done.31
  177.6 5.1 %all-to-all-start.3 = ((bf16[4,2,256,128]{3,2,1,0:T(8,128)(2,1)}), bf16[4,2,256,128]{3,2,1,0:T(8,128)(2,1)S(1)}, u32[]{:S(2)}, u32[]{:S(2)}) async-start(bf16[4,2,256,128]{3,2,1,0:T(8,128)(2,1)} %bitcast.65), calls=%async_computation.3 | async-start | bytes 1048576 | tf_op jit(solution)/shard_map/all_to_all | solution.py:341
  182.9 0.6 collective-permute-start.19
  183.6 1.3 collective-permute-start.20
  185.8 3.6 %collective-permute-done.19.refs_14_ = bf16[128,512]{1,0:T(8,128)(2,1)S(1)} collective-permute-done((bf16[128,512]{1,0:T(8,128)(2,1)}, bf16[128,512]{1,0:T(8,128)(2,1)S(1)}, u32[]{:S(2)}, u32[]{:S(2)}) %collective-permute-start.19) | collective-permute-done | bytes 131104 | tf_op jit(solution)/shard_map/ppermute | solution.py:338
  189.5 7.8 %all-to-all-done.3 = bf16[4,2,256,128]{3,2,1,0:T(8,128)(2,1)S(1)} async-done(((bf16[4,2,256,128]{3,2,1,0:T(8,128)(2,1)}), bf16[4,2,256,128]{3,2,1,0:T(8,128)(2,1)S(1)}, u32[]{:S(2)}, u32[]{:S(2)}) %all-to-all-start.3) | async-done | bytes 524320 | tf_op jit(solution)/shard_map/all_to_all | solution.py:341
  197.2 2.1 pad_maximum_fusion
  199.4 3.0 %gather_fusion.2 = bf16[16,256,128]{2,1,0:T(8,128)(2,1)} fusion(bf16[16,256,128]{2,1,0:T(8,128)(2,1)} %pad_maximum_fusion, s32[1024]{0:T(1024)S(1)} %pad_clamp_fusion), kind=kCustom, calls=%fused_computation.2 | custom fusion | bytes 2097216 | tf_op jit(solution)/shard_map/jit(_take)/gather | solution.py:443
  202.4 2.9 %copy.49 = bf16[2,8,256,128]{3,1,2,0:T(8,128)(2,1)} copy(bf16[2,8,256,128]{3,2,1,0:T(8,128)(2,1)} %bitcast.66) | data formatting | bytes 2097152
  205.5 7.7 %project_out.1 = bf16[512,2048]{1,0:T(8,128)(2,1)} custom-call(s32[4]{0:T(128)S(1)} %select_reduce_fusion.12.at_ref, bf16[128,512]{1,0:T(8,128)(2,1)S(1)} %copy-done.26, bf16[128,512]{1,0:T(8,128)(2,1)S(1)} %copy-done.11, bf16[128,512]{1,0:T(8,128)(2,1)S(1)} %copy-done.13, bf16[128,512]{1,0:T(8,128)(2,1)S(1)} %copy-done.15, bf16[128,512]{1,0:T(8,128)(2,1)S(1)} %copy-done.28, ...), custom_call_target="tpu_custom_call" | custom-call | flops 4294967296 | bytes 12582912 | tf_op jit(solution)/shard_map/project_out/pallas_call | solution.py:289
  (138 shorter events, 5.8 us)
Async XLA Ops:
  7.2 133.3 %all-gather.2.cloned.1.call-start = ((), (), s32[]{:S(2)}) async-start(), calls=%async_computation.4 | async-start | bytes 2359296 | tf_op jit(solution)/shard_map/all_gather | solution.py:409
  7.2 90.2 %collective-permute-start = (bf16[2048,512]{1,0:T(8,128)(2,1)}, bf16[2048,512]{1,0:T(8,128)(2,1)}, u32[]{:S(2)}, u32[]{:S(2)}) collective-permute-start(bf16[2048,512]{1,0:T(8,128)(2,1)} %param.13), channel_id=1, source_target_pairs={{0,1},{1,0},{2,3},{3,2},{4,5},{5,4},{6,7},{7,6},{8,9},{9,8},{10,11... | collective-permute-start | bytes 6291464 | tf_op jit(solution)/shard_map/ppermute | solution.py:338
  8.7 37.7 %collective-permute-start.22 = (bf16[64,2048]{1,0:T(8,128)(2,1)S(1)}, bf16[64,2048]{1,0:T(8,128)(2,1)S(1)}, u32[]{:S(2)}, u32[]{:S(2)}) collective-permute-start(bf16[64,2048]{1,0:T(8,128)(2,1)S(1)} %constant_dynamic-slice_fusion), channel_id=1, source_target_pairs={{0,2},{1,3},{2,0},{3,1},{4,6},{5,7},{6,4},{7,5},{8,10},{9,11},{10,... | collective-permute-start | bytes 786440 | tf_op jit(solution)/shard_map/ppermute | solution.py:338
  46.4 0.7 copy-start.34
  49.0 4.0 %copy-start.33 = (bf16[16,32768]{1,0:T(8,128)(2,1)S(1)}, bf16[16,32768]{1,0:T(8,128)(2,1)}, u32[]{:S(2)}) copy-start(bf16[16,32768]{1,0:T(8,128)(2,1)} %param.22) | copy-start | bytes 3145732
  49.9 77.8 %collective-permute-start.16 = (bf16[512,512]{1,0:T(8,128)(2,1)}, bf16[512,512]{1,0:T(8,128)(2,1)}, u32[]{:S(2)}, u32[]{:S(2)}) collective-permute-start(bf16[512,512]{1,0:T(8,128)(2,1)} %bitcast.32), channel_id=1, source_target_pairs={{0,2},{1,3},{2,0},{3,1},{4,6},{5,7},{6,4},{7,5},{8,10},{9,11},{10,... | collective-permute-start | bytes 1572872 | tf_op jit(solution)/shard_map/ppermute | solution.py:338
  50.8 41.2 %collective-permute-start.6 = (bf16[512,512]{1,0:T(8,128)(2,1)}, bf16[512,512]{1,0:T(8,128)(2,1)}, u32[]{:S(2)}, u32[]{:S(2)}) collective-permute-start(bf16[512,512]{1,0:T(8,128)(2,1)} %bitcast.18), channel_id=1, source_target_pairs={{0,2},{1,3},{2,0},{3,1},{4,6},{5,7},{6,4},{7,5},{8,10},{9,11},{10,... | collective-permute-start | bytes 1572872 | tf_op jit(solution)/shard_map/ppermute | solution.py:338
  52.8 34.6 %collective-permute-start.1 = (bf16[512,512]{1,0:T(8,128)(2,1)S(1)}, bf16[512,512]{1,0:T(8,128)(2,1)}, u32[]{:S(2)}, u32[]{:S(2)}) collective-permute-start(bf16[512,512]{1,0:T(8,128)(2,1)S(1)} %bitcast.73), channel_id=1, source_target_pairs={{0,2},{1,3},{2,0},{3,1},{4,6},{5,7},{6,4},{7,5},{8,10},{9,11},{10,... | collective-permute-start | bytes 1572872 | tf_op jit(solution)/shard_map/ppermute | solution.py:338
  53.1 34.3 %copy-start.35 = (bf16[2048,8]{0,1:T(8,128)(2,1)S(1)}, bf16[2048,8]{0,1:T(8,128)(2,1)}, u32[]{:S(2)}) copy-start(bf16[2048,8]{0,1:T(8,128)(2,1)} %param.17) | copy-start | bytes 98308
  53.1 35.3 %copy-start.36 = (f32[512]{0:T(512)S(1)}, f32[512]{0:T(512)}, u32[]{:S(2)}) copy-start(f32[512]{0:T(512)} %param.20) | copy-start | bytes 6148
  53.1 35.6 %copy-start.37 = (f32[8]{0:T(128)S(1)}, f32[8]{0:T(128)}, u32[]{:S(2)}) copy-start(f32[8]{0:T(128)} %param.18) | copy-start | bytes 100
  53.2 35.7 %copy-start.38 = (f32[8]{0:T(128)S(1)}, f32[8]{0:T(128)}, u32[]{:S(2)}) copy-start(f32[8]{0:T(128)} %param.19) | copy-start | bytes 100
  54.7 37.8 %all-to-all-start = ((bf16[4,2,256,128]{3,2,1,0:T(8,128)(2,1)}), bf16[4,2,256,128]{3,2,1,0:T(8,128)(2,1)}, u32[]{:S(2)}, u32[]{:S(2)}) async-start(bf16[4,2,256,128]{3,2,1,0:T(8,128)(2,1)} %bitcast.11), calls=%async_computation | async-start | bytes 1048576 | tf_op jit(solution)/shard_map/all_to_all | solution.py:341
  61.0 52.2 %collective-permute-start.11 = (bf16[512,512]{1,0:T(8,128)(2,1)}, bf16[512,512]{1,0:T(8,128)(2,1)}, u32[]{:S(2)}, u32[]{:S(2)}) collective-permute-start(bf16[512,512]{1,0:T(8,128)(2,1)} %bitcast.24), channel_id=1, source_target_pairs={{0,2},{1,3},{2,0},{3,1},{4,6},{5,7},{6,4},{7,5},{8,10},{9,11},{10,... | collective-permute-start | bytes 1572872 | tf_op jit(solution)/shard_map/ppermute | solution.py:338
  87.4 10.0 %collective-permute-start.2 = (bf16[512,512]{1,0:T(8,128)(2,1)}, bf16[512,512]{1,0:T(8,128)(2,1)}, u32[]{:S(2)}, u32[]{:S(2)}) collective-permute-start(bf16[512,512]{1,0:T(8,128)(2,1)} %collective-permute-done.1.t2), channel_id=1, source_target_pairs={{0,1},{1,0},{2,3},{3,2},{4,5},{5,4},{6,7},{7,6},{8,9},{9,8},{10,11... | collective-permute-start | bytes 1572872 | tf_op jit(solution)/shard_map/ppermute | solution.py:338
  88.9 8.4 %copy-start = (bf16[2048,512]{1,0:T(8,128)(2,1)S(1)}, bf16[2048,512]{1,0:T(8,128)(2,1)}, u32[]{:S(2)}) copy-start(bf16[2048,512]{1,0:T(8,128)(2,1)} %param.13) | copy-start | bytes 6291460
  92.0 21.2 %collective-permute-start.7 = (bf16[512,512]{1,0:T(8,128)(2,1)}, bf16[512,512]{1,0:T(8,128)(2,1)}, u32[]{:S(2)}, u32[]{:S(2)}) collective-permute-start(bf16[512,512]{1,0:T(8,128)(2,1)} %collective-permute-done.6.t2), channel_id=1, source_target_pairs={{0,1},{1,0},{2,3},{3,2},{4,5},{5,4},{6,7},{7,6},{8,9},{9,8},{10,11... | collective-permute-start | bytes 1572872 | tf_op jit(solution)/shard_map/ppermute | solution.py:338
  92.5 48.0 %all-to-all-start.1 = ((bf16[4,2,256,128]{3,2,1,0:T(8,128)(2,1)}), bf16[4,2,256,128]{3,2,1,0:T(8,128)(2,1)}, u32[]{:S(2)}, u32[]{:S(2)}) async-start(bf16[4,2,256,128]{3,2,1,0:T(8,128)(2,1)} %bitcast.69), calls=%async_computation.1 | async-start | bytes 1048576 | tf_op jit(solution)/shard_map/all_to_all | solution.py:341
  97.4 1.6 copy-start.3
  99.0 1.6 copy-start.5
  100.6 1.0 copy-start.22
  101.6 11.5 %copy-start.23 = (bf16[512,512]{1,0:T(8,128)(2,1)S(1)}, bf16[512,512]{1,0:T(8,128)(2,1)}, u32[]{:S(2)}) copy-start(bf16[512,512]{1,0:T(8,128)(2,1)} %constant.88.clone.order) | copy-start | bytes 1572868
  113.1 32.5 %collective-permute-start.12 = (bf16[512,512]{1,0:T(8,128)(2,1)}, bf16[512,512]{1,0:T(8,128)(2,1)}, u32[]{:S(2)}, u32[]{:S(2)}) collective-permute-start(bf16[512,512]{1,0:T(8,128)(2,1)} %collective-permute-done.11.t2), channel_id=1, source_target_pairs={{0,1},{1,0},{2,3},{3,2},{4,5},{5,4},{6,7},{7,6},{8,9},{9,8},{10,11... | collective-permute-start | bytes 1572872 | tf_op jit(solution)/shard_map/ppermute | solution.py:338
  124.0 0.8 copy-start.1
  125.5 5.2 %collective-permute-start.10 = (bf16[128,512]{1,0:T(8,128)(2,1)S(1)}, bf16[128,512]{1,0:T(8,128)(2,1)S(1)}, u32[]{:S(2)}, u32[]{:S(2)}) collective-permute-start(bf16[128,512]{1,0:T(8,128)(2,1)S(1)} %get-tuple-element.38), channel_id=1, source_target_pairs={{0,3},{1,2},{2,1},{3,0},{4,7},{5,6},{6,5},{7,4},{8,11},{9,10},{10,... | collective-permute-start | bytes 393224 | tf_op jit(solution)/shard_map/ppermute | solution.py:338
  126.1 5.3 %collective-permute-start.8 = (bf16[128,512]{1,0:T(8,128)(2,1)S(1)}, bf16[128,512]{1,0:T(8,128)(2,1)S(1)}, u32[]{:S(2)}, u32[]{:S(2)}) collective-permute-start(bf16[128,512]{1,0:T(8,128)(2,1)S(1)} %get-tuple-element.36), channel_id=1, source_target_pairs={{0,1},{1,0},{2,3},{3,2},{4,5},{5,4},{6,7},{7,6},{8,9},{9,8},{10,11... | collective-permute-start | bytes 393224 | tf_op jit(solution)/shard_map/ppermute | solution.py:338
  126.1 7.9 %collective-permute-start.9 = (bf16[128,512]{1,0:T(8,128)(2,1)S(1)}, bf16[128,512]{1,0:T(8,128)(2,1)S(1)}, u32[]{:S(2)}, u32[]{:S(2)}) collective-permute-start(bf16[128,512]{1,0:T(8,128)(2,1)S(1)} %get-tuple-element.37), channel_id=1, source_target_pairs={{0,2},{1,3},{2,0},{3,1},{4,6},{5,7},{6,4},{7,5},{8,10},{9,11},{10,... | collective-permute-start | bytes 393224 | tf_op jit(solution)/shard_map/ppermute | solution.py:338
  127.6 7.1 %collective-permute-start.3 = (bf16[128,512]{1,0:T(8,128)(2,1)S(1)}, bf16[128,512]{1,0:T(8,128)(2,1)S(1)}, u32[]{:S(2)}, u32[]{:S(2)}) collective-permute-start(bf16[128,512]{1,0:T(8,128)(2,1)S(1)} %get-tuple-element.30), channel_id=1, source_target_pairs={{0,1},{1,0},{2,3},{3,2},{4,5},{5,4},{6,7},{7,6},{8,9},{9,8},{10,11... | collective-permute-start | bytes 393224 | tf_op jit(solution)/shard_map/ppermute | solution.py:338
  130.7 6.3 %collective-permute-start.4 = (bf16[128,512]{1,0:T(8,128)(2,1)S(1)}, bf16[128,512]{1,0:T(8,128)(2,1)S(1)}, u32[]{:S(2)}, u32[]{:S(2)}) collective-permute-start(bf16[128,512]{1,0:T(8,128)(2,1)S(1)} %get-tuple-element.31), channel_id=1, source_target_pairs={{0,2},{1,3},{2,0},{3,1},{4,6},{5,7},{6,4},{7,5},{8,10},{9,11},{10,... | collective-permute-start | bytes 393224 | tf_op jit(solution)/shard_map/ppermute | solution.py:338
  131.4 8.4 %collective-permute-start.5 = (bf16[128,512]{1,0:T(8,128)(2,1)S(1)}, bf16[128,512]{1,0:T(8,128)(2,1)S(1)}, u32[]{:S(2)}, u32[]{:S(2)}) collective-permute-start(bf16[128,512]{1,0:T(8,128)(2,1)S(1)} %get-tuple-element.32), channel_id=1, source_target_pairs={{0,3},{1,2},{2,1},{3,0},{4,7},{5,6},{6,5},{7,4},{8,11},{9,10},{10,... | collective-permute-start | bytes 393224 | tf_op jit(solution)/shard_map/ppermute | solution.py:338
  134.1 0.7 copy-start.8
  134.7 50.2 %collective-permute-start.21 = (bf16[512,2048]{1,0:T(8,128)(2,1)}, bf16[512,2048]{1,0:T(8,128)(2,1)}, u32[]{:S(2)}, u32[]{:S(2)}) collective-permute-start(bf16[512,2048]{1,0:T(8,128)(2,1)} %refs_16_.1), channel_id=1, source_target_pairs={{0,1},{1,0},{2,3},{3,2},{4,5},{5,4},{6,7},{7,6},{8,9},{9,8},{10,11... | collective-permute-start | bytes 6291464 | tf_op jit(solution)/shard_map/ppermute | solution.py:338
  134.7 0.7 copy-start.10
  135.4 27.9 %collective-permute-start.17 = (bf16[512,512]{1,0:T(8,128)(2,1)}, bf16[512,512]{1,0:T(8,128)(2,1)}, u32[]{:S(2)}, u32[]{:S(2)}) collective-permute-start(bf16[512,512]{1,0:T(8,128)(2,1)} %collective-permute-done.16.t2), channel_id=1, source_target_pairs={{0,1},{1,0},{2,3},{3,2},{4,5},{5,4},{6,7},{7,6},{8,9},{9,8},{10,11... | collective-permute-start | bytes 1572872 | tf_op jit(solution)/shard_map/ppermute | solution.py:338
  137.0 0.7 copy-start.12
  139.8 0.6 copy-start.14
  140.5 64.9 %collective-permute-start.23 = (bf16[512,2048]{1,0:T(8,128)(2,1)}, bf16[512,2048]{1,0:T(8,128)(2,1)}, u32[]{:S(2)}, u32[]{:S(2)}) collective-permute-start(bf16[512,2048]{1,0:T(8,128)(2,1)} %all-gather.2.cloned.1.call-done.refs_18_), channel_id=1, source_target_pairs={{0,1},{1,0},{2,3},{3,2},{4,5},{5,4},{6,7},{7,6},{8,9},{9,8},{10,11... | collective-permute-start | bytes 6291464 | tf_op jit(solution)/shard_map/ppermute | solution.py:338
  140.5 37.1 %all-to-all-start.2 = ((bf16[4,2,256,128]{3,2,1,0:T(8,128)(2,1)}), bf16[4,2,256,128]{3,2,1,0:T(8,128)(2,1)}, u32[]{:S(2)}, u32[]{:S(2)}) async-start(bf16[4,2,256,128]{3,2,1,0:T(8,128)(2,1)} %bitcast.64), calls=%async_computation.2 | async-start | bytes 1048576 | tf_op jit(solution)/shard_map/all_to_all | solution.py:341
  145.6 1.6 copy-start.4
  147.2 1.6 copy-start.6
  148.8 1.0 copy-start.24
  162.0 0.7 copy-start.18
  162.6 0.7 copy-start.29
  174.1 0.8 copy-start.2
  174.9 0.7 copy-start.19
  175.6 0.7 copy-start.20
  176.3 0.7 copy-start.21
  176.9 0.7 copy-start.31
  177.6 19.6 %all-to-all-start.3 = ((bf16[4,2,256,128]{3,2,1,0:T(8,128)(2,1)}), bf16[4,2,256,128]{3,2,1,0:T(8,128)(2,1)S(1)}, u32[]{:S(2)}, u32[]{:S(2)}) async-start(bf16[4,2,256,128]{3,2,1,0:T(8,128)(2,1)} %bitcast.65), calls=%async_computation.3 | async-start | bytes 1048576 | tf_op jit(solution)/shard_map/all_to_all | solution.py:341
  182.8 2.5 %collective-permute-start.18 = (bf16[128,512]{1,0:T(8,128)(2,1)}, bf16[128,512]{1,0:T(8,128)(2,1)S(1)}, u32[]{:S(2)}, u32[]{:S(2)}) collective-permute-start(bf16[128,512]{1,0:T(8,128)(2,1)} %copy-done.21), channel_id=1, source_target_pairs={{0,1},{1,0},{2,3},{3,2},{4,5},{5,4},{6,7},{7,6},{8,9},{9,8},{10,11... | collective-permute-start | bytes 393224 | tf_op jit(solution)/shard_map/ppermute | solution.py:338
  182.9 6.6 %collective-permute-start.19 = (bf16[128,512]{1,0:T(8,128)(2,1)}, bf16[128,512]{1,0:T(8,128)(2,1)S(1)}, u32[]{:S(2)}, u32[]{:S(2)}) collective-permute-start(bf16[128,512]{1,0:T(8,128)(2,1)} %copy-done.20), channel_id=1, source_target_pairs={{0,2},{1,3},{2,0},{3,1},{4,6},{5,7},{6,4},{7,5},{8,10},{9,11},{10,... | collective-permute-start | bytes 393224 | tf_op jit(solution)/shard_map/ppermute | solution.py:338
  183.6 21.7 %collective-permute-start.20 = (bf16[128,512]{1,0:T(8,128)(2,1)}, bf16[128,512]{1,0:T(8,128)(2,1)S(1)}, u32[]{:S(2)}, u32[]{:S(2)}) collective-permute-start(bf16[128,512]{1,0:T(8,128)(2,1)} %copy-done.19), channel_id=1, source_target_pairs={{0,3},{1,2},{2,1},{3,0},{4,7},{5,6},{6,5},{7,4},{8,11},{9,10},{10,... | collective-permute-start | bytes 393224 | tf_op jit(solution)/shard_map/ppermute | solution.py:338
  184.9 20.4 %collective-permute-start.13 = (bf16[128,512]{1,0:T(8,128)(2,1)}, bf16[128,512]{1,0:T(8,128)(2,1)S(1)}, u32[]{:S(2)}, u32[]{:S(2)}) collective-permute-start(bf16[128,512]{1,0:T(8,128)(2,1)} %copy-done.18), channel_id=1, source_target_pairs={{0,1},{1,0},{2,3},{3,2},{4,5},{5,4},{6,7},{7,6},{8,9},{9,8},{10,11... | collective-permute-start | bytes 393224 | tf_op jit(solution)/shard_map/ppermute | solution.py:338
  185.3 20.1 %collective-permute-start.14 = (bf16[128,512]{1,0:T(8,128)(2,1)}, bf16[128,512]{1,0:T(8,128)(2,1)S(1)}, u32[]{:S(2)}, u32[]{:S(2)}) collective-permute-start(bf16[128,512]{1,0:T(8,128)(2,1)} %copy-done.17), channel_id=1, source_target_pairs={{0,2},{1,3},{2,0},{3,1},{4,6},{5,7},{6,4},{7,5},{8,10},{9,11},{10,... | collective-permute-start | bytes 393224 | tf_op jit(solution)/shard_map/ppermute | solution.py:338
  189.5 15.9 %collective-permute-start.15 = (bf16[128,512]{1,0:T(8,128)(2,1)}, bf16[128,512]{1,0:T(8,128)(2,1)}, u32[]{:S(2)}, u32[]{:S(2)}) collective-permute-start(bf16[128,512]{1,0:T(8,128)(2,1)} %copy-done.16), channel_id=1, source_target_pairs={{0,3},{1,2},{2,1},{3,0},{4,7},{5,6},{6,5},{7,4},{8,11},{9,10},{10,... | collective-permute-start | bytes 393224 | tf_op jit(solution)/shard_map/ppermute | solution.py:338
  199.3 6.0 %copy-start.7 = (bf16[512,2048]{1,0:T(8,128)(2,1)S(1)}, bf16[512,2048]{1,0:T(8,128)(2,1)}, u32[]{:S(2)}) copy-start(bf16[512,2048]{1,0:T(8,128)(2,1)} %all-gather.2.cloned.1.call-done.refs_18_) | copy-start | bytes 6291460
  199.4 6.0 %copy-start.9 = (bf16[128,512]{1,0:T(8,128)(2,1)S(1)}, bf16[128,512]{1,0:T(8,128)(2,1)}, u32[]{:S(2)}) copy-start(bf16[128,512]{1,0:T(8,128)(2,1)} %copy-done.8) | copy-start | bytes 393220
  199.4 6.0 %copy-start.11 = (bf16[128,512]{1,0:T(8,128)(2,1)S(1)}, bf16[128,512]{1,0:T(8,128)(2,1)}, u32[]{:S(2)}) copy-start(bf16[128,512]{1,0:T(8,128)(2,1)} %copy-done.10) | copy-start | bytes 393220
  199.4 6.1 %copy-start.13 = (bf16[128,512]{1,0:T(8,128)(2,1)S(1)}, bf16[128,512]{1,0:T(8,128)(2,1)}, u32[]{:S(2)}) copy-start(bf16[128,512]{1,0:T(8,128)(2,1)} %copy-done.12) | copy-start | bytes 393220
  199.4 6.1 %copy-start.15 = (bf16[128,512]{1,0:T(8,128)(2,1)S(1)}, bf16[128,512]{1,0:T(8,128)(2,1)}, u32[]{:S(2)}) copy-start(bf16[128,512]{1,0:T(8,128)(2,1)} %copy-done.14) | copy-start | bytes 393220
  202.4 3.0 %copy-start.26 = (bf16[128,512]{1,0:T(8,128)(2,1)S(1)}, bf16[128,512]{1,0:T(8,128)(2,1)}, u32[]{:S(2)}) copy-start(bf16[128,512]{1,0:T(8,128)(2,1)} %copy-done.25) | copy-start | bytes 393220
  202.4 3.0 %copy-start.28 = (bf16[128,512]{1,0:T(8,128)(2,1)S(1)}, bf16[128,512]{1,0:T(8,128)(2,1)}, u32[]{:S(2)}) copy-start(bf16[128,512]{1,0:T(8,128)(2,1)} %copy-done.27) | copy-start | bytes 393220
  202.4 3.0 %copy-start.30 = (bf16[128,512]{1,0:T(8,128)(2,1)S(1)}, bf16[128,512]{1,0:T(8,128)(2,1)}, u32[]{:S(2)}) copy-start(bf16[128,512]{1,0:T(8,128)(2,1)} %copy-done.29) | copy-start | bytes 393220
  202.4 3.1 %copy-start.32 = (bf16[128,512]{1,0:T(8,128)(2,1)S(1)}, bf16[128,512]{1,0:T(8,128)(2,1)}, u32[]{:S(2)}) copy-start(bf16[128,512]{1,0:T(8,128)(2,1)} %copy-done.31) | copy-start | bytes 393220
  (4 other events, 2.6 us)
Sparse Core Ops, SparseCore 0:
  47.2 62.7 all-gather.1

commit v3 on v2

v3 whole, which is shorter than its diff:
```python
import functools

import jax
import jax.numpy as jnp
import numpy as np
from jax import lax
from jax.experimental import pallas as pl
from jax.experimental.pallas import tpu as pltpu
from jax.sharding import PartitionSpec as P

BF = jnp.bfloat16
F32 = jnp.float32
ANY = pl.BlockSpec(memory_space=pl.ANY)
VMEM = pl.BlockSpec(memory_space=pltpu.VMEM)
SMEM = pl.BlockSpec(memory_space=pltpu.SMEM)
NT = (((1,), (1,)), ((), ()))


def pick(values, index):
    chosen = index[..., None] == jnp.arange(values.shape[0], dtype=jnp.int32)
    return jnp.sum(jnp.where(chosen, values, 0), axis=-1, dtype=jnp.int32)


def count_before(same, order):
    earlier = order[None, :] < order[:, None]
    return jnp.sum((same & earlier).astype(jnp.int32), axis=1)


def split_sessions(home_rows, block, per_target):
    total = home_rows.shape[0]
    session = jnp.arange(total, dtype=jnp.int32)
    server = session // block
    shard = home_rows // block
    same_server = server[:, None] == server[None, :]
    same_pair = same_server & (shard[:, None] == shard[None, :])
    rank = count_before(same_pair, session)
    size = jnp.sum(same_pair.astype(jnp.int32), axis=1)
    single = (rank ^ 1) >= size
    both_single = same_server & single[:, None] & single[None, :]
    single_rank = count_before(both_single, session)
    partners = (
        same_pair
        & ~single[:, None]
        & ~single[None, :]
        & (rank[None, :] == (rank ^ 1)[:, None])
    ) | (both_single & (single_rank[None, :] == (single_rank ^ 1)[:, None]))
    partner = jnp.sum(jnp.where(partners, session[None, :], 0), axis=1, dtype=jnp.int32)
    step = partner ^ 1
    lowest = session
    reach = 1
    while reach < block // 2:
        lowest = jnp.minimum(lowest, pick(lowest, step))
        step = pick(step, step)
        reach *= 2
    half = (lowest > pick(lowest, partner)).astype(jnp.int32)
    same_half = half[:, None] == half[None, :]
    target = session // per_target
    turn = count_before(same_half & (target[:, None] == target[None, :]), session)
    chunk = half * (per_target // 2) + turn
    place = count_before(same_half & same_pair, session)
    return server, shard, half, chunk, place


def copy_kernel(groups, index, source, *refs):
    outs, sems = refs[:-1], refs[-1]
    copies = []
    for k, out in enumerate(outs):
        for j in range(groups):
            n = k * groups + j
            copies.append(
                pltpu.make_async_copy(source.at[index[n]], out.at[j], sems.at[n])
            )
            copies[-1].start()
    for copy in copies:
        copy.wait()


def copy_rows(index, source, outs, name):
    groups = index.shape[0] // outs
    return pl.pallas_call(
        functools.partial(copy_kernel, groups),
        out_shape=[jax.ShapeDtypeStruct((groups,) + source.shape[1:], source.dtype)] * outs,
        in_specs=[SMEM, ANY],
        out_specs=[ANY] * outs,
        scratch_shapes=[pltpu.SemaphoreType.DMA((index.shape[0],))],
        compiler_params=pltpu.CompilerParams(vmem_limit_bytes=58 * 2**20),
        cost_estimate=pl.CostEstimate(
            flops=0, bytes_accessed=2 * source.size * 2, transcendentals=0
        ),
        name=name,
    )(index, source)


def layer_kernel(
    heads, span, aliased, meta, tokens, sibling, across, far, xw_any, zw_any, bw_any, bias, rate,
    gain, order, inbound, *refs,
):
    refs = refs[5 if aliased & 2 else (1 if aliased & 1 else 0):]
    n0, n1, n2, n3, outgoing = refs[:5]
    piece0, piece1, piece2, piece3, xw, zw, bw, state4, xs, zs, xt, fresh, sems, out_sems = refs[5:]
    normed_out = (n0, n1, n2, n3)
    pieces = (piece0, piece1, piece2, piece3)
    me = meta[12]
    depth = across.shape[1]
    quads = heads // 4
    copies = []

    def bring(source, target):
        copies.append(pltpu.make_async_copy(source, target, sems.at[len(copies)]))
        copies[-1].start()

    for d in range(4):
        rows = pl.ds(d * span, span)
        bring(tokens.at[meta[d]], piece0.at[rows])
        bring(sibling.at[meta[d]], piece1.at[rows])
    bring(across, piece2)
    for d in range(4):
        bring(far.at[pl.ds((d ^ 1) * span, span)], piece3.at[pl.ds(d * span, span)])
    bring(bw_any, bw)
    early = len(copies)
    bring(xw_any, xw)
    bring(zw_any, zw)
    for d in range(4):
        bring(inbound.at[meta[4 + d]], state4.at[d])

    def project(weight, columns):
        total = None
        for d in range(4):
            first = pl.multiple_of((me ^ d) * depth, depth)
            part = jnp.dot(
                pieces[d][...], weight[pl.ds(first, depth), columns], preferred_element_type=F32
            )
            total = part if total is None else total + part
        return total

    for copy in copies[:early]:
        copy.wait()
    bcs = project(bw, slice(None))

    lane = lax.broadcasted_iota(jnp.int32, (span, 128), 1)
    row = lax.broadcasted_iota(jnp.int32, (span, 128), 0)
    low = lane < 64
    causal = row >= lane
    lane8 = lax.broadcasted_iota(jnp.int32, (heads, span), 1)
    lane32 = lax.broadcasted_iota(jnp.int32, (heads * 4, span), 1)
    raw = jnp.concatenate(
        [jnp.transpose(bcs[d * span : (d + 1) * span, 128:256])[:heads] + bias[...] for d in range(4)],
        axis=0,
    )
    alive = jnp.concatenate([(lane8 < meta[8 + d]).astype(F32) for d in range(4)], axis=0)
    steps = (jnp.maximum(raw, 0.0) + jnp.log1p(jnp.exp(-jnp.abs(raw)))) * alive
    totals = steps * jnp.concatenate([rate[...]] * 4, axis=0)
    shift = 1
    while shift < span:
        totals = totals + jnp.where(lane32 >= shift, pltpu.roll(totals, shift, 1), 0.0)
        shift *= 2
    lasts = totals[:, span - 1 : span]
    weight_rows = jnp.exp(jnp.minimum(totals - lasts, 0.0)) * steps
    kept = jnp.exp(-lasts)
    cum = jnp.transpose(
        jnp.concatenate([totals, jnp.zeros((128 - heads * 4, span), F32)], axis=0)
    )

    copies[early].wait()
    for quad in range(quads):
        columns = slice(quad * 256, quad * 256 + 256)
        xs[:, columns] = project(xw, columns).astype(BF)
    copies[early + 1].wait()
    for quad in range(quads):
        columns = slice(quad * 256, quad * 256 + 256)
        zs[:, columns] = project(zw, columns).astype(BF)
    for copy in copies[early + 2 :]:
        copy.wait()

    wide = lax.broadcasted_iota(jnp.int32, (span, 256), 1) // 64
    head_masks = [(wide == k).astype(F32).astype(BF) for k in range(4)]
    sends = []
    for d in range(4):
        rows = slice(d * span, (d + 1) * span)
        count = meta[8 + d]
        bc = bcs[rows, 0:128]
        turned = pltpu.roll(bc, 64, 1)
        b_low = jnp.where(low, bc, 0.0).astype(BF)
        b_high = jnp.where(low, 0.0, turned).astype(BF)
        c_low = jnp.where(low, turned, 0.0).astype(BF)
        c_high = jnp.where(low, 0.0, bc).astype(BF)
        scores = lax.dot_general(c_low, b_low, NT, preferred_element_type=F32)
        scores = jnp.where(causal, scores, 0.0)
        state = state4[d]
        carried = lax.dot_general(
            jnp.concatenate([c_low, c_high], axis=0), state, NT, preferred_element_type=F32
        ).astype(BF)
        b_both = jnp.concatenate([b_low, b_high], axis=0)
        gated = []
        squares = None
        for quad in range(quads):
            columns = slice(quad * 256, quad * 256 + 256)
            part = slice(quad * 128, quad * 128 + 128)
            x = xs[rows, columns]
            mixes = []
            levels = []
            for k in range(4):
                head = d * heads + quad * 4 + k
                level = jnp.broadcast_to(cum[:, head : head + 1], (span, 128))
                gap = jnp.minimum(totals[head : head + 1, :] - level, 0.0)
                mixes.append((jnp.exp(gap) * steps[head : head + 1, :] * scores).astype(BF))
                levels.append(level)
            diagonal = jnp.dot(
                jnp.concatenate(mixes, axis=1),
                jnp.concatenate([x * head_masks[k] for k in range(4)], axis=0),
                preferred_element_type=F32,
            )
            before = jnp.dot(
                jnp.concatenate([carried[:span, part], carried[span:, part]], axis=1),
                order[...],
                preferred_element_type=F32,
            )
            fade = jnp.exp(
                -jnp.concatenate(
                    [jnp.where(low, levels[0], levels[1]), jnp.where(low, levels[2], levels[3])],
                    axis=1,
                )
            )
            gate = zs[rows, columns].astype(F32)
            value = (diagonal + before * fade) * (gate / (1.0 + jnp.exp(-gate)))
            gated.append(value)
            own = jnp.sum(value * value, axis=1, keepdims=True)
            squares = own if squares is None else squares + own
            flipped = jnp.transpose(x.astype(F32))
            first_head = d * heads + quad * 4
            xt[d, quad] = flipped * jnp.concatenate(
                [
                    jnp.broadcast_to(weight_rows[first_head + k : first_head + k + 1, :], (64, span))
                    for k in range(4)
                ],
                axis=0,
            )
            even = xt[d, quad, pl.ds(0, 128, stride=2), :].astype(BF)
            odd = xt[d, quad, pl.ds(1, 128, stride=2), :].astype(BF)
            added = jnp.dot(
                jnp.concatenate([even, odd], axis=1), b_both, preferred_element_type=F32
            )
            keep_rows = jnp.concatenate(
                [
                    jnp.broadcast_to(kept[first_head + k : first_head + k + 1, :], (32, 128))
                    for k in range(4)
                ],
                axis=0,
            )
            fresh[d, part, :] = (keep_rows * state[part].astype(F32) + added).astype(BF)
        sends.append(
            pltpu.make_async_copy(fresh.at[d], outgoing.at[meta[4 + d]], out_sems.at[d])
        )
        sends[-1].start()
        inverse = lax.rsqrt(squares * (1.0 / (heads * 64)) + 1e-05)
        inverse = jnp.where(row[:, :1] < count, inverse, 0.0)
        for quad in range(quads):
            columns = slice(quad * 256, quad * 256 + 256)
            normed_out[d][:, columns] = (gated[quad] * inverse * gain[:, columns]).astype(BF)
    for send in sends:
        send.wait()


def layer_call(meta, tokens, sibling, across, far, weights, small, inbound, turn, turns, earlier):
    rows, depth = across.shape
    heads = small[0].shape[0]
    width = weights[0].shape[1]
    span = rows // 4
    row_shape = inbound.shape[1:]
    operands = [tokens, sibling, across, far, *weights, *small, inbound]
    aliases = {}
    aliased = 0
    if earlier is not None:
        aliased = 1 if len(earlier) == 1 else 2
        first = 1 + len(operands)
        for k in range(len(earlier)):
            aliases[first + k] = k + 5 - len(earlier)
        operands += list(earlier)
    return pl.pallas_call(
        functools.partial(layer_kernel, heads, span, aliased),
        out_shape=[jax.ShapeDtypeStruct((turns * span, width), BF)] * 4
        + [jax.ShapeDtypeStruct(inbound.shape, BF)],
        grid_spec=pltpu.PrefetchScalarGridSpec(
            num_scalar_prefetch=1,
            grid=(1,),
            in_specs=[ANY] * 7 + [VMEM] * 4 + [ANY] * (len(operands) - 11),
            out_specs=[pl.BlockSpec((span, width), lambda i, meta: (turn, 0))] * 4 + [ANY],
            scratch_shapes=[
                *[pltpu.VMEM((rows, depth), BF)] * 4,
                *[pltpu.VMEM(weight.shape, BF) for weight in weights],
                pltpu.VMEM((4,) + row_shape, BF),
                pltpu.VMEM((rows, width), BF),
                pltpu.VMEM((rows, width), BF),
                pltpu.VMEM((4, heads // 4, 256, span), F32),
                pltpu.VMEM((4,) + row_shape, BF),
                pltpu.SemaphoreType.DMA((20,)),
                pltpu.SemaphoreType.DMA((4,)),
            ],
        ),
        input_output_aliases=aliases,
        compiler_params=pltpu.CompilerParams(vmem_limit_bytes=58 * 2**20),
        cost_estimate=pl.CostEstimate(
            flops=8 * 10**9, bytes_accessed=9 * 2**20, transcendentals=0
        ),
        name="layer",
    )(meta, *operands)


def out_kernel(where, span, at_ref, *refs):
    weights, out = refs[-5:-1], refs[-1]
    for chunk, (first, offset) in enumerate(where):
        total = None
        for d in range(4):
            piece = refs[first * 4 + d][offset * span : (offset + 1) * span, :]
            part = jnp.dot(piece, weights[d][...], preferred_element_type=F32)
            total = part if total is None else total + part
        out[at_ref[chunk]] = total.astype(BF)


def out_call(at, normed, weights, span):
    depth = normed[0].shape[1]
    columns = weights[0].shape[1]
    chunks = at.shape[0]
    block = 512
    where = [
        (k, offset)
        for k in range(len(normed) // 4)
        for offset in range(normed[k * 4].shape[0] // span)
    ]
    return pl.pallas_call(
        functools.partial(out_kernel, where, span),
        grid=(columns // block,),
        out_shape=jax.ShapeDtypeStruct((chunks, span, columns), BF),
        in_specs=[SMEM]
        + [pl.BlockSpec(piece.shape, lambda j: (0, 0)) for piece in normed]
        + [pl.BlockSpec((depth, block), lambda j: (0, j))] * 4,
        out_specs=pl.BlockSpec((chunks, span, block), lambda j: (0, 0, j)),
        compiler_params=pltpu.CompilerParams(vmem_limit_bytes=58 * 2**20),
        cost_estimate=pl.CostEstimate(
            flops=2 * chunks * span * depth * 4 * columns,
            bytes_accessed=12 * 2**20,
            transcendentals=0,
        ),
        name="project_out",
    )(at, *normed, *weights)


def gather_kernel(sessions, slots, index, first, second, out):
    lines = out.shape[1] // 128
    picked = []
    for r in range(sessions):
        slot = index[r]
        inside = jnp.minimum(slot, slots - 1)
        other = jnp.maximum(slot - slots, 0)
        scale = jnp.where(slot < slots, 1.0, 0.0)
        picked.append(
            jnp.where(scale > 0.5, first[inside].astype(F32), second[other].astype(F32))
        )
    block = jnp.stack(picked, axis=0)
    turned = jnp.swapaxes(block, 0, 1)
    for j in range(lines):
        out[:, j * 128 : (j + 1) * 128] = turned[j].astype(BF)


def gather_call(index, first, second):
    sessions = index.shape[0]
    slots, lines, lanes = first.shape
    block = 16
    return pl.pallas_call(
        functools.partial(gather_kernel, sessions, slots),
        grid=(lines // block,),
        out_shape=jax.ShapeDtypeStruct((sessions, lines * lanes), BF),
        in_specs=[SMEM] + [pl.BlockSpec((slots, block, lanes), lambda j: (0, j, 0))] * 2,
        out_specs=pl.BlockSpec((sessions, block * lanes), lambda j: (0, j)),
        compiler_params=pltpu.CompilerParams(vmem_limit_bytes=58 * 2**20),
        cost_estimate=pl.CostEstimate(
            flops=0, bytes_accessed=2 * 2**20, transcendentals=0
        ),
        name="gather_states",
    )(index, first, second)


def after(value, *others):
    return lax.optimization_barrier((value,) + others)[0]


def body(
    tokens,
    x_weight,
    z_weight,
    bc_weight,
    dt_weight,
    dt_bias,
    decay_rate,
    norm_gain,
    out_weight,
    store_states,
    home_rows,
    event_counts,
):
    shard_count = lax.axis_size("dp")
    model_shards = lax.axis_size("mp")
    shard_index = lax.axis_index("dp")
    me = lax.axis_index("mp")
    sessions_here, state_width = store_states.shape
    heads = dt_bias.shape[0]
    width = x_weight.shape[1]
    depth = tokens.shape[1]
    span = tokens.shape[0] // sessions_here
    chunks = sessions_here // model_shards
    capacity = max(2, (sessions_here + shard_count - 1) // shard_count)
    places = (capacity + 1) // 2
    slot_count = shard_count * places
    row_shape = (state_width // 128, 128)

    def exchange(value, distance):
        pairs = [(j, j ^ distance) for j in range(model_shards)]
        return lax.ppermute(value, "mp", pairs)

    def trade(value):
        return lax.all_to_all(
            value.reshape((shard_count, places) + row_shape),
            "dp",
            split_axis=0,
            concat_axis=0,
            tiled=True,
        ).reshape((slot_count,) + row_shape)

    replicas = lax.axis_size("groups") * shard_count
    replica = lax.axis_index("groups") * shard_count + shard_index
    share = width // replicas
    ow_part = exchange(lax.dynamic_slice_in_dim(out_weight, replica * share, share), 2)
    sibling = exchange(tokens, 1).reshape(sessions_here, span, depth)

    server, shard, half, chunk, place = split_sessions(home_rows, sessions_here, chunks)
    local = jnp.arange(sessions_here, dtype=jnp.int32)
    mine = shard_index * sessions_here + local
    my_chunk = pick(chunk, mine)
    my_slot = pick(shard * places + place, mine)
    relative = jnp.arange(model_shards, dtype=jnp.int32) ^ me
    turns_from = jnp.arange(chunks, dtype=jnp.int32)

    def arranged(values, targets):
        by_turn = (turns_from[:, None, None] == my_chunk) & (
            targets[None, :, None] == local // chunks
        )
        return jnp.sum(jnp.where(by_turn, values, 0), axis=2, dtype=jnp.int32)

    turns = arranged(local, relative)
    meta = jnp.concatenate(
        [
            turns,
            arranged(my_slot, relative),
            arranged(event_counts, relative),
            jnp.full((chunks, 4), me, jnp.int32),
        ],
        axis=1,
    )
    at = turns[:, 0] - me * chunks

    by_session = tokens.reshape(sessions_here, span, depth)
    outward = arranged(local, relative ^ 2)
    own = [
        piece.reshape(model_shards * span, depth)
        for piece in copy_rows(outward.reshape(-1), by_session, chunks, "pack_tokens")
    ]
    across = []
    for c in range(chunks):
        ready = own[c]
        if c >= 2:
            ready = after(ready, across[c - 2])
        elif c == 1:
            ready = after(ready, ow_part)
        across.append(exchange(ready, 2))

    store_row = home_rows - shard_index * sessions_here
    here = shard == shard_index
    there = server * places + place
    wanted = jnp.arange(2 * slot_count, dtype=jnp.int32)
    filed = half * slot_count + there
    chosen = (wanted[:, None] == filed[None, :]) & here[None, :]
    source = jnp.sum(jnp.where(chosen, store_row[None, :], 0), axis=1)
    kept = store_states.reshape((sessions_here,) + row_shape)
    inbound = [trade(part) for part in copy_rows(source, kept, 2, "pack_states")]
    owned = here[None, :] & (store_row[None, :] == local[:, None])
    came_back = jnp.sum(jnp.where(owned, filed, 0), axis=1)

    column = np.arange(256)
    natural = (column % 128 // 32) * 64 + column % 32 * 2 + column // 128
    order = jnp.asarray(natural[:, None] == column[None, :], BF)
    bw = jnp.concatenate(
        [bc_weight, dt_weight, jnp.zeros((bc_weight.shape[0], 128 - heads), BF)], axis=1
    )

    ow_across = lax.all_gather(ow_part, ("groups", "dp"), axis=0, tiled=True)
    ow_sibling = exchange(out_weight, 1)
    ow_far = exchange(ow_across, 1)

    small = (
        dt_bias.reshape(heads, 1),
        decay_rate.reshape(heads, 1),
        norm_gain.reshape(1, width),
        order,
    )
    weights = (x_weight, z_weight, bw)
    per_half = chunks // 2
    normed = []
    returned = []
    received = []
    earlier = None
    for c in range(chunks):
        number = c // per_half
        turn = meta[c]
        arrived = across[c]
        if c >= 1:
            turn = after(turn, normed[c - 1][0])
        if c >= 2:
            arrived = after(arrived, normed[c - 2][0])
        far = exchange(arrived, 1)
        merged = number == 0
        parts = layer_call(
            turn,
            by_session,
            sibling,
            arrived,
            far,
            weights,
            small,
            inbound[number],
            c % per_half if merged else 0,
            per_half if merged else 1,
            earlier,
        )
        normed.append(parts)
        last = (c + 1) % per_half == 0
        earlier = None if last else (parts if merged else parts[4:])
        if last:
            returned.append(trade(parts[4]))
        if last or not merged:
            received.append([parts[0]] + [exchange(parts[d], d) for d in range(1, 4)])
    new_store = gather_call(came_back, *returned)
    ow = (out_weight, ow_sibling, ow_across, ow_far)
    pieces = [piece for group in received for piece in group]
    out_tokens = out_call(at, pieces, ow, span).reshape(chunks * span, out_weight.shape[1])
    return (out_tokens, new_store)


def solution(mesh):
    return jax.shard_map(
        body,
        mesh=mesh,
        in_specs=(
            P(("groups", "dp"), "mp"),
            P(None, "mp"),
            P(None, "mp"),
            P(None, "mp"),
            P(None, "mp"),
            P("mp"),
            P("mp"),
            P("mp"),
            P("mp", None),
            P(("groups", "dp"), "mp"),
            P("groups"),
            P(("groups", "dp")),
        ),
        out_specs=(P(("groups", "dp", "mp"), None), P(("groups", "dp"), "mp")),
        check_vma=False,
    )
```

time: 221 us -> 257 us (1.16)
  Pallas kernels: 51.1 us -> 164 us
  between operations: 45.4 us -> 14.4 us
  local copies, waits for them, and re-layouts: 34.1 us -> 9.45 us
  waiting for transfers between devices: 43.4 us -> 25.5 us
  other arithmetic: 10.1 us -> 6.16 us
    pallas_call x5 -> x8, Pallas kernels: 51.1 us -> 164 us  [the longest x2 99.2 us: copy_rows(): pl.pallas_call(functools.partial(copy_kernel, groups), out_shape=[jax.Sha...]
    unnamed x81 -> x42, local copies, waits for them, and re-layouts: 24.1 us -> 5.76 us
    ppermute x24 -> x21, waiting for transfers between devices: 35.6 us -> 25.5 us  [exchange(): return lax.ppermute(value, 'mp', pairs)]
    all_to_all x4, waiting for transfers between devices: 7.78 us -> 0.01 us  [trade(): lax.all_to_all(value.reshape((shard_count, places) + row_shape), 'dp', sp...]
    gather x3 -> x0, local copies, waits for them, and re-layouts: 5.88 us -> none  [the longest x1 3.03 us: body(): jnp.take(jnp.concatenate(returned), came_back, axis=0, mode='clip')]
    concatenate x6 -> x1, other arithmetic: 4.88 us -> 0.08 us  [body(): jnp.concatenate([turns, arranged(my_slot, relative), arranged(event_count...]
    ppermute x24 -> x21, starting transfers between devices: 15.4 us -> 15.6 us  [exchange(): return lax.ppermute(value, 'mp', pairs)]
  transfers between devices with their start and end apart: 29 -> 26, of which waited for: 7 -> 5; matrix products, arithmetic and copies ran while one was open for 11% -> 4% of each run, Pallas kernels for 20% -> 61%
where the time goes in v3:
time: 257 us; the launch traced here: 255 us
  Pallas kernels  164 us (64%)
  starting transfers between devices  36 us (14%)
  waiting for transfers between devices  25.5 us (10%)
  between operations  14.4 us (6%)
  local copies, waits for them, and re-layouts  9.45 us (4%)
  other arithmetic  6.16 us (2%)
    pallas_call x2, Pallas kernels, copy_rows(): pl.pallas_call(functools.partial(copy_kernel, groups), out_shape=[jax.Sha...  99.2 us
    pallas_call x4, Pallas kernels, layer_call(): pl.pallas_call(functools.partial(layer_kernel, heads, span, aliased), out...  46.7 us
    ppermute x21, waiting for transfers between devices, exchange(): return lax.ppermute(value, 'mp', pairs)  25.5 us
    all_to_all x4, starting transfers between devices, trade(): lax.all_to_all(value.reshape((shard_count, places) + row_shape), 'dp', sp...  20.3 us
    ppermute x21, starting transfers between devices, exchange(): return lax.ppermute(value, 'mp', pairs)  15.6 us
    pallas_call x1, Pallas kernels, gather_call(): pl.pallas_call(functools.partial(gather_kernel, sessions, slots), grid=(l...  9.01 us
    pallas_call x1, Pallas kernels, out_call(): pl.pallas_call(functools.partial(out_kernel, where, span), grid=(columns...  8.82 us
    unnamed x42, local copies, waits for them, and re-layouts  5.76 us
  transfers between devices with their start and end apart: 26, of which 5 were waited for; matrix products, arithmetic and copies ran while one was open for 4% of the time, Pallas kernels for 61%

profile of v3, /device:TPU:0, one launch (start us, length us, event | category | flops | bytes accessed | tf_op | source)
XLA Modules:
  0.0 255.2 jit_solution(395151394181927618)
XLA Ops:
  7.2 0.5 collective-permute-start
  7.7 0.1 collective-permute-start.19
  7.8 1.0 constant_dynamic-slice_fusion
  8.8 3.0 %collective-permute-start.3 = (bf16[64,2048]{1,0:T(8,128)(2,1)S(1)}, bf16[64,2048]{1,0:T(8,128)(2,1)S(1)}, u32[]{:S(2)}, u32[]{:S(2)}) collective-permute-start(bf16[64,2048]{1,0:T(8,128)(2,1)S(1)} %constant_dynamic-slice_fusion), channel_id=1, source_target_pairs={{0,2},{1,3},{2,0},{3,1},{4,6},{5,7},{6,4},{7,5},{8,10},{9,11},{10,... | collective-permute-start | bytes 786440 | tf_op jit(solution)/shard_map/ppermute | solution.py:418
  11.8 0.7 broadcast_compare_fusion.2
  12.4 0.2 convert_reduce_fusion.4
  12.6 0.2 convert_reduce_fusion.2
  12.8 0.2 select_reduce_fusion.6
  13.1 0.2 select_reduce_fusion.4
  13.3 0.2 select_reduce_fusion.2
  13.4 0.2 select_reduce_fusion.1
  13.6 0.2 select_reduce_fusion
  13.8 0.2 convert_reduce_fusion
  14.1 4.3 %collective-permute-done.3 = bf16[64,2048]{1,0:T(8,128)(2,1)S(1)} collective-permute-done((bf16[64,2048]{1,0:T(8,128)(2,1)S(1)}, bf16[64,2048]{1,0:T(8,128)(2,1)S(1)}, u32[]{:S(2)}, u32[]{:S(2)}) %collective-permute-start.3) | collective-permute-done | bytes 262176 | tf_op jit(solution)/shard_map/ppermute | solution.py:418
  18.3 0.7 copy-done.6
  19.1 0.2 select_reduce_fusion.10
  19.4 1.0 fusion.6
  20.4 0.6 reshape.313.index
  21.0 65.6 %pack_tokens.1 = (bf16[4,128,512]{2,1,0:T(8,128)(2,1)}, bf16[4,128,512]{2,1,0:T(8,128)(2,1)}, bf16[4,128,512]{2,1,0:T(8,128)(2,1)}, bf16[4,128,512]{2,1,0:T(8,128)(2,1)}) custom-call(s32[16]{0:T(128)} %reshape.313.index, bf16[16,128,512]{2,1,0:T(8,128)(2,1)} %bitcast.31), custom_call_target="tpu_custom_call" | custom-call | bytes 4194304 | tf_op jit(solution)/shard_map/pack_tokens/pallas_call | solution.py:80
  86.5 1.8 collective-permute-start.1
  88.4 1.2 copy.48
  89.5 0.7 select_reduce_fusion.7
  90.2 33.7 %pack_states.1 = (bf16[8,256,128]{2,1,0:T(8,128)(2,1)}, bf16[8,256,128]{2,1,0:T(8,128)(2,1)}) custom-call(s32[16]{0:T(128)} %get-tuple-element.71.index, bf16[16,256,128]{2,1,0:T(8,128)(2,1)} %bitcast.28), custom_call_target="tpu_custom_call" | custom-call | bytes 2097152 | tf_op jit(solution)/shard_map/pack_states/pallas_call | solution.py:80
  123.9 5.0 %all-to-all-start = ((bf16[4,2,256,128]{3,2,1,0:T(8,128)(2,1)}), bf16[4,2,256,128]{3,2,1,0:T(8,128)(2,1)S(1)}, u32[]{:S(2)}, u32[]{:S(2)}) async-start(bf16[4,2,256,128]{3,2,1,0:T(8,128)(2,1)} %bitcast.41), calls=%async_computation | async-start | bytes 1048576 | tf_op jit(solution)/shard_map/all_to_all | solution.py:421
  129.0 0.1 pad.6.clone
  129.0 0.1 add_add_fusion
  129.1 0.5 collective-permute-start.4
  129.7 0.6 slice_bitcast_fusion
  130.3 0.3 copy.39
  130.6 0.7 copy.40.bias
  131.3 0.7 copy.41.rate
  131.9 0.1 pad.2.clone
  132.0 1.2 maximum_maximum_fusion.bw_any
  133.2 1.5 collective-permute-start.9
  134.7 9.6 %collective-permute-done.4.across = bf16[512,512]{1,0:T(8,128)(2,1)} collective-permute-done((bf16[512,512]{1,0:T(8,128)(2,1)}, bf16[512,512]{1,0:T(8,128)(2,1)}, u32[]{:S(2)}, u32[]{:S(2)}) %collective-permute-start.4) | collective-permute-done | bytes 524320 | tf_op jit(solution)/shard_map/ppermute | solution.py:418
  144.3 0.5 collective-permute-start.14
  144.8 5.1 %all-to-all-start.1 = ((bf16[4,2,256,128]{3,2,1,0:T(8,128)(2,1)}), bf16[4,2,256,128]{3,2,1,0:T(8,128)(2,1)S(1)}, u32[]{:S(2)}, u32[]{:S(2)}) async-start(bf16[4,2,256,128]{3,2,1,0:T(8,128)(2,1)} %bitcast.13), calls=%async_computation.1 | async-start | bytes 1048576 | tf_op jit(solution)/shard_map/all_to_all | solution.py:421
  150.0 11.6 %layer.4 = (bf16[256,512]{1,0:T(8,128)(2,1)}, bf16[256,512]{1,0:T(8,128)(2,1)}, bf16[256,512]{1,0:T(8,128)(2,1)}, bf16[256,512]{1,0:T(8,128)(2,1)}, bf16[8,256,128]{2,1,0:T(8,128)(2,1)}) custom-call(s32[16]{0:T(128)} %get-tuple-element.92.meta, bf16[16,128,512]{2,1,0:T(8,128)(2,1)} %bitcast.32, bf16[16,128,512]{2,1,0:T(8,128)(2,1)} %bitcast.3.sibling, ...), custom_call_target="tpu_custom_call" | custom-call | flops 8000000000 | bytes 9437184 | tf_op jit(solution)/shard_map/layer/pallas_call | solution.py:279
  161.6 0.6 collective-permute-start.10
  162.2 0.8 copy-done.15
  163.0 11.6 %layer.5 = (bf16[256,512]{1,0:T(8,128)(2,1)}, bf16[256,512]{1,0:T(8,128)(2,1)}, bf16[256,512]{1,0:T(8,128)(2,1)}, bf16[256,512]{1,0:T(8,128)(2,1)}, bf16[8,256,128]{2,1,0:T(8,128)(2,1)}) custom-call(s32[16]{0:T(128)} %get-tuple-element.39.meta, ...), custom_call_target="tpu_custom_call", output_to_operand_aliasing={{0}: (13, {}), {1}: (14, {}), {2}: (15, {}), {3}: (16, {}),... | custom-call | flops 8000000000 | bytes 9437184 | tf_op jit(solution)/shard_map/layer/pallas_call | solution.py:279
  174.6 0.1 collective-permute-start.15
  174.7 0.5 collective-permute-start.20
  175.2 5.1 %all-to-all-start.2 = ((bf16[4,2,256,128]{3,2,1,0:T(8,128)(2,1)}), bf16[4,2,256,128]{3,2,1,0:T(8,128)(2,1)S(1)}, u32[]{:S(2)}, u32[]{:S(2)}) async-start(bf16[4,2,256,128]{3,2,1,0:T(8,128)(2,1)} %bitcast.42), calls=%async_computation.2 | async-start | bytes 1048576 | tf_op jit(solution)/shard_map/all_to_all | solution.py:421
  180.3 11.7 %layer.6 = (bf16[128,512]{1,0:T(8,128)(2,1)}, bf16[128,512]{1,0:T(8,128)(2,1)}, bf16[128,512]{1,0:T(8,128)(2,1)}, bf16[128,512]{1,0:T(8,128)(2,1)}, bf16[8,256,128]{2,1,0:T(8,128)(2,1)}) custom-call(s32[16]{0:T(128)} %get-tuple-element.50.meta, bf16[16,128,512]{2,1,0:T(8,128)(2,1)} %bitcast.34, bf16[16,128,512]{2,1,0:T(8,128)(2,1)} %bitcast.3.sibling, ...), custom_call_target="tpu_custom_call" | custom-call | flops 8000000000 | bytes 9437184 | tf_op jit(solution)/shard_map/layer/pallas_call | solution.py:279
  192.0 11.7 %layer.7 = (bf16[128,512]{1,0:T(8,128)(2,1)}, bf16[128,512]{1,0:T(8,128)(2,1)}, bf16[128,512]{1,0:T(8,128)(2,1)}, bf16[128,512]{1,0:T(8,128)(2,1)}, bf16[8,256,128]{2,1,0:T(8,128)(2,1)}) custom-call(s32[16]{0:T(128)} %get-tuple-element.59.meta, bf16[16,128,512]{2,1,0:T(8,128)(2,1)} %bitcast.35, ...), custom_call_target="tpu_custom_call", output_to_operand_aliasing={{4}: (13, {})} | custom-call | flops 8000000000 | bytes 9437184 | tf_op jit(solution)/shard_map/layer/pallas_call | solution.py:279
  203.8 5.1 %all-to-all-start.3 = ((bf16[4,2,256,128]{3,2,1,0:T(8,128)(2,1)}), bf16[4,2,256,128]{3,2,1,0:T(8,128)(2,1)S(1)}, u32[]{:S(2)}, u32[]{:S(2)}) async-start(bf16[4,2,256,128]{3,2,1,0:T(8,128)(2,1)} %bitcast.43), calls=%async_computation.3 | async-start | bytes 1048576 | tf_op jit(solution)/shard_map/all_to_all | solution.py:421
  208.9 1.5 collective-permute-start.7
  210.3 0.4 collective-permute-start.8
  210.7 0.3 collective-permute-start.16
  211.0 1.5 collective-permute-start.17
  212.5 5.8 %collective-permute-done.7.refs_2_ = bf16[256,512]{1,0:T(8,128)(2,1)} collective-permute-done((bf16[256,512]{1,0:T(8,128)(2,1)}, bf16[256,512]{1,0:T(8,128)(2,1)}, u32[]{:S(2)}, u32[]{:S(2)}) %collective-permute-start.7) | collective-permute-done | bytes 262176 | tf_op jit(solution)/shard_map/ppermute | solution.py:418
  218.3 0.4 collective-permute-start.18
  218.7 4.4 %collective-permute-done.8.refs_3_ = bf16[256,512]{1,0:T(8,128)(2,1)} collective-permute-done((bf16[256,512]{1,0:T(8,128)(2,1)}, bf16[256,512]{1,0:T(8,128)(2,1)}, u32[]{:S(2)}, u32[]{:S(2)}) %collective-permute-start.8) | collective-permute-done | bytes 262176 | tf_op jit(solution)/shard_map/ppermute | solution.py:418
  223.1 0.6 collective-permute-start.11
  223.7 1.5 collective-permute-start.12
  225.2 1.4 collective-permute-done.17.refs_10_
  226.6 0.7 copy-done.19
  227.3 0.4 collective-permute-start.13
  227.7 0.7 subtract_reduce_fusion.at_ref
  228.4 0.8 copy-done.1
  229.2 9.0 %gather_states.1 = bf16[16,32768]{1,0:T(8,128)(2,1)} custom-call(s32[16]{0:T(128)} %get-tuple-element.70.index, bf16[8,256,128]{2,1,0:T(8,128)(2,1)} %bitcast.29, bf16[8,256,128]{2,1,0:T(8,128)(2,1)} %bitcast.30), custom_call_target="tpu_custom_call" | custom-call | bytes 2097152 | tf_op jit(solution)/shard_map/gather_states/pallas_call | solution.py:369
  238.2 1.3 copy-done.11
  239.5 8.8 %project_out.1 = bf16[4,128,2048]{2,1,0:T(8,128)(2,1)} custom-call(s32[4]{0:T(128)} %subtract_reduce_fusion.at_ref, bf16[256,512]{1,0:T(8,128)(2,1)} %get-tuple-element.46.refs_0_, bf16[256,512]{1,0:T(8,128)(2,1)} %copy-done.16, bf16[256,512]{1,0:T(8,128)(2,1)} %collective-permute-done.7.refs_2_, bf16[256,512]{1,0:T(8,128)(2,1)} %collective-permute-done.8.refs_3_, ...), custom_call_target="tpu_custom_call" | custom-call | flops 4294967296 | bytes 12582912 | tf_op jit(solution)/shard_map/project_out/pallas_call | solution.py:330
  (79 shorter events, 0.3 us)
Async XLA Ops:
  7.2 81.2 %copy-start.2 = (bf16[16,32768]{1,0:T(8,128)(2,1)S(1)}, bf16[16,32768]{1,0:T(8,128)(2,1)}, u32[]{:S(2)}) copy-start(bf16[16,32768]{1,0:T(8,128)(2,1)} %param.22) | copy-start | bytes 3145732
  7.2 167.5 %all-gather.2.cloned.1.call-start = ((), (), s32[]{:S(2)}) async-start(), calls=%async_computation.4 | async-start | bytes 2359296 | tf_op jit(solution)/shard_map/all_gather | solution.py:495
  7.2 142.7 %collective-permute-start = (bf16[2048,512]{1,0:T(8,128)(2,1)}, bf16[2048,512]{1,0:T(8,128)(2,1)}, u32[]{:S(2)}, u32[]{:S(2)}) collective-permute-start(bf16[2048,512]{1,0:T(8,128)(2,1)} %param.13), channel_id=1, source_target_pairs={{0,1},{1,0},{2,3},{3,2},{4,5},{5,4},{6,7},{7,6},{8,9},{9,8},{10,11... | collective-permute-start | bytes 6291464 | tf_op jit(solution)/shard_map/ppermute | solution.py:418
  7.7 203.0 %collective-permute-start.19 = (bf16[512,2048]{1,0:T(8,128)(2,1)}, bf16[512,2048]{1,0:T(8,128)(2,1)}, u32[]{:S(2)}, u32[]{:S(2)}) collective-permute-start(bf16[512,2048]{1,0:T(8,128)(2,1)} %refs_12_.1), channel_id=1, source_target_pairs={{0,1},{1,0},{2,3},{3,2},{4,5},{5,4},{6,7},{7,6},{8,9},{9,8},{10,11... | collective-permute-start | bytes 6291464 | tf_op jit(solution)/shard_map/ppermute | solution.py:418
  8.8 9.5 %collective-permute-start.3 = (bf16[64,2048]{1,0:T(8,128)(2,1)S(1)}, bf16[64,2048]{1,0:T(8,128)(2,1)S(1)}, u32[]{:S(2)}, u32[]{:S(2)}) collective-permute-start(bf16[64,2048]{1,0:T(8,128)(2,1)S(1)} %constant_dynamic-slice_fusion), channel_id=1, source_target_pairs={{0,2},{1,3},{2,0},{3,1},{4,6},{5,7},{6,4},{7,5},{8,10},{9,11},{10,... | collective-permute-start | bytes 786440 | tf_op jit(solution)/shard_map/ppermute | solution.py:418
  18.3 0.7 copy-start.6
  21.0 68.6 %copy-start.10 = (s32[64]{0:T(128)S(1)}, s32[64]{0:T(128)}, u32[]{:S(2)}) copy-start(s32[64]{0:T(128)} %param.23) | copy-start | bytes 772
  86.5 43.1 %collective-permute-start.1 = (bf16[512,512]{1,0:T(8,128)(2,1)}, bf16[512,512]{1,0:T(8,128)(2,1)S(1)}, u32[]{:S(2)}, u32[]{:S(2)}) collective-permute-start(bf16[512,512]{1,0:T(8,128)(2,1)} %bitcast.48), channel_id=1, source_target_pairs={{0,2},{1,3},{2,0},{3,1},{4,6},{5,7},{6,4},{7,5},{8,10},{9,11},{10,... | collective-permute-start | bytes 1572872 | tf_op jit(solution)/shard_map/ppermute | solution.py:418
  88.4 41.9 %copy-start.7 = (bf16[2048,8]{0,1:T(8,128)(2,1)S(1)}, bf16[2048,8]{0,1:T(8,128)(2,1)}, u32[]{:S(2)}) copy-start(bf16[2048,8]{0,1:T(8,128)(2,1)} %param.17) | copy-start | bytes 98308
  88.4 42.2 %copy-start.8 = (f32[8]{0:T(128)S(1)}, f32[8]{0:T(128)}, u32[]{:S(2)}) copy-start(f32[8]{0:T(128)} %param.18) | copy-start | bytes 100
  88.4 42.9 %copy-start.9 = (f32[8]{0:T(128)S(1)}, f32[8]{0:T(128)}, u32[]{:S(2)}) copy-start(f32[8]{0:T(128)} %param.19) | copy-start | bytes 100
  88.4 43.6 %copy-start.3 = (bf16[2048,128]{1,0:T(8,128)(2,1)S(1)}, bf16[2048,128]{1,0:T(8,128)(2,1)}, u32[]{:S(2)}) copy-start(bf16[2048,128]{1,0:T(8,128)(2,1)} %param.16) | copy-start | bytes 1572868
  123.9 9.3 %copy-start.13 = (bf16[4,128,512]{2,1,0:T(8,128)(2,1)S(1)}, bf16[4,128,512]{2,1,0:T(8,128)(2,1)}, u32[]{:S(2)}) copy-start(bf16[4,128,512]{2,1,0:T(8,128)(2,1)} %get-tuple-element.51) | copy-start | bytes 1572868
  123.9 20.4 %copy-start.12 = (bf16[4,128,512]{2,1,0:T(8,128)(2,1)S(1)}, bf16[4,128,512]{2,1,0:T(8,128)(2,1)}, u32[]{:S(2)}) copy-start(bf16[4,128,512]{2,1,0:T(8,128)(2,1)} %get-tuple-element.60) | copy-start | bytes 1572868
  123.9 20.9 %all-to-all-start = ((bf16[4,2,256,128]{3,2,1,0:T(8,128)(2,1)}), bf16[4,2,256,128]{3,2,1,0:T(8,128)(2,1)S(1)}, u32[]{:S(2)}, u32[]{:S(2)}) async-start(bf16[4,2,256,128]{3,2,1,0:T(8,128)(2,1)} %bitcast.41), calls=%async_computation | async-start | bytes 1048576 | tf_op jit(solution)/shard_map/all_to_all | solution.py:421
  129.1 15.2 %collective-permute-start.4 = (bf16[512,512]{1,0:T(8,128)(2,1)}, bf16[512,512]{1,0:T(8,128)(2,1)}, u32[]{:S(2)}, u32[]{:S(2)}) collective-permute-start(bf16[512,512]{1,0:T(8,128)(2,1)} %bitcast.10), channel_id=1, source_target_pairs={{0,2},{1,3},{2,0},{3,1},{4,6},{5,7},{6,4},{7,5},{8,10},{9,11},{10,... | collective-permute-start | bytes 1572872 | tf_op jit(solution)/shard_map/ppermute | solution.py:418
  129.7 20.3 %copy-start.14 = (bf16[512,512]{1,0:T(8,128)(2,1)}, bf16[512,512]{1,0:T(8,128)(2,1)S(1)}, u32[]{:S(2)}) copy-start(bf16[512,512]{1,0:T(8,128)(2,1)S(1)} %collective-permute-done.1.across) | copy-start | bytes 1572868
  129.7 20.3 %collective-permute-start.2 = (bf16[512,512]{1,0:T(8,128)(2,1)S(1)}, bf16[512,512]{1,0:T(8,128)(2,1)}, u32[]{:S(2)}, u32[]{:S(2)}) collective-permute-start(bf16[512,512]{1,0:T(8,128)(2,1)S(1)} %collective-permute-done.1.across), channel_id=1, source_target_pairs={{0,1},{1,0},{2,3},{3,2},{4,5},{5,4},{6,7},{7,6},{8,9},{9,8},{10,11... | collective-permute-start | bytes 1572872 | tf_op jit(solution)/shard_map/ppermute | solution.py:418
  133.2 28.4 %collective-permute-start.9 = (bf16[512,512]{1,0:T(8,128)(2,1)S(1)}, bf16[512,512]{1,0:T(8,128)(2,1)}, u32[]{:S(2)}, u32[]{:S(2)}) collective-permute-start(bf16[512,512]{1,0:T(8,128)(2,1)S(1)} %bitcast.47), channel_id=1, source_target_pairs={{0,2},{1,3},{2,0},{3,1},{4,6},{5,7},{6,4},{7,5},{8,10},{9,11},{10,... | collective-permute-start | bytes 1572872 | tf_op jit(solution)/shard_map/ppermute | solution.py:418
  144.3 30.3 %collective-permute-start.14 = (bf16[512,512]{1,0:T(8,128)(2,1)S(1)}, bf16[512,512]{1,0:T(8,128)(2,1)}, u32[]{:S(2)}, u32[]{:S(2)}) collective-permute-start(bf16[512,512]{1,0:T(8,128)(2,1)S(1)} %bitcast.46), channel_id=1, source_target_pairs={{0,2},{1,3},{2,0},{3,1},{4,6},{5,7},{6,4},{7,5},{8,10},{9,11},{10,... | collective-permute-start | bytes 1572872 | tf_op jit(solution)/shard_map/ppermute | solution.py:418
  144.8 5.1 %copy-start.5 = (bf16[4,2,256,128]{3,2,1,0:T(8,128)(2,1)}, bf16[4,2,256,128]{3,2,1,0:T(8,128)(2,1)S(1)}, u32[]{:S(2)}) copy-start(bf16[4,2,256,128]{3,2,1,0:T(8,128)(2,1)S(1)} %all-to-all-done) | copy-start | bytes 1572868
  144.8 30.4 %all-to-all-start.1 = ((bf16[4,2,256,128]{3,2,1,0:T(8,128)(2,1)}), bf16[4,2,256,128]{3,2,1,0:T(8,128)(2,1)S(1)}, u32[]{:S(2)}, u32[]{:S(2)}) async-start(bf16[4,2,256,128]{3,2,1,0:T(8,128)(2,1)} %bitcast.13), calls=%async_computation.1 | async-start | bytes 1048576 | tf_op jit(solution)/shard_map/all_to_all | solution.py:421
  149.9 12.2 %collective-permute-start.5 = (bf16[512,512]{1,0:T(8,128)(2,1)}, bf16[512,512]{1,0:T(8,128)(2,1)S(1)}, u32[]{:S(2)}, u32[]{:S(2)}) collective-permute-start(bf16[512,512]{1,0:T(8,128)(2,1)} %collective-permute-done.4.across), channel_id=1, source_target_pairs={{0,1},{1,0},{2,3},{3,2},{4,5},{5,4},{6,7},{7,6},{8,9},{9,8},{10,11... | collective-permute-start | bytes 1572872 | tf_op jit(solution)/shard_map/ppermute | solution.py:418
  161.6 18.7 %collective-permute-start.10 = (bf16[512,512]{1,0:T(8,128)(2,1)}, bf16[512,512]{1,0:T(8,128)(2,1)}, u32[]{:S(2)}, u32[]{:S(2)}) collective-permute-start(bf16[512,512]{1,0:T(8,128)(2,1)} %collective-permute-done.9.across), channel_id=1, source_target_pairs={{0,1},{1,0},{2,3},{3,2},{4,5},{5,4},{6,7},{7,6},{8,9},{9,8},{10,11... | collective-permute-start | bytes 1572872 | tf_op jit(solution)/shard_map/ppermute | solution.py:418
  162.2 0.8 copy-start.15
  174.6 17.4 %collective-permute-start.15 = (bf16[512,512]{1,0:T(8,128)(2,1)}, bf16[512,512]{1,0:T(8,128)(2,1)}, u32[]{:S(2)}, u32[]{:S(2)}) collective-permute-start(bf16[512,512]{1,0:T(8,128)(2,1)} %collective-permute-done.14.across), channel_id=1, source_target_pairs={{0,1},{1,0},{2,3},{3,2},{4,5},{5,4},{6,7},{7,6},{8,9},{9,8},{10,11... | collective-permute-start | bytes 1572872 | tf_op jit(solution)/shard_map/ppermute | solution.py:418
  174.7 63.5 %collective-permute-start.20 = (bf16[512,2048]{1,0:T(8,128)(2,1)}, bf16[512,2048]{1,0:T(8,128)(2,1)S(1)}, u32[]{:S(2)}, u32[]{:S(2)}) collective-permute-start(bf16[512,2048]{1,0:T(8,128)(2,1)} %all-gather.2.cloned.1.call-done.refs_14_), channel_id=1, source_target_pairs={{0,1},{1,0},{2,3},{3,2},{4,5},{5,4},{6,7},{7,6},{8,9},{9,8},{10,11... | collective-permute-start | bytes 6291464 | tf_op jit(solution)/shard_map/ppermute | solution.py:418
  175.2 5.1 %copy-start.4 = (bf16[4,2,256,128]{3,2,1,0:T(8,128)(2,1)}, bf16[4,2,256,128]{3,2,1,0:T(8,128)(2,1)S(1)}, u32[]{:S(2)}) copy-start(bf16[4,2,256,128]{3,2,1,0:T(8,128)(2,1)S(1)} %all-to-all-done.1) | copy-start | bytes 1572868
  175.2 28.5 %all-to-all-start.2 = ((bf16[4,2,256,128]{3,2,1,0:T(8,128)(2,1)}), bf16[4,2,256,128]{3,2,1,0:T(8,128)(2,1)S(1)}, u32[]{:S(2)}, u32[]{:S(2)}) async-start(bf16[4,2,256,128]{3,2,1,0:T(8,128)(2,1)} %bitcast.42), calls=%async_computation.2 | async-start | bytes 1048576 | tf_op jit(solution)/shard_map/all_to_all | solution.py:421
  192.0 35.3 %copy-start.17 = (bf16[128,512]{1,0:T(8,128)(2,1)S(1)}, bf16[128,512]{1,0:T(8,128)(2,1)}, u32[]{:S(2)}) copy-start(bf16[128,512]{1,0:T(8,128)(2,1)} %get-tuple-element.58) | copy-start | bytes 393220
  203.8 24.6 %copy-start = (bf16[4,2,256,128]{3,2,1,0:T(8,128)(2,1)}, bf16[4,2,256,128]{3,2,1,0:T(8,128)(2,1)S(1)}, u32[]{:S(2)}) copy-start(bf16[4,2,256,128]{3,2,1,0:T(8,128)(2,1)S(1)} %all-to-all-done.2) | copy-start | bytes 1572868
  203.8 24.6 %all-to-all-start.3 = ((bf16[4,2,256,128]{3,2,1,0:T(8,128)(2,1)}), bf16[4,2,256,128]{3,2,1,0:T(8,128)(2,1)S(1)}, u32[]{:S(2)}, u32[]{:S(2)}) async-start(bf16[4,2,256,128]{3,2,1,0:T(8,128)(2,1)} %bitcast.43), calls=%async_computation.3 | async-start | bytes 1048576 | tf_op jit(solution)/shard_map/all_to_all | solution.py:421
  208.9 2.2 collective-permute-start.6
  208.9 9.4 %collective-permute-start.7 = (bf16[256,512]{1,0:T(8,128)(2,1)}, bf16[256,512]{1,0:T(8,128)(2,1)}, u32[]{:S(2)}, u32[]{:S(2)}) collective-permute-start(bf16[256,512]{1,0:T(8,128)(2,1)} %get-tuple-element.48), channel_id=1, source_target_pairs={{0,2},{1,3},{2,0},{3,1},{4,6},{5,7},{6,4},{7,5},{8,10},{9,11},{10,... | collective-permute-start | bytes 786440 | tf_op jit(solution)/shard_map/ppermute | solution.py:418
  210.3 12.8 %collective-permute-start.8 = (bf16[256,512]{1,0:T(8,128)(2,1)}, bf16[256,512]{1,0:T(8,128)(2,1)}, u32[]{:S(2)}, u32[]{:S(2)}) collective-permute-start(bf16[256,512]{1,0:T(8,128)(2,1)} %get-tuple-element.49), channel_id=1, source_target_pairs={{0,3},{1,2},{2,1},{3,0},{4,7},{5,6},{6,5},{7,4},{8,11},{9,10},{10,... | collective-permute-start | bytes 786440 | tf_op jit(solution)/shard_map/ppermute | solution.py:418
  210.7 13.0 %collective-permute-start.16 = (bf16[128,512]{1,0:T(8,128)(2,1)}, bf16[128,512]{1,0:T(8,128)(2,1)S(1)}, u32[]{:S(2)}, u32[]{:S(2)}) collective-permute-start(bf16[128,512]{1,0:T(8,128)(2,1)} %get-tuple-element.65), channel_id=1, source_target_pairs={{0,1},{1,0},{2,3},{3,2},{4,5},{5,4},{6,7},{7,6},{8,9},{9,8},{10,11... | collective-permute-start | bytes 393224 | tf_op jit(solution)/shard_map/ppermute | solution.py:418
  211.0 27.2 %copy-start.16 = (bf16[256,512]{1,0:T(8,128)(2,1)}, bf16[256,512]{1,0:T(8,128)(2,1)S(1)}, u32[]{:S(2)}) copy-start(bf16[256,512]{1,0:T(8,128)(2,1)S(1)} %collective-permute-done.6.refs_1_) | copy-start | bytes 786436
  211.0 15.6 %collective-permute-start.17 = (bf16[128,512]{1,0:T(8,128)(2,1)}, bf16[128,512]{1,0:T(8,128)(2,1)S(1)}, u32[]{:S(2)}, u32[]{:S(2)}) collective-permute-start(bf16[128,512]{1,0:T(8,128)(2,1)} %get-tuple-element.66), channel_id=1, source_target_pairs={{0,2},{1,3},{2,0},{3,1},{4,6},{5,7},{6,4},{7,5},{8,10},{9,11},{10,... | collective-permute-start | bytes 393224 | tf_op jit(solution)/shard_map/ppermute | solution.py:418
  218.3 19.9 %collective-permute-start.18 = (bf16[128,512]{1,0:T(8,128)(2,1)}, bf16[128,512]{1,0:T(8,128)(2,1)}, u32[]{:S(2)}, u32[]{:S(2)}) collective-permute-start(bf16[128,512]{1,0:T(8,128)(2,1)} %get-tuple-element.67), channel_id=1, source_target_pairs={{0,3},{1,2},{2,1},{3,0},{4,7},{5,6},{6,5},{7,4},{8,11},{9,10},{10,... | collective-permute-start | bytes 393224 | tf_op jit(solution)/shard_map/ppermute | solution.py:418
  223.1 15.1 %collective-permute-start.11 = (bf16[128,512]{1,0:T(8,128)(2,1)}, bf16[128,512]{1,0:T(8,128)(2,1)}, u32[]{:S(2)}, u32[]{:S(2)}) collective-permute-start(bf16[128,512]{1,0:T(8,128)(2,1)} %get-tuple-element.56), channel_id=1, source_target_pairs={{0,1},{1,0},{2,3},{3,2},{4,5},{5,4},{6,7},{7,6},{8,9},{9,8},{10,11... | collective-permute-start | bytes 393224 | tf_op jit(solution)/shard_map/ppermute | solution.py:418
  223.7 2.9 %copy-start.18 = (bf16[128,512]{1,0:T(8,128)(2,1)}, bf16[128,512]{1,0:T(8,128)(2,1)S(1)}, u32[]{:S(2)}) copy-start(bf16[128,512]{1,0:T(8,128)(2,1)S(1)} %collective-permute-done.16.refs_9_) | copy-start | bytes 393220
  223.7 14.5 %collective-permute-start.12 = (bf16[128,512]{1,0:T(8,128)(2,1)}, bf16[128,512]{1,0:T(8,128)(2,1)}, u32[]{:S(2)}, u32[]{:S(2)}) collective-permute-start(bf16[128,512]{1,0:T(8,128)(2,1)} %get-tuple-element.57), channel_id=1, source_target_pairs={{0,2},{1,3},{2,0},{3,1},{4,6},{5,7},{6,4},{7,5},{8,10},{9,11},{10,... | collective-permute-start | bytes 393224 | tf_op jit(solution)/shard_map/ppermute | solution.py:418
  226.6 0.7 copy-start.19
  227.3 10.9 %collective-permute-start.13 = (bf16[128,512]{1,0:T(8,128)(2,1)S(1)}, bf16[128,512]{1,0:T(8,128)(2,1)}, u32[]{:S(2)}, u32[]{:S(2)}) collective-permute-start(bf16[128,512]{1,0:T(8,128)(2,1)S(1)} %copy-done.17), channel_id=1, source_target_pairs={{0,3},{1,2},{2,1},{3,0},{4,7},{5,6},{6,5},{7,4},{8,11},{9,10},{10,... | collective-permute-start | bytes 393224 | tf_op jit(solution)/shard_map/ppermute | solution.py:418
  228.4 0.8 copy-start.1
  238.2 1.3 copy-start.11
Sparse Core Ops, SparseCore 0:
  19.2 50.7 all-gather.1

commit v4 on v3

--- a/solution.py
+++ b/solution.py
@@ -61,80 +61,114 @@
     return server, shard, half, chunk, place
 
 
-def copy_kernel(groups, index, source, *refs):
-    outs, sems = refs[:-1], refs[-1]
-    copies = []
-    for k, out in enumerate(outs):
-        for j in range(groups):
-            n = k * groups + j
-            copies.append(
-                pltpu.make_async_copy(source.at[index[n]], out.at[j], sems.at[n])
-            )
-            copies[-1].start()
-    for copy in copies:
+def pack_tokens_kernel(chunks, meta, source, *refs):
+    outs, held, in_sems, out_sems = refs[:chunks], refs[chunks], refs[-2], refs[-1]
+    groups = held.shape[0] // chunks
+    coming, going = [], []
+    for n in range(chunks * groups):
+        first = n // groups * groups
+        coming.append(
+            pltpu.make_async_copy(
+                source.at[meta[first + (n - first ^ 2)]], held.at[n], in_sems.at[n]
+            )
+        )
+        coming[-1].start()
+    for n in range(chunks * groups):
+        coming[n].wait()
+        going.append(
+            pltpu.make_async_copy(held.at[n], outs[n // groups].at[n % groups], out_sems.at[n])
+        )
+        going[-1].start()
+    for copy in going:
         copy.wait()
 
 
-def copy_rows(index, source, outs, name):
-    groups = index.shape[0] // outs
+def pack_tokens(meta, source, chunks):
+    blocks = source.shape[0]
+    groups = blocks // chunks
     return pl.pallas_call(
-        functools.partial(copy_kernel, groups),
-        out_shape=[jax.ShapeDtypeStruct((groups,) + source.shape[1:], source.dtype)] * outs,
+        functools.partial(pack_tokens_kernel, chunks),
+        out_shape=[jax.ShapeDtypeStruct((groups,) + source.shape[1:], source.dtype)] * chunks,
         in_specs=[SMEM, ANY],
-        out_specs=[ANY] * outs,
-        scratch_shapes=[pltpu.SemaphoreType.DMA((index.shape[0],))],
-        compiler_params=pltpu.CompilerParams(vmem_limit_bytes=58 * 2**20),
+        out_specs=[ANY] * chunks,
+        scratch_shapes=[
+            pltpu.VMEM(source.shape, source.dtype),
+            pltpu.SemaphoreType.DMA((blocks,)),
+            pltpu.SemaphoreType.DMA((blocks,)),
+        ],
+        compiler_params=pltpu.CompilerParams(vmem_limit_bytes=16 * 2**20),
         cost_estimate=pl.CostEstimate(
             flops=0, bytes_accessed=2 * source.size * 2, transcendentals=0
         ),
-        name=name,
-    )(index, source)
+        name="pack_tokens",
+    )(meta, source)
+
+
+def pack_states(source, store, swap, slots):
+    sessions, width = store.shape
+    lines = width // 128
+
+    def kernel(source, store, swap, first, second, held):
+        for part in range(4):
+            base = part * 16 * 128
+            stacked = jnp.concatenate(
+                [store[:, base + j * 128 : base + (j + 1) * 128] for j in range(16)], axis=0
+            )
+            turned = jnp.dot(swap[...], stacked, preferred_element_type=F32).astype(BF)
+            for r in range(sessions):
+                held[r, part * 16 : (part + 1) * 16, :] = turned[r * 16 : (r + 1) * 16]
+        for n in range(slots):
+            first[n] = held[source[n]]
+            second[n] = held[source[slots + n]]
+
+    return pl.pallas_call(
+        kernel,
+        grid=(lines // 64,),
+        out_shape=[jax.ShapeDtypeStruct((slots, lines, 128), BF)] * 2,
+        in_specs=[
+            SMEM,
+            pl.BlockSpec((sessions, 64 * 128), lambda j: (0, j)),
+            pl.BlockSpec(swap.shape, lambda j: (0, 0)),
+        ],
+        out_specs=[pl.BlockSpec((slots, 64, 128), lambda j: (0, j, 0))] * 2,
+        scratch_shapes=[pltpu.VMEM((sessions, 64, 128), BF)],
+        compiler_params=pltpu.CompilerParams(vmem_limit_bytes=16 * 2**20),
+        cost_estimate=pl.CostEstimate(
+            flops=2 * 256 * 256 * width // 16, bytes_accessed=4 * 2**20, transcendentals=0
+        ),
+        name="pack_states",
+    )(source, store, swap)
 
 
 def layer_kernel(
-    heads, span, aliased, meta, tokens, sibling, across, far, xw_any, zw_any, bw_any, bias, rate,
-    gain, order, inbound, *refs,
+    heads, span, chunk, aliased, meta, tokens, sibling, across, far, xw, zw, bw, bias, rate, gain,
+    order, inbound, *refs,
 ):
-    refs = refs[5 if aliased & 2 else (1 if aliased & 1 else 0):]
-    n0, n1, n2, n3, outgoing = refs[:5]
-    piece0, piece1, piece2, piece3, xw, zw, bw, state4, xs, zs, xt, fresh, sems, out_sems = refs[5:]
+    refs = refs[aliased:]
+    n0, n1, n2, n3, outgoing, xs, zs, xt, fresh, out_sems = refs
     normed_out = (n0, n1, n2, n3)
-    pieces = (piece0, piece1, piece2, piece3)
-    me = meta[12]
+    groups = meta.shape[0] // 4
+    turn_at, slot_at, count_at = chunk * 4, groups + chunk * 4, 2 * groups + chunk * 4
+    me = meta[3 * groups]
     depth = across.shape[1]
     quads = heads // 4
-    copies = []
-
-    def bring(source, target):
-        copies.append(pltpu.make_async_copy(source, target, sems.at[len(copies)]))
-        copies[-1].start()
-
-    for d in range(4):
-        rows = pl.ds(d * span, span)
-        bring(tokens.at[meta[d]], piece0.at[rows])
-        bring(sibling.at[meta[d]], piece1.at[rows])
-    bring(across, piece2)
-    for d in range(4):
-        bring(far.at[pl.ds((d ^ 1) * span, span)], piece3.at[pl.ds(d * span, span)])
-    bring(bw_any, bw)
-    early = len(copies)
-    bring(xw_any, xw)
-    bring(zw_any, zw)
-    for d in range(4):
-        bring(inbound.at[meta[4 + d]], state4.at[d])
+    pieces = (
+        jnp.concatenate([tokens[meta[turn_at + d]] for d in range(4)], axis=0),
+        jnp.concatenate([sibling[meta[turn_at + d]] for d in range(4)], axis=0),
+        across[...],
+        jnp.concatenate([far[(d ^ 1) * span : ((d ^ 1) + 1) * span] for d in range(4)], axis=0),
+    )
 
     def project(weight, columns):
         total = None
         for d in range(4):
             first = pl.multiple_of((me ^ d) * depth, depth)
             part = jnp.dot(
-                pieces[d][...], weight[pl.ds(first, depth), columns], preferred_element_type=F32
+                pieces[d], weight[pl.ds(first, depth), columns], preferred_element_type=F32
             )
             total = part if total is None else total + part
         return total
 
-    for copy in copies[:early]:
-        copy.wait()
     bcs = project(bw, slice(None))
 
     lane = lax.broadcasted_iota(jnp.int32, (span, 128), 1)
@@ -147,7 +181,7 @@
         [jnp.transpose(bcs[d * span : (d + 1) * span, 128:256])[:heads] + bias[...] for d in range(4)],
         axis=0,
     )
-    alive = jnp.concatenate([(lane8 < meta[8 + d]).astype(F32) for d in range(4)], axis=0)
+    alive = jnp.concatenate([(lane8 < meta[count_at + d]).astype(F32) for d in range(4)], axis=0)
     steps = (jnp.maximum(raw, 0.0) + jnp.log1p(jnp.exp(-jnp.abs(raw)))) * alive
     totals = steps * jnp.concatenate([rate[...]] * 4, axis=0)
     shift = 1
@@ -161,23 +195,19 @@
         jnp.concatenate([totals, jnp.zeros((128 - heads * 4, span), F32)], axis=0)
     )
 
-    copies[early].wait()
     for quad in range(quads):
         columns = slice(quad * 256, quad * 256 + 256)
         xs[:, columns] = project(xw, columns).astype(BF)
-    copies[early + 1].wait()
     for quad in range(quads):
         columns = slice(quad * 256, quad * 256 + 256)
         zs[:, columns] = project(zw, columns).astype(BF)
-    for copy in copies[early + 2 :]:
-        copy.wait()
 
     wide = lax.broadcasted_iota(jnp.int32, (span, 256), 1) // 64
     head_masks = [(wide == k).astype(F32).astype(BF) for k in range(4)]
     sends = []
     for d in range(4):
         rows = slice(d * span, (d + 1) * span)
-        count = meta[8 + d]
+        count = meta[count_at + d]
         bc = bcs[rows, 0:128]
         turned = pltpu.roll(bc, 64, 1)
         b_low = jnp.where(low, bc, 0.0).astype(BF)
@@ -186,7 +216,7 @@
         c_high = jnp.where(low, 0.0, bc).astype(BF)
         scores = lax.dot_general(c_low, b_low, NT, preferred_element_type=F32)
         scores = jnp.where(causal, scores, 0.0)
-        state = state4[d]
+        state = inbound[meta[slot_at + d]]
         carried = lax.dot_general(
             jnp.concatenate([c_low, c_high], axis=0), state, NT, preferred_element_type=F32
         ).astype(BF)
@@ -222,7 +252,7 @@
                 )
             )
             gate = zs[rows, columns].astype(F32)
-            value = (diagonal + before * fade) * (gate / (1.0 + jnp.exp(-gate)))
+            value = (diagonal + before * fade) * (gate * (0.5 + 0.5 * jnp.tanh(0.5 * gate)))
             gated.append(value)
             own = jnp.sum(value * value, axis=1, keepdims=True)
             squares = own if squares is None else squares + own
@@ -249,7 +279,7 @@
             )
             fresh[d, part, :] = (keep_rows * state[part].astype(F32) + added).astype(BF)
         sends.append(
-            pltpu.make_async_copy(fresh.at[d], outgoing.at[meta[4 + d]], out_sems.at[d])
+            pltpu.make_async_copy(fresh.at[d], outgoing.at[meta[slot_at + d]], out_sems.at[d])
         )
         sends[-1].start()
         inverse = lax.rsqrt(squares * (1.0 / (heads * 64)) + 1e-05)
@@ -261,49 +291,43 @@
         send.wait()
 
 
-def layer_call(meta, tokens, sibling, across, far, weights, small, inbound, turn, turns, earlier):
+def layer_call(
+    meta, chunk, tokens, sibling, across, far, weights, small, inbound, turn, turns, earlier
+):
     rows, depth = across.shape
     heads = small[0].shape[0]
     width = weights[0].shape[1]
     span = rows // 4
     row_shape = inbound.shape[1:]
-    operands = [tokens, sibling, across, far, *weights, *small, inbound]
+    operands = [meta, tokens, sibling, across, far, *weights, *small, inbound]
+    known = len(operands) - 1
     aliases = {}
-    aliased = 0
     if earlier is not None:
-        aliased = 1 if len(earlier) == 1 else 2
-        first = 1 + len(operands)
         for k in range(len(earlier)):
-            aliases[first + k] = k + 5 - len(earlier)
+            aliases[len(operands) + k] = k + 5 - len(earlier)
         operands += list(earlier)
+    extra = len(operands) - 1 - known
     return pl.pallas_call(
-        functools.partial(layer_kernel, heads, span, aliased),
+        functools.partial(layer_kernel, heads, span, chunk, extra),
+        grid=(1,),
         out_shape=[jax.ShapeDtypeStruct((turns * span, width), BF)] * 4
         + [jax.ShapeDtypeStruct(inbound.shape, BF)],
-        grid_spec=pltpu.PrefetchScalarGridSpec(
-            num_scalar_prefetch=1,
-            grid=(1,),
-            in_specs=[ANY] * 7 + [VMEM] * 4 + [ANY] * (len(operands) - 11),
-            out_specs=[pl.BlockSpec((span, width), lambda i, meta: (turn, 0))] * 4 + [ANY],
-            scratch_shapes=[
-                *[pltpu.VMEM((rows, depth), BF)] * 4,
-                *[pltpu.VMEM(weight.shape, BF) for weight in weights],
-                pltpu.VMEM((4,) + row_shape, BF),
-                pltpu.VMEM((rows, width), BF),
-                pltpu.VMEM((rows, width), BF),
-                pltpu.VMEM((4, heads // 4, 256, span), F32),
-                pltpu.VMEM((4,) + row_shape, BF),
-                pltpu.SemaphoreType.DMA((20,)),
-                pltpu.SemaphoreType.DMA((4,)),
-            ],
-        ),
+        in_specs=[SMEM] + [VMEM] * known + [ANY] * extra,
+        out_specs=[pl.BlockSpec((span, width), lambda i: (turn, 0))] * 4 + [ANY],
+        scratch_shapes=[
+            pltpu.VMEM((rows, width), BF),
+            pltpu.VMEM((rows, width), BF),
+            pltpu.VMEM((4, heads // 4, 256, span), F32),
+            pltpu.VMEM((4,) + row_shape, BF),
+            pltpu.SemaphoreType.DMA((4,)),
+        ],
         input_output_aliases=aliases,
-        compiler_params=pltpu.CompilerParams(vmem_limit_bytes=58 * 2**20),
+        compiler_params=pltpu.CompilerParams(vmem_limit_bytes=32 * 2**20),
         cost_estimate=pl.CostEstimate(
             flops=8 * 10**9, bytes_accessed=9 * 2**20, transcendentals=0
         ),
         name="layer",
-    )(meta, *operands)
+    )(*operands)
 
 
 def out_kernel(where, span, at_ref, *refs):
@@ -335,7 +359,7 @@
         + [pl.BlockSpec(piece.shape, lambda j: (0, 0)) for piece in normed]
         + [pl.BlockSpec((depth, block), lambda j: (0, j))] * 4,
         out_specs=pl.BlockSpec((chunks, span, block), lambda j: (0, 0, j)),
-        compiler_params=pltpu.CompilerParams(vmem_limit_bytes=58 * 2**20),
+        compiler_params=pltpu.CompilerParams(vmem_limit_bytes=32 * 2**20),
         cost_estimate=pl.CostEstimate(
             flops=2 * chunks * span * depth * 4 * columns,
             bytes_accessed=12 * 2**20,
@@ -345,39 +369,45 @@
     )(at, *normed, *weights)
 
 
-def gather_kernel(sessions, slots, index, first, second, out):
-    lines = out.shape[1] // 128
-    picked = []
-    for r in range(sessions):
-        slot = index[r]
-        inside = jnp.minimum(slot, slots - 1)
-        other = jnp.maximum(slot - slots, 0)
-        scale = jnp.where(slot < slots, 1.0, 0.0)
-        picked.append(
-            jnp.where(scale > 0.5, first[inside].astype(F32), second[other].astype(F32))
+def gather_kernel(sessions, slots, index, first, second, swap, out):
+    for part in range(4):
+        lines = slice(part * 16, (part + 1) * 16)
+        stacked = jnp.concatenate(
+            [
+                jnp.where(
+                    index[r] < slots,
+                    first[jnp.minimum(index[r], slots - 1), lines, :],
+                    second[jnp.maximum(index[r] - slots, 0), lines, :],
+                )
+                for r in range(sessions)
+            ],
+            axis=0,
         )
-    block = jnp.stack(picked, axis=0)
-    turned = jnp.swapaxes(block, 0, 1)
-    for j in range(lines):
-        out[:, j * 128 : (j + 1) * 128] = turned[j].astype(BF)
-
-
-def gather_call(index, first, second):
+        turned = lax.dot_general(
+            swap[...], stacked, (((0,), (0,)), ((), ())), preferred_element_type=F32
+        ).astype(BF)
+        for j in range(16):
+            column = (part * 16 + j) * 128
+            out[:, column : column + 128] = turned[j * sessions : (j + 1) * sessions]
+
+
+def gather_states(index, first, second, swap):
     sessions = index.shape[0]
     slots, lines, lanes = first.shape
-    block = 16
     return pl.pallas_call(
         functools.partial(gather_kernel, sessions, slots),
-        grid=(lines // block,),
+        grid=(lines // 64,),
         out_shape=jax.ShapeDtypeStruct((sessions, lines * lanes), BF),
-        in_specs=[SMEM] + [pl.BlockSpec((slots, block, lanes), lambda j: (0, j, 0))] * 2,
-        out_specs=pl.BlockSpec((sessions, block * lanes), lambda j: (0, j)),
-        compiler_params=pltpu.CompilerParams(vmem_limit_bytes=58 * 2**20),
+        in_specs=[SMEM]
+        + [pl.BlockSpec((slots, 64, lanes), lambda j: (0, j, 0))] * 2
+        + [pl.BlockSpec(swap.shape, lambda j: (0, 0))],
+        out_specs=pl.BlockSpec((sessions, 64 * lanes), lambda j: (0, j)),
+        compiler_params=pltpu.CompilerParams(vmem_limit_bytes=16 * 2**20),
         cost_estimate=pl.CostEstimate(
             flops=0, bytes_accessed=2 * 2**20, transcendentals=0
         ),
         name="gather_states",
-    )(index, first, second)
+    )(index, first, second, swap)
 
 
 def after(value, *others):
@@ -437,42 +467,29 @@
     mine = shard_index * sessions_here + local
     my_chunk = pick(chunk, mine)
     my_slot = pick(shard * places + place, mine)
-    relative = jnp.arange(model_shards, dtype=jnp.int32) ^ me
-    turns_from = jnp.arange(chunks, dtype=jnp.int32)
-
-    def arranged(values, targets):
-        by_turn = (turns_from[:, None, None] == my_chunk) & (
-            targets[None, :, None] == local // chunks
-        )
-        return jnp.sum(jnp.where(by_turn, values, 0), axis=2, dtype=jnp.int32)
-
-    turns = arranged(local, relative)
+    entry = jnp.arange(sessions_here, dtype=jnp.int32)
+    by_turn = (
+        (entry // model_shards)[:, None] == my_chunk[None, :]
+    ) & ((entry % model_shards ^ me)[:, None] == (local // chunks)[None, :])
+
+    def arranged(values):
+        return jnp.sum(jnp.where(by_turn, values[None, :], 0), axis=1, dtype=jnp.int32)
+
+    turns = arranged(local)
     meta = jnp.concatenate(
         [
             turns,
-            arranged(my_slot, relative),
-            arranged(event_counts, relative),
-            jnp.full((chunks, 4), me, jnp.int32),
-        ],
-        axis=1,
-    )
-    at = turns[:, 0] - me * chunks
+            arranged(my_slot),
+            arranged(event_counts),
+            jnp.full((sessions_here,), me, jnp.int32),
+        ]
+    )
 
     by_session = tokens.reshape(sessions_here, span, depth)
-    outward = arranged(local, relative ^ 2)
     own = [
         piece.reshape(model_shards * span, depth)
-        for piece in copy_rows(outward.reshape(-1), by_session, chunks, "pack_tokens")
+        for piece in pack_tokens(meta, by_session, chunks)
     ]
-    across = []
-    for c in range(chunks):
-        ready = own[c]
-        if c >= 2:
-            ready = after(ready, across[c - 2])
-        elif c == 1:
-            ready = after(ready, ow_part)
-        across.append(exchange(ready, 2))
-
     store_row = home_rows - shard_index * sessions_here
     here = shard == shard_index
     there = server * places + place
@@ -480,10 +497,23 @@
     filed = half * slot_count + there
     chosen = (wanted[:, None] == filed[None, :]) & here[None, :]
     source = jnp.sum(jnp.where(chosen, store_row[None, :], 0), axis=1)
-    kept = store_states.reshape((sessions_here,) + row_shape)
-    inbound = [trade(part) for part in copy_rows(source, kept, 2, "pack_states")]
+    row = np.arange(sessions_here * 16)
+    swap = jnp.asarray(
+        (row % 16 * sessions_here + row // 16)[:, None] == row[None, :], BF
+    )
+    packed = pack_states(after(source, own[0]), store_states, swap, slot_count)
+    inbound = [trade(part) for part in packed]
     owned = here[None, :] & (store_row[None, :] == local[:, None])
     came_back = jnp.sum(jnp.where(owned, filed, 0), axis=1)
+
+    across = []
+    for c in range(chunks):
+        ready = own[c]
+        if c >= 2:
+            ready = after(ready, across[c - 2])
+        elif c == 1:
+            ready = after(ready, packed[0])
+        across.append(exchange(ready, 2))
 
     column = np.arange(256)
     natural = (column % 128 // 32) * 64 + column % 32 * 2 + column // 128
@@ -492,6 +522,7 @@
         [bc_weight, dt_weight, jnp.zeros((bc_weight.shape[0], 128 - heads), BF)], axis=1
     )
 
+    ow_part = after(ow_part, own[0])
     ow_across = lax.all_gather(ow_part, ("groups", "dp"), axis=0, tiled=True)
     ow_sibling = exchange(out_weight, 1)
     ow_far = exchange(ow_across, 1)
@@ -510,16 +541,19 @@
     earlier = None
     for c in range(chunks):
         number = c // per_half
-        turn = meta[c]
+        turn = meta
         arrived = across[c]
         if c >= 1:
             turn = after(turn, normed[c - 1][0])
+        if c == chunks - 1:
+            turn = after(turn, *received[0], returned[0])
         if c >= 2:
             arrived = after(arrived, normed[c - 2][0])
         far = exchange(arrived, 1)
         merged = number == 0
         parts = layer_call(
             turn,
+            c,
             by_session,
             sibling,
             arrived,
@@ -538,9 +572,10 @@
             returned.append(trade(parts[4]))
         if last or not merged:
             received.append([parts[0]] + [exchange(parts[d], d) for d in range(1, 4)])
-    new_store = gather_call(came_back, *returned)
+    new_store = gather_states(came_back, *returned, swap)
     ow = (out_weight, ow_sibling, ow_across, ow_far)
     pieces = [piece for group in received for piece in group]
+    at = (turns - me * chunks).reshape(chunks, model_shards)[:, 0]
     out_tokens = out_call(at, pieces, ow, span).reshape(chunks * span, out_weight.shape[1])
     return (out_tokens, new_store)
 

time: 257 us -> 172 us (0.67)
  Pallas kernels: 164 us -> 51.9 us
  local copies, waits for them, and re-layouts: 9.45 us -> 40.5 us
  starting transfers between devices: 36 us -> 29.4 us
    pallas_call x7, Pallas kernels: 155 us -> 44.1 us  [the longest x4 32.7 us: layer_call(): pl.pallas_call(functools.partial(layer_kernel, heads, span, chunk, extra)...]
    unnamed x42 -> x95, local copies, waits for them, and re-layouts: 5.76 us -> 38.5 us
    all_to_all x4, waiting for transfers between devices: 0.01 us -> 13.7 us  [trade(): lax.all_to_all(value.reshape((shard_count, places) + row_shape), 'dp', sp...]
    ppermute x21, waiting for transfers between devices: 25.5 us -> 14 us  [exchange(): return lax.ppermute(value, 'mp', pairs)]
    ppermute x21, starting transfers between devices: 15.6 us -> 11.8 us  [exchange(): return lax.ppermute(value, 'mp', pairs)]
    all_to_all x4, starting transfers between devices: 20.3 us -> 17.6 us  [trade(): lax.all_to_all(value.reshape((shard_count, places) + row_shape), 'dp', sp...]
  transfers between devices with their start and end apart: 26 -> 26, of which waited for: 5 -> 6; matrix products, arithmetic and copies ran while one was open for 4% -> 6% of each run, Pallas kernels for 61% -> 26%
where the time goes in v4:
time: 172 us; the launch traced here: 170 us
  Pallas kernels  51.9 us (30%)
  local copies, waits for them, and re-layouts  40.5 us (24%)
  starting transfers between devices  29.4 us (17%)
  waiting for transfers between devices  27.7 us (16%)
  between operations  14.4 us (8%)
  other arithmetic  6.55 us (4%)
    unnamed x95, local copies, waits for them, and re-layouts  38.5 us
    pallas_call x4, Pallas kernels, layer_call(): pl.pallas_call(functools.partial(layer_kernel, heads, span, chunk, extra)...  32.7 us
    all_to_all x4, starting transfers between devices, trade(): lax.all_to_all(value.reshape((shard_count, places) + row_shape), 'dp', sp...  17.6 us
    ppermute x21, waiting for transfers between devices, exchange(): return lax.ppermute(value, 'mp', pairs)  14 us
    all_to_all x4, waiting for transfers between devices, trade(): lax.all_to_all(value.reshape((shard_count, places) + row_shape), 'dp', sp...  13.7 us
    ppermute x21, starting transfers between devices, exchange(): return lax.ppermute(value, 'mp', pairs)  11.8 us
    pallas_call x1, Pallas kernels, out_call(): pl.pallas_call(functools.partial(out_kernel, where, span), grid=(columns...  7.81 us
    pallas_call x1, Pallas kernels, pack_tokens(): pl.pallas_call(functools.partial(pack_tokens_kernel, chunks), out_shape=[...  5.23 us
  transfers between devices with their start and end apart: 26, of which 6 were waited for; matrix products, arithmetic and copies ran while one was open for 6% of the time, Pallas kernels for 26%

profile of v4, /device:TPU:0, one launch (start us, length us, event | category | flops | bytes accessed | tf_op | source)
XLA Modules:
  0.0 170.5 jit_solution(6458027944150592678)
XLA Ops:
  7.8 1.0 constant_dynamic-slice_fusion
  8.7 2.6 %collective-permute-start.19 = (bf16[64,2048]{1,0:T(8,128)(2,1)S(1)}, bf16[64,2048]{1,0:T(8,128)(2,1)S(1)}, u32[]{:S(2)}, u32[]{:S(2)}) collective-permute-start(bf16[64,2048]{1,0:T(8,128)(2,1)S(1)} %constant_dynamic-slice_fusion), channel_id=1, source_target_pairs={{0,2},{1,3},{2,0},{3,1},{4,6},{5,7},{6,4},{7,5},{8,10},{9,11},{10,... | collective-permute-start | bytes 786440 | tf_op jit(solution)/shard_map/ppermute | solution.py:448
  11.3 0.7 broadcast_compare_fusion
  13.8 0.9 select_reduce_fusion.10
  14.8 1.6 copy-done
  16.4 5.2 %pack_tokens.1 = (bf16[4,128,512]{2,1,0:T(8,128)(2,1)}, bf16[4,128,512]{2,1,0:T(8,128)(2,1)S(1)}, bf16[4,128,512]{2,1,0:T(8,128)(2,1)}, bf16[4,128,512]{2,1,0:T(8,128)(2,1)}) custom-call(s32[64]{0:T(128)S(1)} %pad_add_fusion.meta, bf16[16,128,512]{2,1,0:T(8,128)(2,1)S(1)} %bitcast.20), custom_call_target="tpu_custom_call" | custom-call | bytes 4194304 | tf_op jit(solution)/shard_map/pack_tokens/pallas_call | solution.py:89
  21.6 0.7 copy-done.43
  22.6 3.0 %pack_states.1 = (bf16[8,256,128]{2,1,0:T(8,128)(2,1)}, bf16[8,256,128]{2,1,0:T(8,128)(2,1)}) custom-call(s32[16]{0:T(128)S(1)} %get-tuple-element.40.source, bf16[16,32768]{1,0:T(8,128)(2,1)S(1)} %copy-done.6, bf16[256,256]{1,0:T(8,128)(2,1)S(1)} %copy-done.7), custom_call_target="tpu_custom_call" | custom-call | flops 268435456 | bytes 4194304 | tf_op jit(solution)/shard_map/pack_states/pallas_call | solution.py:124
  25.6 5.4 %all-to-all-start = ((bf16[4,2,256,128]{3,2,1,0:T(8,128)(2,1)}), bf16[4,2,256,128]{3,2,1,0:T(8,128)(2,1)S(1)}, u32[]{:S(2)}, u32[]{:S(2)}) async-start(bf16[4,2,256,128]{3,2,1,0:T(8,128)(2,1)} %bitcast.6), calls=%async_computation | async-start | bytes 1048576 | tf_op jit(solution)/shard_map/all_to_all | solution.py:451
  31.0 1.5 collective-permute-start.3
  32.5 5.0 %collective-permute-done.1.across = bf16[512,512]{1,0:T(8,128)(2,1)} collective-permute-done((bf16[512,512]{1,0:T(8,128)(2,1)}, bf16[512,512]{1,0:T(8,128)(2,1)}, u32[]{:S(2)}, u32[]{:S(2)}) %collective-permute-start.1) | collective-permute-done | bytes 524320 | tf_op jit(solution)/shard_map/ppermute | solution.py:448
  37.5 1.8 %copy.40 = bf16[2048,8]{1,0:T(8,128)(2,1)} copy(bf16[2048,8]{0,1:T(8,128)(2,1)} %param.18) | data formatting | bytes 65536 | tf_op args[4]
  39.4 0.7 copy.42.rate
  40.2 2.4 %maximum_maximum_fusion.bw = bf16[2048,256]{1,0:T(8,128)(2,1)} fusion(bf16[2048,8]{1,0:T(8,128)(2,1)} %copy.40, bf16[2048,128]{1,0:T(8,128)(2,1)} %param.17, bf16[256]{0:T(256)(128)(2,1)S(1)} %pad.2.clone), kind=kLoop, calls=%fused_computation | loop fusion | flops 3145728 | bytes 1606144 | tf_op jit(solution)/shard_map/concatenate | solution.py:521
  42.6 6.2 %collective-permute-done.3.across = bf16[512,512]{1,0:T(8,128)(2,1)} collective-permute-done((bf16[512,512]{1,0:T(8,128)(2,1)S(1)}, bf16[512,512]{1,0:T(8,128)(2,1)}, u32[]{:S(2)}, u32[]{:S(2)}) %collective-permute-start.3) | collective-permute-done | bytes 524320 | tf_op jit(solution)/shard_map/ppermute | solution.py:448
  48.8 5.3 %all-to-all-done = bf16[4,2,256,128]{3,2,1,0:T(8,128)(2,1)S(1)} async-done(((bf16[4,2,256,128]{3,2,1,0:T(8,128)(2,1)}), bf16[4,2,256,128]{3,2,1,0:T(8,128)(2,1)S(1)}, u32[]{:S(2)}, u32[]{:S(2)}) %all-to-all-start) | async-done | bytes 524320 | tf_op jit(solution)/shard_map/all_to_all | solution.py:451
  54.0 3.6 %all-to-all-start.1 = ((bf16[4,2,256,128]{3,2,1,0:T(8,128)(2,1)}), bf16[4,2,256,128]{3,2,1,0:T(8,128)(2,1)S(1)}, u32[]{:S(2)}, u32[]{:S(2)}) async-start(bf16[4,2,256,128]{3,2,1,0:T(8,128)(2,1)} %bitcast.10), calls=%async_computation.1 | async-start | bytes 1048576 | tf_op jit(solution)/shard_map/all_to_all | solution.py:451
  57.7 1.3 copy-done.2
  59.0 1.6 copy-done.12
  60.6 1.6 copy-done.15
  62.2 0.7 copy-done.31
  62.9 0.9 copy-done.34
  63.8 8.6 %layer.4 = (bf16[256,512]{1,0:T(8,128)(2,1)S(1)}, bf16[256,512]{1,0:T(8,128)(2,1)}, bf16[256,512]{1,0:T(8,128)(2,1)S(1)}, bf16[256,512]{1,0:T(8,128)(2,1)S(1)}, bf16[8,256,128]{2,1,0:T(8,128)(2,1)S(1)}) custom-call(s32[64]{0:T(128)S(1)} %pad_add_fusion.meta, bf16[16,128,512]{2,1,0:T(8,128)(2,1)S(1)} %bitcast.21, bf16[16,128,512]{2,1,0:T(8,128)(2,1)} %bitcast.1.sibling, ...), custom_call_target="tpu_custom_call" | custom-call | flops 8000000000 | bytes 9437184 | tf_op jit(solution)/shard_map/layer/pallas_call | solution.py:310
  72.4 8.5 %layer.5 = (bf16[256,512]{1,0:T(8,128)(2,1)S(1)}, bf16[256,512]{1,0:T(8,128)(2,1)}, bf16[256,512]{1,0:T(8,128)(2,1)S(1)}, bf16[256,512]{1,0:T(8,128)(2,1)S(1)}, bf16[8,256,128]{2,1,0:T(8,128)(2,1)S(1)}) custom-call(s32[64]{0:T(128)S(1)} %pad_add_fusion.meta, ...), custom_call_target="tpu_custom_call", output_to_operand_aliasing={{0}: (13, {}), {1}: (14, {}), {2}: (15, {}), {3}: (16, {}),... | custom-call | flops 8000000000 | bytes 9437184 | tf_op jit(solution)/shard_map/layer/pallas_call | solution.py:310
  80.9 0.8 copy-done.11
  81.7 0.7 copy-done.19
  82.4 0.7 copy-done.20
  83.1 0.7 copy-done.37
  84.3 1.5 all-to-all-done.1
  85.8 3.7 %all-to-all-start.2 = ((bf16[4,2,256,128]{3,2,1,0:T(8,128)(2,1)}), bf16[4,2,256,128]{3,2,1,0:T(8,128)(2,1)S(1)}, u32[]{:S(2)}, u32[]{:S(2)}) async-start(bf16[4,2,256,128]{3,2,1,0:T(8,128)(2,1)} %bitcast.30), calls=%async_computation.2 | async-start | bytes 1048576 | tf_op jit(solution)/shard_map/all_to_all | solution.py:451
  89.6 1.6 collective-permute-start.6
  91.8 1.2 copy-done.4
  93.0 1.6 copy-done.13
  94.6 1.6 copy-done.16
  96.2 0.7 copy-done.32
  96.9 0.9 copy-done.35
  97.8 7.8 %layer.6 = (bf16[128,512]{1,0:T(8,128)(2,1)S(1)}, bf16[128,512]{1,0:T(8,128)(2,1)S(1)}, bf16[128,512]{1,0:T(8,128)(2,1)S(1)}, bf16[128,512]{1,0:T(8,128)(2,1)S(1)}, bf16[8,256,128]{2,1,0:T(8,128)(2,1)S(1)}) custom-call(s32[64]{0:T(128)S(1)} %pad_add_fusion.meta, bf16[16,128,512]{2,1,0:T(8,128)(2,1)S(1)} %bitcast.23, bf16[16,128,512]{2,1,0:T(8,128)(2,1)} %bitcast.1.sibling, ...), custom_call_target="tpu_custom_call" | custom-call | flops 8000000000 | bytes 9437184 | tf_op jit(solution)/shard_map/layer/pallas_call | solution.py:310
  105.6 0.8 copy-done.8
  106.4 0.7 copy-done.21
  107.1 0.7 copy-done.25
  107.7 0.7 copy-done.26
  108.4 0.7 copy-done.39
  109.1 1.2 copy-done.5
  110.3 1.0 copy-done.9
  111.3 1.6 copy-done.14
  112.9 1.6 copy-done.17
  114.5 0.7 copy-done.33
  115.2 0.9 copy-done.36
  116.1 7.9 %layer.7 = (bf16[128,512]{1,0:T(8,128)(2,1)S(1)}, bf16[128,512]{1,0:T(8,128)(2,1)S(1)}, bf16[128,512]{1,0:T(8,128)(2,1)S(1)}, bf16[128,512]{1,0:T(8,128)(2,1)S(1)}, bf16[8,256,128]{2,1,0:T(8,128)(2,1)S(1)}) custom-call(s32[64]{0:T(128)S(1)} %pad_add_fusion.meta, bf16[16,128,512]{2,1,0:T(8,128)(2,1)S(1)} %bitcast.24, ...), custom_call_target="tpu_custom_call", output_to_operand_aliasing={{4}: (13, {})} | custom-call | flops 8000000000 | bytes 9437184 | tf_op jit(solution)/shard_map/layer/pallas_call | solution.py:310
  124.0 0.8 copy-done.10
  125.4 0.6 copy-done.23
  126.7 0.7 copy-done.41
  127.4 4.9 %all-to-all-start.3 = ((bf16[4,2,256,128]{3,2,1,0:T(8,128)(2,1)}), bf16[4,2,256,128]{3,2,1,0:T(8,128)(2,1)S(1)}, u32[]{:S(2)}, u32[]{:S(2)}) async-start(bf16[4,2,256,128]{3,2,1,0:T(8,128)(2,1)} %bitcast.29), calls=%async_computation.3 | async-start | bytes 1048576 | tf_op jit(solution)/shard_map/all_to_all | solution.py:451
  132.3 1.6 collective-permute-start.11
  134.4 1.6 collective-permute-start.16
  136.0 2.8 %collective-permute-done.11.refs_6_ = bf16[128,512]{1,0:T(8,128)(2,1)S(1)} collective-permute-done((bf16[128,512]{1,0:T(8,128)(2,1)}, bf16[128,512]{1,0:T(8,128)(2,1)S(1)}, u32[]{:S(2)}, u32[]{:S(2)}) %collective-permute-start.11) | collective-permute-done | bytes 131104 | tf_op jit(solution)/shard_map/ppermute | solution.py:448
  139.3 0.7 broadcast_subtract_fusion.1
  140.1 6.9 %all-to-all-done.3 = bf16[4,2,256,128]{3,2,1,0:T(8,128)(2,1)S(1)} async-done(((bf16[4,2,256,128]{3,2,1,0:T(8,128)(2,1)}), bf16[4,2,256,128]{3,2,1,0:T(8,128)(2,1)S(1)}, u32[]{:S(2)}, u32[]{:S(2)}) %all-to-all-start.3) | async-done | bytes 524320 | tf_op jit(solution)/shard_map/all_to_all | solution.py:451
  147.1 3.1 %gather_states.1 = bf16[16,32768]{1,0:T(8,128)(2,1)} custom-call(s32[16]{0:T(128)S(1)} %get-tuple-element.76.index, bf16[8,256,128]{2,1,0:T(8,128)(2,1)S(1)} %bitcast.18, bf16[8,256,128]{2,1,0:T(8,128)(2,1)S(1)} %bitcast.19, bf16[256,256]{1,0:T(8,128)(2,1)S(1)} %copy-done.7), custom_call_target="tpu_custom_call" | custom-call | bytes 2097152 | tf_op jit(solution)/shard_map/gather_states/pallas_call | solution.py:397
  151.5 1.6 copy-done.18
  153.1 0.9 copy-done.28
  154.0 0.9 copy-done.30
  154.9 0.9 copy-done.38
  155.8 7.8 %project_out.1 = bf16[4,128,2048]{2,1,0:T(8,128)(2,1)} custom-call(s32[4]{0:T(128)S(1)} %slice_reduce_fusion.at_ref, bf16[256,512]{1,0:T(8,128)(2,1)S(1)} %copy-done.38, bf16[256,512]{1,0:T(8,128)(2,1)S(1)} %collective-permute-done.5.refs_1_, bf16[256,512]{1,0:T(8,128)(2,1)} %collective-permute-done.6.refs_2_, ...), custom_call_target="tpu_custom_call" | custom-call | flops 4294967296 | bytes 12582912 | tf_op jit(solution)/shard_map/project_out/pallas_call | solution.py:354
  (128 shorter events, 8.1 us)
Async XLA Ops:
  7.2 15.5 %copy-start.7 = (bf16[256,256]{1,0:T(8,128)(2,1)S(1)}, bf16[256,256]{1,0:T(8,128)(2,1)}, u32[]{:S(2)}) copy-start(bf16[256,256]{1,0:T(8,128)(2,1)} %constant.104.clone.swap) | copy-start | bytes 393220
  7.2 15.3 %copy-start.46 = (s32[64]{0:T(128)S(1)}, s32[64]{0:T(128)}, u32[]{:S(2)}) copy-start(s32[64]{0:T(128)} %param.24) | copy-start | bytes 772
  7.2 84.3 %all-gather.2.cloned.1.call-start = ((), (), s32[]{:S(2)}) async-start(), calls=%async_computation.4 | async-start | bytes 2359296 | tf_op jit(solution)/shard_map/all_gather | solution.py:526
  7.2 50.5 %collective-permute-start = (bf16[2048,512]{1,0:T(8,128)(2,1)}, bf16[2048,512]{1,0:T(8,128)(2,1)}, u32[]{:S(2)}, u32[]{:S(2)}) collective-permute-start(bf16[2048,512]{1,0:T(8,128)(2,1)} %param.14), channel_id=1, source_target_pairs={{0,1},{1,0},{2,3},{3,2},{4,5},{5,4},{6,7},{7,6},{8,9},{9,8},{10,11... | collective-permute-start | bytes 6291464 | tf_op jit(solution)/shard_map/ppermute | solution.py:448
  8.7 12.9 %collective-permute-start.19 = (bf16[64,2048]{1,0:T(8,128)(2,1)S(1)}, bf16[64,2048]{1,0:T(8,128)(2,1)S(1)}, u32[]{:S(2)}, u32[]{:S(2)}) collective-permute-start(bf16[64,2048]{1,0:T(8,128)(2,1)S(1)} %constant_dynamic-slice_fusion), channel_id=1, source_target_pairs={{0,2},{1,3},{2,0},{3,1},{4,6},{5,7},{6,4},{7,5},{8,10},{9,11},{10,... | collective-permute-start | bytes 786440 | tf_op jit(solution)/shard_map/ppermute | solution.py:448
  14.7 7.8 %copy-start.44 = (s32[16]{0:T(128)}, s32[16]{0:T(128)S(1)}, u32[]{:S(2)}) copy-start(s32[16]{0:T(128)S(1)} %get-tuple-element.79) | copy-start | bytes 196
  14.8 1.6 copy-start
  16.4 6.3 %copy-start.6 = (bf16[16,32768]{1,0:T(8,128)(2,1)S(1)}, bf16[16,32768]{1,0:T(8,128)(2,1)}, u32[]{:S(2)}) copy-start(bf16[16,32768]{1,0:T(8,128)(2,1)} %store.1) | copy-start | bytes 3145732
  16.4 22.9 %copy-start.45 = (f32[8]{0:T(128)S(1)}, f32[8]{0:T(128)}, u32[]{:S(2)}) copy-start(f32[8]{0:T(128)} %param.19) | copy-start | bytes 100
  21.6 0.8 copy-start.43
  22.4 15.1 %collective-permute-start.1 = (bf16[512,512]{1,0:T(8,128)(2,1)}, bf16[512,512]{1,0:T(8,128)(2,1)}, u32[]{:S(2)}, u32[]{:S(2)}) collective-permute-start(bf16[512,512]{1,0:T(8,128)(2,1)} %bitcast.2), channel_id=1, source_target_pairs={{0,2},{1,3},{2,0},{3,1},{4,6},{5,7},{6,4},{7,5},{8,10},{9,11},{10,... | collective-permute-start | bytes 1572872 | tf_op jit(solution)/shard_map/ppermute | solution.py:448
  25.6 28.4 %all-to-all-start = ((bf16[4,2,256,128]{3,2,1,0:T(8,128)(2,1)}), bf16[4,2,256,128]{3,2,1,0:T(8,128)(2,1)S(1)}, u32[]{:S(2)}, u32[]{:S(2)}) async-start(bf16[4,2,256,128]{3,2,1,0:T(8,128)(2,1)} %bitcast.6), calls=%async_computation | async-start | bytes 1048576 | tf_op jit(solution)/shard_map/all_to_all | solution.py:451
  31.0 26.7 %copy-start.1 = (bf16[2048,512]{1,0:T(8,128)(2,1)S(1)}, bf16[2048,512]{1,0:T(8,128)(2,1)}, u32[]{:S(2)}) copy-start(bf16[2048,512]{1,0:T(8,128)(2,1)} %param.14) | copy-start | bytes 6291460
  31.0 17.7 %collective-permute-start.3 = (bf16[512,512]{1,0:T(8,128)(2,1)S(1)}, bf16[512,512]{1,0:T(8,128)(2,1)}, u32[]{:S(2)}, u32[]{:S(2)}) collective-permute-start(bf16[512,512]{1,0:T(8,128)(2,1)S(1)} %bitcast.31), channel_id=1, source_target_pairs={{0,2},{1,3},{2,0},{3,1},{4,6},{5,7},{6,4},{7,5},{8,10},{9,11},{10,... | collective-permute-start | bytes 1572872 | tf_op jit(solution)/shard_map/ppermute | solution.py:448
  37.5 20.2 %collective-permute-start.2 = (bf16[512,512]{1,0:T(8,128)(2,1)}, bf16[512,512]{1,0:T(8,128)(2,1)}, u32[]{:S(2)}, u32[]{:S(2)}) collective-permute-start(bf16[512,512]{1,0:T(8,128)(2,1)} %collective-permute-done.1.across), channel_id=1, source_target_pairs={{0,1},{1,0},{2,3},{3,2},{4,5},{5,4},{6,7},{7,6},{8,9},{9,8},{10,11... | collective-permute-start | bytes 1572872 | tf_op jit(solution)/shard_map/ppermute | solution.py:448
  42.6 29.8 %collective-permute-start.8 = (bf16[512,512]{1,0:T(8,128)(2,1)}, bf16[512,512]{1,0:T(8,128)(2,1)}, u32[]{:S(2)}, u32[]{:S(2)}) collective-permute-start(bf16[512,512]{1,0:T(8,128)(2,1)} %bitcast.9), channel_id=1, source_target_pairs={{0,2},{1,3},{2,0},{3,1},{4,6},{5,7},{6,4},{7,5},{8,10},{9,11},{10,... | collective-permute-start | bytes 1572872 | tf_op jit(solution)/shard_map/ppermute | solution.py:448
  48.8 40.7 %collective-permute-start.13 = (bf16[512,512]{1,0:T(8,128)(2,1)}, bf16[512,512]{1,0:T(8,128)(2,1)}, u32[]{:S(2)}, u32[]{:S(2)}) collective-permute-start(bf16[512,512]{1,0:T(8,128)(2,1)} %bitcast.14), channel_id=1, source_target_pairs={{0,2},{1,3},{2,0},{3,1},{4,6},{5,7},{6,4},{7,5},{8,10},{9,11},{10,... | collective-permute-start | bytes 1572872 | tf_op jit(solution)/shard_map/ppermute | solution.py:448
  48.8 23.7 %collective-permute-start.4 = (bf16[512,512]{1,0:T(8,128)(2,1)}, bf16[512,512]{1,0:T(8,128)(2,1)}, u32[]{:S(2)}, u32[]{:S(2)}) collective-permute-start(bf16[512,512]{1,0:T(8,128)(2,1)} %collective-permute-done.3.across), channel_id=1, source_target_pairs={{0,1},{1,0},{2,3},{3,2},{4,5},{5,4},{6,7},{7,6},{8,9},{9,8},{10,11... | collective-permute-start | bytes 1572872 | tf_op jit(solution)/shard_map/ppermute | solution.py:448
  54.0 31.8 %all-to-all-start.1 = ((bf16[4,2,256,128]{3,2,1,0:T(8,128)(2,1)}), bf16[4,2,256,128]{3,2,1,0:T(8,128)(2,1)S(1)}, u32[]{:S(2)}, u32[]{:S(2)}) async-start(bf16[4,2,256,128]{3,2,1,0:T(8,128)(2,1)} %bitcast.10), calls=%async_computation.1 | async-start | bytes 1048576 | tf_op jit(solution)/shard_map/all_to_all | solution.py:451
  57.7 1.3 copy-start.2
  59.0 1.6 copy-start.12
  60.6 1.6 copy-start.15
  62.2 0.7 copy-start.31
  62.9 0.9 copy-start.34
  63.8 8.7 %copy-start.3 = (bf16[2048,256]{1,0:T(8,128)(2,1)S(1)}, bf16[2048,256]{1,0:T(8,128)(2,1)}, u32[]{:S(2)}) copy-start(bf16[2048,256]{1,0:T(8,128)(2,1)} %maximum_maximum_fusion.bw) | copy-start | bytes 3145732
  72.3 19.1 %collective-permute-start.9 = (bf16[512,512]{1,0:T(8,128)(2,1)}, bf16[512,512]{1,0:T(8,128)(2,1)}, u32[]{:S(2)}, u32[]{:S(2)}) collective-permute-start(bf16[512,512]{1,0:T(8,128)(2,1)} %collective-permute-done.8.across), channel_id=1, source_target_pairs={{0,1},{1,0},{2,3},{3,2},{4,5},{5,4},{6,7},{7,6},{8,9},{9,8},{10,11... | collective-permute-start | bytes 1572872 | tf_op jit(solution)/shard_map/ppermute | solution.py:448
  80.9 0.8 copy-start.11
  81.7 0.7 copy-start.19
  82.4 0.7 copy-start.20
  83.1 0.7 copy-start.37
  83.8 7.4 %collective-permute-start.5 = (bf16[256,512]{1,0:T(8,128)(2,1)}, bf16[256,512]{1,0:T(8,128)(2,1)S(1)}, u32[]{:S(2)}, u32[]{:S(2)}) collective-permute-start(bf16[256,512]{1,0:T(8,128)(2,1)} %get-tuple-element.51), channel_id=1, source_target_pairs={{0,1},{1,0},{2,3},{3,2},{4,5},{5,4},{6,7},{7,6},{8,9},{9,8},{10,11... | collective-permute-start | bytes 786440 | tf_op jit(solution)/shard_map/ppermute | solution.py:448
  84.3 49.9 %collective-permute-start.18 = (bf16[512,2048]{1,0:T(8,128)(2,1)}, bf16[512,2048]{1,0:T(8,128)(2,1)}, u32[]{:S(2)}, u32[]{:S(2)}) collective-permute-start(bf16[512,2048]{1,0:T(8,128)(2,1)} %refs_12_.1), channel_id=1, source_target_pairs={{0,1},{1,0},{2,3},{3,2},{4,5},{5,4},{6,7},{7,6},{8,9},{9,8},{10,11... | collective-permute-start | bytes 6291464 | tf_op jit(solution)/shard_map/ppermute | solution.py:448
  85.8 23.2 %all-to-all-start.2 = ((bf16[4,2,256,128]{3,2,1,0:T(8,128)(2,1)}), bf16[4,2,256,128]{3,2,1,0:T(8,128)(2,1)S(1)}, u32[]{:S(2)}, u32[]{:S(2)}) async-start(bf16[4,2,256,128]{3,2,1,0:T(8,128)(2,1)} %bitcast.30), calls=%async_computation.2 | async-start | bytes 1048576 | tf_op jit(solution)/shard_map/all_to_all | solution.py:451
  89.5 19.5 %collective-permute-start.14 = (bf16[512,512]{1,0:T(8,128)(2,1)}, bf16[512,512]{1,0:T(8,128)(2,1)}, u32[]{:S(2)}, u32[]{:S(2)}) collective-permute-start(bf16[512,512]{1,0:T(8,128)(2,1)} %collective-permute-done.13.across), channel_id=1, source_target_pairs={{0,1},{1,0},{2,3},{3,2},{4,5},{5,4},{6,7},{7,6},{8,9},{9,8},{10,11... | collective-permute-start | bytes 1572872 | tf_op jit(solution)/shard_map/ppermute | solution.py:448
  89.6 19.4 %collective-permute-start.6 = (bf16[256,512]{1,0:T(8,128)(2,1)}, bf16[256,512]{1,0:T(8,128)(2,1)}, u32[]{:S(2)}, u32[]{:S(2)}) collective-permute-start(bf16[256,512]{1,0:T(8,128)(2,1)} %copy-done.19), channel_id=1, source_target_pairs={{0,2},{1,3},{2,0},{3,1},{4,6},{5,7},{6,4},{7,5},{8,10},{9,11},{10,... | collective-permute-start | bytes 786440 | tf_op jit(solution)/shard_map/ppermute | solution.py:448
  91.2 17.8 %collective-permute-start.7 = (bf16[256,512]{1,0:T(8,128)(2,1)}, bf16[256,512]{1,0:T(8,128)(2,1)}, u32[]{:S(2)}, u32[]{:S(2)}) collective-permute-start(bf16[256,512]{1,0:T(8,128)(2,1)} %copy-done.20), channel_id=1, source_target_pairs={{0,3},{1,2},{2,1},{3,0},{4,7},{5,6},{6,5},{7,4},{8,11},{9,10},{10,... | collective-permute-start | bytes 786440 | tf_op jit(solution)/shard_map/ppermute | solution.py:448
  91.5 60.0 %collective-permute-start.20 = (bf16[512,2048]{1,0:T(8,128)(2,1)}, bf16[512,2048]{1,0:T(8,128)(2,1)}, u32[]{:S(2)}, u32[]{:S(2)}) collective-permute-start(bf16[512,2048]{1,0:T(8,128)(2,1)} %all-gather.2.cloned.1.call-done.refs_14_), channel_id=1, source_target_pairs={{0,1},{1,0},{2,3},{3,2},{4,5},{5,4},{6,7},{7,6},{8,9},{9,8},{10,11... | collective-permute-start | bytes 6291464 | tf_op jit(solution)/shard_map/ppermute | solution.py:448
  91.8 1.2 copy-start.4
  93.0 1.6 copy-start.13
  94.6 1.6 copy-start.16
  96.2 0.7 copy-start.32
  96.9 0.9 copy-start.35
  105.6 0.8 copy-start.8
  106.4 0.7 copy-start.21
  109.0 1.2 copy-start.5
  110.3 1.0 copy-start.9
  111.3 1.6 copy-start.14
  112.9 1.6 copy-start.17
  114.5 0.7 copy-start.33
  115.2 0.9 copy-start.36
  124.0 0.8 copy-start.10
  127.4 24.1 %copy-start.40 = (bf16[128,512]{1,0:T(8,128)(2,1)S(1)}, bf16[128,512]{1,0:T(8,128)(2,1)}, u32[]{:S(2)}) copy-start(bf16[128,512]{1,0:T(8,128)(2,1)} %copy-done.39) | copy-start | bytes 393220
  127.4 19.7 %all-to-all-start.3 = ((bf16[4,2,256,128]{3,2,1,0:T(8,128)(2,1)}), bf16[4,2,256,128]{3,2,1,0:T(8,128)(2,1)S(1)}, u32[]{:S(2)}, u32[]{:S(2)}) async-start(bf16[4,2,256,128]{3,2,1,0:T(8,128)(2,1)} %bitcast.29), calls=%async_computation.3 | async-start | bytes 1048576 | tf_op jit(solution)/shard_map/all_to_all | solution.py:451
  132.3 2.2 %collective-permute-start.10 = (bf16[128,512]{1,0:T(8,128)(2,1)}, bf16[128,512]{1,0:T(8,128)(2,1)S(1)}, u32[]{:S(2)}, u32[]{:S(2)}) collective-permute-start(bf16[128,512]{1,0:T(8,128)(2,1)} %copy-done.26), channel_id=1, source_target_pairs={{0,1},{1,0},{2,3},{3,2},{4,5},{5,4},{6,7},{7,6},{8,9},{9,8},{10,11... | collective-permute-start | bytes 393224 | tf_op jit(solution)/shard_map/ppermute | solution.py:448
  132.3 6.5 %collective-permute-start.11 = (bf16[128,512]{1,0:T(8,128)(2,1)}, bf16[128,512]{1,0:T(8,128)(2,1)S(1)}, u32[]{:S(2)}, u32[]{:S(2)}) collective-permute-start(bf16[128,512]{1,0:T(8,128)(2,1)} %copy-done.25), channel_id=1, source_target_pairs={{0,2},{1,3},{2,0},{3,1},{4,6},{5,7},{6,4},{7,5},{8,10},{9,11},{10,... | collective-permute-start | bytes 393224 | tf_op jit(solution)/shard_map/ppermute | solution.py:448
  133.8 16.3 %collective-permute-start.12 = (bf16[128,512]{1,0:T(8,128)(2,1)}, bf16[128,512]{1,0:T(8,128)(2,1)S(1)}, u32[]{:S(2)}, u32[]{:S(2)}) collective-permute-start(bf16[128,512]{1,0:T(8,128)(2,1)} %copy-done.21), channel_id=1, source_target_pairs={{0,3},{1,2},{2,1},{3,0},{4,7},{5,6},{6,5},{7,4},{8,11},{9,10},{10,... | collective-permute-start | bytes 393224 | tf_op jit(solution)/shard_map/ppermute | solution.py:448
  134.1 16.0 %collective-permute-start.15 = (bf16[128,512]{1,0:T(8,128)(2,1)}, bf16[128,512]{1,0:T(8,128)(2,1)S(1)}, u32[]{:S(2)}, u32[]{:S(2)}) collective-permute-start(bf16[128,512]{1,0:T(8,128)(2,1)} %copy-done.24), channel_id=1, source_target_pairs={{0,1},{1,0},{2,3},{3,2},{4,5},{5,4},{6,7},{7,6},{8,9},{9,8},{10,11... | collective-permute-start | bytes 393224 | tf_op jit(solution)/shard_map/ppermute | solution.py:448
  134.4 15.7 %collective-permute-start.16 = (bf16[128,512]{1,0:T(8,128)(2,1)}, bf16[128,512]{1,0:T(8,128)(2,1)S(1)}, u32[]{:S(2)}, u32[]{:S(2)}) collective-permute-start(bf16[128,512]{1,0:T(8,128)(2,1)} %copy-done.23), channel_id=1, source_target_pairs={{0,2},{1,3},{2,0},{3,1},{4,6},{5,7},{6,4},{7,5},{8,10},{9,11},{10,... | collective-permute-start | bytes 393224 | tf_op jit(solution)/shard_map/ppermute | solution.py:448
  138.8 12.0 %collective-permute-start.17 = (bf16[128,512]{1,0:T(8,128)(2,1)}, bf16[128,512]{1,0:T(8,128)(2,1)S(1)}, u32[]{:S(2)}, u32[]{:S(2)}) collective-permute-start(bf16[128,512]{1,0:T(8,128)(2,1)} %copy-done.22), channel_id=1, source_target_pairs={{0,3},{1,2},{2,1},{3,0},{4,7},{5,6},{6,5},{7,4},{8,11},{9,10},{10,... | collective-permute-start | bytes 393224 | tf_op jit(solution)/shard_map/ppermute | solution.py:448
  147.1 4.4 %copy-start.42 = (bf16[128,512]{1,0:T(8,128)(2,1)S(1)}, bf16[128,512]{1,0:T(8,128)(2,1)}, u32[]{:S(2)}) copy-start(bf16[128,512]{1,0:T(8,128)(2,1)} %copy-done.41) | copy-start | bytes 393220
  151.5 1.6 copy-start.18
  153.1 0.9 copy-start.28
  154.0 0.9 copy-start.30
  154.9 0.9 copy-start.38
  (9 other events, 5.9 us)
Sparse Core Ops, SparseCore 0:
  22.5 66.9 all-gather.1

commit v5 on v0

v5 whole, which is shorter than its diff:
```python
import jax
import jax.numpy as jnp
import numpy as np
from jax import lax
from jax.experimental import pallas as pl
from jax.experimental.pallas import tpu as pltpu
from jax.sharding import PartitionSpec as P

BF = jnp.bfloat16
F32 = jnp.float32
ANY = pl.BlockSpec(memory_space=pl.ANY)
VMEM = pl.BlockSpec(memory_space=pltpu.VMEM)
SMEM = pl.BlockSpec(memory_space=pltpu.SMEM)
NT = (((1,), (1,)), ((), ()))


def rank_within(keys, order):
    earlier = (keys[None, :] == keys[:, None]) & (order[None, :] < order[:, None])
    return jnp.sum(earlier.astype(jnp.int32), axis=1)


def pack_states(source, store, swap, slots):
    sessions, width = store.shape
    lines = width // 128

    def kernel(source, store, swap, out, held):
        for part in range(4):
            base = part * 16 * 128
            stacked = jnp.concatenate(
                [store[:, base + j * 128 : base + (j + 1) * 128] for j in range(16)], axis=0
            )
            turned = jnp.dot(swap[...], stacked, preferred_element_type=F32).astype(BF)
            for r in range(sessions):
                held[r, part * 16 : (part + 1) * 16, :] = turned[r * 16 : (r + 1) * 16]
        for n in range(slots):
            out[n] = held[source[n]]

    return pl.pallas_call(
        kernel,
        grid=(lines // 64,),
        out_shape=jax.ShapeDtypeStruct((slots, lines, 128), BF),
        in_specs=[
            SMEM,
            pl.BlockSpec((sessions, 64 * 128), lambda j: (0, j)),
            pl.BlockSpec(swap.shape, lambda j: (0, 0)),
        ],
        out_specs=pl.BlockSpec((slots, 64, 128), lambda j: (0, j, 0)),
        scratch_shapes=[pltpu.VMEM((sessions, 64, 128), BF)],
        compiler_params=pltpu.CompilerParams(vmem_limit_bytes=16 * 2**20),
        cost_estimate=pl.CostEstimate(
            flops=2 * 256 * 256 * width // 16, bytes_accessed=4 * 2**20, transcendentals=0
        ),
        name="pack_states",
    )(source, store, swap)


def gather_states(index, returned, swap):
    sessions = index.shape[0]
    slots, lines, lanes = returned.shape

    def kernel(index, returned, swap, out):
        for part in range(4):
            rows = slice(part * 16, (part + 1) * 16)
            stacked = jnp.concatenate(
                [returned[index[r], rows, :] for r in range(sessions)], axis=0
            )
            turned = lax.dot_general(
                swap[...], stacked, (((0,), (0,)), ((), ())), preferred_element_type=F32
            ).astype(BF)
            for j in range(16):
                column = (part * 16 + j) * 128
                out[:, column : column + 128] = turned[j * sessions : (j + 1) * sessions]

    return pl.pallas_call(
        kernel,
        grid=(lines // 64,),
        out_shape=jax.ShapeDtypeStruct((sessions, lines * lanes), BF),
        in_specs=[
            SMEM,
            pl.BlockSpec((slots, 64, lanes), lambda j: (0, j, 0)),
            pl.BlockSpec(swap.shape, lambda j: (0, 0)),
        ],
        out_specs=pl.BlockSpec((sessions, 64 * lanes), lambda j: (0, j)),
        compiler_params=pltpu.CompilerParams(vmem_limit_bytes=16 * 2**20),
        cost_estimate=pl.CostEstimate(flops=0, bytes_accessed=2 * 2**20, transcendentals=0),
        name="gather_states",
    )(index, returned, swap)


def project(me, pieces, weight, columns):
    depth = pieces[0].shape[1]
    total = None
    for k in range(4):
        first = pl.multiple_of((me ^ k) * depth, depth)
        part = jnp.dot(
            pieces[k][...], weight[pl.ds(first, depth), columns], preferred_element_type=F32
        )
        total = part if total is None else total + part
    return total


def state_kernel(
    heads, span, pairs, half, meta, own, sibling, across, far, xw, bw, small, s0, s1, *refs
):
    xs, bc_out, steps_out, totals_out, outgoing, fresh, sems = refs[-7:]
    me = meta[0]
    step = pl.program_id(0)
    target = me ^ step
    pieces = (own, sibling, across, far)
    quads = heads // 4
    states = (s0, s1)
    bcs = project(me, pieces, bw, slice(None))
    for quad in range(quads):
        columns = slice(quad * 256, quad * 256 + 256)
        xs[:, columns] = project(me, pieces, xw, columns).astype(BF)
    bc_out[...] = bcs[:, :128].astype(BF)

    lane = lax.broadcasted_iota(jnp.int32, (span, 128), 1)
    low = lane < 64
    lane8 = lax.broadcasted_iota(jnp.int32, (heads, span), 1)
    lane_all = lax.broadcasted_iota(jnp.int32, (heads * pairs, span), 1)
    first_session = (target * 2 + half) * pairs
    raw = jnp.concatenate(
        [
            jnp.transpose(bcs[i * span : (i + 1) * span, 128:256])[:heads] + small[:, 0:1]
            for i in range(pairs)
        ],
        axis=0,
    )
    counts_at = 1 + meta.shape[0] // 2
    alive = jnp.concatenate(
        [(lane8 < meta[counts_at + first_session + i]).astype(F32) for i in range(pairs)], axis=0
    )
    steps = (jnp.maximum(raw, 0.0) + jnp.log1p(jnp.exp(-jnp.abs(raw)))) * alive
    totals = steps * jnp.concatenate([small[:, 1:2]] * pairs, axis=0)
    shift = 1
    while shift < span:
        totals = totals + jnp.where(lane_all >= shift, pltpu.roll(totals, shift, 1), 0.0)
        shift *= 2
    steps_out[...] = steps
    totals_out[...] = totals
    lasts = totals[:, span - 1 : span]
    weight_rows = jnp.exp(jnp.minimum(totals - lasts, 0.0)) * steps
    kept = jnp.exp(-lasts)

    for i in range(pairs):
        rows = slice(i * span, (i + 1) * span)
        bc = bcs[rows, 0:128]
        b_low = jnp.where(low, bc, 0.0).astype(BF)
        b_high = jnp.where(low, 0.0, pltpu.roll(bc, 64, 1)).astype(BF)
        b_both = jnp.concatenate([b_low, b_high], axis=0)
        for quad in range(quads):
            head = i * heads + quad * 4
            scale = jnp.concatenate(
                [
                    jnp.broadcast_to(weight_rows[head + k : head + k + 1, :], (32, span))
                    for k in range(4)
                ],
                axis=0,
            )
            x = xs[rows, quad * 256 : quad * 256 + 256].astype(F32)
            even = (jnp.transpose(x[:, :128]) * scale).astype(BF)
            odd = (jnp.transpose(x[:, 128:]) * scale).astype(BF)
            added = jnp.dot(
                jnp.concatenate([even, odd], axis=1), b_both, preferred_element_type=F32
            )
            keep = jnp.concatenate(
                [
                    jnp.broadcast_to(kept[head + k : head + k + 1, :], (32, 128))
                    for k in range(4)
                ],
                axis=0,
            )
            part = slice(quad * 128, quad * 128 + 128)
            fresh[step * pairs + i, part, :] = (
                keep * states[i][part, :].astype(F32) + added
            ).astype(BF)

    def sending(at, i):
        session = ((me ^ at) * 2 + half) * pairs + i
        number = at * pairs + i
        return pltpu.make_async_copy(
            fresh.at[number], outgoing.at[meta[1 + session]], sems.at[number]
        )

    for i in range(pairs):
        sending(step, i).start()

    @pl.when(step == 3)
    def _():
        for at in range(4):
            for i in range(pairs):
                sending(at, i).wait()


def scan_kernel(
    heads, span, pairs, half, meta, own, sibling, across, far, zw, gain, order, xs, bcs,
    steps_in, totals_in, s0, s1, n0, n1, n2, n3, zs,
):
    normed_out = (n0, n1, n2, n3)
    me = meta[0]
    step = pl.program_id(0)
    target = me ^ step
    pieces = (own, sibling, across, far)
    quads = heads // 4
    states = (s0, s1)
    for quad in range(quads):
        columns = slice(quad * 256, quad * 256 + 256)
        zs[:, columns] = project(me, pieces, zw, columns).astype(BF)

    lane = lax.broadcasted_iota(jnp.int32, (span, 128), 1)
    row = lax.broadcasted_iota(jnp.int32, (span, 128), 0)
    low = lane < 64
    causal = row >= lane
    head_masks = []
    for k in range(4):
        mask = (lane // 32 == k).astype(F32).astype(BF)
        head_masks.append(jnp.concatenate([mask, mask], axis=1))
    steps = steps_in[...]
    totals = totals_in[...]
    cum = jnp.transpose(
        jnp.concatenate([totals, jnp.zeros((128 - heads * pairs, span), F32)], axis=0)
    )
    counts_at = 1 + meta.shape[0] // 2
    for i in range(pairs):
        rows = slice(i * span, (i + 1) * span)
        count = meta[counts_at + (target * 2 + half) * pairs + i]
        bc = bcs[rows, :].astype(F32)
        turned = pltpu.roll(bc, 64, 1)
        b_low = jnp.where(low, bc, 0.0).astype(BF)
        c_low = jnp.where(low, turned, 0.0).astype(BF)
        c_high = jnp.where(low, 0.0, bc).astype(BF)
        scores = lax.dot_general(c_low, b_low, NT, preferred_element_type=F32)
        scores = jnp.where(causal, scores, 0.0)
        carried = lax.dot_general(
            jnp.concatenate([c_low, c_high], axis=0),
            states[i][...],
            NT,
            preferred_element_type=F32,
        )
        gated = []
        squares = None
        for quad in range(quads):
            columns = slice(quad * 256, quad * 256 + 256)
            part = slice(quad * 128, quad * 128 + 128)
            x = xs[rows, columns]
            mixes = []
            spread = None
            for k in range(4):
                head = i * heads + quad * 4 + k
                level = jnp.broadcast_to(cum[:, head : head + 1], (span, 128))
                gap = jnp.minimum(totals[head : head + 1, :] - level, 0.0)
                mixes.append((jnp.exp(gap) * steps[head : head + 1, :] * scores).astype(BF))
                spread = level if spread is None else jnp.where(lane >= 32 * k, level, spread)
            diagonal = jnp.dot(
                jnp.concatenate(mixes, axis=1),
                jnp.concatenate([x * head_masks[k] for k in range(4)], axis=0),
                preferred_element_type=F32,
            )
            fade = jnp.exp(-spread)
            before = jnp.concatenate(
                [carried[:span, part] * fade, carried[span:, part] * fade], axis=1
            )
            gate = zs[rows, columns].astype(F32)
            value = (diagonal + before) * (gate * (0.5 + 0.5 * jnp.tanh(0.5 * gate)))
            gated.append(value)
            own_squares = jnp.sum(value * value, axis=1, keepdims=True)
            squares = own_squares if squares is None else squares + own_squares
        inverse = lax.rsqrt(squares * (1.0 / (heads * 64)) + 1e-05)
        inverse = jnp.where(row[:, :1] < count, inverse, 0.0)
        for quad in range(quads):
            columns = slice(quad * 256, quad * 256 + 256)
            normed = (gated[quad] * inverse * gain[:, columns]).astype(BF)
            zs[rows, columns] = lax.dot_general(
                normed, order[...], NT, preferred_element_type=F32
            ).astype(BF)
    for d in range(4):

        @pl.when(step == d)
        def _():
            normed_out[d][...] = zs[...]


def whole(array):
    return pl.BlockSpec(array.shape, lambda i, meta: (0,) * array.ndim)


def token_specs(half, rows, depth):
    def near(i, meta):
        return (meta[0] ^ i, half, 0, 0)

    def arrived(i, meta):
        return (meta[0] ^ i, 0, 0)

    return [pl.BlockSpec((None, None, rows, depth), near)] * 2 + [
        pl.BlockSpec((None, rows, depth), arrived)
    ] * 2


def state_specs(inbound, pairs, half):
    def slot_of(n):
        return lambda i, meta: (meta[1 + ((meta[0] ^ i) * 2 + half) * pairs + n], 0, 0)

    return [pl.BlockSpec((None,) + inbound.shape[1:], slot_of(n)) for n in range(pairs)]


def by_step(shape, dtype=None):
    return pl.BlockSpec((None,) + tuple(shape), lambda i, meta: (i,) + (0,) * len(shape))


def state_call(half, meta, pieces, xw, bw, small, inbound, span, earlier):
    rows, depth = pieces[2].shape[1:]
    pairs = rows // span
    heads = small.shape[0]
    width = xw.shape[1]
    operands = [meta, *pieces, xw, bw, small] + [inbound] * pairs
    aliases = {}
    extra = []
    if earlier is not None:
        aliases = {len(operands): 4}
        operands.append(earlier)
        extra = [ANY]
    return pl.pallas_call(
        lambda *refs: state_kernel(heads, span, pairs, half, *refs),
        out_shape=[
            jax.ShapeDtypeStruct((4, rows, width), BF),
            jax.ShapeDtypeStruct((4, rows, 128), BF),
            jax.ShapeDtypeStruct((4, heads * pairs, span), F32),
            jax.ShapeDtypeStruct((4, heads * pairs, span), F32),
            jax.ShapeDtypeStruct(inbound.shape, BF),
        ],
        grid_spec=pltpu.PrefetchScalarGridSpec(
            num_scalar_prefetch=1,
            grid=(4,),
            in_specs=token_specs(half, rows, depth)
            + [whole(xw), whole(bw), whole(small)]
            + state_specs(inbound, pairs, half)
            + extra,
            out_specs=[
                by_step((rows, width)),
                by_step((rows, 128)),
                by_step((heads * pairs, span)),
                by_step((heads * pairs, span)),
                ANY,
            ],
            scratch_shapes=[
                pltpu.VMEM((4 * pairs,) + inbound.shape[1:], BF),
                pltpu.SemaphoreType.DMA((4 * pairs,)),
            ],
        ),
        input_output_aliases=aliases,
        compiler_params=pltpu.CompilerParams(vmem_limit_bytes=32 * 2**20),
        cost_estimate=pl.CostEstimate(
            flops=8 * 10**9, bytes_accessed=9 * 2**20, transcendentals=0
        ),
        name="states",
    )(*operands)


def scan_call(half, meta, pieces, zw, gain, order, mid, inbound, span):
    rows, depth = pieces[2].shape[1:]
    pairs = rows // span
    xs, bcs, steps, totals = mid
    heads = steps.shape[1] // pairs
    width = zw.shape[1]
    return pl.pallas_call(
        lambda *refs: scan_kernel(heads, span, pairs, half, *refs),
        out_shape=[jax.ShapeDtypeStruct((rows, width), BF)] * 4,
        grid_spec=pltpu.PrefetchScalarGridSpec(
            num_scalar_prefetch=1,
            grid=(4,),
            in_specs=token_specs(half, rows, depth)
            + [whole(zw), whole(gain), whole(order)]
            + [by_step(part.shape[1:]) for part in mid]
            + state_specs(inbound, pairs, half),
            out_specs=[pl.BlockSpec((rows, width), lambda i, meta: (0, 0))] * 4,
            scratch_shapes=[pltpu.VMEM((rows, width), BF)],
        ),
        compiler_params=pltpu.CompilerParams(vmem_limit_bytes=32 * 2**20),
        cost_estimate=pl.CostEstimate(
            flops=10 * 10**9, bytes_accessed=9 * 2**20, transcendentals=0
        ),
        name="scan",
    )(meta, *pieces, zw, gain, order, *mid, *[inbound] * pairs)


def out_call(half, halves, normed, weights, earlier):
    rows, depth = normed[0].shape
    columns = weights[0].shape[1]
    block = 512

    def kernel(*refs):
        out = refs[-1]
        total = None
        for d in range(4):
            part = jnp.dot(refs[d][...], refs[4 + d][...], preferred_element_type=F32)
            total = part if total is None else total + part
        out[...] = total.astype(BF)

    operands = [*normed, *weights]
    extra = []
    aliases = {}
    if earlier is not None:
        aliases = {len(operands): 0}
        operands.append(earlier)
        extra = [ANY]
    return pl.pallas_call(
        kernel,
        grid=(columns // block,),
        out_shape=jax.ShapeDtypeStruct((halves * rows, columns), BF),
        in_specs=[pl.BlockSpec((rows, depth), lambda j: (0, 0))] * 4
        + [pl.BlockSpec((depth, block), lambda j: (0, j))] * 4
        + extra,
        out_specs=pl.BlockSpec((rows, block), lambda j: (half, j)),
        input_output_aliases=aliases,
        compiler_params=pltpu.CompilerParams(vmem_limit_bytes=24 * 2**20),
        cost_estimate=pl.CostEstimate(
            flops=2 * rows * depth * 4 * columns, bytes_accessed=10 * 2**20, transcendentals=0
        ),
        name="project_out",
    )(*operands)


def after(value, *others):
    return lax.optimization_barrier((value,) + others)[0]


def body(
    tokens,
    x_weight,
    z_weight,
    bc_weight,
    dt_weight,
    dt_bias,
    decay_rate,
    norm_gain,
    out_weight,
    store_states,
    home_rows,
    event_counts,
):
    shard_count = lax.axis_size("dp")
    model_shards = lax.axis_size("mp")
    shard_index = lax.axis_index("dp")
    me = lax.axis_index("mp")
    sessions_here, state_width = store_states.shape
    heads = dt_bias.shape[0]
    width = x_weight.shape[1]
    depth = tokens.shape[1]
    span = tokens.shape[0] // sessions_here
    halves = 2
    rows = tokens.shape[0] // (model_shards * halves)
    capacity = max(2, (sessions_here + shard_count - 1) // shard_count)
    slot_count = shard_count * capacity
    row_shape = (state_width // 128, 128)

    def exchange(value, distance):
        pairs = [(j, j ^ distance) for j in range(model_shards)]
        return lax.ppermute(value, "mp", pairs)

    def trade(value):
        return lax.all_to_all(
            value.reshape((shard_count, capacity) + row_shape),
            "dp",
            split_axis=0,
            concat_axis=0,
            tiled=True,
        ).reshape((slot_count,) + row_shape)

    blocks = tokens.reshape(model_shards, halves, rows, depth)
    across = [exchange(blocks[:, h], 2) for h in range(halves)]
    sibling = exchange(tokens, 1).reshape(blocks.shape)
    replicas = lax.axis_size("groups") * shard_count
    replica = lax.axis_index("groups") * shard_count + shard_index
    share = width // replicas
    ow_part = exchange(lax.dynamic_slice_in_dim(out_weight, replica * share, share), 2)

    local = jnp.arange(sessions_here, dtype=jnp.int32)
    store_rows = shard_index * sessions_here + local
    everyone = jnp.arange(home_rows.shape[0], dtype=jnp.int32)
    owner = jnp.sum(
        jnp.where(home_rows[None, :] == store_rows[:, None], everyone[None, :], 0), axis=1
    )
    server = owner // sessions_here
    row_slot = server * capacity + rank_within(server, local)
    wanted_slots = jnp.arange(slot_count, dtype=jnp.int32)
    source = jnp.sum(
        jnp.where(row_slot[None, :] == wanted_slots[:, None], local[None, :], 0), axis=1
    )
    swap_row = np.arange(sessions_here * 16)
    swap = jnp.asarray(
        (swap_row % 16 * sessions_here + swap_row // 16)[:, None] == swap_row[None, :], BF
    )
    packed = pack_states(source, store_states, swap, slot_count)
    inbound = trade(packed)
    wanted = lax.dynamic_slice_in_dim(home_rows, shard_index * sessions_here, sessions_here)
    home_shard = wanted // sessions_here
    session_slot = home_shard * capacity + rank_within(home_shard, wanted % sessions_here)
    meta = jnp.concatenate([me.reshape(1).astype(jnp.int32), session_slot, event_counts])

    new_column = np.arange(width)
    old_column = (
        new_column // 256 * 256
        + new_column // 32 % 4 * 64
        + new_column % 32 * 2
        + new_column // 128 % 2
    )
    turn = jnp.asarray(old_column[None, :] == np.arange(width)[:, None], BF)
    xw = jnp.dot(x_weight, turn, preferred_element_type=F32).astype(BF)
    zw = jnp.dot(z_weight, turn, preferred_element_type=F32).astype(BF)
    order = turn[:256, :256]
    bw = jnp.concatenate(
        [bc_weight, dt_weight, jnp.zeros((bc_weight.shape[0], 128 - heads), BF)], axis=1
    )
    gain = norm_gain.reshape(heads // 4, 4, 32, 2).transpose(0, 3, 1, 2).reshape(1, width)
    small = jnp.stack([dt_bias, decay_rate], axis=1)

    ow_part = after(ow_part, packed)
    ow_across = lax.all_gather(ow_part, ("groups", "dp"), axis=0, tiled=True)
    ow_sibling = exchange(out_weight, 1)
    ow_far = exchange(ow_across, 1)

    outgoing = None
    received = []
    done = []
    for h in range(halves):
        arrived = across[h]
        turn_meta = meta
        if h:
            turn_meta = after(meta, done[-1])
            arrived = after(arrived, done[-1])
        pieces = (blocks, sibling, arrived, exchange(arrived, 1))
        *mid, outgoing = state_call(
            h, turn_meta, pieces, xw, bw, small, inbound, span, outgoing
        )
        parts = scan_call(h, turn_meta, pieces, zw, gain, order, mid, inbound, span)
        done.append(parts[0])
        received.append([parts[0]] + [exchange(parts[d], d) for d in range(1, 4)])
    returned = trade(outgoing)
    new_store = gather_states(row_slot, returned, swap)
    ow = (out_weight, ow_sibling, ow_across, ow_far)
    out_tokens = None
    for h in range(halves):
        normed = list(received[h])
        if h == 0:
            normed[0] = after(normed[0], done[-1])
        out_tokens = out_call(h, halves, normed, ow, out_tokens)
    return (out_tokens, new_store)


def solution(mesh):
    return jax.shard_map(
        body,
        mesh=mesh,
        in_specs=(
            P(("groups", "dp"), "mp"),
            P(None, "mp"),
            P(None, "mp"),
            P(None, "mp"),
            P(None, "mp"),
            P("mp"),
            P("mp"),
            P("mp"),
            P("mp", None),
            P(("groups", "dp"), "mp"),
            P("groups"),
            P(("groups", "dp")),
        ),
        out_specs=(P(("groups", "dp", "mp"), None), P(("groups", "dp"), "mp")),
        check_vma=False,
    )
```

time: 220 us -> 188 us (0.85)
  Pallas kernels: 0 us -> 53.4 us
  matrix products: 51.3 us -> 7.94 us
  waiting for transfers between devices: 85.3 us -> 59.6 us
  other arithmetic: 15.7 us -> 1.11 us
  local copies, waits for them, and re-layouts: 41.3 us -> 32.8 us
  starting transfers between devices: 11.1 us -> 18.3 us
    pallas_call x0 -> x8, Pallas kernels: none -> 53.4 us  [the longest x2 18.1 us: scan_call(): pl.pallas_call(lambda *refs: scan_kernel(heads, span, pairs, half, *refs)...]
    all_to_all x2, waiting for transfers between devices: 48.4 us -> 3.01 us  [trade(): lax.all_to_all(value.reshape((shard_count, capacity) + row_shape), 'dp',...]
    dot_general x9 -> x2, matrix products: 51.3 us -> 7.94 us  [the longest x1 4.26 us: body(): zw = jnp.dot(z_weight, turn, preferred_element_type=F32).astype(BF)]
    ppermute x0 -> x14, waiting for transfers between devices: none -> 36.6 us  [exchange(): return lax.ppermute(value, 'mp', pairs)]
    unnamed x43 -> x87, local copies, waits for them, and re-layouts: 3.34 us -> 28.2 us
    reshape x8 -> x2, local copies, waits for them, and re-layouts: 22.7 us -> 0.22 us  [body(): norm_gain.reshape(heads // 4, 4, 32, 2).transpose(0, 3, 1, 2)]
    reduce_scatter x1 -> x0, waiting for transfers between devices: 21.1 us -> none  [body(): lax.psum_scatter(jnp.dot(normed, out_weight, preferred_element_type=jnp.f...]
    ppermute x0 -> x14, starting transfers between devices: none -> 9.7 us  [exchange(): return lax.ppermute(value, 'mp', pairs)]
  transfers between devices with their start and end apart: 4 -> 17, of which waited for: 4 -> 4; matrix products, arithmetic and copies ran while one was open for 17% -> 8% of each run, Pallas kernels for 0% -> 25%
where the time goes in v5:
time: 188 us; the launch traced here: 187 us
  waiting for transfers between devices  59.6 us (32%)
  Pallas kernels  53.4 us (28%)
  local copies, waits for them, and re-layouts  32.8 us (17%)
  starting transfers between devices  18.3 us (10%)
  between operations  14.3 us (8%)
  matrix products  7.94 us (4%)
    ppermute x14, waiting for transfers between devices, exchange(): return lax.ppermute(value, 'mp', pairs)  36.6 us
    unnamed x87, local copies, waits for them, and re-layouts  28.2 us
    all_gather x1, waiting for transfers between devices, body(): ow_across = lax.all_gather(ow_part, ('groups', 'dp'), axis=0, tiled=True)  20 us
    pallas_call x2, Pallas kernels, scan_call(): pl.pallas_call(lambda *refs: scan_kernel(heads, span, pairs, half, *refs)...  18.1 us
    pallas_call x2, Pallas kernels, state_call(): pl.pallas_call(lambda *refs: state_kernel(heads, span, pairs, half, *refs...  17.1 us
    pallas_call x2, Pallas kernels, out_call(): pl.pallas_call(kernel, grid=(columns // block,), out_shape=jax.ShapeDtype...  12.1 us
    ppermute x14, starting transfers between devices, exchange(): return lax.ppermute(value, 'mp', pairs)  9.7 us
    all_to_all x2, starting transfers between devices, trade(): lax.all_to_all(value.reshape((shard_count, capacity) + row_shape), 'dp',...  8.59 us
  transfers between devices with their start and end apart: 17, of which 4 were waited for; matrix products, arithmetic and copies ran while one was open for 8% of the time, Pallas kernels for 25%

profile of v5, /device:TPU:0, one launch (start us, length us, event | category | flops | bytes accessed | tf_op | source)
XLA Modules:
  0.0 187.4 jit_solution(2923128019014594818)
XLA Ops:
  7.2 0.5 collective-permute-start
  7.7 3.1 %slice_bitcast_fusion = (bf16[4,256,512]{2,1,0:T(8,128)(2,1)}, bf16[4,256,512]{2,1,0:T(8,128)(2,1)}) fusion(bf16[4,2,256,512]{3,2,1,0:T(8,128)(2,1)} %bitcast.27), kind=kLoop, calls=%fused_computation.4 | loop fusion | bytes 4194304 | tf_op jit(solution)/shard_map/squeeze | solution.py:471
  10.8 2.6 %collective-permute-start.1 = (bf16[4,256,512]{2,1,0:T(8,128)(2,1)}, bf16[4,256,512]{2,1,0:T(8,128)(2,1)}, u32[]{:S(2)}, u32[]{:S(2)}) collective-permute-start(bf16[4,256,512]{2,1,0:T(8,128)(2,1)} %get-tuple-element.49), channel_id=1, source_target_pairs={{0,2},{1,3},{2,0},{3,1},{4,6},{5,7},{6,4},{7,5},{8,10},{9,11},{10,... | collective-permute-start | bytes 3145736 | tf_op jit(solution)/shard_map/ppermute | solution.py:459
  13.4 0.2 select_reduce_fusion.1
  13.6 0.2 convert_reduce_fusion
  13.8 0.1 select_reduce_fusion.source
  13.9 3.0 %pack_states.1 = bf16[16,256,128]{2,1,0:T(8,128)(2,1)} custom-call(s32[16]{0:T(128)S(1)} %select_reduce_fusion.source, bf16[16,32768]{1,0:T(8,128)(2,1)S(1)} %copy-done.5, bf16[256,256]{1,0:T(8,128)(2,1)S(1)} %copy-done.9), custom_call_target="tpu_custom_call" | custom-call | flops 268435456 | bytes 4194304 | tf_op jit(solution)/shard_map/pack_states/pallas_call | solution.py:38
  16.9 4.9 %all-to-all-start = ((bf16[4,4,256,128]{3,2,1,0:T(8,128)(2,1)}), bf16[4,4,256,128]{3,2,1,0:T(8,128)(2,1)}, u32[]{:S(2)}, u32[]{:S(2)}) async-start(bf16[4,4,256,128]{3,2,1,0:T(8,128)(2,1)} %bitcast.9), calls=%async_computation | async-start | bytes 2097152 | tf_op jit(solution)/shard_map/all_to_all | solution.py:462
  21.8 0.5 collective-permute-start.3
  22.3 1.0 constant_dynamic-slice_fusion
  23.3 1.6 collective-permute-start.9
  25.0 3.7 %fusion.1.refs_5_ = bf16[2048,512]{1,0:T(8,128)(2,1)} fusion(bf16[2048,512]{1,0:T(8,128)(2,1)S(1)} %copy-done, bf16[512,512]{1,0:T(8,128)(2,1)} %constant.62.clone), kind=kOutput, calls=%fused_computation.3 | convolution fusion | flops 1074790400 | bytes 4718592 | tf_op jit(solution)/shard_map/dot_general | solution.py:509
  28.7 0.2 convert_reduce_fusion.1
  28.9 8.8 %collective-permute-done.1.refs_3_ = bf16[4,256,512]{2,1,0:T(8,128)(2,1)} collective-permute-done((bf16[4,256,512]{2,1,0:T(8,128)(2,1)}, bf16[4,256,512]{2,1,0:T(8,128)(2,1)}, u32[]{:S(2)}, u32[]{:S(2)}) %collective-permute-start.1) | collective-permute-done | bytes 1048608 | tf_op jit(solution)/shard_map/ppermute | solution.py:459
  37.7 27.7 %collective-permute-done.9 = bf16[64,2048]{1,0:T(8,128)(2,1)S(1)} collective-permute-done((bf16[64,2048]{1,0:T(8,128)(2,1)S(1)}, bf16[64,2048]{1,0:T(8,128)(2,1)S(1)}, u32[]{:S(2)}, u32[]{:S(2)}) %collective-permute-start.9) | collective-permute-done | bytes 262176 | tf_op jit(solution)/shard_map/ppermute | solution.py:459
  65.4 0.7 copy-done.35
  66.2 1.0 copy.47
  67.3 0.1 reshape.83
  67.4 0.1 copy.45
  67.5 0.1 reshape.84.refs_6_
  67.6 0.1 pad.4.clone
  67.8 4.3 %fusion.refs_5_ = bf16[2048,512]{1,0:T(8,128)(2,1)} fusion(bf16[2048,512]{1,0:T(8,128)(2,1)} %param.16, bf16[512,512]{1,0:T(8,128)(2,1)S(1)} %copy-done.42), kind=kOutput, calls=%fused_computation.2 | convolution fusion | flops 1074790400 | bytes 4718592 | tf_op jit(solution)/shard_map/dot_general | solution.py:510
  72.1 0.2 maximum_maximum_fusion.refs_6_
  72.3 1.6 copy-done.2
  73.9 1.7 copy-done.21
  75.6 8.6 %states.2 = (bf16[4,256,512]{2,1,0:T(8,128)(2,1)S(1)}, bf16[4,256,128]{2,1,0:T(8,128)(2,1)S(1)}, f32[4,16,128]{2,1,0:T(8,128)S(1)}, f32[4,16,128]{2,1,0:T(8,128)S(1)}, bf16[16,256,128]{2,1,0:T(8,128)(2,1)S(1)}) custom-call(s32[33]{0:T(128)S(1)} %pad_add_fusion.refs_0_, bf16[4,2,256,512]{3,2,1,0:T(8,128)(2,1)S(1)} %bitcast.28, ...), custom_call_target="tpu_custom_call" | custom-call | flops 8000000000 | bytes 9437184 | tf_op jit(solution)/shard_map/states/pallas_call | solution.py:323
  84.3 1.0 copy-done.6
  85.2 8.6 %scan.2 = (bf16[256,512]{1,0:T(8,128)(2,1)S(1)}, bf16[256,512]{1,0:T(8,128)(2,1)S(1)}, bf16[256,512]{1,0:T(8,128)(2,1)S(1)}, bf16[256,512]{1,0:T(8,128)(2,1)S(1)}) custom-call(s32[33]{0:T(128)S(1)} %pad_add_fusion.refs_0_, bf16[4,2,256,512]{3,2,1,0:T(8,128)(2,1)S(1)} %bitcast.29, bf16[4,2,256,512]{3,2,1,0:T(8,128)(2,1)} %bitcast.2.refs_2_, ...), custom_call_target="tpu_custom_call" | custom-call | flops 10000000000 | bytes 9437184 | tf_op jit(solution)/shard_map/scan/pallas_call | solution.py:366
  93.9 0.7 copy-done.16
  94.6 0.7 copy-done.17
  95.3 0.7 copy-done.18
  96.0 0.5 collective-permute-start.8
  96.5 20.0 %all-gather.2.cloned.1.call-done.refs_6_ = bf16[512,2048]{1,0:T(8,128)(2,1)} async-done(((bf16[64,2048]{1,0:T(8,128)(2,1)}), bf16[512,2048]{1,0:T(8,128)(2,1)}) %all-gather.2.cloned.1.call-update) | async-done | bytes 2097168 | tf_op jit(solution)/shard_map/all_gather | solution.py:519
  116.5 1.6 copy-done.3
  118.1 1.2 copy-done.7
  119.4 1.6 copy-done.22
  120.9 8.4 %states.3 = (bf16[4,256,512]{2,1,0:T(8,128)(2,1)S(1)}, bf16[4,256,128]{2,1,0:T(8,128)(2,1)S(1)}, f32[4,16,128]{2,1,0:T(8,128)S(1)}, f32[4,16,128]{2,1,0:T(8,128)S(1)}, bf16[16,256,128]{2,1,0:T(8,128)(2,1)S(1)}) custom-call(s32[33]{0:T(128)S(1)} %pad_add_fusion.refs_0_, bf16[4,2,256,512]{3,2,1,0:T(8,128)(2,1)S(1)} %bitcast.30, ...), custom_call_target="tpu_custom_call", output_to_operand_aliasing={{4}: (10, {})} | custom-call | flops 8000000000 | bytes 9437184 | tf_op jit(solution)/shard_map/states/pallas_call | solution.py:323
  129.4 1.0 copy-done.8
  130.4 1.0 copy-done.25
  131.3 0.7 copy-done.27
  132.0 0.6 copy-done.29
  132.7 0.6 copy-done.31
  133.3 3.7 %all-to-all-start.1 = ((bf16[4,4,256,128]{3,2,1,0:T(8,128)(2,1)}), bf16[4,4,256,128]{3,2,1,0:T(8,128)(2,1)S(1)}, u32[]{:S(2)}, u32[]{:S(2)}) async-start(bf16[4,4,256,128]{3,2,1,0:T(8,128)(2,1)} %bitcast.32), calls=%async_computation.1 | async-start | bytes 2097152 | tf_op jit(solution)/shard_map/all_to_all | solution.py:462
  137.0 0.3 collective-permute-start.11
  137.3 1.5 collective-permute-start.12
  138.9 1.6 copy-done.4
  140.5 0.9 copy-done.20
  141.4 1.6 copy-done.24
  143.0 1.2 copy-done.26
  144.2 0.9 copy-done.28
  145.2 0.8 copy-done.30
  145.9 0.8 copy-done.32
  146.7 9.5 %scan.3 = (bf16[256,512]{1,0:T(8,128)(2,1)S(1)}, bf16[256,512]{1,0:T(8,128)(2,1)}, bf16[256,512]{1,0:T(8,128)(2,1)}, bf16[256,512]{1,0:T(8,128)(2,1)}) custom-call(s32[33]{0:T(128)S(1)} %pad_add_fusion.refs_0_, bf16[4,2,256,512]{3,2,1,0:T(8,128)(2,1)S(1)} %bitcast.31, bf16[4,2,256,512]{3,2,1,0:T(8,128)(2,1)} %bitcast.2.refs_2_, ...), custom_call_target="tpu_custom_call" | custom-call | flops 10000000000 | bytes 9437184 | tf_op jit(solution)/shard_map/scan/pallas_call | solution.py:366
  156.1 0.7 copy-done.14
  156.9 0.6 collective-permute-start.5
  157.5 0.7 copy-done.10
  158.2 1.5 collective-permute-start.6
  159.7 0.7 copy-done.12
  160.4 3.0 %all-to-all-done.1 = bf16[4,4,256,128]{3,2,1,0:T(8,128)(2,1)S(1)} async-done(((bf16[4,4,256,128]{3,2,1,0:T(8,128)(2,1)}), bf16[4,4,256,128]{3,2,1,0:T(8,128)(2,1)S(1)}, u32[]{:S(2)}, u32[]{:S(2)}) %all-to-all-start.1) | async-done | bytes 1048608 | tf_op jit(solution)/shard_map/all_to_all | solution.py:462
  163.4 3.1 %gather_states.1 = bf16[16,32768]{1,0:T(8,128)(2,1)} custom-call(s32[16]{0:T(128)S(1)} %multiply_add_fusion.index, bf16[16,256,128]{2,1,0:T(8,128)(2,1)S(1)} %bitcast.26, bf16[256,256]{1,0:T(8,128)(2,1)S(1)} %copy-done.9), custom_call_target="tpu_custom_call" | custom-call | bytes 2097152 | tf_op jit(solution)/shard_map/gather_states/pallas_call | solution.py:74
  166.5 0.9 copy-done.11
  167.5 0.9 copy-done.13
  168.4 6.0 %project_out.2.refs_8_ = bf16[512,2048]{1,0:T(8,128)(2,1)} custom-call(bf16[256,512]{1,0:T(8,128)(2,1)S(1)} %get-tuple-element.41.refs_0_, bf16[256,512]{1,0:T(8,128)(2,1)S(1)} %copy-done.11, bf16[256,512]{1,0:T(8,128)(2,1)S(1)} %copy-done.13, bf16[256,512]{1,0:T(8,128)(2,1)} %collective-permute-done.13.refs_3_, bf16[512,2048]{1,0:T(8,128)(2,1)} %refs_4_.3, ...), custom_call_target="tpu_custom_call" | custom-call | flops 2147483648 | bytes 10485760 | tf_op jit(solution)/shard_map/project_out/pallas_call | solution.py:407
  174.4 6.1 %project_out.3 = bf16[512,2048]{1,0:T(8,128)(2,1)} custom-call(bf16[256,512]{1,0:T(8,128)(2,1)S(1)} %copy-done.15, bf16[256,512]{1,0:T(8,128)(2,1)} %collective-permute-done.5.refs_1_, bf16[256,512]{1,0:T(8,128)(2,1)} %collective-permute-done.6.refs_2_, bf16[256,512]{1,0:T(8,128)(2,1)} %collective-permute-done.7.refs_3_, ...), custom_call_target="tpu_custom_call", output_to_operand_aliasing={{}: (8, {})} | custom-call | flops 2147483648 | bytes 10485760 | tf_op jit(solution)/shard_map/project_out/pallas_call | solution.py:407
  (89 shorter events, 0.5 us)
Async XLA Ops:
  7.2 17.8 %copy-start = (bf16[2048,512]{1,0:T(8,128)(2,1)S(1)}, bf16[2048,512]{1,0:T(8,128)(2,1)}, u32[]{:S(2)}) copy-start(bf16[2048,512]{1,0:T(8,128)(2,1)} %param.15) | copy-start | bytes 6291460
  7.2 65.1 %collective-permute-start = (bf16[2048,512]{1,0:T(8,128)(2,1)}, bf16[2048,512]{1,0:T(8,128)(2,1)}, u32[]{:S(2)}, u32[]{:S(2)}) collective-permute-start(bf16[2048,512]{1,0:T(8,128)(2,1)} %param.14), channel_id=1, source_target_pairs={{0,1},{1,0},{2,3},{3,2},{4,5},{5,4},{6,7},{7,6},{8,9},{9,8},{10,11... | collective-permute-start | bytes 6291464 | tf_op jit(solution)/shard_map/ppermute | solution.py:459
  7.7 5.7 %copy-start.38 = (s32[64]{0:T(128)S(1)}, s32[64]{0:T(128)}, u32[]{:S(2)}) copy-start(s32[64]{0:T(128)} %param.24) | copy-start | bytes 772
  7.7 6.2 %copy-start.5 = (bf16[16,32768]{1,0:T(8,128)(2,1)S(1)}, bf16[16,32768]{1,0:T(8,128)(2,1)}, u32[]{:S(2)}) copy-start(bf16[16,32768]{1,0:T(8,128)(2,1)} %store.1) | copy-start | bytes 3145732
  7.7 6.2 %copy-start.9 = (bf16[256,256]{1,0:T(8,128)(2,1)S(1)}, bf16[256,256]{1,0:T(8,128)(2,1)}, u32[]{:S(2)}) copy-start(bf16[256,256]{1,0:T(8,128)(2,1)} %constant.61.clone.swap) | copy-start | bytes 393220
  10.8 26.9 %collective-permute-start.1 = (bf16[4,256,512]{2,1,0:T(8,128)(2,1)}, bf16[4,256,512]{2,1,0:T(8,128)(2,1)}, u32[]{:S(2)}, u32[]{:S(2)}) collective-permute-start(bf16[4,256,512]{2,1,0:T(8,128)(2,1)} %get-tuple-element.49), channel_id=1, source_target_pairs={{0,2},{1,3},{2,0},{3,1},{4,6},{5,7},{6,4},{7,5},{8,10},{9,11},{10,... | collective-permute-start | bytes 3145736 | tf_op jit(solution)/shard_map/ppermute | solution.py:459
  16.9 55.4 %all-to-all-start = ((bf16[4,4,256,128]{3,2,1,0:T(8,128)(2,1)}), bf16[4,4,256,128]{3,2,1,0:T(8,128)(2,1)}, u32[]{:S(2)}, u32[]{:S(2)}) async-start(bf16[4,4,256,128]{3,2,1,0:T(8,128)(2,1)} %bitcast.9), calls=%async_computation | async-start | bytes 2097152 | tf_op jit(solution)/shard_map/all_to_all | solution.py:462
  21.8 94.7 %all-gather.2.cloned.1.call-start = ((), (), s32[]{:S(2)}) async-start(), calls=%async_computation.2 | async-start | bytes 2359296 | tf_op jit(solution)/shard_map/all_gather | solution.py:519
  21.8 74.2 %collective-permute-start.3 = (bf16[4,256,512]{2,1,0:T(8,128)(2,1)}, bf16[4,256,512]{2,1,0:T(8,128)(2,1)}, u32[]{:S(2)}, u32[]{:S(2)}) collective-permute-start(bf16[4,256,512]{2,1,0:T(8,128)(2,1)} %get-tuple-element.48), channel_id=1, source_target_pairs={{0,2},{1,3},{2,0},{3,1},{4,6},{5,7},{6,4},{7,5},{8,10},{9,11},{10,... | collective-permute-start | bytes 3145736 | tf_op jit(solution)/shard_map/ppermute | solution.py:459
  23.3 42.1 %collective-permute-start.9 = (bf16[64,2048]{1,0:T(8,128)(2,1)S(1)}, bf16[64,2048]{1,0:T(8,128)(2,1)S(1)}, u32[]{:S(2)}, u32[]{:S(2)}) collective-permute-start(bf16[64,2048]{1,0:T(8,128)(2,1)S(1)} %constant_dynamic-slice_fusion), channel_id=1, source_target_pairs={{0,2},{1,3},{2,0},{3,1},{4,6},{5,7},{6,4},{7,5},{8,10},{9,11},{10,... | collective-permute-start | bytes 786440 | tf_op jit(solution)/shard_map/ppermute | solution.py:459
  24.9 41.2 %copy-start.39 = (f32[8]{0:T(128)S(1)}, f32[8]{0:T(128)}, u32[]{:S(2)}) copy-start(f32[8]{0:T(128)} %param.20) | copy-start | bytes 100
  25.0 41.2 %copy-start.40 = (f32[8]{0:T(128)S(1)}, f32[8]{0:T(128)}, u32[]{:S(2)}) copy-start(f32[8]{0:T(128)} %param.19) | copy-start | bytes 100
  25.0 41.2 %copy-start.36 = (bf16[2048,8]{0,1:T(8,128)(2,1)S(1)}, bf16[2048,8]{0,1:T(8,128)(2,1)}, u32[]{:S(2)}) copy-start(bf16[2048,8]{0,1:T(8,128)(2,1)} %param.18) | copy-start | bytes 98308
  25.0 42.3 %copy-start.37 = (f32[512]{0:T(512)S(1)}, f32[512]{0:T(512)}, u32[]{:S(2)}) copy-start(f32[512]{0:T(512)} %param.21) | copy-start | bytes 6148
  25.0 42.7 %copy-start.41 = (s32[16]{0:T(128)S(1)}, s32[16]{0:T(128)}, u32[]{:S(2)}) copy-start(s32[16]{0:T(128)} %param.25) | copy-start | bytes 196
  25.0 42.8 %copy-start.42 = (bf16[512,512]{1,0:T(8,128)(2,1)S(1)}, bf16[512,512]{1,0:T(8,128)(2,1)}, u32[]{:S(2)}) copy-start(bf16[512,512]{1,0:T(8,128)(2,1)} %constant.62.clone) | copy-start | bytes 1572868
  37.7 34.6 %collective-permute-start.2 = (bf16[4,256,512]{2,1,0:T(8,128)(2,1)}, bf16[4,256,512]{2,1,0:T(8,128)(2,1)}, u32[]{:S(2)}, u32[]{:S(2)}) collective-permute-start(bf16[4,256,512]{2,1,0:T(8,128)(2,1)} %collective-permute-done.1.refs_3_), channel_id=1, source_target_pairs={{0,1},{1,0},{2,3},{3,2},{4,5},{5,4},{6,7},{7,6},{8,9},{9,8},{10,11... | collective-permute-start | bytes 3145736 | tf_op jit(solution)/shard_map/ppermute | solution.py:459
  65.4 0.7 copy-start.35
  67.8 4.3 %copy-start.33 = (bf16[2048,8]{1,0:T(8,128)(2,1)S(1)}, bf16[2048,8]{1,0:T(8,128)(2,1)}, u32[]{:S(2)}) copy-start(bf16[2048,8]{1,0:T(8,128)(2,1)} %copy.47) | copy-start | bytes 98308
  67.8 4.3 %copy-start.34 = (bf16[2048,128]{1,0:T(8,128)(2,1)S(1)}, bf16[2048,128]{1,0:T(8,128)(2,1)}, u32[]{:S(2)}) copy-start(bf16[2048,128]{1,0:T(8,128)(2,1)} %param.17) | copy-start | bytes 1572868
  72.3 1.6 copy-start.2
  73.9 1.7 copy-start.21
  75.6 9.6 %copy-start.19 = (bf16[256,256]{1,0:T(8,128)(2,1)S(1)}, bf16[256,256]{1,0:T(8,128)(2,1)}, u32[]{:S(2)}) copy-start(bf16[256,256]{1,0:T(8,128)(2,1)} %constant.63.refs_7_) | copy-start | bytes 393220
  75.6 9.6 %copy-start.23 = (bf16[2048,512]{1,0:T(8,128)(2,1)S(1)}, bf16[2048,512]{1,0:T(8,128)(2,1)}, u32[]{:S(2)}) copy-start(bf16[2048,512]{1,0:T(8,128)(2,1)} %fusion.refs_5_) | copy-start | bytes 6291460
  84.3 1.0 copy-start.6
  93.9 0.7 copy-start.16
  94.6 0.7 copy-start.17
  95.3 0.7 copy-start.18
  96.0 20.5 %collective-permute-start.4 = (bf16[4,256,512]{2,1,0:T(8,128)(2,1)}, bf16[4,256,512]{2,1,0:T(8,128)(2,1)}, u32[]{:S(2)}, u32[]{:S(2)}) collective-permute-start(bf16[4,256,512]{2,1,0:T(8,128)(2,1)} %collective-permute-done.3.refs_3_), channel_id=1, source_target_pairs={{0,1},{1,0},{2,3},{3,2},{4,5},{5,4},{6,7},{7,6},{8,9},{9,8},{10,11... | collective-permute-start | bytes 3145736 | tf_op jit(solution)/shard_map/ppermute | solution.py:459
  96.0 60.8 %collective-permute-start.8 = (bf16[512,2048]{1,0:T(8,128)(2,1)}, bf16[512,2048]{1,0:T(8,128)(2,1)}, u32[]{:S(2)}, u32[]{:S(2)}) collective-permute-start(bf16[512,2048]{1,0:T(8,128)(2,1)} %refs_4_.3), channel_id=1, source_target_pairs={{0,1},{1,0},{2,3},{3,2},{4,5},{5,4},{6,7},{7,6},{8,9},{9,8},{10,11... | collective-permute-start | bytes 6291464 | tf_op jit(solution)/shard_map/ppermute | solution.py:459
  116.5 50.0 %collective-permute-start.10 = (bf16[512,2048]{1,0:T(8,128)(2,1)}, bf16[512,2048]{1,0:T(8,128)(2,1)}, u32[]{:S(2)}, u32[]{:S(2)}) collective-permute-start(bf16[512,2048]{1,0:T(8,128)(2,1)} %all-gather.2.cloned.1.call-done.refs_6_), channel_id=1, source_target_pairs={{0,1},{1,0},{2,3},{3,2},{4,5},{5,4},{6,7},{7,6},{8,9},{9,8},{10,11... | collective-permute-start | bytes 6291464 | tf_op jit(solution)/shard_map/ppermute | solution.py:459
  116.5 1.6 copy-start.3
  118.1 1.2 copy-start.7
  119.4 1.6 copy-start.22
  129.4 1.0 copy-start.8
  130.4 1.0 copy-start.25
  131.3 0.7 copy-start.27
  132.0 0.6 copy-start.29
  132.7 0.6 copy-start.31
  133.3 30.1 %all-to-all-start.1 = ((bf16[4,4,256,128]{3,2,1,0:T(8,128)(2,1)}), bf16[4,4,256,128]{3,2,1,0:T(8,128)(2,1)S(1)}, u32[]{:S(2)}, u32[]{:S(2)}) async-start(bf16[4,4,256,128]{3,2,1,0:T(8,128)(2,1)} %bitcast.32), calls=%async_computation.1 | async-start | bytes 2097152 | tf_op jit(solution)/shard_map/all_to_all | solution.py:462
  137.0 20.5 %collective-permute-start.11 = (bf16[256,512]{1,0:T(8,128)(2,1)}, bf16[256,512]{1,0:T(8,128)(2,1)S(1)}, u32[]{:S(2)}, u32[]{:S(2)}) collective-permute-start(bf16[256,512]{1,0:T(8,128)(2,1)} %copy-done.18), channel_id=1, source_target_pairs={{0,1},{1,0},{2,3},{3,2},{4,5},{5,4},{6,7},{7,6},{8,9},{9,8},{10,11... | collective-permute-start | bytes 786440 | tf_op jit(solution)/shard_map/ppermute | solution.py:459
  137.3 22.4 %collective-permute-start.12 = (bf16[256,512]{1,0:T(8,128)(2,1)}, bf16[256,512]{1,0:T(8,128)(2,1)S(1)}, u32[]{:S(2)}, u32[]{:S(2)}) collective-permute-start(bf16[256,512]{1,0:T(8,128)(2,1)} %copy-done.17), channel_id=1, source_target_pairs={{0,2},{1,3},{2,0},{3,1},{4,6},{5,7},{6,4},{7,5},{8,10},{9,11},{10,... | collective-permute-start | bytes 786440 | tf_op jit(solution)/shard_map/ppermute | solution.py:459
  138.9 27.6 %collective-permute-start.13 = (bf16[256,512]{1,0:T(8,128)(2,1)}, bf16[256,512]{1,0:T(8,128)(2,1)}, u32[]{:S(2)}, u32[]{:S(2)}) collective-permute-start(bf16[256,512]{1,0:T(8,128)(2,1)} %copy-done.16), channel_id=1, source_target_pairs={{0,3},{1,2},{2,1},{3,0},{4,7},{5,6},{6,5},{7,4},{8,11},{9,10},{10,... | collective-permute-start | bytes 786440 | tf_op jit(solution)/shard_map/ppermute | solution.py:459
  138.9 1.6 copy-start.4
  140.5 0.9 copy-start.20
  141.4 1.6 copy-start.24
  143.0 1.2 copy-start.26
  144.2 0.9 copy-start.28
  145.2 0.8 copy-start.30
  145.9 0.8 copy-start.32
  156.1 0.7 copy-start.14
  156.9 17.5 %collective-permute-start.5 = (bf16[256,512]{1,0:T(8,128)(2,1)}, bf16[256,512]{1,0:T(8,128)(2,1)}, u32[]{:S(2)}, u32[]{:S(2)}) collective-permute-start(bf16[256,512]{1,0:T(8,128)(2,1)} %get-tuple-element.37), channel_id=1, source_target_pairs={{0,1},{1,0},{2,3},{3,2},{4,5},{5,4},{6,7},{7,6},{8,9},{9,8},{10,11... | collective-permute-start | bytes 786440 | tf_op jit(solution)/shard_map/ppermute | solution.py:459
  157.5 0.7 copy-start.10
  158.2 16.2 %collective-permute-start.6 = (bf16[256,512]{1,0:T(8,128)(2,1)}, bf16[256,512]{1,0:T(8,128)(2,1)}, u32[]{:S(2)}, u32[]{:S(2)}) collective-permute-start(bf16[256,512]{1,0:T(8,128)(2,1)} %get-tuple-element.38), channel_id=1, source_target_pairs={{0,2},{1,3},{2,0},{3,1},{4,6},{5,7},{6,4},{7,5},{8,10},{9,11},{10,... | collective-permute-start | bytes 786440 | tf_op jit(solution)/shard_map/ppermute | solution.py:459
  159.7 0.7 copy-start.12
  160.4 14.0 %collective-permute-start.7 = (bf16[256,512]{1,0:T(8,128)(2,1)}, bf16[256,512]{1,0:T(8,128)(2,1)}, u32[]{:S(2)}, u32[]{:S(2)}) collective-permute-start(bf16[256,512]{1,0:T(8,128)(2,1)} %get-tuple-element.39), channel_id=1, source_target_pairs={{0,3},{1,2},{2,1},{3,0},{4,7},{5,6},{6,5},{7,4},{8,11},{9,10},{10,... | collective-permute-start | bytes 786440 | tf_op jit(solution)/shard_map/ppermute | solution.py:459
  163.4 3.1 %copy-start.1 = (bf16[512,2048]{1,0:T(8,128)(2,1)S(1)}, bf16[512,2048]{1,0:T(8,128)(2,1)}, u32[]{:S(2)}) copy-start(bf16[512,2048]{1,0:T(8,128)(2,1)} %all-gather.2.cloned.1.call-done.refs_6_) | copy-start | bytes 6291460
  166.5 1.0 copy-start.11
  167.5 0.9 copy-start.13
  168.4 6.0 %copy-start.15 = (bf16[256,512]{1,0:T(8,128)(2,1)S(1)}, bf16[256,512]{1,0:T(8,128)(2,1)}, u32[]{:S(2)}) copy-start(bf16[256,512]{1,0:T(8,128)(2,1)} %copy-done.14) | copy-start | bytes 786436
Sparse Core Ops, SparseCore 0:
  66.3 50.2 all-gather.1

commit v6 on v5

--- a/solution.py
+++ b/solution.py
@@ -12,6 +12,7 @@
 VMEM = pl.BlockSpec(memory_space=pltpu.VMEM)
 SMEM = pl.BlockSpec(memory_space=pltpu.SMEM)
 NT = (((1,), (1,)), ((), ()))
+VMEM_LIMIT = 58 * 2**20
 
 
 def rank_within(keys, order):
@@ -46,9 +47,9 @@
         ],
         out_specs=pl.BlockSpec((slots, 64, 128), lambda j: (0, j, 0)),
         scratch_shapes=[pltpu.VMEM((sessions, 64, 128), BF)],
-        compiler_params=pltpu.CompilerParams(vmem_limit_bytes=16 * 2**20),
+        compiler_params=pltpu.CompilerParams(vmem_limit_bytes=VMEM_LIMIT),
         cost_estimate=pl.CostEstimate(
-            flops=2 * 256 * 256 * width // 16, bytes_accessed=4 * 2**20, transcendentals=0
+            flops=1, bytes_accessed=1, transcendentals=0
         ),
         name="pack_states",
     )(source, store, swap)
@@ -81,8 +82,8 @@
             pl.BlockSpec(swap.shape, lambda j: (0, 0)),
         ],
         out_specs=pl.BlockSpec((sessions, 64 * lanes), lambda j: (0, j)),
-        compiler_params=pltpu.CompilerParams(vmem_limit_bytes=16 * 2**20),
-        cost_estimate=pl.CostEstimate(flops=0, bytes_accessed=2 * 2**20, transcendentals=0),
+        compiler_params=pltpu.CompilerParams(vmem_limit_bytes=VMEM_LIMIT),
+        cost_estimate=pl.CostEstimate(flops=1, bytes_accessed=1, transcendentals=0),
         name="gather_states",
     )(index, returned, swap)
 
@@ -100,39 +101,48 @@
 
 
 def state_kernel(
-    heads, span, pairs, half, meta, own, sibling, across, far, xw, bw, small, s0, s1, *refs
+    heads, span, pairs, half, meta, own, sibling, across, far, bw, xw, zw, small, s0, s1, s2, s3,
+    *refs
 ):
-    xs, bc_out, steps_out, totals_out, outgoing, fresh, sems = refs[-7:]
+    xs, zs, bc_out, steps_out, totals_out, outgoing, fresh, sems = refs[-8:]
     me = meta[0]
     step = pl.program_id(0)
-    target = me ^ step
-    pieces = (own, sibling, across, far)
+    side = (me // 2) ^ 1 ^ step
+    count = 2 * pairs
+    rows_all = count * span
+    depth = across.shape[-1]
+    pieces = [piece[...].reshape(rows_all, depth) for piece in (own, sibling, across, far)]
     quads = heads // 4
-    states = (s0, s1)
+    states = (s0, s1, s2, s3)
+
+    def session_of(at, n):
+        return ((((me // 2) ^ 1 ^ at) * 2 + n // pairs) * 2 + half) * pairs + n % pairs
+
     bcs = project(me, pieces, bw, slice(None))
     for quad in range(quads):
         columns = slice(quad * 256, quad * 256 + 256)
         xs[:, columns] = project(me, pieces, xw, columns).astype(BF)
+        zs[:, columns] = project(me, pieces, zw, columns).astype(BF)
     bc_out[...] = bcs[:, :128].astype(BF)
 
     lane = lax.broadcasted_iota(jnp.int32, (span, 128), 1)
     low = lane < 64
     lane8 = lax.broadcasted_iota(jnp.int32, (heads, span), 1)
-    lane_all = lax.broadcasted_iota(jnp.int32, (heads * pairs, span), 1)
-    first_session = (target * 2 + half) * pairs
+    lane_all = lax.broadcasted_iota(jnp.int32, (heads * count, span), 1)
     raw = jnp.concatenate(
         [
-            jnp.transpose(bcs[i * span : (i + 1) * span, 128:256])[:heads] + small[:, 0:1]
-            for i in range(pairs)
+            jnp.transpose(bcs[n * span : (n + 1) * span, 128:256])[:heads] + small[:, 0:1]
+            for n in range(count)
         ],
         axis=0,
     )
     counts_at = 1 + meta.shape[0] // 2
     alive = jnp.concatenate(
-        [(lane8 < meta[counts_at + first_session + i]).astype(F32) for i in range(pairs)], axis=0
+        [(lane8 < meta[counts_at + session_of(step, n)]).astype(F32) for n in range(count)],
+        axis=0,
     )
     steps = (jnp.maximum(raw, 0.0) + jnp.log1p(jnp.exp(-jnp.abs(raw)))) * alive
-    totals = steps * jnp.concatenate([small[:, 1:2]] * pairs, axis=0)
+    totals = steps * jnp.concatenate([small[:, 1:2]] * count, axis=0)
     shift = 1
     while shift < span:
         totals = totals + jnp.where(lane_all >= shift, pltpu.roll(totals, shift, 1), 0.0)
@@ -143,14 +153,14 @@
     weight_rows = jnp.exp(jnp.minimum(totals - lasts, 0.0)) * steps
     kept = jnp.exp(-lasts)
 
-    for i in range(pairs):
-        rows = slice(i * span, (i + 1) * span)
+    for n in range(count):
+        rows = slice(n * span, (n + 1) * span)
         bc = bcs[rows, 0:128]
         b_low = jnp.where(low, bc, 0.0).astype(BF)
         b_high = jnp.where(low, 0.0, pltpu.roll(bc, 64, 1)).astype(BF)
         b_both = jnp.concatenate([b_low, b_high], axis=0)
         for quad in range(quads):
-            head = i * heads + quad * 4
+            head = n * heads + quad * 4
             scale = jnp.concatenate(
                 [
                     jnp.broadcast_to(weight_rows[head + k : head + k + 1, :], (32, span))
@@ -172,42 +182,35 @@
                 axis=0,
             )
             part = slice(quad * 128, quad * 128 + 128)
-            fresh[step * pairs + i, part, :] = (
-                keep * states[i][part, :].astype(F32) + added
+            fresh[step * count + n, part, :] = (
+                keep * states[n][part, :].astype(F32) + added
             ).astype(BF)
 
-    def sending(at, i):
-        session = ((me ^ at) * 2 + half) * pairs + i
-        number = at * pairs + i
+    def sending(at, n):
+        number = at * count + n
         return pltpu.make_async_copy(
-            fresh.at[number], outgoing.at[meta[1 + session]], sems.at[number]
+            fresh.at[number], outgoing.at[meta[1 + session_of(at, n)]], sems.at[number]
         )
 
-    for i in range(pairs):
-        sending(step, i).start()
-
-    @pl.when(step == 3)
+    for n in range(count):
+        sending(step, n).start()
+
+    @pl.when(step == 1)
     def _():
-        for at in range(4):
-            for i in range(pairs):
-                sending(at, i).wait()
+        for at in range(2):
+            for n in range(count):
+                sending(at, n).wait()
 
 
 def scan_kernel(
-    heads, span, pairs, half, meta, own, sibling, across, far, zw, gain, order, xs, bcs,
-    steps_in, totals_in, s0, s1, n0, n1, n2, n3, zs,
+    heads, span, pairs, half, side, meta, gain, order, xs, zs, bcs, steps_in, totals_in, s0, s1,
+    na, nb, result,
 ):
-    normed_out = (n0, n1, n2, n3)
     me = meta[0]
     step = pl.program_id(0)
-    target = me ^ step
-    pieces = (own, sibling, across, far)
+    target = me ^ (2 * (1 - side) + step)
     quads = heads // 4
     states = (s0, s1)
-    for quad in range(quads):
-        columns = slice(quad * 256, quad * 256 + 256)
-        zs[:, columns] = project(me, pieces, zw, columns).astype(BF)
-
     lane = lax.broadcasted_iota(jnp.int32, (span, 128), 1)
     row = lax.broadcasted_iota(jnp.int32, (span, 128), 0)
     low = lane < 64
@@ -271,117 +274,130 @@
         for quad in range(quads):
             columns = slice(quad * 256, quad * 256 + 256)
             normed = (gated[quad] * inverse * gain[:, columns]).astype(BF)
-            zs[rows, columns] = lax.dot_general(
+            result[rows, columns] = lax.dot_general(
                 normed, order[...], NT, preferred_element_type=F32
             ).astype(BF)
-    for d in range(4):
-
-        @pl.when(step == d)
-        def _():
-            normed_out[d][...] = zs[...]
+
+    @pl.when(step == 0)
+    def _():
+        na[...] = result[...]
+
+    @pl.when(step == 1)
+    def _():
+        nb[...] = result[...]
 
 
 def whole(array):
     return pl.BlockSpec(array.shape, lambda i, meta: (0,) * array.ndim)
 
 
-def token_specs(half, rows, depth):
+def state_call(half, meta, pieces, weights, small, inbound, span, earlier):
+    rows, depth = pieces[2].shape[-2:]
+    pairs = rows // span
+    count = 2 * pairs
+    heads = small.shape[0]
+    width = weights[1].shape[1]
+
     def near(i, meta):
-        return (meta[0] ^ i, half, 0, 0)
+        return ((meta[0] // 2) ^ 1 ^ i, 0, half, 0, 0)
 
     def arrived(i, meta):
-        return (meta[0] ^ i, 0, 0)
-
-    return [pl.BlockSpec((None, None, rows, depth), near)] * 2 + [
-        pl.BlockSpec((None, rows, depth), arrived)
-    ] * 2
-
-
-def state_specs(inbound, pairs, half):
+        return ((meta[0] // 2) ^ 1 ^ i, 0, 0, 0)
+
     def slot_of(n):
-        return lambda i, meta: (meta[1 + ((meta[0] ^ i) * 2 + half) * pairs + n], 0, 0)
-
-    return [pl.BlockSpec((None,) + inbound.shape[1:], slot_of(n)) for n in range(pairs)]
-
-
-def by_step(shape, dtype=None):
-    return pl.BlockSpec((None,) + tuple(shape), lambda i, meta: (i,) + (0,) * len(shape))
-
-
-def state_call(half, meta, pieces, xw, bw, small, inbound, span, earlier):
-    rows, depth = pieces[2].shape[1:]
-    pairs = rows // span
-    heads = small.shape[0]
-    width = xw.shape[1]
-    operands = [meta, *pieces, xw, bw, small] + [inbound] * pairs
+        def index(i, meta):
+            target = ((meta[0] // 2) ^ 1 ^ i) * 2 + n // pairs
+            return (meta[1 + (target * 2 + half) * pairs + n % pairs], 0, 0)
+
+        return index
+
+    def by_step(shape):
+        return pl.BlockSpec((None,) + shape, lambda i, meta: (i, 0, 0))
+
+    operands = [meta, *pieces, *weights, small] + [inbound] * count
     aliases = {}
     extra = []
     if earlier is not None:
-        aliases = {len(operands): 4}
+        aliases = {len(operands): 5}
         operands.append(earlier)
         extra = [ANY]
     return pl.pallas_call(
         lambda *refs: state_kernel(heads, span, pairs, half, *refs),
         out_shape=[
-            jax.ShapeDtypeStruct((4, rows, width), BF),
-            jax.ShapeDtypeStruct((4, rows, 128), BF),
-            jax.ShapeDtypeStruct((4, heads * pairs, span), F32),
-            jax.ShapeDtypeStruct((4, heads * pairs, span), F32),
+            jax.ShapeDtypeStruct((2, count * span, width), BF),
+            jax.ShapeDtypeStruct((2, count * span, width), BF),
+            jax.ShapeDtypeStruct((2, count * span, 128), BF),
+            jax.ShapeDtypeStruct((2, heads * count, span), F32),
+            jax.ShapeDtypeStruct((2, heads * count, span), F32),
             jax.ShapeDtypeStruct(inbound.shape, BF),
         ],
         grid_spec=pltpu.PrefetchScalarGridSpec(
             num_scalar_prefetch=1,
-            grid=(4,),
-            in_specs=token_specs(half, rows, depth)
-            + [whole(xw), whole(bw), whole(small)]
-            + state_specs(inbound, pairs, half)
+            grid=(2,),
+            in_specs=[pl.BlockSpec((None, 2, None, rows, depth), near)] * 2
+            + [pl.BlockSpec((None, 2, rows, depth), arrived)] * 2
+            + [whole(weight) for weight in weights]
+            + [whole(small)]
+            + [pl.BlockSpec((None,) + inbound.shape[1:], slot_of(n)) for n in range(count)]
             + extra,
             out_specs=[
-                by_step((rows, width)),
-                by_step((rows, 128)),
-                by_step((heads * pairs, span)),
-                by_step((heads * pairs, span)),
+                by_step((count * span, width)),
+                by_step((count * span, width)),
+                by_step((count * span, 128)),
+                by_step((heads * count, span)),
+                by_step((heads * count, span)),
                 ANY,
             ],
             scratch_shapes=[
-                pltpu.VMEM((4 * pairs,) + inbound.shape[1:], BF),
-                pltpu.SemaphoreType.DMA((4 * pairs,)),
+                pltpu.VMEM((2 * count,) + inbound.shape[1:], BF),
+                pltpu.SemaphoreType.DMA((2 * count,)),
             ],
         ),
         input_output_aliases=aliases,
-        compiler_params=pltpu.CompilerParams(vmem_limit_bytes=32 * 2**20),
+        compiler_params=pltpu.CompilerParams(vmem_limit_bytes=VMEM_LIMIT),
         cost_estimate=pl.CostEstimate(
-            flops=8 * 10**9, bytes_accessed=9 * 2**20, transcendentals=0
+            flops=1, bytes_accessed=1, transcendentals=0
         ),
         name="states",
     )(*operands)
 
 
-def scan_call(half, meta, pieces, zw, gain, order, mid, inbound, span):
-    rows, depth = pieces[2].shape[1:]
+def scan_call(half, side, meta, gain, order, mid, inbound, span, rows):
     pairs = rows // span
-    xs, bcs, steps, totals = mid
-    heads = steps.shape[1] // pairs
-    width = zw.shape[1]
+    heads = mid[-1].shape[1] // (2 * pairs)
+    width = mid[0].shape[2]
+    mid = [part.reshape(2, 2, part.shape[1] // 2, part.shape[2]) for part in mid]
+
+    def block_of(part):
+        return pl.BlockSpec(
+            (None, None) + part.shape[2:], lambda i, meta: (side, i ^ (meta[0] % 2), 0, 0)
+        )
+
+    def slot_of(n):
+        def index(i, meta):
+            target = meta[0] ^ (2 * (1 - side) + i)
+            return (meta[1 + (target * 2 + half) * pairs + n], 0, 0)
+
+        return index
+
     return pl.pallas_call(
-        lambda *refs: scan_kernel(heads, span, pairs, half, *refs),
-        out_shape=[jax.ShapeDtypeStruct((rows, width), BF)] * 4,
+        lambda *refs: scan_kernel(heads, span, pairs, half, side, *refs),
+        out_shape=[jax.ShapeDtypeStruct((rows, width), BF)] * 2,
         grid_spec=pltpu.PrefetchScalarGridSpec(
             num_scalar_prefetch=1,
-            grid=(4,),
-            in_specs=token_specs(half, rows, depth)
-            + [whole(zw), whole(gain), whole(order)]
-            + [by_step(part.shape[1:]) for part in mid]
-            + state_specs(inbound, pairs, half),
-            out_specs=[pl.BlockSpec((rows, width), lambda i, meta: (0, 0))] * 4,
+            grid=(2,),
+            in_specs=[whole(gain), whole(order)]
+            + [block_of(part) for part in mid]
+            + [pl.BlockSpec((None,) + inbound.shape[1:], slot_of(n)) for n in range(pairs)],
+            out_specs=[pl.BlockSpec((rows, width), lambda i, meta: (0, 0))] * 2,
             scratch_shapes=[pltpu.VMEM((rows, width), BF)],
         ),
-        compiler_params=pltpu.CompilerParams(vmem_limit_bytes=32 * 2**20),
+        compiler_params=pltpu.CompilerParams(vmem_limit_bytes=VMEM_LIMIT),
         cost_estimate=pl.CostEstimate(
-            flops=10 * 10**9, bytes_accessed=9 * 2**20, transcendentals=0
+            flops=1, bytes_accessed=1, transcendentals=0
         ),
         name="scan",
-    )(meta, *pieces, zw, gain, order, *mid, *[inbound] * pairs)
+    )(meta, gain, order, *mid, *[inbound] * pairs)
 
 
 def out_call(half, halves, normed, weights, earlier):
@@ -413,9 +429,9 @@
         + extra,
         out_specs=pl.BlockSpec((rows, block), lambda j: (half, j)),
         input_output_aliases=aliases,
-        compiler_params=pltpu.CompilerParams(vmem_limit_bytes=24 * 2**20),
+        compiler_params=pltpu.CompilerParams(vmem_limit_bytes=VMEM_LIMIT),
         cost_estimate=pl.CostEstimate(
-            flops=2 * rows * depth * 4 * columns, bytes_accessed=10 * 2**20, transcendentals=0
+            flops=1, bytes_accessed=1, transcendentals=0
         ),
         name="project_out",
     )(*operands)
@@ -467,13 +483,12 @@
             tiled=True,
         ).reshape((slot_count,) + row_shape)
 
-    blocks = tokens.reshape(model_shards, halves, rows, depth)
-    across = [exchange(blocks[:, h], 2) for h in range(halves)]
-    sibling = exchange(tokens, 1).reshape(blocks.shape)
     replicas = lax.axis_size("groups") * shard_count
     replica = lax.axis_index("groups") * shard_count + shard_index
     share = width // replicas
     ow_part = exchange(lax.dynamic_slice_in_dim(out_weight, replica * share, share), 2)
+    blocks = tokens.reshape(model_shards // 2, 2, halves, rows, depth)
+    sibling = exchange(tokens, 1).reshape(blocks.shape)
 
     local = jnp.arange(sessions_here, dtype=jnp.int32)
     store_rows = shard_index * sessions_here + local
@@ -493,6 +508,9 @@
     )
     packed = pack_states(source, store_states, swap, slot_count)
     inbound = trade(packed)
+    first = after(blocks[:, :, 0], ow_part)
+    across = [exchange(first, 2)]
+    across.append(exchange(after(blocks[:, :, 1], across[0]), 2))
     wanted = lax.dynamic_slice_in_dim(home_rows, shard_index * sessions_here, sessions_here)
     home_shard = wanted // sessions_here
     session_slot = home_shard * capacity + rank_within(home_shard, wanted % sessions_here)
@@ -515,28 +533,39 @@
     gain = norm_gain.reshape(heads // 4, 4, 32, 2).transpose(0, 3, 1, 2).reshape(1, width)
     small = jnp.stack([dt_bias, decay_rate], axis=1)
 
-    ow_part = after(ow_part, packed)
     ow_across = lax.all_gather(ow_part, ("groups", "dp"), axis=0, tiled=True)
     ow_sibling = exchange(out_weight, 1)
-    ow_far = exchange(ow_across, 1)
 
     outgoing = None
     received = []
     done = []
     for h in range(halves):
         arrived = across[h]
-        turn_meta = meta
+        start = meta
         if h:
-            turn_meta = after(meta, done[-1])
-            arrived = after(arrived, done[-1])
+            start = after(meta, done[-1])
+            arrived = after(arrived, mid[0])
+        else:
+            arrived = after(arrived, xw, zw, bw)
         pieces = (blocks, sibling, arrived, exchange(arrived, 1))
         *mid, outgoing = state_call(
-            h, turn_meta, pieces, xw, bw, small, inbound, span, outgoing
+            h, start, pieces, (bw, xw, zw), small, inbound, span, outgoing
         )
-        parts = scan_call(h, turn_meta, pieces, zw, gain, order, mid, inbound, span)
-        done.append(parts[0])
-        received.append([parts[0]] + [exchange(parts[d], d) for d in range(1, 4)])
+        far_part = scan_call(h, 0, start, gain, order, mid, inbound, span, rows)
+        start = after(start, far_part[0])
+        near_part = scan_call(h, 1, start, gain, order, mid, inbound, span, rows)
+        done.append(near_part[0])
+        received.append(
+            [
+                near_part[0],
+                exchange(near_part[1], 1),
+                exchange(far_part[0], 2),
+                exchange(far_part[1], 3),
+            ]
+        )
     returned = trade(outgoing)
+    ow_across = after(ow_across, done[-1])
+    ow_far = exchange(ow_across, 1)
     new_store = gather_states(row_slot, returned, swap)
     ow = (out_weight, ow_sibling, ow_across, ow_far)
     out_tokens = None

time: 188 us -> 177 us (0.941)
  local copies, waits for them, and re-layouts: 32.8 us -> 11.3 us
  Pallas kernels: 53.4 us -> 67.6 us
  waiting for transfers between devices: 59.6 us -> 52.4 us
  other arithmetic: 1.11 us -> 4.99 us
  matrix products: 7.94 us -> 5.2 us
  starting transfers between devices: 18.3 us -> 20.5 us
    unnamed x87 -> x33, local copies, waits for them, and re-layouts: 28.2 us -> 5.41 us
    all_gather x1, waiting for transfers between devices: 20 us -> 0.01 us  [body(): ow_across = lax.all_gather(ow_part, ('groups', 'dp'), axis=0, tiled=True)]
    all_to_all x2, waiting for transfers between devices: 3.01 us -> 17.3 us  [trade(): lax.all_to_all(value.reshape((shard_count, capacity) + row_shape), 'dp',...]
    pallas_call x2, Pallas kernels: 17.1 us -> 24.5 us  [state_call(): pl.pallas_call(lambda *refs: state_kernel(heads, span, pairs, half, *refs...]
    pallas_call x2 -> x4, Pallas kernels: 18.1 us -> 21.6 us  [scan_call(): pl.pallas_call(lambda *refs: scan_kernel(heads, span, pairs, half, side,...]
    concatenate x1, other arithmetic: 0.24 us -> 2.4 us  [body(): jnp.concatenate([bc_weight, dt_weight, jnp.zeros((bc_weight.shape[0], 128...]
  transfers between devices with their start and end apart: 17 -> 17, of which waited for: 4 -> 6; matrix products, arithmetic and copies ran while one was open for 8% -> 9% of each run, Pallas kernels for 25% -> 35%
where the time goes in v6:
time: 177 us; the launch traced here: 176 us
  Pallas kernels  67.6 us (38%)
  waiting for transfers between devices  52.4 us (30%)
  starting transfers between devices  20.5 us (12%)
  between operations  14.2 us (8%)
  local copies, waits for them, and re-layouts  11.3 us (6%)
  matrix products  5.2 us (3%)
  other arithmetic  4.99 us (3%)
    ppermute x14, waiting for transfers between devices, exchange(): return lax.ppermute(value, 'mp', pairs)  35.1 us
    pallas_call x2, Pallas kernels, state_call(): pl.pallas_call(lambda *refs: state_kernel(heads, span, pairs, half, *refs...  24.5 us
    pallas_call x4, Pallas kernels, scan_call(): pl.pallas_call(lambda *refs: scan_kernel(heads, span, pairs, half, side,...  21.6 us
    all_to_all x2, waiting for transfers between devices, trade(): lax.all_to_all(value.reshape((shard_count, capacity) + row_shape), 'dp',...  17.3 us
    pallas_call x2, Pallas kernels, out_call(): pl.pallas_call(kernel, grid=(columns // block,), out_shape=jax.ShapeDtype...  13.4 us
    ppermute x14, starting transfers between devices, exchange(): return lax.ppermute(value, 'mp', pairs)  10.2 us
    all_to_all x2, starting transfers between devices, trade(): lax.all_to_all(value.reshape((shard_count, capacity) + row_shape), 'dp',...  10.2 us
    unnamed x33, local copies, waits for them, and re-layouts  5.41 us
  transfers between devices with their start and end apart: 17, of which 6 were waited for; matrix products, arithmetic and copies ran while one was open for 9% of the time, Pallas kernels for 35%

profile of v6, /device:TPU:0, one launch (start us, length us, event | category | flops | bytes accessed | tf_op | source)
XLA Modules:
  0.0 176.1 jit_solution(8493630745255487854)
XLA Ops:
  7.2 0.0 copy-start
  7.2 0.0 all-gather.2.cloned.1.call-start
  7.2 1.1 constant_dynamic-slice_fusion
  8.3 3.0 %collective-permute-start.1 = (bf16[64,2048]{1,0:T(8,128)(2,1)S(1)}, bf16[64,2048]{1,0:T(8,128)(2,1)S(1)}, u32[]{:S(2)}, u32[]{:S(2)}) collective-permute-start(bf16[64,2048]{1,0:T(8,128)(2,1)S(1)} %constant_dynamic-slice_fusion), channel_id=1, source_target_pairs={{0,2},{1,3},{2,0},{3,1},{4,6},{5,7},{6,4},{7,5},{8,10},{9,11},{10,... | collective-permute-start | bytes 786440 | tf_op jit(solution)/shard_map/ppermute | solution.py:475
  11.4 0.8 select_reduce_fusion.1
  12.2 0.2 convert_reduce_fusion
  12.4 5.2 %collective-permute-done.1 = bf16[64,2048]{1,0:T(8,128)(2,1)S(1)} collective-permute-done((bf16[64,2048]{1,0:T(8,128)(2,1)S(1)}, bf16[64,2048]{1,0:T(8,128)(2,1)S(1)}, u32[]{:S(2)}, u32[]{:S(2)}) %collective-permute-start.1) | collective-permute-done | bytes 262176 | tf_op jit(solution)/shard_map/ppermute | solution.py:475
  17.7 0.7 copy-done.6
  18.4 0.0 all-gather.2.cloned.1.call-update
  18.4 0.6 select_reduce_fusion.source
  19.0 4.0 %pack_states.1 = bf16[16,256,128]{2,1,0:T(8,128)(2,1)} custom-call(s32[16]{0:T(128)} %select_reduce_fusion.source, bf16[16,32768]{1,0:T(8,128)(2,1)} %store.1, bf16[256,256]{1,0:T(8,128)(2,1)} %constant.61.clone.swap), custom_call_target="tpu_custom_call" | custom-call | flops 1 | bytes 1 | tf_op jit(solution)/shard_map/pack_states/pallas_call | solution.py:39
  23.0 5.1 %all-to-all-start = ((bf16[4,4,256,128]{3,2,1,0:T(8,128)(2,1)}), bf16[4,4,256,128]{3,2,1,0:T(8,128)(2,1)S(1)}, u32[]{:S(2)}, u32[]{:S(2)}) async-start(bf16[4,4,256,128]{3,2,1,0:T(8,128)(2,1)} %bitcast.55), calls=%async_computation | async-start | bytes 2097152 | tf_op jit(solution)/shard_map/all_to_all | solution.py:478
  28.2 0.0 collective-permute-start
  28.2 3.1 %slice_bitcast_fusion = (bf16[2,2,256,512]{3,2,1,0:T(8,128)(2,1)}, bf16[2,2,256,512]{3,2,1,0:T(8,128)(2,1)}) fusion(bf16[2,2,2,256,512]{4,3,2,1,0:T(8,128)(2,1)} %bitcast.52), kind=kLoop, calls=%fused_computation.4 | loop fusion | bytes 4194304 | tf_op jit(solution)/shard_map/squeeze | solution.py:513
  31.3 1.5 collective-permute-start.2
  32.8 2.6 %fusion.refs_6_ = bf16[2048,512]{1,0:T(8,128)(2,1)} fusion(bf16[2048,512]{1,0:T(8,128)(2,1)S(1)} %copy-done, bf16[512,512]{1,0:T(8,128)(2,1)S(1)} %copy-done.15), kind=kOutput, calls=%fused_computation.2 | convolution fusion | flops 1074790400 | bytes 4718592 | tf_op jit(solution)/shard_map/dot_general | solution.py:527
  35.4 2.6 %fusion.1.refs_7_ = bf16[2048,512]{1,0:T(8,128)(2,1)} fusion(bf16[2048,512]{1,0:T(8,128)(2,1)S(1)} %copy-done.14, bf16[512,512]{1,0:T(8,128)(2,1)S(1)} %copy-done.15), kind=kOutput, calls=%fused_computation.3 | convolution fusion | flops 1074790400 | bytes 4718592 | tf_op jit(solution)/shard_map/dot_general | solution.py:528
  38.0 0.0 copy-start.13
  38.0 1.0 copy.45
  39.1 0.1 pad.4.clone
  39.1 2.4 %maximum_maximum_fusion.refs_5_ = bf16[2048,256]{1,0:T(8,128)(2,1)} fusion(bf16[2048,8]{1,0:T(8,128)(2,1)} %copy.45, bf16[2048,128]{1,0:T(8,128)(2,1)} %param.17, bf16[256]{0:T(256)(128)(2,1)S(1)} %pad.4.clone), kind=kLoop, calls=%fused_computation.6 | loop fusion | flops 3145728 | bytes 1606144 | tf_op jit(solution)/shard_map/concatenate | solution.py:530
  41.6 15.6 %collective-permute-done.2.refs_3_ = bf16[2,2,256,512]{3,2,1,0:T(8,128)(2,1)} collective-permute-done((bf16[2,2,256,512]{3,2,1,0:T(8,128)(2,1)}, bf16[2,2,256,512]{3,2,1,0:T(8,128)(2,1)}, u32[]{:S(2)}, u32[]{:S(2)}) %collective-permute-start.2) | collective-permute-done | bytes 1048608 | tf_op jit(solution)/shard_map/ppermute | solution.py:475
  57.1 0.0 collective-permute-start.3
  57.1 1.5 collective-permute-start.4
  58.7 0.7 copy.46.refs_8_
  59.3 0.1 and_select_fusion.2
  59.4 0.2 convert_reduce_fusion.1
  59.6 0.6 pad_add_fusion.refs_0_
  60.3 1.2 all-to-all-done
  61.4 0.0 collective-permute-done
  61.4 0.0 collective-permute-done.3.refs_4_
  61.5 1.0 copy-done.1
  62.5 12.3 %states.2 = (bf16[2,512,512]{2,1,0:T(8,128)(2,1)}, bf16[2,512,512]{2,1,0:T(8,128)(2,1)}, bf16[2,512,128]{2,1,0:T(8,128)(2,1)}, f32[2,32,128]{2,1,0:T(8,128)}, f3...) custom-call(s32[33]{0:T(128)} %pad_add_fusion.refs_0_, bf16[2,2,2,256,512]{4,3,2,1,0:T(8,128)(2,1)} %bitcast.53, ...), custom_call_target="tpu_custom_call" | custom-call | flops 1 | bytes 1 | tf_op jit(solution)/shard_map/states/pallas_call | solution.py:324
  74.8 8.3 %collective-permute-done.4.refs_3_ = bf16[2,2,256,512]{3,2,1,0:T(8,128)(2,1)} collective-permute-done((bf16[2,2,256,512]{3,2,1,0:T(8,128)(2,1)}, bf16[2,2,256,512]{3,2,1,0:T(8,128)(2,1)}, u32[]{:S(2)}, u32[]{:S(2)}) %collective-permute-start.4) | collective-permute-done | bytes 1048608 | tf_op jit(solution)/shard_map/ppermute | solution.py:475
  83.0 0.5 collective-permute-start.9
  83.5 0.1 reshape.121
  83.7 0.1 copy.41
  83.8 0.7 reshape.122.refs_1_
  84.5 5.4 %scan.4 = (bf16[256,512]{1,0:T(8,128)(2,1)}, bf16[256,512]{1,0:T(8,128)(2,1)}) custom-call(s32[33]{0:T(128)} %pad_add_fusion.refs_0_, f32[1,512]{1,0:T(1,128)} %reshape.122.refs_1_, bf16[256,256]{1,0:T(8,128)(2,1)} %constant.63.refs_2_, bf16[2,2,256,512]{3,2,1,0:T(8,128)(2,1)} %bitcast.57, bf16[2,2,256,512]{3,2,1,0:T(8,128)(2,1)} %bitcast.59, ...), custom_call_target="tpu_custom_call" | custom-call | flops 1 | bytes 1 | tf_op jit(solution)/shard_map/scan/pallas_call | solution.py:383
  89.9 5.4 %scan.5 = (bf16[256,512]{1,0:T(8,128)(2,1)}, bf16[256,512]{1,0:T(8,128)(2,1)}) custom-call(s32[33]{0:T(128)} %pad_add_fusion.refs_0_, f32[1,512]{1,0:T(1,128)} %reshape.122.refs_1_, bf16[256,256]{1,0:T(8,128)(2,1)} %constant.63.refs_2_, bf16[2,2,256,512]{3,2,1,0:T(8,128)(2,1)} %bitcast.58, bf16[2,2,256,512]{3,2,1,0:T(8,128)(2,1)} %bitcast.60, ...), custom_call_target="tpu_custom_call" | custom-call | flops 1 | bytes 1 | tf_op jit(solution)/shard_map/scan/pallas_call | solution.py:383
  95.2 0.0 collective-permute-done.5.refs_4_
  95.2 0.0 copy-start.3
  95.2 1.0 copy-done.3
  96.2 12.2 %states.3 = (bf16[2,512,512]{2,1,0:T(8,128)(2,1)}, bf16[2,512,512]{2,1,0:T(8,128)(2,1)}, bf16[2,512,128]{2,1,0:T(8,128)(2,1)}, f32[2,32,128]{2,1,0:T(8,128)}, f3...) custom-call(s32[33]{0:T(128)} %pad_add_fusion.refs_0_, ...), custom_call_target="tpu_custom_call", output_to_operand_aliasing={{5}: (13, {})} | custom-call | flops 1 | bytes 1 | tf_op jit(solution)/shard_map/states/pallas_call | solution.py:324
  108.4 5.5 %scan.6 = (bf16[256,512]{1,0:T(8,128)(2,1)}, bf16[256,512]{1,0:T(8,128)(2,1)}) custom-call(s32[33]{0:T(128)} %pad_add_fusion.refs_0_, f32[1,512]{1,0:T(1,128)} %reshape.122.refs_1_, bf16[256,256]{1,0:T(8,128)(2,1)} %constant.63.refs_2_, bf16[2,2,256,512]{3,2,1,0:T(8,128)(2,1)} %bitcast.61, bf16[2,2,256,512]{3,2,1,0:T(8,128)(2,1)} %bitcast.63, ...), custom_call_target="tpu_custom_call" | custom-call | flops 1 | bytes 1 | tf_op jit(solution)/shard_map/scan/pallas_call | solution.py:383
  113.9 5.3 %scan.7 = (bf16[256,512]{1,0:T(8,128)(2,1)}, bf16[256,512]{1,0:T(8,128)(2,1)}) custom-call(s32[33]{0:T(128)} %pad_add_fusion.refs_0_, f32[1,512]{1,0:T(1,128)} %reshape.122.refs_1_, bf16[256,256]{1,0:T(8,128)(2,1)} %constant.63.refs_2_, bf16[2,2,256,512]{3,2,1,0:T(8,128)(2,1)} %bitcast.62, bf16[2,2,256,512]{3,2,1,0:T(8,128)(2,1)} %bitcast.64, ...), custom_call_target="tpu_custom_call" | custom-call | flops 1 | bytes 1 | tf_op jit(solution)/shard_map/scan/pallas_call | solution.py:383
  119.2 0.1 collective-permute-start.10
  119.3 5.1 %all-to-all-start.1 = ((bf16[4,4,256,128]{3,2,1,0:T(8,128)(2,1)}), bf16[4,4,256,128]{3,2,1,0:T(8,128)(2,1)S(1)}, u32[]{:S(2)}, u32[]{:S(2)}) async-start(bf16[4,4,256,128]{3,2,1,0:T(8,128)(2,1)} %bitcast.22), calls=%async_computation.1 | async-start | bytes 2097152 | tf_op jit(solution)/shard_map/all_to_all | solution.py:478
  124.4 0.2 collective-permute-start.11
  124.6 1.5 collective-permute-start.12
  126.1 0.2 collective-permute-start.13
  126.3 1.5 collective-permute-start.7
  127.8 0.0 collective-permute-done.11.refs_1_
  127.8 0.2 collective-permute-start.6
  128.0 6.0 %collective-permute-done.12.refs_2_ = bf16[256,512]{1,0:T(8,128)(2,1)S(1)} collective-permute-done((bf16[256,512]{1,0:T(8,128)(2,1)}, bf16[256,512]{1,0:T(8,128)(2,1)S(1)}, u32[]{:S(2)}, u32[]{:S(2)}) %collective-permute-start.12) | collective-permute-done | bytes 262176 | tf_op jit(solution)/shard_map/ppermute | solution.py:475
  133.9 0.7 copy-done.5
  134.7 16.1 %all-to-all-done.1 = bf16[4,4,256,128]{3,2,1,0:T(8,128)(2,1)S(1)} async-done(((bf16[4,4,256,128]{3,2,1,0:T(8,128)(2,1)}), bf16[4,4,256,128]{3,2,1,0:T(8,128)(2,1)S(1)}, u32[]{:S(2)}, u32[]{:S(2)}) %all-to-all-start.1) | async-done | bytes 1048608 | tf_op jit(solution)/shard_map/all_to_all | solution.py:478
  150.8 1.0 copy-done.2
  151.8 4.1 %gather_states.1 = bf16[16,32768]{1,0:T(8,128)(2,1)} custom-call(s32[16]{0:T(128)} %copy-done.9, bf16[16,256,128]{2,1,0:T(8,128)(2,1)} %bitcast.56, bf16[256,256]{1,0:T(8,128)(2,1)} %constant.61.clone.swap), custom_call_target="tpu_custom_call" | custom-call | flops 1 | bytes 1 | tf_op jit(solution)/shard_map/gather_states/pallas_call | solution.py:75
  155.8 0.0 collective-permute-done.13.refs_3_
  155.8 0.0 collective-permute-done.10.refs_7_
  155.8 6.7 %project_out.2.refs_8_ = bf16[512,2048]{1,0:T(8,128)(2,1)} custom-call(bf16[256,512]{1,0:T(8,128)(2,1)} %get-tuple-element.56.refs_0_, bf16[256,512]{1,0:T(8,128)(2,1)} %copy-done.4, bf16[256,512]{1,0:T(8,128)(2,1)} %copy-done.5, bf16[256,512]{1,0:T(8,128)(2,1)} %collective-permute-done.13.refs_3_, bf16[512,2048]{1,0:T(8,128)(2,1)} %refs_4_.3, ...), custom_call_target="tpu_custom_call" | custom-call | flops 1 | bytes 1 | tf_op jit(solution)/shard_map/project_out/pallas_call | solution.py:423
  162.5 0.0 collective-permute-done.7.refs_2_
  162.6 6.7 %project_out.3 = bf16[512,2048]{1,0:T(8,128)(2,1)} custom-call(bf16[256,512]{1,0:T(8,128)(2,1)} %get-tuple-element.52.refs_0_, bf16[256,512]{1,0:T(8,128)(2,1)} %collective-permute-done.6.refs_1_, bf16[256,512]{1,0:T(8,128)(2,1)} %collective-permute-done.7.refs_2_, bf16[256,512]{1,0:T(8,128)(2,1)} %collective-permute-done.8.refs_3_, ...), custom_call_target="tpu_custom_call", output_to_operand_aliasing={{}: (8, {})} | custom-call | flops 1 | bytes 1 | tf_op jit(solution)/shard_map/project_out/pallas_call | solution.py:423
  (37 shorter events, 0.1 us)
Async XLA Ops:
  7.2 25.7 %copy-start = (bf16[2048,512]{1,0:T(8,128)(2,1)S(1)}, bf16[2048,512]{1,0:T(8,128)(2,1)}, u32[]{:S(2)}) copy-start(bf16[2048,512]{1,0:T(8,128)(2,1)} %param.15) | copy-start | bytes 6291460
  7.2 112.1 %all-gather.2.cloned.1.call-start = ((), (), s32[]{:S(2)}) async-start(), calls=%async_computation.2 | async-start | bytes 2359296 | tf_op jit(solution)/shard_map/all_gather | solution.py:536
  8.3 9.3 %collective-permute-start.1 = (bf16[64,2048]{1,0:T(8,128)(2,1)S(1)}, bf16[64,2048]{1,0:T(8,128)(2,1)S(1)}, u32[]{:S(2)}, u32[]{:S(2)}) collective-permute-start(bf16[64,2048]{1,0:T(8,128)(2,1)S(1)} %constant_dynamic-slice_fusion), channel_id=1, source_target_pairs={{0,2},{1,3},{2,0},{3,1},{4,6},{5,7},{6,4},{7,5},{8,10},{9,11},{10,... | collective-permute-start | bytes 786440 | tf_op jit(solution)/shard_map/ppermute | solution.py:475
  12.4 10.6 %copy-start.9 = (s32[16]{0:T(128)}, s32[16]{0:T(128)S(1)}, u32[]{:S(2)}) copy-start(s32[16]{0:T(128)S(1)} %multiply_add_fusion.index) | copy-start | bytes 196
  17.7 0.7 copy-start.6
  23.0 38.4 %all-to-all-start = ((bf16[4,4,256,128]{3,2,1,0:T(8,128)(2,1)}), bf16[4,4,256,128]{3,2,1,0:T(8,128)(2,1)S(1)}, u32[]{:S(2)}, u32[]{:S(2)}) async-start(bf16[4,4,256,128]{3,2,1,0:T(8,128)(2,1)} %bitcast.55), calls=%async_computation | async-start | bytes 2097152 | tf_op jit(solution)/shard_map/all_to_all | solution.py:478
  28.2 33.3 %collective-permute-start = (bf16[2048,512]{1,0:T(8,128)(2,1)}, bf16[2048,512]{1,0:T(8,128)(2,1)}, u32[]{:S(2)}, u32[]{:S(2)}) collective-permute-start(bf16[2048,512]{1,0:T(8,128)(2,1)} %param.14), channel_id=1, source_target_pairs={{0,1},{1,0},{2,3},{3,2},{4,5},{5,4},{6,7},{7,6},{8,9},{9,8},{10,11... | collective-permute-start | bytes 6291464 | tf_op jit(solution)/shard_map/ppermute | solution.py:475
  28.2 4.7 %copy-start.15 = (bf16[512,512]{1,0:T(8,128)(2,1)S(1)}, bf16[512,512]{1,0:T(8,128)(2,1)}, u32[]{:S(2)}) copy-start(bf16[512,512]{1,0:T(8,128)(2,1)} %constant.62.clone) | copy-start | bytes 1572868
  31.3 4.1 %copy-start.14 = (bf16[2048,512]{1,0:T(8,128)(2,1)S(1)}, bf16[2048,512]{1,0:T(8,128)(2,1)}, u32[]{:S(2)}) copy-start(bf16[2048,512]{1,0:T(8,128)(2,1)} %param.16) | copy-start | bytes 6291460
  31.3 25.8 %collective-permute-start.2 = (bf16[2,2,256,512]{3,2,1,0:T(8,128)(2,1)}, bf16[2,2,256,512]{3,2,1,0:T(8,128)(2,1)}, u32[]{:S(2)}, u32[]{:S(2)}) collective-permute-start(bf16[2,2,256,512]{3,2,1,0:T(8,128)(2,1)} %get-tuple-element.31), channel_id=1, source_target_pairs={{0,2},{1,3},{2,0},{3,1},{4,6},{5,7},{6,4},{7,5},{8,10},{9,11},{10,... | collective-permute-start | bytes 3145736 | tf_op jit(solution)/shard_map/ppermute | solution.py:475
  35.4 2.6 %copy-start.7 = (bf16[2048,8]{0,1:T(8,128)(2,1)S(1)}, bf16[2048,8]{0,1:T(8,128)(2,1)}, u32[]{:S(2)}) copy-start(bf16[2048,8]{0,1:T(8,128)(2,1)} %param.18) | copy-start | bytes 98308
  38.0 20.6 %copy-start.10 = (f32[8]{0:T(128)S(1)}, f32[8]{0:T(128)}, u32[]{:S(2)}) copy-start(f32[8]{0:T(128)} %param.20) | copy-start | bytes 100
  38.0 20.6 %copy-start.11 = (f32[8]{0:T(128)S(1)}, f32[8]{0:T(128)}, u32[]{:S(2)}) copy-start(f32[8]{0:T(128)} %param.19) | copy-start | bytes 100
  38.0 21.3 %copy-start.12 = (s32[64]{0:T(128)S(1)}, s32[64]{0:T(128)}, u32[]{:S(2)}) copy-start(s32[64]{0:T(128)} %param.24) | copy-start | bytes 772
  38.0 21.6 %copy-start.13 = (s32[16]{0:T(128)S(1)}, s32[16]{0:T(128)}, u32[]{:S(2)}) copy-start(s32[16]{0:T(128)} %param.25) | copy-start | bytes 196
  57.1 4.3 %collective-permute-start.3 = (bf16[2,2,256,512]{3,2,1,0:T(8,128)(2,1)}, bf16[2,2,256,512]{3,2,1,0:T(8,128)(2,1)}, u32[]{:S(2)}, u32[]{:S(2)}) collective-permute-start(bf16[2,2,256,512]{3,2,1,0:T(8,128)(2,1)} %collective-permute-done.2.refs_3_), channel_id=1, source_target_pairs={{0,1},{1,0},{2,3},{3,2},{4,5},{5,4},{6,7},{7,6},{8,9},{9,8},{10,11... | collective-permute-start | bytes 3145736 | tf_op jit(solution)/shard_map/ppermute | solution.py:475
  57.1 25.9 %collective-permute-start.4 = (bf16[2,2,256,512]{3,2,1,0:T(8,128)(2,1)}, bf16[2,2,256,512]{3,2,1,0:T(8,128)(2,1)}, u32[]{:S(2)}, u32[]{:S(2)}) collective-permute-start(bf16[2,2,256,512]{3,2,1,0:T(8,128)(2,1)} %get-tuple-element.42), channel_id=1, source_target_pairs={{0,2},{1,3},{2,0},{3,1},{4,6},{5,7},{6,4},{7,5},{8,10},{9,11},{10,... | collective-permute-start | bytes 3145736 | tf_op jit(solution)/shard_map/ppermute | solution.py:475
  61.4 1.0 copy-start.1
  62.5 21.1 %copy-start.8 = (f32[512]{0:T(512)S(1)}, f32[512]{0:T(512)}, u32[]{:S(2)}) copy-start(f32[512]{0:T(512)} %param.21) | copy-start | bytes 6148
  83.0 12.2 %collective-permute-start.5 = (bf16[2,2,256,512]{3,2,1,0:T(8,128)(2,1)}, bf16[2,2,256,512]{3,2,1,0:T(8,128)(2,1)S(1)}, u32[]{:S(2)}, u32[]{:S(2)}) collective-permute-start(bf16[2,2,256,512]{3,2,1,0:T(8,128)(2,1)} %collective-permute-done.4.refs_3_), channel_id=1, source_target_pairs={{0,1},{1,0},{2,3},{3,2},{4,5},{5,4},{6,7},{7,6},{8,9},{9,8},{10,11... | collective-permute-start | bytes 3145736 | tf_op jit(solution)/shard_map/ppermute | solution.py:475
  83.0 43.2 %collective-permute-start.9 = (bf16[512,2048]{1,0:T(8,128)(2,1)}, bf16[512,2048]{1,0:T(8,128)(2,1)}, u32[]{:S(2)}, u32[]{:S(2)}) collective-permute-start(bf16[512,2048]{1,0:T(8,128)(2,1)} %refs_4_.3), channel_id=1, source_target_pairs={{0,1},{1,0},{2,3},{3,2},{4,5},{5,4},{6,7},{7,6},{8,9},{9,8},{10,11... | collective-permute-start | bytes 6291464 | tf_op jit(solution)/shard_map/ppermute | solution.py:475
  95.2 1.0 copy-start.3
  119.2 36.6 %collective-permute-start.10 = (bf16[512,2048]{1,0:T(8,128)(2,1)}, bf16[512,2048]{1,0:T(8,128)(2,1)}, u32[]{:S(2)}, u32[]{:S(2)}) collective-permute-start(bf16[512,2048]{1,0:T(8,128)(2,1)} %all-gather.2.cloned.1.call-done.refs_6_), channel_id=1, source_target_pairs={{0,1},{1,0},{2,3},{3,2},{4,5},{5,4},{6,7},{7,6},{8,9},{9,8},{10,11... | collective-permute-start | bytes 6291464 | tf_op jit(solution)/shard_map/ppermute | solution.py:475
  119.3 31.5 %all-to-all-start.1 = ((bf16[4,4,256,128]{3,2,1,0:T(8,128)(2,1)}), bf16[4,4,256,128]{3,2,1,0:T(8,128)(2,1)S(1)}, u32[]{:S(2)}, u32[]{:S(2)}) async-start(bf16[4,4,256,128]{3,2,1,0:T(8,128)(2,1)} %bitcast.22), calls=%async_computation.1 | async-start | bytes 2097152 | tf_op jit(solution)/shard_map/all_to_all | solution.py:478
  124.4 3.4 %collective-permute-start.11 = (bf16[256,512]{1,0:T(8,128)(2,1)}, bf16[256,512]{1,0:T(8,128)(2,1)S(1)}, u32[]{:S(2)}, u32[]{:S(2)}) collective-permute-start(bf16[256,512]{1,0:T(8,128)(2,1)} %get-tuple-element.57), channel_id=1, source_target_pairs={{0,1},{1,0},{2,3},{3,2},{4,5},{5,4},{6,7},{7,6},{8,9},{9,8},{10,11... | collective-permute-start | bytes 786440 | tf_op jit(solution)/shard_map/ppermute | solution.py:475
  124.6 9.3 %collective-permute-start.12 = (bf16[256,512]{1,0:T(8,128)(2,1)}, bf16[256,512]{1,0:T(8,128)(2,1)S(1)}, u32[]{:S(2)}, u32[]{:S(2)}) collective-permute-start(bf16[256,512]{1,0:T(8,128)(2,1)} %get-tuple-element.38), channel_id=1, source_target_pairs={{0,2},{1,3},{2,0},{3,1},{4,6},{5,7},{6,4},{7,5},{8,10},{9,11},{10,... | collective-permute-start | bytes 786440 | tf_op jit(solution)/shard_map/ppermute | solution.py:475
  126.1 29.7 %collective-permute-start.13 = (bf16[256,512]{1,0:T(8,128)(2,1)}, bf16[256,512]{1,0:T(8,128)(2,1)}, u32[]{:S(2)}, u32[]{:S(2)}) collective-permute-start(bf16[256,512]{1,0:T(8,128)(2,1)} %get-tuple-element.58), channel_id=1, source_target_pairs={{0,3},{1,2},{2,1},{3,0},{4,7},{5,6},{6,5},{7,4},{8,11},{9,10},{10,... | collective-permute-start | bytes 786440 | tf_op jit(solution)/shard_map/ppermute | solution.py:475
  126.3 36.3 %collective-permute-start.7 = (bf16[256,512]{1,0:T(8,128)(2,1)}, bf16[256,512]{1,0:T(8,128)(2,1)}, u32[]{:S(2)}, u32[]{:S(2)}) collective-permute-start(bf16[256,512]{1,0:T(8,128)(2,1)} %get-tuple-element.50), channel_id=1, source_target_pairs={{0,2},{1,3},{2,0},{3,1},{4,6},{5,7},{6,4},{7,5},{8,10},{9,11},{10,... | collective-permute-start | bytes 786440 | tf_op jit(solution)/shard_map/ppermute | solution.py:475
  127.8 28.1 %copy-start.4 = (bf16[256,512]{1,0:T(8,128)(2,1)}, bf16[256,512]{1,0:T(8,128)(2,1)S(1)}, u32[]{:S(2)}) copy-start(bf16[256,512]{1,0:T(8,128)(2,1)S(1)} %collective-permute-done.11.refs_1_) | copy-start | bytes 786436
  127.8 34.8 %collective-permute-start.6 = (bf16[256,512]{1,0:T(8,128)(2,1)}, bf16[256,512]{1,0:T(8,128)(2,1)}, u32[]{:S(2)}, u32[]{:S(2)}) collective-permute-start(bf16[256,512]{1,0:T(8,128)(2,1)} %get-tuple-element.53), channel_id=1, source_target_pairs={{0,1},{1,0},{2,3},{3,2},{4,5},{5,4},{6,7},{7,6},{8,9},{9,8},{10,11... | collective-permute-start | bytes 786440 | tf_op jit(solution)/shard_map/ppermute | solution.py:475
  133.9 0.7 copy-start.5
  134.6 27.9 %collective-permute-start.8 = (bf16[256,512]{1,0:T(8,128)(2,1)}, bf16[256,512]{1,0:T(8,128)(2,1)}, u32[]{:S(2)}, u32[]{:S(2)}) collective-permute-start(bf16[256,512]{1,0:T(8,128)(2,1)} %get-tuple-element.54), channel_id=1, source_target_pairs={{0,3},{1,2},{2,1},{3,0},{4,7},{5,6},{6,5},{7,4},{8,11},{9,10},{10,... | collective-permute-start | bytes 786440 | tf_op jit(solution)/shard_map/ppermute | solution.py:475
  150.8 1.0 copy-start.2
Sparse Core Ops, SparseCore 0:
  18.5 65.3 all-gather.1

commit v7 on v6

--- a/solution.py
+++ b/solution.py
@@ -104,7 +104,7 @@
     heads, span, pairs, half, meta, own, sibling, across, far, bw, xw, zw, small, s0, s1, s2, s3,
     *refs
 ):
-    xs, zs, bc_out, steps_out, totals_out, outgoing, fresh, sems = refs[-8:]
+    xs, zs, bc_out, steps_out, totals_out, outgoing, fresh, xw_held, zw_held, sems, in_sems = refs[-11:]
     me = meta[0]
     step = pl.program_id(0)
     side = (me // 2) ^ 1 ^ step
@@ -118,11 +118,15 @@
     def session_of(at, n):
         return ((((me // 2) ^ 1 ^ at) * 2 + n // pairs) * 2 + half) * pairs + n % pairs
 
+    x_copy = pltpu.make_async_copy(xw, xw_held, in_sems.at[0])
+    z_copy = pltpu.make_async_copy(zw, zw_held, in_sems.at[1])
+
+    @pl.when(step == 0)
+    def _():
+        x_copy.start()
+        z_copy.start()
+
     bcs = project(me, pieces, bw, slice(None))
-    for quad in range(quads):
-        columns = slice(quad * 256, quad * 256 + 256)
-        xs[:, columns] = project(me, pieces, xw, columns).astype(BF)
-        zs[:, columns] = project(me, pieces, zw, columns).astype(BF)
     bc_out[...] = bcs[:, :128].astype(BF)
 
     lane = lax.broadcasted_iota(jnp.int32, (span, 128), 1)
@@ -152,6 +156,22 @@
     lasts = totals[:, span - 1 : span]
     weight_rows = jnp.exp(jnp.minimum(totals - lasts, 0.0)) * steps
     kept = jnp.exp(-lasts)
+
+    @pl.when(step == 0)
+    def _():
+        x_copy.wait()
+
+    for quad in range(quads):
+        columns = slice(quad * 256, quad * 256 + 256)
+        xs[:, columns] = project(me, pieces, xw_held, columns).astype(BF)
+
+    @pl.when(step == 0)
+    def _():
+        z_copy.wait()
+
+    for quad in range(quads):
+        columns = slice(quad * 256, quad * 256 + 256)
+        zs[:, columns] = project(me, pieces, zw_held, columns).astype(BF)
 
     for n in range(count):
         rows = slice(n * span, (n + 1) * span)
@@ -336,7 +356,7 @@
             grid=(2,),
             in_specs=[pl.BlockSpec((None, 2, None, rows, depth), near)] * 2
             + [pl.BlockSpec((None, 2, rows, depth), arrived)] * 2
-            + [whole(weight) for weight in weights]
+            + [whole(weights[0]), ANY, ANY]
             + [whole(small)]
             + [pl.BlockSpec((None,) + inbound.shape[1:], slot_of(n)) for n in range(count)]
             + extra,
@@ -350,13 +370,15 @@
             ],
             scratch_shapes=[
                 pltpu.VMEM((2 * count,) + inbound.shape[1:], BF),
+                *[pltpu.VMEM(weight.shape, BF) for weight in weights[1:]],
                 pltpu.SemaphoreType.DMA((2 * count,)),
+                pltpu.SemaphoreType.DMA((2,)),
             ],
         ),
         input_output_aliases=aliases,
         compiler_params=pltpu.CompilerParams(vmem_limit_bytes=VMEM_LIMIT),
         cost_estimate=pl.CostEstimate(
-            flops=1, bytes_accessed=1, transcendentals=0
+            flops=4 * 10**9, bytes_accessed=1, transcendentals=0
         ),
         name="states",
     )(*operands)
@@ -394,7 +416,7 @@
         ),
         compiler_params=pltpu.CompilerParams(vmem_limit_bytes=VMEM_LIMIT),
         cost_estimate=pl.CostEstimate(
-            flops=1, bytes_accessed=1, transcendentals=0
+            flops=2 * 10**9, bytes_accessed=1, transcendentals=0
         ),
         name="scan",
     )(meta, gain, order, *mid, *[inbound] * pairs)
@@ -431,7 +453,7 @@
         input_output_aliases=aliases,
         compiler_params=pltpu.CompilerParams(vmem_limit_bytes=VMEM_LIMIT),
         cost_estimate=pl.CostEstimate(
-            flops=1, bytes_accessed=1, transcendentals=0
+            flops=2 * 10**9, bytes_accessed=1, transcendentals=0
         ),
         name="project_out",
     )(*operands)
@@ -486,7 +508,8 @@
     replicas = lax.axis_size("groups") * shard_count
     replica = lax.axis_index("groups") * shard_count + shard_index
     share = width // replicas
-    ow_part = exchange(lax.dynamic_slice_in_dim(out_weight, replica * share, share), 2)
+    ow_share = lax.dynamic_slice_in_dim(out_weight, replica * share, share)
+    ow_part = exchange(ow_share, 2)
     blocks = tokens.reshape(model_shards // 2, 2, halves, rows, depth)
     sibling = exchange(tokens, 1).reshape(blocks.shape)
 
@@ -506,11 +529,11 @@
     swap = jnp.asarray(
         (swap_row % 16 * sessions_here + swap_row // 16)[:, None] == swap_row[None, :], BF
     )
-    packed = pack_states(source, store_states, swap, slot_count)
+    first = after(blocks, ow_share)[:, :, 0]
+    packed = pack_states(after(source, first), store_states, swap, slot_count)
+    second = after(blocks, packed)[:, :, 1]
+    across = [exchange(first, 2), exchange(second, 2)]
     inbound = trade(packed)
-    first = after(blocks[:, :, 0], ow_part)
-    across = [exchange(first, 2)]
-    across.append(exchange(after(blocks[:, :, 1], across[0]), 2))
     wanted = lax.dynamic_slice_in_dim(home_rows, shard_index * sessions_here, sessions_here)
     home_shard = wanted // sessions_here
     session_slot = home_shard * capacity + rank_within(home_shard, wanted % sessions_here)
@@ -533,6 +556,7 @@
     gain = norm_gain.reshape(heads // 4, 4, 32, 2).transpose(0, 3, 1, 2).reshape(1, width)
     small = jnp.stack([dt_bias, decay_rate], axis=1)
 
+    ow_part = after(ow_part, packed)
     ow_across = lax.all_gather(ow_part, ("groups", "dp"), axis=0, tiled=True)
     ow_sibling = exchange(out_weight, 1)
 
@@ -543,7 +567,7 @@
         arrived = across[h]
         start = meta
         if h:
-            start = after(meta, done[-1])
+            start = after(meta, done[-1], ow_sibling)
             arrived = after(arrived, mid[0])
         else:
             arrived = after(arrived, xw, zw, bw)
@@ -553,6 +577,8 @@
         )
         far_part = scan_call(h, 0, start, gain, order, mid, inbound, span, rows)
         start = after(start, far_part[0])
+        if h:
+            start = after(start, *received[0])
         near_part = scan_call(h, 1, start, gain, order, mid, inbound, span, rows)
         done.append(near_part[0])
         received.append(

time: 177 us -> 173 us (0.977)
  waiting for transfers between devices: 52.4 us -> 43 us
  Pallas kernels: 67.6 us -> 72.2 us
  matrix products: 5.2 us -> 7.03 us
    ppermute x14, waiting for transfers between devices: 35.1 us -> 5.73 us  [exchange(): return lax.ppermute(value, 'mp', pairs)]
    all_to_all x2, waiting for transfers between devices: 17.3 us -> 37.2 us  [trade(): lax.all_to_all(value.reshape((shard_count, capacity) + row_shape), 'dp',...]
    pallas_call x2, Pallas kernels: 24.5 us -> 29.3 us  [state_call(): pl.pallas_call(lambda *refs: state_kernel(heads, span, pairs, half, *refs...]
    dot_general x1, matrix products: 2.62 us -> 4.46 us  [body(): zw = jnp.dot(z_weight, turn, preferred_element_type=F32).astype(BF)]
    unnamed x33 -> x37, local copies, waits for them, and re-layouts: 5.41 us -> 6.17 us
  transfers between devices with their start and end apart: 17 -> 17, of which waited for: 6 -> 3; matrix products, arithmetic and copies ran while one was open for 9% -> 11% of each run, Pallas kernels for 35% -> 38%
where the time goes in v7:
time: 173 us; the launch traced here: 172 us
  Pallas kernels  72.2 us (42%)
  waiting for transfers between devices  43 us (25%)
  starting transfers between devices  19.1 us (11%)
  between operations  14.2 us (8%)
  local copies, waits for them, and re-layouts  12.1 us (7%)
  matrix products  7.03 us (4%)
  other arithmetic  4.44 us (3%)
    all_to_all x2, waiting for transfers between devices, trade(): lax.all_to_all(value.reshape((shard_count, capacity) + row_shape), 'dp',...  37.2 us
    pallas_call x2, Pallas kernels, state_call(): pl.pallas_call(lambda *refs: state_kernel(heads, span, pairs, half, *refs...  29.3 us
    pallas_call x4, Pallas kernels, scan_call(): pl.pallas_call(lambda *refs: scan_kernel(heads, span, pairs, half, side,...  21.4 us
    pallas_call x2, Pallas kernels, out_call(): pl.pallas_call(kernel, grid=(columns // block,), out_shape=jax.ShapeDtype...  13.3 us
    ppermute x14, starting transfers between devices, exchange(): return lax.ppermute(value, 'mp', pairs)  10.2 us
    all_to_all x2, starting transfers between devices, trade(): lax.all_to_all(value.reshape((shard_count, capacity) + row_shape), 'dp',...  8.9 us
    unnamed x37, local copies, waits for them, and re-layouts  6.17 us
    ppermute x14, waiting for transfers between devices, exchange(): return lax.ppermute(value, 'mp', pairs)  5.73 us
  transfers between devices with their start and end apart: 17, of which 3 were waited for; matrix products, arithmetic and copies ran while one was open for 11% of the time, Pallas kernels for 38%

profile of v7, /device:TPU:0, one launch (start us, length us, event | category | flops | bytes accessed | tf_op | source)
XLA Modules:
  0.0 172.1 jit_solution(3575325931860188682)
XLA Ops:
  7.2 0.0 copy-start
  7.2 0.5 collective-permute-start
  7.7 0.1 collective-permute-start.3
  7.8 1.0 constant_dynamic-slice_fusion
  8.8 3.0 %collective-permute-start.12 = (bf16[64,2048]{1,0:T(8,128)(2,1)S(1)}, bf16[64,2048]{1,0:T(8,128)(2,1)}, u32[]{:S(2)}, u32[]{:S(2)}) collective-permute-start(bf16[64,2048]{1,0:T(8,128)(2,1)S(1)} %constant_dynamic-slice_fusion), channel_id=1, source_target_pairs={{0,2},{1,3},{2,0},{3,1},{4,6},{5,7},{6,4},{7,5},{8,10},{9,11},{10,... | collective-permute-start | bytes 786440 | tf_op jit(solution)/shard_map/ppermute | solution.py:497
  11.8 2.3 %slice_bitcast_fusion.1 = bf16[2,2,256,512]{3,2,1,0:T(8,128)(2,1)} fusion(bf16[2,2,2,256,512]{4,3,2,1,0:T(8,128)(2,1)} %bitcast.48), kind=kLoop, calls=%fused_computation.5 | loop fusion | bytes 2097152 | tf_op jit(solution)/shard_map/squeeze | solution.py:532
  14.1 0.0 collective-permute-start.1
  14.1 0.2 select_reduce_fusion.1
  14.3 0.2 convert_reduce_fusion
  14.5 0.6 select_reduce_fusion.source
  15.1 4.0 %pack_states.1 = bf16[16,256,128]{2,1,0:T(8,128)(2,1)} custom-call(s32[16]{0:T(128)} %select_reduce_fusion.source, bf16[16,32768]{1,0:T(8,128)(2,1)} %store.1, bf16[256,256]{1,0:T(8,128)(2,1)} %constant.61.clone.swap), custom_call_target="tpu_custom_call" | custom-call | flops 1 | bytes 1 | tf_op jit(solution)/shard_map/pack_states/pallas_call | solution.py:39
  19.1 5.4 %all-to-all-start = ((bf16[4,4,256,128]{3,2,1,0:T(8,128)(2,1)}), bf16[4,4,256,128]{3,2,1,0:T(8,128)(2,1)S(1)}, u32[]{:S(2)}, u32[]{:S(2)}) async-start(bf16[4,4,256,128]{3,2,1,0:T(8,128)(2,1)} %bitcast.52), calls=%async_computation | async-start | bytes 2097152 | tf_op jit(solution)/shard_map/all_to_all | solution.py:500
  24.5 1.0 copy.45
  25.5 0.1 pad.4.clone
  25.6 2.5 %maximum_maximum_fusion.refs_5_ = bf16[2048,256]{1,0:T(8,128)(2,1)} fusion(bf16[2048,8]{1,0:T(8,128)(2,1)} %copy.45, bf16[2048,128]{1,0:T(8,128)(2,1)} %param.17, bf16[256]{0:T(256)(128)(2,1)S(1)} %pad.4.clone), kind=kLoop, calls=%fused_computation.6 | loop fusion | flops 3145728 | bytes 1606144 | tf_op jit(solution)/shard_map/concatenate | solution.py:553
  28.1 2.6 %fusion.refs_6_ = bf16[2048,512]{1,0:T(8,128)(2,1)} fusion(bf16[2048,512]{1,0:T(8,128)(2,1)S(1)} %copy-done, bf16[512,512]{1,0:T(8,128)(2,1)S(1)} %copy-done.17), kind=kOutput, calls=%fused_computation.2 | convolution fusion | flops 1074790400 | bytes 4718592 | tf_op jit(solution)/shard_map/dot_general | solution.py:550
  30.7 0.0 all-gather.2.cloned.1.call-update
  30.7 0.0 copy-start.2
  30.7 4.5 %fusion.1.refs_7_ = bf16[2048,512]{1,0:T(8,128)(2,1)} fusion(bf16[2048,512]{1,0:T(8,128)(2,1)} %param.16, bf16[512,512]{1,0:T(8,128)(2,1)} %constant.62.clone), kind=kOutput, calls=%fused_computation.3 | convolution fusion | flops 1074790400 | bytes 4718592 | tf_op jit(solution)/shard_map/dot_general | solution.py:551
  35.2 5.7 %collective-permute-done.1.refs_3_ = bf16[2,2,256,512]{3,2,1,0:T(8,128)(2,1)} collective-permute-done((bf16[2,2,256,512]{3,2,1,0:T(8,128)(2,1)}, bf16[2,2,256,512]{3,2,1,0:T(8,128)(2,1)}, u32[]{:S(2)}, u32[]{:S(2)}) %collective-permute-start.1) | collective-permute-done | bytes 1048608 | tf_op jit(solution)/shard_map/ppermute | solution.py:497
  40.9 0.0 collective-permute-start.2
  40.9 1.0 slice_bitcast_fusion
  41.9 1.7 %collective-permute-start.4 = (bf16[2,2,256,512]{3,2,1,0:T(8,128)(2,1)}, bf16[2,2,256,512]{3,2,1,0:T(8,128)(2,1)}, u32[]{:S(2)}, u32[]{:S(2)}) collective-permute-start(bf16[2,2,256,512]{3,2,1,0:T(8,128)(2,1)} %slice_bitcast_fusion), channel_id=1, source_target_pairs={{0,2},{1,3},{2,0},{3,1},{4,6},{5,7},{6,4},{7,5},{8,10},{9,11},{10,... | collective-permute-start | bytes 3145736 | tf_op jit(solution)/shard_map/ppermute | solution.py:497
  43.7 0.7 copy.46.refs_8_
  44.3 0.1 and_select_fusion.2
  44.4 0.2 convert_reduce_fusion.1
  44.6 0.7 pad_add_fusion.refs_0_
  45.3 13.0 %all-to-all-done = bf16[4,4,256,128]{3,2,1,0:T(8,128)(2,1)S(1)} async-done(((bf16[4,4,256,128]{3,2,1,0:T(8,128)(2,1)}), bf16[4,4,256,128]{3,2,1,0:T(8,128)(2,1)S(1)}, u32[]{:S(2)}, u32[]{:S(2)}) %all-to-all-start) | async-done | bytes 1048608 | tf_op jit(solution)/shard_map/all_to_all | solution.py:500
  58.3 0.0 collective-permute-done.2.refs_4_
  58.3 1.0 copy-done.1
  59.3 14.7 %states.2 = (bf16[2,512,512]{2,1,0:T(8,128)(2,1)}, bf16[2,512,512]{2,1,0:T(8,128)(2,1)}, bf16[2,512,128]{2,1,0:T(8,128)(2,1)}, f32[2,32,128]{2,1,0:T(8,128)}, f3...) custom-call(s32[33]{0:T(128)} %pad_add_fusion.refs_0_, bf16[2,2,2,256,512]{4,3,2,1,0:T(8,128)(2,1)} %bitcast.49, ...), custom_call_target="tpu_custom_call" | custom-call | flops 4000000000 | bytes 1 | tf_op jit(solution)/shard_map/states/pallas_call | solution.py:344
  74.0 0.0 collective-permute-done.4.refs_3_
  74.0 0.1 collective-permute-start.5
  74.1 0.1 reshape.121
  74.2 0.1 copy.41
  74.4 0.7 reshape.122.refs_1_
  75.0 5.3 %scan.4 = (bf16[256,512]{1,0:T(8,128)(2,1)}, bf16[256,512]{1,0:T(8,128)(2,1)}) custom-call(s32[33]{0:T(128)} %pad_add_fusion.refs_0_, f32[1,512]{1,0:T(1,128)} %reshape.122.refs_1_, bf16[256,256]{1,0:T(8,128)(2,1)} %constant.63.refs_2_, bf16[2,2,256,512]{3,2,1,0:T(8,128)(2,1)} %bitcast.61, bf16[2,2,256,512]{3,2,1,0:T(8,128)(2,1)} %bitcast.63, ...), custom_call_target="tpu_custom_call" | custom-call | flops 2000000000 | bytes 1 | tf_op jit(solution)/shard_map/scan/pallas_call | solution.py:405
  80.4 1.6 collective-permute-start.7
  81.9 5.4 %scan.5 = (bf16[256,512]{1,0:T(8,128)(2,1)}, bf16[256,512]{1,0:T(8,128)(2,1)}) custom-call(s32[33]{0:T(128)} %pad_add_fusion.refs_0_, f32[1,512]{1,0:T(1,128)} %reshape.122.refs_1_, bf16[256,256]{1,0:T(8,128)(2,1)} %constant.63.refs_2_, bf16[2,2,256,512]{3,2,1,0:T(8,128)(2,1)} %bitcast.62, bf16[2,2,256,512]{3,2,1,0:T(8,128)(2,1)} %bitcast.64, ...), custom_call_target="tpu_custom_call" | custom-call | flops 2000000000 | bytes 1 | tf_op jit(solution)/shard_map/scan/pallas_call | solution.py:405
  87.3 0.0 collective-permute-done.3.refs_5_
  87.3 0.3 collective-permute-start.6
  87.6 0.4 collective-permute-start.8
  88.0 0.0 collective-permute-done.5.refs_4_
  88.0 1.0 copy-done.4
  89.0 14.7 %states.3 = (bf16[2,512,512]{2,1,0:T(8,128)(2,1)}, bf16[2,512,512]{2,1,0:T(8,128)(2,1)}, bf16[2,512,128]{2,1,0:T(8,128)(2,1)}, f32[2,32,128]{2,1,0:T(8,128)}, f3...) custom-call(s32[33]{0:T(128)} %pad_add_fusion.refs_0_, ...), custom_call_target="tpu_custom_call", output_to_operand_aliasing={{5}: (13, {})} | custom-call | flops 4000000000 | bytes 1 | tf_op jit(solution)/shard_map/states/pallas_call | solution.py:344
  103.6 5.4 %scan.6 = (bf16[256,512]{1,0:T(8,128)(2,1)}, bf16[256,512]{1,0:T(8,128)(2,1)}) custom-call(s32[33]{0:T(128)} %pad_add_fusion.refs_0_, f32[1,512]{1,0:T(1,128)} %reshape.122.refs_1_, bf16[256,256]{1,0:T(8,128)(2,1)} %constant.63.refs_2_, bf16[2,2,256,512]{3,2,1,0:T(8,128)(2,1)} %bitcast.57, bf16[2,2,256,512]{3,2,1,0:T(8,128)(2,1)} %bitcast.59, ...), custom_call_target="tpu_custom_call" | custom-call | flops 2000000000 | bytes 1 | tf_op jit(solution)/shard_map/scan/pallas_call | solution.py:405
  109.0 0.0 collective-permute-done.6.refs_1_
  109.0 0.0 collective-permute-done.7.refs_2_
  109.0 0.7 copy-done.6
  109.7 0.8 copy-done.7
  110.5 5.3 %scan.7 = (bf16[256,512]{1,0:T(8,128)(2,1)}, bf16[256,512]{1,0:T(8,128)(2,1)}) custom-call(s32[33]{0:T(128)} %pad_add_fusion.refs_0_, f32[1,512]{1,0:T(1,128)} %reshape.122.refs_1_, bf16[256,256]{1,0:T(8,128)(2,1)} %constant.63.refs_2_, bf16[2,2,256,512]{3,2,1,0:T(8,128)(2,1)} %bitcast.58, bf16[2,2,256,512]{3,2,1,0:T(8,128)(2,1)} %bitcast.60, ...), custom_call_target="tpu_custom_call" | custom-call | flops 2000000000 | bytes 1 | tf_op jit(solution)/shard_map/scan/pallas_call | solution.py:405
  115.8 0.0 all-gather.2.cloned.1.call-done.refs_6_
  115.9 0.3 collective-permute-start.13
  116.1 3.5 %all-to-all-start.1 = ((bf16[4,4,256,128]{3,2,1,0:T(8,128)(2,1)}), bf16[4,4,256,128]{3,2,1,0:T(8,128)(2,1)S(1)}, u32[]{:S(2)}, u32[]{:S(2)}) async-start(bf16[4,4,256,128]{3,2,1,0:T(8,128)(2,1)} %bitcast.22), calls=%async_computation.1 | async-start | bytes 2097152 | tf_op jit(solution)/shard_map/all_to_all | solution.py:500
  119.7 1.6 collective-permute-start.10
  121.3 0.0 collective-permute-start.9
  121.3 0.6 collective-permute-start.11
  121.9 24.2 %all-to-all-done.1 = bf16[4,4,256,128]{3,2,1,0:T(8,128)(2,1)S(1)} async-done(((bf16[4,4,256,128]{3,2,1,0:T(8,128)(2,1)}), bf16[4,4,256,128]{3,2,1,0:T(8,128)(2,1)S(1)}, u32[]{:S(2)}, u32[]{:S(2)}) %all-to-all-start.1) | async-done | bytes 1048608 | tf_op jit(solution)/shard_map/all_to_all | solution.py:500
  146.1 1.0 copy-done.3
  147.1 4.1 %gather_states.1 = bf16[16,32768]{1,0:T(8,128)(2,1)} custom-call(s32[16]{0:T(128)} %copy-done.11, bf16[16,256,128]{2,1,0:T(8,128)(2,1)} %bitcast.53, bf16[256,256]{1,0:T(8,128)(2,1)} %constant.61.clone.swap), custom_call_target="tpu_custom_call" | custom-call | flops 1 | bytes 1 | tf_op jit(solution)/shard_map/gather_states/pallas_call | solution.py:75
  151.2 6.7 %project_out.2.refs_8_ = bf16[512,2048]{1,0:T(8,128)(2,1)} custom-call(bf16[256,512]{1,0:T(8,128)(2,1)} %get-tuple-element.64.refs_0_, bf16[256,512]{1,0:T(8,128)(2,1)} %copy-done.6, bf16[256,512]{1,0:T(8,128)(2,1)} %copy-done.5, bf16[256,512]{1,0:T(8,128)(2,1)} %copy-done.7, bf16[512,2048]{1,0:T(8,128)(2,1)} %refs_4_.3, ...), custom_call_target="tpu_custom_call" | custom-call | flops 2000000000 | bytes 1 | tf_op jit(solution)/shard_map/project_out/pallas_call | solution.py:445
  157.8 0.0 collective-permute-done.9.refs_1_
  157.9 0.7 copy-done.8
  158.6 6.7 %project_out.3 = bf16[512,2048]{1,0:T(8,128)(2,1)} custom-call(bf16[256,512]{1,0:T(8,128)(2,1)} %get-tuple-element.59.refs_0_, bf16[256,512]{1,0:T(8,128)(2,1)} %collective-permute-done.9.refs_1_, bf16[256,512]{1,0:T(8,128)(2,1)} %copy-done.8, bf16[256,512]{1,0:T(8,128)(2,1)} %collective-permute-done.11.refs_3_, ...), custom_call_target="tpu_custom_call", output_to_operand_aliasing={{}: (8, {})} | custom-call | flops 2000000000 | bytes 1 | tf_op jit(solution)/shard_map/project_out/pallas_call | solution.py:445
  (42 shorter events, 0.1 us)
Async XLA Ops:
  7.2 20.9 %copy-start = (bf16[2048,512]{1,0:T(8,128)(2,1)S(1)}, bf16[2048,512]{1,0:T(8,128)(2,1)}, u32[]{:S(2)}) copy-start(bf16[2048,512]{1,0:T(8,128)(2,1)} %param.15) | copy-start | bytes 6291460
  7.2 6.9 %copy-start.14 = (s32[64]{0:T(128)S(1)}, s32[64]{0:T(128)}, u32[]{:S(2)}) copy-start(s32[64]{0:T(128)} %param.24) | copy-start | bytes 772
  7.2 51.1 %collective-permute-start = (bf16[2048,512]{1,0:T(8,128)(2,1)}, bf16[2048,512]{1,0:T(8,128)(2,1)}, u32[]{:S(2)}, u32[]{:S(2)}) collective-permute-start(bf16[2048,512]{1,0:T(8,128)(2,1)} %param.14), channel_id=1, source_target_pairs={{0,1},{1,0},{2,3},{3,2},{4,5},{5,4},{6,7},{7,6},{8,9},{9,8},{10,11... | collective-permute-start | bytes 6291464 | tf_op jit(solution)/shard_map/ppermute | solution.py:497
  7.7 79.6 %collective-permute-start.3 = (bf16[512,2048]{1,0:T(8,128)(2,1)}, bf16[512,2048]{1,0:T(8,128)(2,1)}, u32[]{:S(2)}, u32[]{:S(2)}) collective-permute-start(bf16[512,2048]{1,0:T(8,128)(2,1)} %refs_4_.3), channel_id=1, source_target_pairs={{0,1},{1,0},{2,3},{3,2},{4,5},{5,4},{6,7},{7,6},{8,9},{9,8},{10,11... | collective-permute-start | bytes 6291464 | tf_op jit(solution)/shard_map/ppermute | solution.py:497
  8.8 21.9 %collective-permute-start.12 = (bf16[64,2048]{1,0:T(8,128)(2,1)S(1)}, bf16[64,2048]{1,0:T(8,128)(2,1)}, u32[]{:S(2)}, u32[]{:S(2)}) collective-permute-start(bf16[64,2048]{1,0:T(8,128)(2,1)S(1)} %constant_dynamic-slice_fusion), channel_id=1, source_target_pairs={{0,2},{1,3},{2,0},{3,1},{4,6},{5,7},{6,4},{7,5},{8,10},{9,11},{10,... | collective-permute-start | bytes 786440 | tf_op jit(solution)/shard_map/ppermute | solution.py:497
  14.1 26.8 %collective-permute-start.1 = (bf16[2,2,256,512]{3,2,1,0:T(8,128)(2,1)}, bf16[2,2,256,512]{3,2,1,0:T(8,128)(2,1)}, u32[]{:S(2)}, u32[]{:S(2)}) collective-permute-start(bf16[2,2,256,512]{3,2,1,0:T(8,128)(2,1)} %slice_bitcast_fusion.1), channel_id=1, source_target_pairs={{0,2},{1,3},{2,0},{3,1},{4,6},{5,7},{6,4},{7,5},{8,10},{9,11},{10,... | collective-permute-start | bytes 3145736 | tf_op jit(solution)/shard_map/ppermute | solution.py:497
  14.5 4.7 %copy-start.11 = (s32[16]{0:T(128)}, s32[16]{0:T(128)S(1)}, u32[]{:S(2)}) copy-start(s32[16]{0:T(128)S(1)} %multiply_add_fusion.index) | copy-start | bytes 196
  15.1 9.4 %copy-start.9 = (bf16[2048,8]{0,1:T(8,128)(2,1)S(1)}, bf16[2048,8]{0,1:T(8,128)(2,1)}, u32[]{:S(2)}) copy-start(bf16[2048,8]{0,1:T(8,128)(2,1)} %param.18) | copy-start | bytes 98308
  19.1 39.2 %all-to-all-start = ((bf16[4,4,256,128]{3,2,1,0:T(8,128)(2,1)}), bf16[4,4,256,128]{3,2,1,0:T(8,128)(2,1)S(1)}, u32[]{:S(2)}, u32[]{:S(2)}) async-start(bf16[4,4,256,128]{3,2,1,0:T(8,128)(2,1)} %bitcast.52), calls=%async_computation | async-start | bytes 2097152 | tf_op jit(solution)/shard_map/all_to_all | solution.py:500
  24.5 91.3 %all-gather.2.cloned.1.call-start = ((), (), s32[]{:S(2)}) async-start(), calls=%async_computation.2 | async-start | bytes 2359296 | tf_op jit(solution)/shard_map/all_gather | solution.py:560
  25.5 2.6 %copy-start.17 = (bf16[512,512]{1,0:T(8,128)(2,1)S(1)}, bf16[512,512]{1,0:T(8,128)(2,1)}, u32[]{:S(2)}) copy-start(bf16[512,512]{1,0:T(8,128)(2,1)} %constant.62.clone) | copy-start | bytes 1572868
  30.7 10.2 %copy-start.2 = (bf16[2048,512]{1,0:T(8,128)(2,1)S(1)}, bf16[2048,512]{1,0:T(8,128)(2,1)}, u32[]{:S(2)}) copy-start(bf16[2048,512]{1,0:T(8,128)(2,1)} %param.14) | copy-start | bytes 6291460
  35.2 8.5 %copy-start.12 = (f32[8]{0:T(128)S(1)}, f32[8]{0:T(128)}, u32[]{:S(2)}) copy-start(f32[8]{0:T(128)} %param.20) | copy-start | bytes 100
  35.2 8.5 %copy-start.13 = (f32[8]{0:T(128)S(1)}, f32[8]{0:T(128)}, u32[]{:S(2)}) copy-start(f32[8]{0:T(128)} %param.19) | copy-start | bytes 100
  35.2 9.5 %copy-start.15 = (s32[16]{0:T(128)S(1)}, s32[16]{0:T(128)}, u32[]{:S(2)}) copy-start(s32[16]{0:T(128)} %param.25) | copy-start | bytes 196
  40.9 17.4 %collective-permute-start.2 = (bf16[2,2,256,512]{3,2,1,0:T(8,128)(2,1)}, bf16[2,2,256,512]{3,2,1,0:T(8,128)(2,1)}, u32[]{:S(2)}, u32[]{:S(2)}) collective-permute-start(bf16[2,2,256,512]{3,2,1,0:T(8,128)(2,1)} %collective-permute-done.1.refs_3_), channel_id=1, source_target_pairs={{0,1},{1,0},{2,3},{3,2},{4,5},{5,4},{6,7},{7,6},{8,9},{9,8},{10,11... | collective-permute-start | bytes 3145736 | tf_op jit(solution)/shard_map/ppermute | solution.py:497
  41.9 32.1 %collective-permute-start.4 = (bf16[2,2,256,512]{3,2,1,0:T(8,128)(2,1)}, bf16[2,2,256,512]{3,2,1,0:T(8,128)(2,1)}, u32[]{:S(2)}, u32[]{:S(2)}) collective-permute-start(bf16[2,2,256,512]{3,2,1,0:T(8,128)(2,1)} %slice_bitcast_fusion), channel_id=1, source_target_pairs={{0,2},{1,3},{2,0},{3,1},{4,6},{5,7},{6,4},{7,5},{8,10},{9,11},{10,... | collective-permute-start | bytes 3145736 | tf_op jit(solution)/shard_map/ppermute | solution.py:497
  58.3 1.0 copy-start.1
  59.3 14.8 %copy-start.10 = (f32[512]{0:T(512)S(1)}, f32[512]{0:T(512)}, u32[]{:S(2)}) copy-start(f32[512]{0:T(512)} %param.21) | copy-start | bytes 6148
  74.0 14.0 %collective-permute-start.5 = (bf16[2,2,256,512]{3,2,1,0:T(8,128)(2,1)}, bf16[2,2,256,512]{3,2,1,0:T(8,128)(2,1)S(1)}, u32[]{:S(2)}, u32[]{:S(2)}) collective-permute-start(bf16[2,2,256,512]{3,2,1,0:T(8,128)(2,1)} %collective-permute-done.4.refs_3_), channel_id=1, source_target_pairs={{0,1},{1,0},{2,3},{3,2},{4,5},{5,4},{6,7},{7,6},{8,9},{9,8},{10,11... | collective-permute-start | bytes 3145736 | tf_op jit(solution)/shard_map/ppermute | solution.py:497
  80.4 7.2 %copy-start.16 = (bf16[256,512]{1,0:T(8,128)(2,1)S(1)}, bf16[256,512]{1,0:T(8,128)(2,1)}, u32[]{:S(2)}) copy-start(bf16[256,512]{1,0:T(8,128)(2,1)} %get-tuple-element.57) | copy-start | bytes 786436
  80.4 28.7 %collective-permute-start.7 = (bf16[256,512]{1,0:T(8,128)(2,1)}, bf16[256,512]{1,0:T(8,128)(2,1)S(1)}, u32[]{:S(2)}, u32[]{:S(2)}) collective-permute-start(bf16[256,512]{1,0:T(8,128)(2,1)} %get-tuple-element.42), channel_id=1, source_target_pairs={{0,2},{1,3},{2,0},{3,1},{4,6},{5,7},{6,4},{7,5},{8,10},{9,11},{10,... | collective-permute-start | bytes 786440 | tf_op jit(solution)/shard_map/ppermute | solution.py:497
  87.3 21.7 %collective-permute-start.6 = (bf16[256,512]{1,0:T(8,128)(2,1)}, bf16[256,512]{1,0:T(8,128)(2,1)S(1)}, u32[]{:S(2)}, u32[]{:S(2)}) collective-permute-start(bf16[256,512]{1,0:T(8,128)(2,1)} %get-tuple-element.56), channel_id=1, source_target_pairs={{0,1},{1,0},{2,3},{3,2},{4,5},{5,4},{6,7},{7,6},{8,9},{9,8},{10,11... | collective-permute-start | bytes 786440 | tf_op jit(solution)/shard_map/ppermute | solution.py:497
  87.6 22.1 %collective-permute-start.8 = (bf16[256,512]{1,0:T(8,128)(2,1)S(1)}, bf16[256,512]{1,0:T(8,128)(2,1)S(1)}, u32[]{:S(2)}, u32[]{:S(2)}) collective-permute-start(bf16[256,512]{1,0:T(8,128)(2,1)S(1)} %copy-done.16), channel_id=1, source_target_pairs={{0,3},{1,2},{2,1},{3,0},{4,7},{5,6},{6,5},{7,4},{8,11},{9,10},{10,... | collective-permute-start | bytes 786440 | tf_op jit(solution)/shard_map/ppermute | solution.py:497
  88.0 1.0 copy-start.4
  109.0 0.7 copy-start.6
  109.7 6.1 %copy-start.5 = (bf16[256,512]{1,0:T(8,128)(2,1)}, bf16[256,512]{1,0:T(8,128)(2,1)S(1)}, u32[]{:S(2)}) copy-start(bf16[256,512]{1,0:T(8,128)(2,1)S(1)} %collective-permute-done.7.refs_2_) | copy-start | bytes 786436
  109.7 0.8 copy-start.7
  115.9 35.3 %collective-permute-start.13 = (bf16[512,2048]{1,0:T(8,128)(2,1)}, bf16[512,2048]{1,0:T(8,128)(2,1)}, u32[]{:S(2)}, u32[]{:S(2)}) collective-permute-start(bf16[512,2048]{1,0:T(8,128)(2,1)} %all-gather.2.cloned.1.call-done.refs_6_), channel_id=1, source_target_pairs={{0,1},{1,0},{2,3},{3,2},{4,5},{5,4},{6,7},{7,6},{8,9},{9,8},{10,11... | collective-permute-start | bytes 6291464 | tf_op jit(solution)/shard_map/ppermute | solution.py:497
  116.1 30.0 %all-to-all-start.1 = ((bf16[4,4,256,128]{3,2,1,0:T(8,128)(2,1)}), bf16[4,4,256,128]{3,2,1,0:T(8,128)(2,1)S(1)}, u32[]{:S(2)}, u32[]{:S(2)}) async-start(bf16[4,4,256,128]{3,2,1,0:T(8,128)(2,1)} %bitcast.22), calls=%async_computation.1 | async-start | bytes 2097152 | tf_op jit(solution)/shard_map/all_to_all | solution.py:500
  119.7 38.2 %collective-permute-start.10 = (bf16[256,512]{1,0:T(8,128)(2,1)}, bf16[256,512]{1,0:T(8,128)(2,1)S(1)}, u32[]{:S(2)}, u32[]{:S(2)}) collective-permute-start(bf16[256,512]{1,0:T(8,128)(2,1)} %get-tuple-element.54), channel_id=1, source_target_pairs={{0,2},{1,3},{2,0},{3,1},{4,6},{5,7},{6,4},{7,5},{8,10},{9,11},{10,... | collective-permute-start | bytes 786440 | tf_op jit(solution)/shard_map/ppermute | solution.py:497
  121.3 36.6 %collective-permute-start.9 = (bf16[256,512]{1,0:T(8,128)(2,1)}, bf16[256,512]{1,0:T(8,128)(2,1)}, u32[]{:S(2)}, u32[]{:S(2)}) collective-permute-start(bf16[256,512]{1,0:T(8,128)(2,1)} %get-tuple-element.60), channel_id=1, source_target_pairs={{0,1},{1,0},{2,3},{3,2},{4,5},{5,4},{6,7},{7,6},{8,9},{9,8},{10,11... | collective-permute-start | bytes 786440 | tf_op jit(solution)/shard_map/ppermute | solution.py:497
  121.3 36.6 %collective-permute-start.11 = (bf16[256,512]{1,0:T(8,128)(2,1)}, bf16[256,512]{1,0:T(8,128)(2,1)}, u32[]{:S(2)}, u32[]{:S(2)}) collective-permute-start(bf16[256,512]{1,0:T(8,128)(2,1)} %get-tuple-element.61), channel_id=1, source_target_pairs={{0,3},{1,2},{2,1},{3,0},{4,7},{5,6},{6,5},{7,4},{8,11},{9,10},{10,... | collective-permute-start | bytes 786440 | tf_op jit(solution)/shard_map/ppermute | solution.py:497
  146.1 1.0 copy-start.3
  157.8 0.7 copy-start.8
Sparse Core Ops, SparseCore 0:
  30.8 54.1 all-gather.1

commit v8 on v6

--- a/solution.py
+++ b/solution.py
@@ -100,14 +100,15 @@
     return total
 
 
-def state_kernel(
-    heads, span, pairs, half, meta, own, sibling, across, far, bw, xw, zw, small, s0, s1, s2, s3,
+def layer_kernel(
+    heads, span, pairs, half, meta, own, sibling, across, far, bw, xw, zw, small, gain, order, s0,
+    s1, s2, s3,
     *refs
 ):
-    xs, zs, bc_out, steps_out, totals_out, outgoing, fresh, sems = refs[-8:]
+    n0, n1, n2, n3, outgoing, xs, zs, fresh, sems = refs[-9:]
+    normed_out = (n0, n1, n2, n3)
     me = meta[0]
     step = pl.program_id(0)
-    side = (me // 2) ^ 1 ^ step
     count = 2 * pairs
     rows_all = count * span
     depth = across.shape[-1]
@@ -123,7 +124,6 @@
         columns = slice(quad * 256, quad * 256 + 256)
         xs[:, columns] = project(me, pieces, xw, columns).astype(BF)
         zs[:, columns] = project(me, pieces, zw, columns).astype(BF)
-    bc_out[...] = bcs[:, :128].astype(BF)
 
     lane = lax.broadcasted_iota(jnp.int32, (span, 128), 1)
     low = lane < 64
@@ -147,97 +147,35 @@
     while shift < span:
         totals = totals + jnp.where(lane_all >= shift, pltpu.roll(totals, shift, 1), 0.0)
         shift *= 2
-    steps_out[...] = steps
-    totals_out[...] = totals
     lasts = totals[:, span - 1 : span]
     weight_rows = jnp.exp(jnp.minimum(totals - lasts, 0.0)) * steps
     kept = jnp.exp(-lasts)
 
-    for n in range(count):
-        rows = slice(n * span, (n + 1) * span)
-        bc = bcs[rows, 0:128]
-        b_low = jnp.where(low, bc, 0.0).astype(BF)
-        b_high = jnp.where(low, 0.0, pltpu.roll(bc, 64, 1)).astype(BF)
-        b_both = jnp.concatenate([b_low, b_high], axis=0)
-        for quad in range(quads):
-            head = n * heads + quad * 4
-            scale = jnp.concatenate(
-                [
-                    jnp.broadcast_to(weight_rows[head + k : head + k + 1, :], (32, span))
-                    for k in range(4)
-                ],
-                axis=0,
-            )
-            x = xs[rows, quad * 256 : quad * 256 + 256].astype(F32)
-            even = (jnp.transpose(x[:, :128]) * scale).astype(BF)
-            odd = (jnp.transpose(x[:, 128:]) * scale).astype(BF)
-            added = jnp.dot(
-                jnp.concatenate([even, odd], axis=1), b_both, preferred_element_type=F32
-            )
-            keep = jnp.concatenate(
-                [
-                    jnp.broadcast_to(kept[head + k : head + k + 1, :], (32, 128))
-                    for k in range(4)
-                ],
-                axis=0,
-            )
-            part = slice(quad * 128, quad * 128 + 128)
-            fresh[step * count + n, part, :] = (
-                keep * states[n][part, :].astype(F32) + added
-            ).astype(BF)
-
-    def sending(at, n):
-        number = at * count + n
-        return pltpu.make_async_copy(
-            fresh.at[number], outgoing.at[meta[1 + session_of(at, n)]], sems.at[number]
-        )
-
-    for n in range(count):
-        sending(step, n).start()
-
-    @pl.when(step == 1)
-    def _():
-        for at in range(2):
-            for n in range(count):
-                sending(at, n).wait()
-
-
-def scan_kernel(
-    heads, span, pairs, half, side, meta, gain, order, xs, zs, bcs, steps_in, totals_in, s0, s1,
-    na, nb, result,
-):
-    me = meta[0]
-    step = pl.program_id(0)
-    target = me ^ (2 * (1 - side) + step)
-    quads = heads // 4
-    states = (s0, s1)
-    lane = lax.broadcasted_iota(jnp.int32, (span, 128), 1)
+    cum = jnp.transpose(
+        jnp.concatenate([totals, jnp.zeros((128 - heads * count, span), F32)], axis=0)
+    )
     row = lax.broadcasted_iota(jnp.int32, (span, 128), 0)
-    low = lane < 64
     causal = row >= lane
     head_masks = []
     for k in range(4):
         mask = (lane // 32 == k).astype(F32).astype(BF)
         head_masks.append(jnp.concatenate([mask, mask], axis=1))
-    steps = steps_in[...]
-    totals = totals_in[...]
-    cum = jnp.transpose(
-        jnp.concatenate([totals, jnp.zeros((128 - heads * pairs, span), F32)], axis=0)
-    )
-    counts_at = 1 + meta.shape[0] // 2
-    for i in range(pairs):
-        rows = slice(i * span, (i + 1) * span)
-        count = meta[counts_at + (target * 2 + half) * pairs + i]
-        bc = bcs[rows, :].astype(F32)
+
+    for n in range(count):
+        rows = slice(n * span, (n + 1) * span)
+        length = meta[counts_at + session_of(step, n)]
+        bc = bcs[rows, 0:128]
         turned = pltpu.roll(bc, 64, 1)
         b_low = jnp.where(low, bc, 0.0).astype(BF)
+        b_high = jnp.where(low, 0.0, turned).astype(BF)
         c_low = jnp.where(low, turned, 0.0).astype(BF)
         c_high = jnp.where(low, 0.0, bc).astype(BF)
+        b_both = jnp.concatenate([b_low, b_high], axis=0)
         scores = lax.dot_general(c_low, b_low, NT, preferred_element_type=F32)
         scores = jnp.where(causal, scores, 0.0)
         carried = lax.dot_general(
             jnp.concatenate([c_low, c_high], axis=0),
-            states[i][...],
+            states[n][...],
             NT,
             preferred_element_type=F32,
         )
@@ -246,11 +184,12 @@
         for quad in range(quads):
             columns = slice(quad * 256, quad * 256 + 256)
             part = slice(quad * 128, quad * 128 + 128)
+            first_head = n * heads + quad * 4
             x = xs[rows, columns]
             mixes = []
             spread = None
             for k in range(4):
-                head = i * heads + quad * 4 + k
+                head = first_head + k
                 level = jnp.broadcast_to(cum[:, head : head + 1], (span, 128))
                 gap = jnp.minimum(totals[head : head + 1, :] - level, 0.0)
                 mixes.append((jnp.exp(gap) * steps[head : head + 1, :] * scores).astype(BF))
@@ -269,33 +208,73 @@
             gated.append(value)
             own_squares = jnp.sum(value * value, axis=1, keepdims=True)
             squares = own_squares if squares is None else squares + own_squares
+            scale = jnp.concatenate(
+                [
+                    jnp.broadcast_to(
+                        weight_rows[first_head + k : first_head + k + 1, :], (32, span)
+                    )
+                    for k in range(4)
+                ],
+                axis=0,
+            )
+            xf = x.astype(F32)
+            even = (jnp.transpose(xf[:, :128]) * scale).astype(BF)
+            odd = (jnp.transpose(xf[:, 128:]) * scale).astype(BF)
+            added = jnp.dot(
+                jnp.concatenate([even, odd], axis=1), b_both, preferred_element_type=F32
+            )
+            keep = jnp.concatenate(
+                [
+                    jnp.broadcast_to(kept[first_head + k : first_head + k + 1, :], (32, 128))
+                    for k in range(4)
+                ],
+                axis=0,
+            )
+            fresh[step * count + n, part, :] = (
+                keep * states[n][part, :].astype(F32) + added
+            ).astype(BF)
         inverse = lax.rsqrt(squares * (1.0 / (heads * 64)) + 1e-05)
-        inverse = jnp.where(row[:, :1] < count, inverse, 0.0)
+        inverse = jnp.where(row[:, :1] < length, inverse, 0.0)
         for quad in range(quads):
             columns = slice(quad * 256, quad * 256 + 256)
             normed = (gated[quad] * inverse * gain[:, columns]).astype(BF)
-            result[rows, columns] = lax.dot_general(
+            zs[rows, columns] = lax.dot_general(
                 normed, order[...], NT, preferred_element_type=F32
             ).astype(BF)
 
-    @pl.when(step == 0)
-    def _():
-        na[...] = result[...]
+    def sending(at, n):
+        number = at * count + n
+        return pltpu.make_async_copy(
+            fresh.at[number], outgoing.at[meta[1 + session_of(at, n)]], sems.at[number]
+        )
+
+    for n in range(count):
+        sending(step, n).start()
+
+    for at in range(2):
+
+        @pl.when(step == at)
+        def _():
+            for near in range(2):
+                first = pl.multiple_of((near ^ (me % 2)) * (pairs * span), pairs * span)
+                normed_out[2 * (1 - at) + near][...] = zs[pl.ds(first, pairs * span), :]
 
     @pl.when(step == 1)
     def _():
-        nb[...] = result[...]
+        for at in range(2):
+            for n in range(count):
+                sending(at, n).wait()
 
 
 def whole(array):
     return pl.BlockSpec(array.shape, lambda i, meta: (0,) * array.ndim)
 
 
-def state_call(half, meta, pieces, weights, small, inbound, span, earlier):
+def layer_call(half, meta, pieces, weights, smalls, inbound, span, earlier):
     rows, depth = pieces[2].shape[-2:]
     pairs = rows // span
     count = 2 * pairs
-    heads = small.shape[0]
+    heads = smalls[0].shape[0]
     width = weights[1].shape[1]
 
     def near(i, meta):
@@ -311,44 +290,30 @@
 
         return index
 
-    def by_step(shape):
-        return pl.BlockSpec((None,) + shape, lambda i, meta: (i, 0, 0))
-
-    operands = [meta, *pieces, *weights, small] + [inbound] * count
+    operands = [meta, *pieces, *weights, *smalls] + [inbound] * count
     aliases = {}
     extra = []
     if earlier is not None:
-        aliases = {len(operands): 5}
+        aliases = {len(operands): 4}
         operands.append(earlier)
         extra = [ANY]
     return pl.pallas_call(
-        lambda *refs: state_kernel(heads, span, pairs, half, *refs),
-        out_shape=[
-            jax.ShapeDtypeStruct((2, count * span, width), BF),
-            jax.ShapeDtypeStruct((2, count * span, width), BF),
-            jax.ShapeDtypeStruct((2, count * span, 128), BF),
-            jax.ShapeDtypeStruct((2, heads * count, span), F32),
-            jax.ShapeDtypeStruct((2, heads * count, span), F32),
-            jax.ShapeDtypeStruct(inbound.shape, BF),
-        ],
+        lambda *refs: layer_kernel(heads, span, pairs, half, *refs),
+        out_shape=[jax.ShapeDtypeStruct((rows, width), BF)] * 4
+        + [jax.ShapeDtypeStruct(inbound.shape, BF)],
         grid_spec=pltpu.PrefetchScalarGridSpec(
             num_scalar_prefetch=1,
             grid=(2,),
             in_specs=[pl.BlockSpec((None, 2, None, rows, depth), near)] * 2
             + [pl.BlockSpec((None, 2, rows, depth), arrived)] * 2
             + [whole(weight) for weight in weights]
-            + [whole(small)]
+            + [whole(small) for small in smalls]
             + [pl.BlockSpec((None,) + inbound.shape[1:], slot_of(n)) for n in range(count)]
             + extra,
-            out_specs=[
-                by_step((count * span, width)),
-                by_step((count * span, width)),
-                by_step((count * span, 128)),
-                by_step((heads * count, span)),
-                by_step((heads * count, span)),
-                ANY,
-            ],
+            out_specs=[pl.BlockSpec((rows, width), lambda i, meta: (0, 0))] * 4 + [ANY],
             scratch_shapes=[
+                pltpu.VMEM((count * span, width), BF),
+                pltpu.VMEM((count * span, width), BF),
                 pltpu.VMEM((2 * count,) + inbound.shape[1:], BF),
                 pltpu.SemaphoreType.DMA((2 * count,)),
             ],
@@ -356,48 +321,10 @@
         input_output_aliases=aliases,
         compiler_params=pltpu.CompilerParams(vmem_limit_bytes=VMEM_LIMIT),
         cost_estimate=pl.CostEstimate(
-            flops=1, bytes_accessed=1, transcendentals=0
+            flops=6 * 10**9, bytes_accessed=1, transcendentals=0
         ),
-        name="states",
+        name="layer",
     )(*operands)
-
-
-def scan_call(half, side, meta, gain, order, mid, inbound, span, rows):
-    pairs = rows // span
-    heads = mid[-1].shape[1] // (2 * pairs)
-    width = mid[0].shape[2]
-    mid = [part.reshape(2, 2, part.shape[1] // 2, part.shape[2]) for part in mid]
-
-    def block_of(part):
-        return pl.BlockSpec(
-            (None, None) + part.shape[2:], lambda i, meta: (side, i ^ (meta[0] % 2), 0, 0)
-        )
-
-    def slot_of(n):
-        def index(i, meta):
-            target = meta[0] ^ (2 * (1 - side) + i)
-            return (meta[1 + (target * 2 + half) * pairs + n], 0, 0)
-
-        return index
-
-    return pl.pallas_call(
-        lambda *refs: scan_kernel(heads, span, pairs, half, side, *refs),
-        out_shape=[jax.ShapeDtypeStruct((rows, width), BF)] * 2,
-        grid_spec=pltpu.PrefetchScalarGridSpec(
-            num_scalar_prefetch=1,
-            grid=(2,),
-            in_specs=[whole(gain), whole(order)]
-            + [block_of(part) for part in mid]
-            + [pl.BlockSpec((None,) + inbound.shape[1:], slot_of(n)) for n in range(pairs)],
-            out_specs=[pl.BlockSpec((rows, width), lambda i, meta: (0, 0))] * 2,
-            scratch_shapes=[pltpu.VMEM((rows, width), BF)],
-        ),
-        compiler_params=pltpu.CompilerParams(vmem_limit_bytes=VMEM_LIMIT),
-        cost_estimate=pl.CostEstimate(
-            flops=1, bytes_accessed=1, transcendentals=0
-        ),
-        name="scan",
-    )(meta, gain, order, *mid, *[inbound] * pairs)
 
 
 def out_call(half, halves, normed, weights, earlier):
@@ -431,7 +358,7 @@
         input_output_aliases=aliases,
         compiler_params=pltpu.CompilerParams(vmem_limit_bytes=VMEM_LIMIT),
         cost_estimate=pl.CostEstimate(
-            flops=1, bytes_accessed=1, transcendentals=0
+            flops=2 * 10**9, bytes_accessed=1, transcendentals=0
         ),
         name="project_out",
     )(*operands)
@@ -486,7 +413,8 @@
     replicas = lax.axis_size("groups") * shard_count
     replica = lax.axis_index("groups") * shard_count + shard_index
     share = width // replicas
-    ow_part = exchange(lax.dynamic_slice_in_dim(out_weight, replica * share, share), 2)
+    ow_share = lax.dynamic_slice_in_dim(out_weight, replica * share, share)
+    ow_part = exchange(ow_share, 2)
     blocks = tokens.reshape(model_shards // 2, 2, halves, rows, depth)
     sibling = exchange(tokens, 1).reshape(blocks.shape)
 
@@ -506,11 +434,11 @@
     swap = jnp.asarray(
         (swap_row % 16 * sessions_here + swap_row // 16)[:, None] == swap_row[None, :], BF
     )
-    packed = pack_states(source, store_states, swap, slot_count)
+    first = after(blocks, ow_share)[:, :, 0]
+    packed = pack_states(after(source, first), store_states, swap, slot_count)
+    second = after(blocks, packed)[:, :, 1]
+    across = [exchange(first, 2), exchange(second, 2)]
     inbound = trade(packed)
-    first = after(blocks[:, :, 0], ow_part)
-    across = [exchange(first, 2)]
-    across.append(exchange(after(blocks[:, :, 1], across[0]), 2))
     wanted = lax.dynamic_slice_in_dim(home_rows, shard_index * sessions_here, sessions_here)
     home_shard = wanted // sessions_here
     session_slot = home_shard * capacity + rank_within(home_shard, wanted % sessions_here)
@@ -533,6 +461,7 @@
     gain = norm_gain.reshape(heads // 4, 4, 32, 2).transpose(0, 3, 1, 2).reshape(1, width)
     small = jnp.stack([dt_bias, decay_rate], axis=1)
 
+    ow_part = after(ow_part, inbound)
     ow_across = lax.all_gather(ow_part, ("groups", "dp"), axis=0, tiled=True)
     ow_sibling = exchange(out_weight, 1)
 
@@ -543,26 +472,16 @@
         arrived = across[h]
         start = meta
         if h:
-            start = after(meta, done[-1])
-            arrived = after(arrived, mid[0])
+            start = after(meta, done[-1], ow_sibling)
+            arrived = after(arrived, done[-1])
         else:
             arrived = after(arrived, xw, zw, bw)
         pieces = (blocks, sibling, arrived, exchange(arrived, 1))
-        *mid, outgoing = state_call(
-            h, start, pieces, (bw, xw, zw), small, inbound, span, outgoing
+        *parts, outgoing = layer_call(
+            h, start, pieces, (bw, xw, zw), (small, gain, order), inbound, span, outgoing
         )
-        far_part = scan_call(h, 0, start, gain, order, mid, inbound, span, rows)
-        start = after(start, far_part[0])
-        near_part = scan_call(h, 1, start, gain, order, mid, inbound, span, rows)
-        done.append(near_part[0])
-        received.append(
-            [
-                near_part[0],
-                exchange(near_part[1], 1),
-                exchange(far_part[0], 2),
-                exchange(far_part[1], 3),
-            ]
-        )
+        done.append(parts[0])
+        received.append([parts[0]] + [exchange(parts[d], d) for d in range(1, 4)])
     returned = trade(outgoing)
     ow_across = after(ow_across, done[-1])
     ow_far = exchange(ow_across, 1)

time: 177 us -> 160 us (0.904)
  Pallas kernels: 67.6 us -> 54.4 us
  local copies, waits for them, and re-layouts: 11.3 us -> 8.09 us
  other arithmetic: 4.99 us -> 3.1 us
  matrix products: 5.2 us -> 6.98 us
    pallas_call x6 -> x2, Pallas kernels: 46.1 us -> 32.9 us  [layer_call(): pl.pallas_call(lambda *refs: layer_kernel(heads, span, pairs, half, *refs...]
    ppermute x14, waiting for transfers between devices: 35.1 us -> 37.5 us  [exchange(): return lax.ppermute(value, 'mp', pairs)]
    unnamed x33, local copies, waits for them, and re-layouts: 5.41 us -> 2.96 us
    ppermute x14, starting transfers between devices: 10.2 us -> 8.31 us  [exchange(): return lax.ppermute(value, 'mp', pairs)]
    dot_general x1, matrix products: 2.62 us -> 4.4 us  [body(): zw = jnp.dot(z_weight, turn, preferred_element_type=F32).astype(BF)]
  transfers between devices with their start and end apart: 17 -> 17, of which waited for: 6 -> 6; matrix products, arithmetic and copies ran while one was open for 9% -> 7% of each run, Pallas kernels for 35% -> 27%
where the time goes in v8:
time: 160 us
  Pallas kernels  54.4 us (34%)
  waiting for transfers between devices  53.5 us (33%)
  starting transfers between devices  19.5 us (12%)
  between operations  14.3 us (9%)
  local copies, waits for them, and re-layouts  8.09 us (5%)
  matrix products  6.98 us (4%)
  other arithmetic  3.1 us (2%)
    ppermute x14, waiting for transfers between devices, exchange(): return lax.ppermute(value, 'mp', pairs)  37.5 us
    pallas_call x2, Pallas kernels, layer_call(): pl.pallas_call(lambda *refs: layer_kernel(heads, span, pairs, half, *refs...  32.9 us
    all_to_all x2, waiting for transfers between devices, trade(): lax.all_to_all(value.reshape((shard_count, capacity) + row_shape), 'dp',...  15.9 us
    pallas_call x2, Pallas kernels, out_call(): pl.pallas_call(kernel, grid=(columns // block,), out_shape=jax.ShapeDtype...  13.4 us
    all_to_all x2, starting transfers between devices, trade(): lax.all_to_all(value.reshape((shard_count, capacity) + row_shape), 'dp',...  11.1 us
    ppermute x14, starting transfers between devices, exchange(): return lax.ppermute(value, 'mp', pairs)  8.31 us
    dot_general x1, matrix products, body(): zw = jnp.dot(z_weight, turn, preferred_element_type=F32).astype(BF)  4.4 us
    pallas_call x1, Pallas kernels, gather_states(): pl.pallas_call(kernel, grid=(lines // 64,), out_shape=jax.ShapeDtypeStruc...  4.08 us
  transfers between devices with their start and end apart: 17, of which 6 were waited for; matrix products, arithmetic and copies ran while one was open for 7% of the time, Pallas kernels for 27%

profile of v8, /device:TPU:0, one launch (start us, length us, event | category | flops | bytes accessed | tf_op | source)
XLA Modules:
  0.0 159.7 jit_solution(14525591735069612936)
XLA Ops:
  7.2 0.0 copy-start
  7.2 1.1 constant_dynamic-slice_fusion
  8.3 2.3 %slice_bitcast_fusion.1 = bf16[2,2,256,512]{3,2,1,0:T(8,128)(2,1)} fusion(bf16[2,2,2,256,512]{4,3,2,1,0:T(8,128)(2,1)} %bitcast.24), kind=kLoop, calls=%fused_computation.5 | loop fusion | bytes 2097152 | tf_op jit(solution)/shard_map/squeeze | solution.py:437
  10.6 0.2 select_reduce_fusion.1
  10.8 0.2 convert_reduce_fusion
  11.0 0.6 select_reduce_fusion.source
  11.6 4.0 %pack_states.1 = bf16[16,256,128]{2,1,0:T(8,128)(2,1)} custom-call(s32[16]{0:T(128)} %select_reduce_fusion.source, bf16[16,32768]{1,0:T(8,128)(2,1)} %store.1, bf16[256,256]{1,0:T(8,128)(2,1)} %constant.61.clone.swap), custom_call_target="tpu_custom_call" | custom-call | flops 1 | bytes 1 | tf_op jit(solution)/shard_map/pack_states/pallas_call | solution.py:39
  15.7 6.3 %all-to-all-start = ((bf16[4,4,256,128]{3,2,1,0:T(8,128)(2,1)}), bf16[4,4,256,128]{3,2,1,0:T(8,128)(2,1)}, u32[]{:S(2)}, u32[]{:S(2)}) async-start(bf16[4,4,256,128]{3,2,1,0:T(8,128)(2,1)} %bitcast.23), calls=%async_computation | async-start | bytes 2097152 | tf_op jit(solution)/shard_map/all_to_all | solution.py:405
  22.0 1.5 collective-permute-start.1
  23.5 0.0 collective-permute-start
  23.5 0.5 collective-permute-start.3
  24.0 0.5 collective-permute-start.9
  24.5 0.3 copy.44
  24.8 0.0 copy-start.14
  24.8 0.1 pad.4.clone
  24.9 1.2 maximum_maximum_fusion.refs_5_
  26.2 2.6 %fusion.refs_6_ = bf16[2048,512]{1,0:T(8,128)(2,1)} fusion(bf16[2048,512]{1,0:T(8,128)(2,1)S(1)} %copy-done, bf16[512,512]{1,0:T(8,128)(2,1)S(1)} %copy-done.14), kind=kOutput, calls=%fused_computation.2 | convolution fusion | flops 1074790400 | bytes 4718592 | tf_op jit(solution)/shard_map/dot_general | solution.py:455
  28.7 23.8 %collective-permute-done.9 = bf16[64,2048]{1,0:T(8,128)(2,1)} collective-permute-done((bf16[64,2048]{1,0:T(8,128)(2,1)S(1)}, bf16[64,2048]{1,0:T(8,128)(2,1)}, u32[]{:S(2)}, u32[]{:S(2)}) %collective-permute-start.9) | collective-permute-done | bytes 262176 | tf_op jit(solution)/shard_map/ppermute | solution.py:402
  52.5 0.0 all-to-all-done
  52.5 0.0 all-gather.2.cloned.1.call-update
  52.6 0.0 copy-start.2
  52.6 4.4 %fusion.1.refs_7_ = bf16[2048,512]{1,0:T(8,128)(2,1)} fusion(bf16[2048,512]{1,0:T(8,128)(2,1)} %param.16, bf16[512,512]{1,0:T(8,128)(2,1)S(1)} %copy-done.15), kind=kOutput, calls=%fused_computation.3 | convolution fusion | flops 1074790400 | bytes 4718592 | tf_op jit(solution)/shard_map/dot_general | solution.py:456
  57.0 0.0 collective-permute-done.1.refs_3_
  57.0 0.1 collective-permute-start.2
  57.1 0.1 slice_bitcast_fusion
  57.2 1.6 collective-permute-start.4
  58.7 0.1 and_select_fusion.2
  58.9 0.1 reshape.83
  59.0 0.1 copy.45
  59.1 0.7 reshape.84.refs_9_
  59.8 0.7 copy.46.refs_8_
  60.5 0.2 convert_reduce_fusion.1
  60.7 0.6 pad_add_fusion.refs_0_
  61.2 0.0 collective-permute-done.2.refs_4_
  61.2 0.0 collective-permute-done
  61.2 16.5 %layer.2 = (bf16[256,512]{1,0:T(8,128)(2,1)}, bf16[256,512]{1,0:T(8,128)(2,1)}, bf16[256,512]{1,0:T(8,128)(2,1)}, bf16[256,512]{1,0:T(8,128)(2,1)}, bf16[16,256,128]{2,1,0:T(8,128)(2,1)}) custom-call(s32[33]{0:T(128)} %pad_add_fusion.refs_0_, bf16[2,2,2,256,512]{4,3,2,1,0:T(8,128)(2,1)} %bitcast.25, bf16[2,2,2,256,512]{4,3,2,1,0:T(8,128)(2,1)} %bitcast.2.refs_2_, ...), custom_call_target="tpu_custom_call" | custom-call | flops 6000000000 | bytes 1 | tf_op jit(solution)/shard_map/layer/pallas_call | solution.py:300
  77.8 5.1 %collective-permute-done.4.refs_3_ = bf16[2,2,256,512]{3,2,1,0:T(8,128)(2,1)} collective-permute-done((bf16[2,2,256,512]{3,2,1,0:T(8,128)(2,1)S(1)}, bf16[2,2,256,512]{3,2,1,0:T(8,128)(2,1)}, u32[]{:S(2)}, u32[]{:S(2)}) %collective-permute-start.4) | collective-permute-done | bytes 1048608 | tf_op jit(solution)/shard_map/ppermute | solution.py:402
  82.9 0.0 collective-permute-start.5
  82.9 0.0 collective-permute-done.3.refs_5_
  82.9 2.9 %collective-permute-done.5.refs_4_ = bf16[2,2,256,512]{3,2,1,0:T(8,128)(2,1)S(1)} collective-permute-done((bf16[2,2,256,512]{3,2,1,0:T(8,128)(2,1)}, bf16[2,2,256,512]{3,2,1,0:T(8,128)(2,1)S(1)}, u32[]{:S(2)}, u32[]{:S(2)}) %collective-permute-start.5) | collective-permute-done | bytes 1048608 | tf_op jit(solution)/shard_map/ppermute | solution.py:402
  85.8 1.0 copy-done.13
  86.7 16.4 %layer.3 = (bf16[256,512]{1,0:T(8,128)(2,1)}, bf16[256,512]{1,0:T(8,128)(2,1)}, bf16[256,512]{1,0:T(8,128)(2,1)}, bf16[256,512]{1,0:T(8,128)(2,1)}, bf16[16,256,128]{2,1,0:T(8,128)(2,1)}) custom-call(s32[33]{0:T(128)} %pad_add_fusion.refs_0_, bf16[2,2,2,256,512]{4,3,2,1,0:T(8,128)(2,1)} %bitcast.26, ...), custom_call_target="tpu_custom_call", output_to_operand_aliasing={{4}: (15, {})} | custom-call | flops 6000000000 | bytes 1 | tf_op jit(solution)/shard_map/layer/pallas_call | solution.py:300
  103.1 0.1 all-gather.2.cloned.1.call-done.refs_6_
  103.2 0.1 collective-permute-start.10
  103.3 4.8 %all-to-all-start.1 = ((bf16[4,4,256,128]{3,2,1,0:T(8,128)(2,1)}), bf16[4,4,256,128]{3,2,1,0:T(8,128)(2,1)S(1)}, u32[]{:S(2)}, u32[]{:S(2)}) async-start(bf16[4,4,256,128]{3,2,1,0:T(8,128)(2,1)} %bitcast.28), calls=%async_computation.1 | async-start | bytes 2097152 | tf_op jit(solution)/shard_map/all_to_all | solution.py:405
  108.2 0.1 collective-permute-start.11
  108.2 1.5 collective-permute-start.12
  109.7 0.3 collective-permute-start.13
  110.0 0.4 collective-permute-start.6
  110.4 0.0 collective-permute-done.11.refs_1_
  110.4 1.5 collective-permute-start.7
  111.9 5.7 %collective-permute-done.12.refs_2_ = bf16[256,512]{1,0:T(8,128)(2,1)S(1)} collective-permute-done((bf16[256,512]{1,0:T(8,128)(2,1)}, bf16[256,512]{1,0:T(8,128)(2,1)S(1)}, u32[]{:S(2)}, u32[]{:S(2)}) %collective-permute-start.12) | collective-permute-done | bytes 262176 | tf_op jit(solution)/shard_map/ppermute | solution.py:402
  117.6 0.7 copy-done.5
  118.3 0.3 collective-permute-start.8
  118.6 15.9 %all-to-all-done.1 = bf16[4,4,256,128]{3,2,1,0:T(8,128)(2,1)S(1)} async-done(((bf16[4,4,256,128]{3,2,1,0:T(8,128)(2,1)}), bf16[4,4,256,128]{3,2,1,0:T(8,128)(2,1)S(1)}, u32[]{:S(2)}, u32[]{:S(2)}) %all-to-all-start.1) | async-done | bytes 1048608 | tf_op jit(solution)/shard_map/all_to_all | solution.py:405
  134.4 1.0 copy-done.1
  135.4 4.1 %gather_states.1 = bf16[16,32768]{1,0:T(8,128)(2,1)} custom-call(s32[16]{0:T(128)} %copy-done.8, bf16[16,256,128]{2,1,0:T(8,128)(2,1)} %bitcast.22, bf16[256,256]{1,0:T(8,128)(2,1)} %constant.61.clone.swap), custom_call_target="tpu_custom_call" | custom-call | flops 1 | bytes 1 | tf_op jit(solution)/shard_map/gather_states/pallas_call | solution.py:75
  139.5 0.0 collective-permute-done.13.refs_3_
  139.5 0.0 collective-permute-done.10.refs_7_
  139.5 6.7 %project_out.2.refs_8_ = bf16[512,2048]{1,0:T(8,128)(2,1)} custom-call(bf16[256,512]{1,0:T(8,128)(2,1)} %get-tuple-element.35.refs_0_, bf16[256,512]{1,0:T(8,128)(2,1)} %copy-done.4, bf16[256,512]{1,0:T(8,128)(2,1)} %copy-done.5, bf16[256,512]{1,0:T(8,128)(2,1)} %collective-permute-done.13.refs_3_, bf16[512,2048]{1,0:T(8,128)(2,1)} %refs_4_.3, ...), custom_call_target="tpu_custom_call" | custom-call | flops 2000000000 | bytes 1 | tf_op jit(solution)/shard_map/project_out/pallas_call | solution.py:350
  146.2 0.0 collective-permute-done.6.refs_1_
  146.2 0.0 collective-permute-done.7.refs_2_
  146.2 0.0 collective-permute-done.8.refs_3_
  146.2 6.7 %project_out.3 = bf16[512,2048]{1,0:T(8,128)(2,1)} custom-call(bf16[256,512]{1,0:T(8,128)(2,1)} %get-tuple-element.29.refs_0_, bf16[256,512]{1,0:T(8,128)(2,1)} %collective-permute-done.6.refs_1_, bf16[256,512]{1,0:T(8,128)(2,1)} %collective-permute-done.7.refs_2_, bf16[256,512]{1,0:T(8,128)(2,1)} %collective-permute-done.8.refs_3_, ...), custom_call_target="tpu_custom_call", output_to_operand_aliasing={{}: (8, {})} | custom-call | flops 2000000000 | bytes 1 | tf_op jit(solution)/shard_map/project_out/pallas_call | solution.py:350
  (34 shorter events, 0.1 us)
Async XLA Ops:
  7.2 19.0 %copy-start = (bf16[2048,512]{1,0:T(8,128)(2,1)S(1)}, bf16[2048,512]{1,0:T(8,128)(2,1)}, u32[]{:S(2)}) copy-start(bf16[2048,512]{1,0:T(8,128)(2,1)} %param.15) | copy-start | bytes 6291460
  7.2 3.4 %copy-start.9 = (s32[64]{0:T(128)S(1)}, s32[64]{0:T(128)}, u32[]{:S(2)}) copy-start(s32[64]{0:T(128)} %param.24) | copy-start | bytes 772
  11.0 4.7 %copy-start.8 = (s32[16]{0:T(128)}, s32[16]{0:T(128)S(1)}, u32[]{:S(2)}) copy-start(s32[16]{0:T(128)S(1)} %multiply_add_fusion.index) | copy-start | bytes 196
  11.6 12.9 %copy-start.6 = (bf16[2048,8]{0,1:T(8,128)(2,1)S(1)}, bf16[2048,8]{0,1:T(8,128)(2,1)}, u32[]{:S(2)}) copy-start(bf16[2048,8]{0,1:T(8,128)(2,1)} %param.18) | copy-start | bytes 98308
  11.6 13.3 %copy-start.3 = (bf16[2048,128]{1,0:T(8,128)(2,1)S(1)}, bf16[2048,128]{1,0:T(8,128)(2,1)}, u32[]{:S(2)}) copy-start(bf16[2048,128]{1,0:T(8,128)(2,1)} %param.17) | copy-start | bytes 1572868
  15.7 36.9 %all-to-all-start = ((bf16[4,4,256,128]{3,2,1,0:T(8,128)(2,1)}), bf16[4,4,256,128]{3,2,1,0:T(8,128)(2,1)}, u32[]{:S(2)}, u32[]{:S(2)}) async-start(bf16[4,4,256,128]{3,2,1,0:T(8,128)(2,1)} %bitcast.23), calls=%async_computation | async-start | bytes 2097152 | tf_op jit(solution)/shard_map/all_to_all | solution.py:405
  22.0 81.2 %all-gather.2.cloned.1.call-start = ((), (), s32[]{:S(2)}) async-start(), calls=%async_computation.2 | async-start | bytes 2359296 | tf_op jit(solution)/shard_map/all_gather | solution.py:465
  22.0 35.0 %collective-permute-start.1 = (bf16[2,2,256,512]{3,2,1,0:T(8,128)(2,1)}, bf16[2,2,256,512]{3,2,1,0:T(8,128)(2,1)}, u32[]{:S(2)}, u32[]{:S(2)}) collective-permute-start(bf16[2,2,256,512]{3,2,1,0:T(8,128)(2,1)} %slice_bitcast_fusion.1), channel_id=1, source_target_pairs={{0,2},{1,3},{2,0},{3,1},{4,6},{5,7},{6,4},{7,5},{8,10},{9,11},{10,... | collective-permute-start | bytes 3145736 | tf_op jit(solution)/shard_map/ppermute | solution.py:402
  23.5 37.8 %collective-permute-start = (bf16[2048,512]{1,0:T(8,128)(2,1)}, bf16[2048,512]{1,0:T(8,128)(2,1)}, u32[]{:S(2)}, u32[]{:S(2)}) collective-permute-start(bf16[2048,512]{1,0:T(8,128)(2,1)} %param.14), channel_id=1, source_target_pairs={{0,1},{1,0},{2,3},{3,2},{4,5},{5,4},{6,7},{7,6},{8,9},{9,8},{10,11... | collective-permute-start | bytes 6291464 | tf_op jit(solution)/shard_map/ppermute | solution.py:402
  23.5 59.4 %collective-permute-start.3 = (bf16[512,2048]{1,0:T(8,128)(2,1)}, bf16[512,2048]{1,0:T(8,128)(2,1)}, u32[]{:S(2)}, u32[]{:S(2)}) collective-permute-start(bf16[512,2048]{1,0:T(8,128)(2,1)} %refs_4_.3), channel_id=1, source_target_pairs={{0,1},{1,0},{2,3},{3,2},{4,5},{5,4},{6,7},{7,6},{8,9},{9,8},{10,11... | collective-permute-start | bytes 6291464 | tf_op jit(solution)/shard_map/ppermute | solution.py:402
  24.0 28.5 %collective-permute-start.9 = (bf16[64,2048]{1,0:T(8,128)(2,1)S(1)}, bf16[64,2048]{1,0:T(8,128)(2,1)}, u32[]{:S(2)}, u32[]{:S(2)}) collective-permute-start(bf16[64,2048]{1,0:T(8,128)(2,1)S(1)} %constant_dynamic-slice_fusion), channel_id=1, source_target_pairs={{0,2},{1,3},{2,0},{3,1},{4,6},{5,7},{6,4},{7,5},{8,10},{9,11},{10,... | collective-permute-start | bytes 786440 | tf_op jit(solution)/shard_map/ppermute | solution.py:402
  24.8 1.3 copy-start.14
  26.2 26.4 %copy-start.15 = (bf16[512,512]{1,0:T(8,128)(2,1)S(1)}, bf16[512,512]{1,0:T(8,128)(2,1)}, u32[]{:S(2)}) copy-start(bf16[512,512]{1,0:T(8,128)(2,1)} %constant.62.clone) | copy-start | bytes 1572868
  52.6 4.5 %copy-start.2 = (bf16[2048,512]{1,0:T(8,128)(2,1)S(1)}, bf16[2048,512]{1,0:T(8,128)(2,1)}, u32[]{:S(2)}) copy-start(bf16[2048,512]{1,0:T(8,128)(2,1)} %param.14) | copy-start | bytes 6291460
  57.0 1.8 %copy-start.10 = (f32[8]{0:T(128)S(1)}, f32[8]{0:T(128)}, u32[]{:S(2)}) copy-start(f32[8]{0:T(128)} %param.20) | copy-start | bytes 100
  57.0 1.8 %copy-start.11 = (f32[8]{0:T(128)S(1)}, f32[8]{0:T(128)}, u32[]{:S(2)}) copy-start(f32[8]{0:T(128)} %param.19) | copy-start | bytes 100
  57.0 1.9 %copy-start.7 = (f32[512]{0:T(512)S(1)}, f32[512]{0:T(512)}, u32[]{:S(2)}) copy-start(f32[512]{0:T(512)} %param.21) | copy-start | bytes 6148
  57.0 3.7 %copy-start.12 = (s32[16]{0:T(128)S(1)}, s32[16]{0:T(128)}, u32[]{:S(2)}) copy-start(s32[16]{0:T(128)} %param.25) | copy-start | bytes 196
  57.0 4.2 %collective-permute-start.2 = (bf16[2,2,256,512]{3,2,1,0:T(8,128)(2,1)}, bf16[2,2,256,512]{3,2,1,0:T(8,128)(2,1)}, u32[]{:S(2)}, u32[]{:S(2)}) collective-permute-start(bf16[2,2,256,512]{3,2,1,0:T(8,128)(2,1)} %collective-permute-done.1.refs_3_), channel_id=1, source_target_pairs={{0,1},{1,0},{2,3},{3,2},{4,5},{5,4},{6,7},{7,6},{8,9},{9,8},{10,11... | collective-permute-start | bytes 3145736 | tf_op jit(solution)/shard_map/ppermute | solution.py:402
  57.2 25.7 %collective-permute-start.4 = (bf16[2,2,256,512]{3,2,1,0:T(8,128)(2,1)S(1)}, bf16[2,2,256,512]{3,2,1,0:T(8,128)(2,1)}, u32[]{:S(2)}, u32[]{:S(2)}) collective-permute-start(bf16[2,2,256,512]{3,2,1,0:T(8,128)(2,1)S(1)} %slice_bitcast_fusion), channel_id=1, source_target_pairs={{0,2},{1,3},{2,0},{3,1},{4,6},{5,7},{6,4},{7,5},{8,10},{9,11},{10,... | collective-permute-start | bytes 3145736 | tf_op jit(solution)/shard_map/ppermute | solution.py:402
  82.9 2.9 %collective-permute-start.5 = (bf16[2,2,256,512]{3,2,1,0:T(8,128)(2,1)}, bf16[2,2,256,512]{3,2,1,0:T(8,128)(2,1)S(1)}, u32[]{:S(2)}, u32[]{:S(2)}) collective-permute-start(bf16[2,2,256,512]{3,2,1,0:T(8,128)(2,1)} %collective-permute-done.4.refs_3_), channel_id=1, source_target_pairs={{0,1},{1,0},{2,3},{3,2},{4,5},{5,4},{6,7},{7,6},{8,9},{9,8},{10,11... | collective-permute-start | bytes 3145736 | tf_op jit(solution)/shard_map/ppermute | solution.py:402
  85.8 1.0 copy-start.13
  103.2 36.3 %collective-permute-start.10 = (bf16[512,2048]{1,0:T(8,128)(2,1)}, bf16[512,2048]{1,0:T(8,128)(2,1)}, u32[]{:S(2)}, u32[]{:S(2)}) collective-permute-start(bf16[512,2048]{1,0:T(8,128)(2,1)} %all-gather.2.cloned.1.call-done.refs_6_), channel_id=1, source_target_pairs={{0,1},{1,0},{2,3},{3,2},{4,5},{5,4},{6,7},{7,6},{8,9},{9,8},{10,11... | collective-permute-start | bytes 6291464 | tf_op jit(solution)/shard_map/ppermute | solution.py:402
  103.3 31.1 %all-to-all-start.1 = ((bf16[4,4,256,128]{3,2,1,0:T(8,128)(2,1)}), bf16[4,4,256,128]{3,2,1,0:T(8,128)(2,1)S(1)}, u32[]{:S(2)}, u32[]{:S(2)}) async-start(bf16[4,4,256,128]{3,2,1,0:T(8,128)(2,1)} %bitcast.28), calls=%async_computation.1 | async-start | bytes 2097152 | tf_op jit(solution)/shard_map/all_to_all | solution.py:405
  108.2 2.2 %collective-permute-start.11 = (bf16[256,512]{1,0:T(8,128)(2,1)}, bf16[256,512]{1,0:T(8,128)(2,1)S(1)}, u32[]{:S(2)}, u32[]{:S(2)}) collective-permute-start(bf16[256,512]{1,0:T(8,128)(2,1)} %get-tuple-element.36), channel_id=1, source_target_pairs={{0,1},{1,0},{2,3},{3,2},{4,5},{5,4},{6,7},{7,6},{8,9},{9,8},{10,11... | collective-permute-start | bytes 786440 | tf_op jit(solution)/shard_map/ppermute | solution.py:402
  108.2 9.3 %collective-permute-start.12 = (bf16[256,512]{1,0:T(8,128)(2,1)}, bf16[256,512]{1,0:T(8,128)(2,1)S(1)}, u32[]{:S(2)}, u32[]{:S(2)}) collective-permute-start(bf16[256,512]{1,0:T(8,128)(2,1)} %get-tuple-element.37), channel_id=1, source_target_pairs={{0,2},{1,3},{2,0},{3,1},{4,6},{5,7},{6,4},{7,5},{8,10},{9,11},{10,... | collective-permute-start | bytes 786440 | tf_op jit(solution)/shard_map/ppermute | solution.py:402
  109.7 29.7 %collective-permute-start.13 = (bf16[256,512]{1,0:T(8,128)(2,1)}, bf16[256,512]{1,0:T(8,128)(2,1)}, u32[]{:S(2)}, u32[]{:S(2)}) collective-permute-start(bf16[256,512]{1,0:T(8,128)(2,1)} %get-tuple-element.38), channel_id=1, source_target_pairs={{0,3},{1,2},{2,1},{3,0},{4,7},{5,6},{6,5},{7,4},{8,11},{9,10},{10,... | collective-permute-start | bytes 786440 | tf_op jit(solution)/shard_map/ppermute | solution.py:402
  110.0 36.1 %collective-permute-start.6 = (bf16[256,512]{1,0:T(8,128)(2,1)}, bf16[256,512]{1,0:T(8,128)(2,1)}, u32[]{:S(2)}, u32[]{:S(2)}) collective-permute-start(bf16[256,512]{1,0:T(8,128)(2,1)} %get-tuple-element.30), channel_id=1, source_target_pairs={{0,1},{1,0},{2,3},{3,2},{4,5},{5,4},{6,7},{7,6},{8,9},{9,8},{10,11... | collective-permute-start | bytes 786440 | tf_op jit(solution)/shard_map/ppermute | solution.py:402
  110.4 29.1 %copy-start.4 = (bf16[256,512]{1,0:T(8,128)(2,1)}, bf16[256,512]{1,0:T(8,128)(2,1)S(1)}, u32[]{:S(2)}) copy-start(bf16[256,512]{1,0:T(8,128)(2,1)S(1)} %collective-permute-done.11.refs_1_) | copy-start | bytes 786436
  110.4 35.8 %collective-permute-start.7 = (bf16[256,512]{1,0:T(8,128)(2,1)}, bf16[256,512]{1,0:T(8,128)(2,1)}, u32[]{:S(2)}, u32[]{:S(2)}) collective-permute-start(bf16[256,512]{1,0:T(8,128)(2,1)} %get-tuple-element.31), channel_id=1, source_target_pairs={{0,2},{1,3},{2,0},{3,1},{4,6},{5,7},{6,4},{7,5},{8,10},{9,11},{10,... | collective-permute-start | bytes 786440 | tf_op jit(solution)/shard_map/ppermute | solution.py:402
  117.6 0.7 copy-start.5
  118.3 27.9 %collective-permute-start.8 = (bf16[256,512]{1,0:T(8,128)(2,1)}, bf16[256,512]{1,0:T(8,128)(2,1)}, u32[]{:S(2)}, u32[]{:S(2)}) collective-permute-start(bf16[256,512]{1,0:T(8,128)(2,1)} %get-tuple-element.32), channel_id=1, source_target_pairs={{0,3},{1,2},{2,1},{3,0},{4,7},{5,6},{6,5},{7,4},{8,11},{9,10},{10,... | collective-permute-start | bytes 786440 | tf_op jit(solution)/shard_map/ppermute | solution.py:402
  134.4 1.0 copy-start.1
Sparse Core Ops, SparseCore 0:
  52.7 50.4 all-gather.1

commit v9 on v8

--- a/solution.py
+++ b/solution.py
@@ -321,7 +321,7 @@
         input_output_aliases=aliases,
         compiler_params=pltpu.CompilerParams(vmem_limit_bytes=VMEM_LIMIT),
         cost_estimate=pl.CostEstimate(
-            flops=6 * 10**9, bytes_accessed=1, transcendentals=0
+            flops=1, bytes_accessed=1, transcendentals=0
         ),
         name="layer",
     )(*operands)
@@ -358,7 +358,7 @@
         input_output_aliases=aliases,
         compiler_params=pltpu.CompilerParams(vmem_limit_bytes=VMEM_LIMIT),
         cost_estimate=pl.CostEstimate(
-            flops=2 * 10**9, bytes_accessed=1, transcendentals=0
+            flops=1, bytes_accessed=1, transcendentals=0
         ),
         name="project_out",
     )(*operands)
@@ -452,6 +452,9 @@
         + new_column // 128 % 2
     )
     turn = jnp.asarray(old_column[None, :] == np.arange(width)[:, None], BF)
+    x_weight, z_weight, bc_weight, across[0], ow_part = lax.optimization_barrier(
+        (x_weight, z_weight, bc_weight, across[0], ow_part)
+    )
     xw = jnp.dot(x_weight, turn, preferred_element_type=F32).astype(BF)
     zw = jnp.dot(z_weight, turn, preferred_element_type=F32).astype(BF)
     order = turn[:256, :256]
@@ -474,8 +477,6 @@
         if h:
             start = after(meta, done[-1], ow_sibling)
             arrived = after(arrived, done[-1])
-        else:
-            arrived = after(arrived, xw, zw, bw)
         pieces = (blocks, sibling, arrived, exchange(arrived, 1))
         *parts, outgoing = layer_call(
             h, start, pieces, (bw, xw, zw), (small, gain, order), inbound, span, outgoing
@@ -485,7 +486,6 @@
     returned = trade(outgoing)
     ow_across = after(ow_across, done[-1])
     ow_far = exchange(ow_across, 1)
-    new_store = gather_states(row_slot, returned, swap)
     ow = (out_weight, ow_sibling, ow_across, ow_far)
     out_tokens = None
     for h in range(halves):
@@ -493,6 +493,8 @@
         if h == 0:
             normed[0] = after(normed[0], done[-1])
         out_tokens = out_call(h, halves, normed, ow, out_tokens)
+    returned, out_tokens = lax.optimization_barrier((returned, out_tokens))
+    new_store = gather_states(row_slot, returned, swap)
     return (out_tokens, new_store)
 
 

time: 160 us -> 157 us (0.981)
  waiting for transfers between devices: 53.5 us -> 46.5 us
  local copies, waits for them, and re-layouts: 8.09 us -> 12.7 us
    all_to_all x2, waiting for transfers between devices: 15.9 us -> 0.01 us  [trade(): lax.all_to_all(value.reshape((shard_count, capacity) + row_shape), 'dp',...]
    ppermute x14, waiting for transfers between devices: 37.5 us -> 46.4 us  [exchange(): return lax.ppermute(value, 'mp', pairs)]
    unnamed x33 -> x47, local copies, waits for them, and re-layouts: 2.96 us -> 5.37 us
    squeeze x1, local copies, waits for them, and re-layouts: 0.07 us -> 2.26 us  [body(): second = after(blocks, packed)[:, :, 1]]
  transfers between devices with their start and end apart: 17 -> 17, of which waited for: 6 -> 5; matrix products, arithmetic and copies ran while one was open for 7% -> 9% of each run, Pallas kernels for 27% -> 30%
where the time goes in v9:
time: 157 us; the launch traced here: 156 us
  Pallas kernels  54.3 us (35%)
  waiting for transfers between devices  46.5 us (30%)
  starting transfers between devices  19 us (12%)
  between operations  14.3 us (9%)
  local copies, waits for them, and re-layouts  12.7 us (8%)
  matrix products  6.43 us (4%)
  other arithmetic  3.13 us (2%)
    ppermute x14, waiting for transfers between devices, exchange(): return lax.ppermute(value, 'mp', pairs)  46.4 us
    pallas_call x2, Pallas kernels, layer_call(): pl.pallas_call(lambda *refs: layer_kernel(heads, span, pairs, half, *refs...  32.9 us
    pallas_call x2, Pallas kernels, out_call(): pl.pallas_call(kernel, grid=(columns // block,), out_shape=jax.ShapeDtype...  13.3 us
    all_to_all x2, starting transfers between devices, trade(): lax.all_to_all(value.reshape((shard_count, capacity) + row_shape), 'dp',...  11.2 us
    ppermute x14, starting transfers between devices, exchange(): return lax.ppermute(value, 'mp', pairs)  7.76 us
    unnamed x47, local copies, waits for them, and re-layouts  5.37 us
    pallas_call x1, Pallas kernels, gather_states(): pl.pallas_call(kernel, grid=(lines // 64,), out_shape=jax.ShapeDtypeStruc...  4.08 us
    pallas_call x1, Pallas kernels, pack_states(): pl.pallas_call(kernel, grid=(lines // 64,), out_shape=jax.ShapeDtypeStruc...  3.98 us
  transfers between devices with their start and end apart: 17, of which 5 were waited for; matrix products, arithmetic and copies ran while one was open for 9% of the time, Pallas kernels for 30%

profile of v9, /device:TPU:0, one launch (start us, length us, event | category | flops | bytes accessed | tf_op | source)
XLA Modules:
  0.0 156.3 jit_solution(2151408309528323812)
XLA Ops:
  7.2 0.0 copy-start
  7.2 1.1 constant_dynamic-slice_fusion
  8.3 2.3 %slice_bitcast_fusion.1 = bf16[2,2,256,512]{3,2,1,0:T(8,128)(2,1)} fusion(bf16[2,2,2,256,512]{4,3,2,1,0:T(8,128)(2,1)} %bitcast.26), kind=kLoop, calls=%fused_computation.3 | loop fusion | bytes 2097152 | tf_op jit(solution)/shard_map/squeeze | solution.py:437
  10.6 0.2 select_reduce_fusion.1
  10.8 0.2 convert_reduce_fusion
  11.0 0.6 select_reduce_fusion.source
  11.6 4.0 %pack_states.1 = bf16[16,256,128]{2,1,0:T(8,128)(2,1)} custom-call(s32[16]{0:T(128)} %select_reduce_fusion.source, bf16[16,32768]{1,0:T(8,128)(2,1)} %store.1, bf16[256,256]{1,0:T(8,128)(2,1)} %constant.61.clone.swap), custom_call_target="tpu_custom_call" | custom-call | flops 1 | bytes 1 | tf_op jit(solution)/shard_map/pack_states/pallas_call | solution.py:39
  15.6 6.5 %all-to-all-start = ((bf16[4,4,256,128]{3,2,1,0:T(8,128)(2,1)}), bf16[4,4,256,128]{3,2,1,0:T(8,128)(2,1)S(1)}, u32[]{:S(2)}, u32[]{:S(2)}) async-start(bf16[4,4,256,128]{3,2,1,0:T(8,128)(2,1)} %bitcast.32), calls=%async_computation | async-start | bytes 2097152 | tf_op jit(solution)/shard_map/all_to_all | solution.py:405
  22.1 0.0 all-gather.2.cloned.1.call-start
  22.1 1.6 collective-permute-start.1
  23.7 0.5 collective-permute-start.2
  24.2 28.5 %collective-permute-done.2 = bf16[64,2048]{1,0:T(8,128)(2,1)} collective-permute-done((bf16[64,2048]{1,0:T(8,128)(2,1)S(1)}, bf16[64,2048]{1,0:T(8,128)(2,1)}, u32[]{:S(2)}, u32[]{:S(2)}) %collective-permute-start.2) | collective-permute-done | bytes 262176 | tf_op jit(solution)/shard_map/ppermute | solution.py:402
  52.7 0.0 collective-permute-done.1.refs_3_
  52.8 0.0 all-to-all-done
  52.8 0.0 all-gather.2.cloned.1.call-update
  52.8 0.1 collective-permute-start
  52.9 0.5 collective-permute-start.4
  53.4 2.3 %slice_bitcast_fusion = bf16[2,2,256,512]{3,2,1,0:T(8,128)(2,1)} fusion(bf16[2,2,2,256,512]{4,3,2,1,0:T(8,128)(2,1)} %bitcast.27), kind=kLoop, calls=%fused_computation.2 | loop fusion | bytes 2097152 | tf_op jit(solution)/shard_map/squeeze | solution.py:439
  55.6 1.5 collective-permute-start.5
  57.1 1.0 copy.36
  58.1 0.1 reshape.83
  58.3 0.1 copy.37
  58.4 0.7 reshape.84.refs_9_
  59.1 0.7 copy.38.refs_8_
  59.8 0.1 pad.4.clone
  59.8 0.1 and_select_fusion.2
  59.9 0.2 convert_reduce_fusion.1
  60.1 0.6 pad_add_fusion.refs_0_
  60.8 0.0 collective-permute-start.3
  60.8 3.9 %convolution_convert_fusion.refs_7_ = bf16[2048,512]{1,0:T(8,128)(2,1)} fusion(bf16[2048,512]{1,0:T(8,128)(2,1)S(1)} %copy-done, bf16[512,512]{1,0:T(8,128)(2,1)} %constant.62.clone), kind=kOutput, calls=%fused_computation | convolution fusion | flops 1074790400 | bytes 4718592 | tf_op jit(solution)/shard_map/dot_general | solution.py:459
  64.6 0.0 copy-start.6
  64.6 2.6 %convolution_convert_fusion.1.refs_6_ = bf16[2048,512]{1,0:T(8,128)(2,1)} fusion(bf16[2048,512]{1,0:T(8,128)(2,1)S(1)} %copy-done.20, bf16[512,512]{1,0:T(8,128)(2,1)S(1)} %copy-done.22), kind=kOutput, calls=%fused_computation.1 | convolution fusion | flops 1074790400 | bytes 4718592 | tf_op jit(solution)/shard_map/dot_general | solution.py:458
  67.2 1.2 maximum_maximum_fusion.refs_5_
  68.4 0.0 collective-permute-done.3.refs_4_
  68.4 0.0 collective-permute-done
  68.4 1.0 copy-done.5
  69.4 16.5 %layer.2 = (bf16[256,512]{1,0:T(8,128)(2,1)}, bf16[256,512]{1,0:T(8,128)(2,1)}, bf16[256,512]{1,0:T(8,128)(2,1)}, bf16[256,512]{1,0:T(8,128)(2,1)}, bf16[16,256,128]{2,1,0:T(8,128)(2,1)}) custom-call(s32[33]{0:T(128)} %pad_add_fusion.refs_0_, bf16[2,2,2,256,512]{4,3,2,1,0:T(8,128)(2,1)} %bitcast.28, bf16[2,2,2,256,512]{4,3,2,1,0:T(8,128)(2,1)} %bitcast.2.refs_2_, ...), custom_call_target="tpu_custom_call" | custom-call | flops 1 | bytes 1 | tf_op jit(solution)/shard_map/layer/pallas_call | solution.py:300
  86.0 0.0 collective-permute-done.5.refs_3_
  86.0 0.6 collective-permute-start.6
  86.5 0.0 collective-permute-done.4.refs_5_
  86.6 2.5 %collective-permute-done.6.refs_4_ = bf16[2,2,256,512]{3,2,1,0:T(8,128)(2,1)S(1)} collective-permute-done((bf16[2,2,256,512]{3,2,1,0:T(8,128)(2,1)}, bf16[2,2,256,512]{3,2,1,0:T(8,128)(2,1)S(1)}, u32[]{:S(2)}, u32[]{:S(2)}) %collective-permute-start.6) | collective-permute-done | bytes 1048608 | tf_op jit(solution)/shard_map/ppermute | solution.py:402
  89.0 1.0 copy-done.4
  90.0 16.4 %layer.3 = (bf16[256,512]{1,0:T(8,128)(2,1)}, bf16[256,512]{1,0:T(8,128)(2,1)}, bf16[256,512]{1,0:T(8,128)(2,1)}, bf16[256,512]{1,0:T(8,128)(2,1)}, bf16[16,256,128]{2,1,0:T(8,128)(2,1)}) custom-call(s32[33]{0:T(128)} %pad_add_fusion.refs_0_, bf16[2,2,2,256,512]{4,3,2,1,0:T(8,128)(2,1)} %bitcast.29, ...), custom_call_target="tpu_custom_call", output_to_operand_aliasing={{4}: (15, {})} | custom-call | flops 1 | bytes 1 | tf_op jit(solution)/shard_map/layer/pallas_call | solution.py:300
  106.4 0.0 all-gather.2.cloned.1.call-done.refs_6_
  106.4 0.4 collective-permute-start.10
  106.9 4.8 %all-to-all-start.1 = ((bf16[4,4,256,128]{3,2,1,0:T(8,128)(2,1)}), bf16[4,4,256,128]{3,2,1,0:T(8,128)(2,1)S(1)}, u32[]{:S(2)}, u32[]{:S(2)}) async-start(bf16[4,4,256,128]{3,2,1,0:T(8,128)(2,1)} %bitcast.30), calls=%async_computation.1 | async-start | bytes 2097152 | tf_op jit(solution)/shard_map/all_to_all | solution.py:405
  111.7 0.0 collective-permute-start.11
  111.7 0.4 collective-permute-start.12
  112.1 1.4 collective-permute-start.13
  113.5 0.3 collective-permute-start.7
  113.8 0.0 collective-permute-done.11.refs_1_
  113.8 0.4 collective-permute-start.8
  114.2 6.7 %collective-permute-done.12.refs_2_ = bf16[256,512]{1,0:T(8,128)(2,1)S(1)} collective-permute-done((bf16[256,512]{1,0:T(8,128)(2,1)}, bf16[256,512]{1,0:T(8,128)(2,1)S(1)}, u32[]{:S(2)}, u32[]{:S(2)}) %collective-permute-start.12) | collective-permute-done | bytes 262176 | tf_op jit(solution)/shard_map/ppermute | solution.py:402
  121.0 0.0 collective-permute-start.9
  121.0 4.8 %collective-permute-done.13.refs_3_ = bf16[256,512]{1,0:T(8,128)(2,1)S(1)} collective-permute-done((bf16[256,512]{1,0:T(8,128)(2,1)S(1)}, bf16[256,512]{1,0:T(8,128)(2,1)S(1)}, u32[]{:S(2)}, u32[]{:S(2)}) %collective-permute-start.13) | collective-permute-done | bytes 262176 | tf_op jit(solution)/shard_map/ppermute | solution.py:402
  125.8 0.7 copy-done.9
  126.5 6.7 %project_out.2.refs_8_ = bf16[512,2048]{1,0:T(8,128)(2,1)} custom-call(bf16[256,512]{1,0:T(8,128)(2,1)} %get-tuple-element.46.refs_0_, bf16[256,512]{1,0:T(8,128)(2,1)} %copy-done.7, bf16[256,512]{1,0:T(8,128)(2,1)} %copy-done.8, bf16[256,512]{1,0:T(8,128)(2,1)} %copy-done.9, bf16[512,2048]{1,0:T(8,128)(2,1)} %refs_4_.3, ...), custom_call_target="tpu_custom_call" | custom-call | flops 1 | bytes 1 | tf_op jit(solution)/shard_map/project_out/pallas_call | solution.py:350
  133.2 0.0 copy-start.10
  133.2 0.0 collective-permute-done.8.refs_2_
  133.2 3.8 %collective-permute-done.9.refs_3_ = bf16[256,512]{1,0:T(8,128)(2,1)S(1)} collective-permute-done((bf16[256,512]{1,0:T(8,128)(2,1)}, bf16[256,512]{1,0:T(8,128)(2,1)S(1)}, u32[]{:S(2)}, u32[]{:S(2)}) %collective-permute-start.9) | collective-permute-done | bytes 262176 | tf_op jit(solution)/shard_map/ppermute | solution.py:402
  137.1 0.7 copy-done.12
  137.7 6.7 %project_out.3 = bf16[512,2048]{1,0:T(8,128)(2,1)} custom-call(bf16[256,512]{1,0:T(8,128)(2,1)} %get-tuple-element.39.refs_0_, bf16[256,512]{1,0:T(8,128)(2,1)} %copy-done.10, bf16[256,512]{1,0:T(8,128)(2,1)} %copy-done.11, bf16[256,512]{1,0:T(8,128)(2,1)} %copy-done.12, bf16[512,2048]{1,0:T(8,128)(2,1)} %refs_4_.3, ...), custom_call_target="tpu_custom_call", output_to_operand_aliasing={{}: (8, {})} | custom-call | flops 1 | bytes 1 | tf_op jit(solution)/shard_map/project_out/pallas_call | solution.py:350
  144.4 1.0 copy-done.2
  145.4 4.1 %gather_states.1 = bf16[16,32768]{1,0:T(8,128)(2,1)} custom-call(s32[16]{0:T(128)} %copy-done.15, bf16[16,256,128]{2,1,0:T(8,128)(2,1)} %bitcast.31, bf16[256,256]{1,0:T(8,128)(2,1)} %constant.61.clone.swap), custom_call_target="tpu_custom_call" | custom-call | flops 1 | bytes 1 | tf_op jit(solution)/shard_map/gather_states/pallas_call | solution.py:75
  (48 shorter events, 0.1 us)
Async XLA Ops:
  7.2 53.6 %copy-start = (bf16[2048,512]{1,0:T(8,128)(2,1)S(1)}, bf16[2048,512]{1,0:T(8,128)(2,1)}, u32[]{:S(2)}) copy-start(bf16[2048,512]{1,0:T(8,128)(2,1)} %param.16) | copy-start | bytes 6291460
  7.2 3.4 %copy-start.18 = (s32[64]{0:T(128)S(1)}, s32[64]{0:T(128)}, u32[]{:S(2)}) copy-start(s32[64]{0:T(128)} %param.24) | copy-start | bytes 772
  11.0 4.6 %copy-start.15 = (s32[16]{0:T(128)}, s32[16]{0:T(128)S(1)}, u32[]{:S(2)}) copy-start(s32[16]{0:T(128)S(1)} %multiply_add_fusion.index) | copy-start | bytes 196
  15.6 41.5 %copy-start.13 = (bf16[2048,8]{0,1:T(8,128)(2,1)S(1)}, bf16[2048,8]{0,1:T(8,128)(2,1)}, u32[]{:S(2)}) copy-start(bf16[2048,8]{0,1:T(8,128)(2,1)} %param.18) | copy-start | bytes 98308
  15.6 42.5 %copy-start.14 = (f32[512]{0:T(512)S(1)}, f32[512]{0:T(512)}, u32[]{:S(2)}) copy-start(f32[512]{0:T(512)} %param.21) | copy-start | bytes 6148
  15.6 37.1 %all-to-all-start = ((bf16[4,4,256,128]{3,2,1,0:T(8,128)(2,1)}), bf16[4,4,256,128]{3,2,1,0:T(8,128)(2,1)S(1)}, u32[]{:S(2)}, u32[]{:S(2)}) async-start(bf16[4,4,256,128]{3,2,1,0:T(8,128)(2,1)} %bitcast.32), calls=%async_computation | async-start | bytes 2097152 | tf_op jit(solution)/shard_map/all_to_all | solution.py:405
  22.1 37.0 %copy-start.16 = (f32[8]{0:T(128)S(1)}, f32[8]{0:T(128)}, u32[]{:S(2)}) copy-start(f32[8]{0:T(128)} %param.20) | copy-start | bytes 100
  22.1 37.0 %copy-start.17 = (f32[8]{0:T(128)S(1)}, f32[8]{0:T(128)}, u32[]{:S(2)}) copy-start(f32[8]{0:T(128)} %param.19) | copy-start | bytes 100
  22.1 38.0 %copy-start.19 = (s32[16]{0:T(128)S(1)}, s32[16]{0:T(128)}, u32[]{:S(2)}) copy-start(s32[16]{0:T(128)} %param.25) | copy-start | bytes 196
  22.1 84.3 %all-gather.2.cloned.1.call-start = ((), (), s32[]{:S(2)}) async-start(), calls=%async_computation.2 | async-start | bytes 2359296 | tf_op jit(solution)/shard_map/all_gather | solution.py:468
  22.1 30.6 %collective-permute-start.1 = (bf16[2,2,256,512]{3,2,1,0:T(8,128)(2,1)}, bf16[2,2,256,512]{3,2,1,0:T(8,128)(2,1)}, u32[]{:S(2)}, u32[]{:S(2)}) collective-permute-start(bf16[2,2,256,512]{3,2,1,0:T(8,128)(2,1)} %slice_bitcast_fusion.1), channel_id=1, source_target_pairs={{0,2},{1,3},{2,0},{3,1},{4,6},{5,7},{6,4},{7,5},{8,10},{9,11},{10,... | collective-permute-start | bytes 3145736 | tf_op jit(solution)/shard_map/ppermute | solution.py:402
  23.7 29.1 %collective-permute-start.2 = (bf16[64,2048]{1,0:T(8,128)(2,1)S(1)}, bf16[64,2048]{1,0:T(8,128)(2,1)}, u32[]{:S(2)}, u32[]{:S(2)}) collective-permute-start(bf16[64,2048]{1,0:T(8,128)(2,1)S(1)} %constant_dynamic-slice_fusion), channel_id=1, source_target_pairs={{0,2},{1,3},{2,0},{3,1},{4,6},{5,7},{6,4},{7,5},{8,10},{9,11},{10,... | collective-permute-start | bytes 786440 | tf_op jit(solution)/shard_map/ppermute | solution.py:402
  52.8 11.9 %copy-start.1 = (bf16[4,4,256,128]{3,2,1,0:T(8,128)(2,1)}, bf16[4,4,256,128]{3,2,1,0:T(8,128)(2,1)S(1)}, u32[]{:S(2)}) copy-start(bf16[4,4,256,128]{3,2,1,0:T(8,128)(2,1)S(1)} %all-to-all-done) | copy-start | bytes 3145732
  52.8 15.7 %collective-permute-start = (bf16[2048,512]{1,0:T(8,128)(2,1)}, bf16[2048,512]{1,0:T(8,128)(2,1)}, u32[]{:S(2)}, u32[]{:S(2)}) collective-permute-start(bf16[2048,512]{1,0:T(8,128)(2,1)} %param.14), channel_id=1, source_target_pairs={{0,1},{1,0},{2,3},{3,2},{4,5},{5,4},{6,7},{7,6},{8,9},{9,8},{10,11... | collective-permute-start | bytes 6291464 | tf_op jit(solution)/shard_map/ppermute | solution.py:402
  52.9 33.7 %collective-permute-start.4 = (bf16[512,2048]{1,0:T(8,128)(2,1)}, bf16[512,2048]{1,0:T(8,128)(2,1)}, u32[]{:S(2)}, u32[]{:S(2)}) collective-permute-start(bf16[512,2048]{1,0:T(8,128)(2,1)} %refs_4_.3), channel_id=1, source_target_pairs={{0,1},{1,0},{2,3},{3,2},{4,5},{5,4},{6,7},{7,6},{8,9},{9,8},{10,11... | collective-permute-start | bytes 6291464 | tf_op jit(solution)/shard_map/ppermute | solution.py:402
  55.6 30.3 %collective-permute-start.5 = (bf16[2,2,256,512]{3,2,1,0:T(8,128)(2,1)}, bf16[2,2,256,512]{3,2,1,0:T(8,128)(2,1)}, u32[]{:S(2)}, u32[]{:S(2)}) collective-permute-start(bf16[2,2,256,512]{3,2,1,0:T(8,128)(2,1)} %slice_bitcast_fusion), channel_id=1, source_target_pairs={{0,2},{1,3},{2,0},{3,1},{4,6},{5,7},{6,4},{7,5},{8,10},{9,11},{10,... | collective-permute-start | bytes 3145736 | tf_op jit(solution)/shard_map/ppermute | solution.py:402
  60.7 3.9 %copy-start.20 = (bf16[2048,512]{1,0:T(8,128)(2,1)S(1)}, bf16[2048,512]{1,0:T(8,128)(2,1)}, u32[]{:S(2)}) copy-start(bf16[2048,512]{1,0:T(8,128)(2,1)} %param.15) | copy-start | bytes 6291460
  60.7 3.9 %copy-start.22 = (bf16[512,512]{1,0:T(8,128)(2,1)S(1)}, bf16[512,512]{1,0:T(8,128)(2,1)}, u32[]{:S(2)}) copy-start(bf16[512,512]{1,0:T(8,128)(2,1)} %constant.62.clone) | copy-start | bytes 1572868
  60.8 7.7 %collective-permute-start.3 = (bf16[2,2,256,512]{3,2,1,0:T(8,128)(2,1)}, bf16[2,2,256,512]{3,2,1,0:T(8,128)(2,1)S(1)}, u32[]{:S(2)}, u32[]{:S(2)}) collective-permute-start(bf16[2,2,256,512]{3,2,1,0:T(8,128)(2,1)} %collective-permute-done.1.refs_3_), channel_id=1, source_target_pairs={{0,1},{1,0},{2,3},{3,2},{4,5},{5,4},{6,7},{7,6},{8,9},{9,8},{10,11... | collective-permute-start | bytes 3145736 | tf_op jit(solution)/shard_map/ppermute | solution.py:402
  64.6 2.6 %copy-start.3 = (bf16[2048,8]{1,0:T(8,128)(2,1)S(1)}, bf16[2048,8]{1,0:T(8,128)(2,1)}, u32[]{:S(2)}) copy-start(bf16[2048,8]{1,0:T(8,128)(2,1)} %copy.36) | copy-start | bytes 98308
  64.6 2.6 %copy-start.6 = (bf16[2048,128]{1,0:T(8,128)(2,1)S(1)}, bf16[2048,128]{1,0:T(8,128)(2,1)}, u32[]{:S(2)}) copy-start(bf16[2048,128]{1,0:T(8,128)(2,1)} %param.17) | copy-start | bytes 1572868
  68.4 1.0 copy-start.5
  86.0 3.1 %collective-permute-start.6 = (bf16[2,2,256,512]{3,2,1,0:T(8,128)(2,1)}, bf16[2,2,256,512]{3,2,1,0:T(8,128)(2,1)S(1)}, u32[]{:S(2)}, u32[]{:S(2)}) collective-permute-start(bf16[2,2,256,512]{3,2,1,0:T(8,128)(2,1)} %collective-permute-done.5.refs_3_), channel_id=1, source_target_pairs={{0,1},{1,0},{2,3},{3,2},{4,5},{5,4},{6,7},{7,6},{8,9},{9,8},{10,11... | collective-permute-start | bytes 3145736 | tf_op jit(solution)/shard_map/ppermute | solution.py:402
  89.0 1.0 copy-start.4
  106.4 5.7 %copy-start.21 = (bf16[256,512]{1,0:T(8,128)(2,1)S(1)}, bf16[256,512]{1,0:T(8,128)(2,1)}, u32[]{:S(2)}) copy-start(bf16[256,512]{1,0:T(8,128)(2,1)} %get-tuple-element.49) | copy-start | bytes 786436
  106.4 19.4 %collective-permute-start.10 = (bf16[512,2048]{1,0:T(8,128)(2,1)}, bf16[512,2048]{1,0:T(8,128)(2,1)}, u32[]{:S(2)}, u32[]{:S(2)}) collective-permute-start(bf16[512,2048]{1,0:T(8,128)(2,1)} %all-gather.2.cloned.1.call-done.refs_6_), channel_id=1, source_target_pairs={{0,1},{1,0},{2,3},{3,2},{4,5},{5,4},{6,7},{7,6},{8,9},{9,8},{10,11... | collective-permute-start | bytes 6291464 | tf_op jit(solution)/shard_map/ppermute | solution.py:402
  106.9 37.6 %all-to-all-start.1 = ((bf16[4,4,256,128]{3,2,1,0:T(8,128)(2,1)}), bf16[4,4,256,128]{3,2,1,0:T(8,128)(2,1)S(1)}, u32[]{:S(2)}, u32[]{:S(2)}) async-start(bf16[4,4,256,128]{3,2,1,0:T(8,128)(2,1)} %bitcast.30), calls=%async_computation.1 | async-start | bytes 2097152 | tf_op jit(solution)/shard_map/all_to_all | solution.py:405
  111.7 2.2 %collective-permute-start.11 = (bf16[256,512]{1,0:T(8,128)(2,1)}, bf16[256,512]{1,0:T(8,128)(2,1)S(1)}, u32[]{:S(2)}, u32[]{:S(2)}) collective-permute-start(bf16[256,512]{1,0:T(8,128)(2,1)} %get-tuple-element.47), channel_id=1, source_target_pairs={{0,1},{1,0},{2,3},{3,2},{4,5},{5,4},{6,7},{7,6},{8,9},{9,8},{10,11... | collective-permute-start | bytes 786440 | tf_op jit(solution)/shard_map/ppermute | solution.py:402
  111.7 9.3 %collective-permute-start.12 = (bf16[256,512]{1,0:T(8,128)(2,1)}, bf16[256,512]{1,0:T(8,128)(2,1)S(1)}, u32[]{:S(2)}, u32[]{:S(2)}) collective-permute-start(bf16[256,512]{1,0:T(8,128)(2,1)} %get-tuple-element.48), channel_id=1, source_target_pairs={{0,2},{1,3},{2,0},{3,1},{4,6},{5,7},{6,4},{7,5},{8,10},{9,11},{10,... | collective-permute-start | bytes 786440 | tf_op jit(solution)/shard_map/ppermute | solution.py:402
  112.1 13.7 %collective-permute-start.13 = (bf16[256,512]{1,0:T(8,128)(2,1)S(1)}, bf16[256,512]{1,0:T(8,128)(2,1)S(1)}, u32[]{:S(2)}, u32[]{:S(2)}) collective-permute-start(bf16[256,512]{1,0:T(8,128)(2,1)S(1)} %copy-done.21), channel_id=1, source_target_pairs={{0,3},{1,2},{2,1},{3,0},{4,7},{5,6},{6,5},{7,4},{8,11},{9,10},{10,... | collective-permute-start | bytes 786440 | tf_op jit(solution)/shard_map/ppermute | solution.py:402
  113.5 19.7 %collective-permute-start.7 = (bf16[256,512]{1,0:T(8,128)(2,1)}, bf16[256,512]{1,0:T(8,128)(2,1)S(1)}, u32[]{:S(2)}, u32[]{:S(2)}) collective-permute-start(bf16[256,512]{1,0:T(8,128)(2,1)} %get-tuple-element.40), channel_id=1, source_target_pairs={{0,1},{1,0},{2,3},{3,2},{4,5},{5,4},{6,7},{7,6},{8,9},{9,8},{10,11... | collective-permute-start | bytes 786440 | tf_op jit(solution)/shard_map/ppermute | solution.py:402
  113.8 12.0 %copy-start.7 = (bf16[256,512]{1,0:T(8,128)(2,1)}, bf16[256,512]{1,0:T(8,128)(2,1)S(1)}, u32[]{:S(2)}) copy-start(bf16[256,512]{1,0:T(8,128)(2,1)S(1)} %collective-permute-done.11.refs_1_) | copy-start | bytes 786436
  113.8 19.4 %collective-permute-start.8 = (bf16[256,512]{1,0:T(8,128)(2,1)}, bf16[256,512]{1,0:T(8,128)(2,1)S(1)}, u32[]{:S(2)}, u32[]{:S(2)}) collective-permute-start(bf16[256,512]{1,0:T(8,128)(2,1)} %get-tuple-element.41), channel_id=1, source_target_pairs={{0,2},{1,3},{2,0},{3,1},{4,6},{5,7},{6,4},{7,5},{8,10},{9,11},{10,... | collective-permute-start | bytes 786440 | tf_op jit(solution)/shard_map/ppermute | solution.py:402
  121.0 4.9 %copy-start.8 = (bf16[256,512]{1,0:T(8,128)(2,1)}, bf16[256,512]{1,0:T(8,128)(2,1)S(1)}, u32[]{:S(2)}) copy-start(bf16[256,512]{1,0:T(8,128)(2,1)S(1)} %collective-permute-done.12.refs_2_) | copy-start | bytes 786436
  121.0 16.1 %collective-permute-start.9 = (bf16[256,512]{1,0:T(8,128)(2,1)}, bf16[256,512]{1,0:T(8,128)(2,1)S(1)}, u32[]{:S(2)}, u32[]{:S(2)}) collective-permute-start(bf16[256,512]{1,0:T(8,128)(2,1)} %get-tuple-element.42), channel_id=1, source_target_pairs={{0,3},{1,2},{2,1},{3,0},{4,7},{5,6},{6,5},{7,4},{8,11},{9,10},{10,... | collective-permute-start | bytes 786440 | tf_op jit(solution)/shard_map/ppermute | solution.py:402
  125.8 0.7 copy-start.9
  133.2 3.9 %copy-start.10 = (bf16[256,512]{1,0:T(8,128)(2,1)}, bf16[256,512]{1,0:T(8,128)(2,1)S(1)}, u32[]{:S(2)}) copy-start(bf16[256,512]{1,0:T(8,128)(2,1)S(1)} %collective-permute-done.7.refs_1_) | copy-start | bytes 786436
  133.2 3.9 %copy-start.11 = (bf16[256,512]{1,0:T(8,128)(2,1)}, bf16[256,512]{1,0:T(8,128)(2,1)S(1)}, u32[]{:S(2)}) copy-start(bf16[256,512]{1,0:T(8,128)(2,1)S(1)} %collective-permute-done.8.refs_2_) | copy-start | bytes 786436
  137.1 0.7 copy-start.12
  144.4 1.0 copy-start.2
Sparse Core Ops, SparseCore 0:
  52.9 50.5 all-gather.1

commit v10 on v9

--- a/solution.py
+++ b/solution.py
@@ -434,10 +434,11 @@
     swap = jnp.asarray(
         (swap_row % 16 * sessions_here + swap_row // 16)[:, None] == swap_row[None, :], BF
     )
-    first = after(blocks, ow_share)[:, :, 0]
-    packed = pack_states(after(source, first), store_states, swap, slot_count)
-    second = after(blocks, packed)[:, :, 1]
+    halved = after(blocks, ow_share)
+    first, second = halved[:, :, 0], halved[:, :, 1]
+    packed = pack_states(after(source, first, second), store_states, swap, slot_count)
     across = [exchange(first, 2), exchange(second, 2)]
+    packed, ow_part = lax.optimization_barrier((packed, ow_part))
     inbound = trade(packed)
     wanted = lax.dynamic_slice_in_dim(home_rows, shard_index * sessions_here, sessions_here)
     home_shard = wanted // sessions_here
@@ -452,8 +453,8 @@
         + new_column // 128 % 2
     )
     turn = jnp.asarray(old_column[None, :] == np.arange(width)[:, None], BF)
-    x_weight, z_weight, bc_weight, across[0], ow_part = lax.optimization_barrier(
-        (x_weight, z_weight, bc_weight, across[0], ow_part)
+    x_weight, z_weight, bc_weight, packed = lax.optimization_barrier(
+        (x_weight, z_weight, bc_weight, packed)
     )
     xw = jnp.dot(x_weight, turn, preferred_element_type=F32).astype(BF)
     zw = jnp.dot(z_weight, turn, preferred_element_type=F32).astype(BF)
@@ -464,7 +465,8 @@
     gain = norm_gain.reshape(heads // 4, 4, 32, 2).transpose(0, 3, 1, 2).reshape(1, width)
     small = jnp.stack([dt_bias, decay_rate], axis=1)
 
-    ow_part = after(ow_part, inbound)
+    across[0], xw, zw, bw = lax.optimization_barrier((across[0], xw, zw, bw))
+    ow_part, across[0] = lax.optimization_barrier((ow_part, across[0]))
     ow_across = lax.all_gather(ow_part, ("groups", "dp"), axis=0, tiled=True)
     ow_sibling = exchange(out_weight, 1)
 

time: 157 us -> 167 us (1.064)
  waiting for transfers between devices: 46.5 us -> 59.6 us
  local copies, waits for them, and re-layouts: 12.7 us -> 10.5 us
    all_to_all x2, waiting for transfers between devices: 0.01 us -> 30.5 us  [trade(): lax.all_to_all(value.reshape((shard_count, capacity) + row_shape), 'dp',...]
    ppermute x14, waiting for transfers between devices: 46.4 us -> 29 us  [exchange(): return lax.ppermute(value, 'mp', pairs)]
    all_to_all x2, starting transfers between devices: 11.2 us -> 8.65 us  [trade(): lax.all_to_all(value.reshape((shard_count, capacity) + row_shape), 'dp',...]
    squeeze x2 -> x1, local copies, waits for them, and re-layouts: 4.53 us -> 3.04 us  [body(): first, second = (halved[:, :, 0], halved[:, :, 1])]
    unnamed x47 -> x45, local copies, waits for them, and re-layouts: 5.37 us -> 4.67 us
  transfers between devices with their start and end apart: 17 -> 17, of which waited for: 5 -> 6; matrix products, arithmetic and copies ran while one was open for 9% -> 9% of each run, Pallas kernels for 30% -> 30%
where the time goes in v10:
time: 167 us; the launch traced here: 166 us
  waiting for transfers between devices  59.6 us (36%)
  Pallas kernels  54.2 us (32%)
  starting transfers between devices  18 us (11%)
  between operations  14.3 us (9%)
  local copies, waits for them, and re-layouts  10.5 us (6%)
  matrix products  6.39 us (4%)
  other arithmetic  3.2 us (2%)
    pallas_call x2, Pallas kernels, layer_call(): pl.pallas_call(lambda *refs: layer_kernel(heads, span, pairs, half, *refs...  32.7 us
    all_to_all x2, waiting for transfers between devices, trade(): lax.all_to_all(value.reshape((shard_count, capacity) + row_shape), 'dp',...  30.5 us
    ppermute x14, waiting for transfers between devices, exchange(): return lax.ppermute(value, 'mp', pairs)  29 us
    pallas_call x2, Pallas kernels, out_call(): pl.pallas_call(kernel, grid=(columns // block,), out_shape=jax.ShapeDtype...  13.3 us
    ppermute x14, starting transfers between devices, exchange(): return lax.ppermute(value, 'mp', pairs)  9.29 us
    all_to_all x2, starting transfers between devices, trade(): lax.all_to_all(value.reshape((shard_count, capacity) + row_shape), 'dp',...  8.65 us
    unnamed x45, local copies, waits for them, and re-layouts  4.67 us
    pallas_call x1, Pallas kernels, gather_states(): pl.pallas_call(kernel, grid=(lines // 64,), out_shape=jax.ShapeDtypeStruc...  4.08 us
  transfers between devices with their start and end apart: 17, of which 6 were waited for; matrix products, arithmetic and copies ran while one was open for 9% of the time, Pallas kernels for 30%

profile of v10, /device:TPU:0, one launch (start us, length us, event | category | flops | bytes accessed | tf_op | source)
XLA Modules:
  0.0 166.1 jit_solution(15447250374993020394)
XLA Ops:
  7.2 0.0 copy-start
  7.2 0.0 all-gather.2.cloned.1.call-start
  7.2 1.1 constant_dynamic-slice_fusion
  8.3 3.0 %collective-permute-start.1 = (bf16[64,2048]{1,0:T(8,128)(2,1)S(1)}, bf16[64,2048]{1,0:T(8,128)(2,1)S(1)}, u32[]{:S(2)}, u32[]{:S(2)}) collective-permute-start(bf16[64,2048]{1,0:T(8,128)(2,1)S(1)} %constant_dynamic-slice_fusion), channel_id=1, source_target_pairs={{0,2},{1,3},{2,0},{3,1},{4,6},{5,7},{6,4},{7,5},{8,10},{9,11},{10,... | collective-permute-start | bytes 786440 | tf_op jit(solution)/shard_map/ppermute | solution.py:402
  11.4 3.0 %slice_bitcast_fusion = (bf16[2,2,256,512]{3,2,1,0:T(8,128)(2,1)}, bf16[2,2,256,512]{3,2,1,0:T(8,128)(2,1)}) fusion(bf16[2,2,2,256,512]{4,3,2,1,0:T(8,128)(2,1)} %bitcast.26), kind=kLoop, calls=%fused_computation.2 | loop fusion | bytes 4194304 | tf_op jit(solution)/shard_map/squeeze | solution.py:438
  14.4 0.0 collective-permute-start.2
  14.4 0.2 select_reduce_fusion.1
  14.6 0.2 convert_reduce_fusion
  14.8 0.6 select_reduce_fusion.source
  15.4 4.0 %pack_states.1 = bf16[16,256,128]{2,1,0:T(8,128)(2,1)} custom-call(s32[16]{0:T(128)} %select_reduce_fusion.source, bf16[16,32768]{1,0:T(8,128)(2,1)} %store.1, bf16[256,256]{1,0:T(8,128)(2,1)} %constant.61.clone.swap), custom_call_target="tpu_custom_call" | custom-call | flops 1 | bytes 1 | tf_op jit(solution)/shard_map/pack_states/pallas_call | solution.py:39
  19.5 0.3 copy.37
  19.8 0.1 pad.4.clone
  19.8 0.0 collective-permute-done.1
  19.9 0.0 copy-start.21
  19.9 3.8 %convolution_convert_fusion.refs_7_ = bf16[2048,512]{1,0:T(8,128)(2,1)} fusion(bf16[2048,512]{1,0:T(8,128)(2,1)S(1)} %copy-done, bf16[512,512]{1,0:T(8,128)(2,1)} %constant.62.clone), kind=kOutput, calls=%fused_computation | convolution fusion | flops 1074790400 | bytes 4718592 | tf_op jit(solution)/shard_map/dot_general | solution.py:460
  23.7 0.0 copy-start.4
  23.7 2.6 %convolution_convert_fusion.1.refs_6_ = bf16[2048,512]{1,0:T(8,128)(2,1)} fusion(bf16[2048,512]{1,0:T(8,128)(2,1)S(1)} %copy-done.19, bf16[512,512]{1,0:T(8,128)(2,1)S(1)} %copy-done.21), kind=kOutput, calls=%fused_computation.1 | convolution fusion | flops 1074790400 | bytes 4718592 | tf_op jit(solution)/shard_map/dot_general | solution.py:459
  26.3 0.0 copy-start.18
  26.3 1.3 maximum_maximum_fusion.refs_5_
  27.6 12.6 %collective-permute-done.2.refs_3_ = bf16[2,2,256,512]{3,2,1,0:T(8,128)(2,1)} collective-permute-done((bf16[2,2,256,512]{3,2,1,0:T(8,128)(2,1)}, bf16[2,2,256,512]{3,2,1,0:T(8,128)(2,1)}, u32[]{:S(2)}, u32[]{:S(2)}) %collective-permute-start.2) | collective-permute-done | bytes 1048608 | tf_op jit(solution)/shard_map/ppermute | solution.py:402
  40.2 0.0 all-gather.2.cloned.1.call-update
  40.3 0.1 collective-permute-start
  40.3 5.1 %all-to-all-start = ((bf16[4,4,256,128]{3,2,1,0:T(8,128)(2,1)}), bf16[4,4,256,128]{3,2,1,0:T(8,128)(2,1)S(1)}, u32[]{:S(2)}, u32[]{:S(2)}) async-start(bf16[4,4,256,128]{3,2,1,0:T(8,128)(2,1)} %bitcast.30), calls=%async_computation | async-start | bytes 2097152 | tf_op jit(solution)/shard_map/all_to_all | solution.py:405
  45.5 0.2 collective-permute-start.3
  45.7 1.5 collective-permute-start.5
  47.2 0.0 collective-permute-start.4
  47.2 0.1 reshape.83
  47.3 0.1 copy.38
  47.5 0.7 reshape.84.refs_9_
  48.1 0.7 copy.39.refs_8_
  48.8 0.1 and_select_fusion.2
  48.9 0.2 convert_reduce_fusion.1
  49.1 0.6 pad_add_fusion.refs_0_
  49.7 30.5 %all-to-all-done = bf16[4,4,256,128]{3,2,1,0:T(8,128)(2,1)S(1)} async-done(((bf16[4,4,256,128]{3,2,1,0:T(8,128)(2,1)}), bf16[4,4,256,128]{3,2,1,0:T(8,128)(2,1)S(1)}, u32[]{:S(2)}, u32[]{:S(2)}) %all-to-all-start) | async-done | bytes 1048608 | tf_op jit(solution)/shard_map/all_to_all | solution.py:405
  80.3 0.0 collective-permute-done.3.refs_4_
  80.3 1.0 copy-done.1
  81.3 16.4 %layer.2 = (bf16[256,512]{1,0:T(8,128)(2,1)}, bf16[256,512]{1,0:T(8,128)(2,1)}, bf16[256,512]{1,0:T(8,128)(2,1)}, bf16[256,512]{1,0:T(8,128)(2,1)}, bf16[16,256,128]{2,1,0:T(8,128)(2,1)}) custom-call(s32[33]{0:T(128)} %pad_add_fusion.refs_0_, bf16[2,2,2,256,512]{4,3,2,1,0:T(8,128)(2,1)} %bitcast.27, bf16[2,2,2,256,512]{4,3,2,1,0:T(8,128)(2,1)} %bitcast.2.refs_2_, ...), custom_call_target="tpu_custom_call" | custom-call | flops 1 | bytes 1 | tf_op jit(solution)/shard_map/layer/pallas_call | solution.py:300
  97.7 0.0 collective-permute-done.5.refs_3_
  97.7 0.1 collective-permute-start.6
  97.8 2.8 %collective-permute-done.6.refs_4_ = bf16[2,2,256,512]{3,2,1,0:T(8,128)(2,1)S(1)} collective-permute-done((bf16[2,2,256,512]{3,2,1,0:T(8,128)(2,1)}, bf16[2,2,256,512]{3,2,1,0:T(8,128)(2,1)S(1)}, u32[]{:S(2)}, u32[]{:S(2)}) %collective-permute-start.6) | collective-permute-done | bytes 1048608 | tf_op jit(solution)/shard_map/ppermute | solution.py:402
  100.7 1.0 copy-done.3
  101.6 16.3 %layer.3 = (bf16[256,512]{1,0:T(8,128)(2,1)}, bf16[256,512]{1,0:T(8,128)(2,1)}, bf16[256,512]{1,0:T(8,128)(2,1)}, bf16[256,512]{1,0:T(8,128)(2,1)}, bf16[16,256,128]{2,1,0:T(8,128)(2,1)}) custom-call(s32[33]{0:T(128)} %pad_add_fusion.refs_0_, bf16[2,2,2,256,512]{4,3,2,1,0:T(8,128)(2,1)} %bitcast.28, ...), custom_call_target="tpu_custom_call", output_to_operand_aliasing={{4}: (15, {})} | custom-call | flops 1 | bytes 1 | tf_op jit(solution)/shard_map/layer/pallas_call | solution.py:300
  117.9 0.0 all-gather.2.cloned.1.call-done.refs_6_
  118.0 0.2 collective-permute-start.10
  118.2 3.5 %all-to-all-start.1 = ((bf16[4,4,256,128]{3,2,1,0:T(8,128)(2,1)}), bf16[4,4,256,128]{3,2,1,0:T(8,128)(2,1)S(1)}, u32[]{:S(2)}, u32[]{:S(2)}) async-start(bf16[4,4,256,128]{3,2,1,0:T(8,128)(2,1)} %bitcast.29), calls=%async_computation.1 | async-start | bytes 2097152 | tf_op jit(solution)/shard_map/all_to_all | solution.py:405
  121.7 0.4 collective-permute-start.11
  122.1 1.6 collective-permute-start.12
  123.8 0.0 collective-permute-start.13
  123.8 0.5 collective-permute-start.7
  124.3 1.6 collective-permute-start.8
  125.9 5.6 %collective-permute-done.12.refs_2_ = bf16[256,512]{1,0:T(8,128)(2,1)S(1)} collective-permute-done((bf16[256,512]{1,0:T(8,128)(2,1)}, bf16[256,512]{1,0:T(8,128)(2,1)S(1)}, u32[]{:S(2)}, u32[]{:S(2)}) %collective-permute-start.12) | collective-permute-done | bytes 262176 | tf_op jit(solution)/shard_map/ppermute | solution.py:402
  131.5 0.0 collective-permute-start.9
  131.5 4.8 %collective-permute-done.13.refs_3_ = bf16[256,512]{1,0:T(8,128)(2,1)S(1)} collective-permute-done((bf16[256,512]{1,0:T(8,128)(2,1)S(1)}, bf16[256,512]{1,0:T(8,128)(2,1)S(1)}, u32[]{:S(2)}, u32[]{:S(2)}) %collective-permute-start.13) | collective-permute-done | bytes 262176 | tf_op jit(solution)/shard_map/ppermute | solution.py:402
  136.3 0.0 collective-permute-done.10.refs_7_
  136.3 0.7 copy-done.7
  136.9 6.7 %project_out.2.refs_8_ = bf16[512,2048]{1,0:T(8,128)(2,1)} custom-call(bf16[256,512]{1,0:T(8,128)(2,1)} %get-tuple-element.54.refs_0_, bf16[256,512]{1,0:T(8,128)(2,1)} %copy-done.5, bf16[256,512]{1,0:T(8,128)(2,1)} %copy-done.6, bf16[256,512]{1,0:T(8,128)(2,1)} %copy-done.7, bf16[512,2048]{1,0:T(8,128)(2,1)} %refs_4_.3, ...), custom_call_target="tpu_custom_call" | custom-call | flops 1 | bytes 1 | tf_op jit(solution)/shard_map/project_out/pallas_call | solution.py:350
  143.6 0.0 collective-permute-done.7.refs_1_
  143.6 0.0 copy-start.9
  143.7 3.1 %collective-permute-done.9.refs_3_ = bf16[256,512]{1,0:T(8,128)(2,1)S(1)} collective-permute-done((bf16[256,512]{1,0:T(8,128)(2,1)}, bf16[256,512]{1,0:T(8,128)(2,1)S(1)}, u32[]{:S(2)}, u32[]{:S(2)}) %collective-permute-start.9) | collective-permute-done | bytes 262176 | tf_op jit(solution)/shard_map/ppermute | solution.py:402
  146.8 0.7 copy-done.11
  147.5 6.7 %project_out.3 = bf16[512,2048]{1,0:T(8,128)(2,1)} custom-call(bf16[256,512]{1,0:T(8,128)(2,1)} %get-tuple-element.48.refs_0_, bf16[256,512]{1,0:T(8,128)(2,1)} %copy-done.9, bf16[256,512]{1,0:T(8,128)(2,1)} %copy-done.10, bf16[256,512]{1,0:T(8,128)(2,1)} %copy-done.11, bf16[512,2048]{1,0:T(8,128)(2,1)} %refs_4_.3, ...), custom_call_target="tpu_custom_call", output_to_operand_aliasing={{}: (8, {})} | custom-call | flops 1 | bytes 1 | tf_op jit(solution)/shard_map/project_out/pallas_call | solution.py:350
  154.2 0.0 all-to-all-done.1
  154.2 1.0 copy-done.2
  155.2 4.1 %gather_states.1 = bf16[16,32768]{1,0:T(8,128)(2,1)} custom-call(s32[16]{0:T(128)} %copy-done.14, bf16[16,256,128]{2,1,0:T(8,128)(2,1)} %bitcast.31, bf16[256,256]{1,0:T(8,128)(2,1)} %constant.61.clone.swap), custom_call_target="tpu_custom_call" | custom-call | flops 1 | bytes 1 | tf_op jit(solution)/shard_map/gather_states/pallas_call | solution.py:75
  (45 shorter events, 0.1 us)
Async XLA Ops:
  7.2 12.7 %copy-start = (bf16[2048,512]{1,0:T(8,128)(2,1)S(1)}, bf16[2048,512]{1,0:T(8,128)(2,1)}, u32[]{:S(2)}) copy-start(bf16[2048,512]{1,0:T(8,128)(2,1)} %param.16) | copy-start | bytes 6291460
  7.2 110.8 %all-gather.2.cloned.1.call-start = ((), (), s32[]{:S(2)}) async-start(), calls=%async_computation.2 | async-start | bytes 2359296 | tf_op jit(solution)/shard_map/all_gather | solution.py:470
  8.3 11.5 %collective-permute-start.1 = (bf16[64,2048]{1,0:T(8,128)(2,1)S(1)}, bf16[64,2048]{1,0:T(8,128)(2,1)S(1)}, u32[]{:S(2)}, u32[]{:S(2)}) collective-permute-start(bf16[64,2048]{1,0:T(8,128)(2,1)S(1)} %constant_dynamic-slice_fusion), channel_id=1, source_target_pairs={{0,2},{1,3},{2,0},{3,1},{4,6},{5,7},{6,4},{7,5},{8,10},{9,11},{10,... | collective-permute-start | bytes 786440 | tf_op jit(solution)/shard_map/ppermute | solution.py:402
  11.3 3.1 %copy-start.17 = (s32[64]{0:T(128)S(1)}, s32[64]{0:T(128)}, u32[]{:S(2)}) copy-start(s32[64]{0:T(128)} %param.24) | copy-start | bytes 772
  14.4 5.1 %copy-start.12 = (bf16[2048,8]{0,1:T(8,128)(2,1)S(1)}, bf16[2048,8]{0,1:T(8,128)(2,1)}, u32[]{:S(2)}) copy-start(bf16[2048,8]{0,1:T(8,128)(2,1)} %param.18) | copy-start | bytes 98308
  14.4 25.8 %collective-permute-start.2 = (bf16[2,2,256,512]{3,2,1,0:T(8,128)(2,1)}, bf16[2,2,256,512]{3,2,1,0:T(8,128)(2,1)}, u32[]{:S(2)}, u32[]{:S(2)}) collective-permute-start(bf16[2,2,256,512]{3,2,1,0:T(8,128)(2,1)} %get-tuple-element.63), channel_id=1, source_target_pairs={{0,2},{1,3},{2,0},{3,1},{4,6},{5,7},{6,4},{7,5},{8,10},{9,11},{10,... | collective-permute-start | bytes 3145736 | tf_op jit(solution)/shard_map/ppermute | solution.py:402
  14.8 8.9 %copy-start.14 = (s32[16]{0:T(128)}, s32[16]{0:T(128)S(1)}, u32[]{:S(2)}) copy-start(s32[16]{0:T(128)S(1)} %multiply_add_fusion.index) | copy-start | bytes 196
  19.8 3.9 %copy-start.8 = (bf16[64,2048]{1,0:T(8,128)(2,1)}, bf16[64,2048]{1,0:T(8,128)(2,1)S(1)}, u32[]{:S(2)}) copy-start(bf16[64,2048]{1,0:T(8,128)(2,1)S(1)} %collective-permute-done.1) | copy-start | bytes 786436
  19.8 3.9 %copy-start.19 = (bf16[2048,512]{1,0:T(8,128)(2,1)S(1)}, bf16[2048,512]{1,0:T(8,128)(2,1)}, u32[]{:S(2)}) copy-start(bf16[2048,512]{1,0:T(8,128)(2,1)} %param.15) | copy-start | bytes 6291460
  19.9 3.8 %copy-start.21 = (bf16[512,512]{1,0:T(8,128)(2,1)S(1)}, bf16[512,512]{1,0:T(8,128)(2,1)}, u32[]{:S(2)}) copy-start(bf16[512,512]{1,0:T(8,128)(2,1)} %constant.62.clone) | copy-start | bytes 1572868
  23.7 2.6 %copy-start.4 = (bf16[2048,128]{1,0:T(8,128)(2,1)S(1)}, bf16[2048,128]{1,0:T(8,128)(2,1)}, u32[]{:S(2)}) copy-start(bf16[2048,128]{1,0:T(8,128)(2,1)} %param.17) | copy-start | bytes 1572868
  26.3 20.9 %copy-start.13 = (f32[512]{0:T(512)S(1)}, f32[512]{0:T(512)}, u32[]{:S(2)}) copy-start(f32[512]{0:T(512)} %param.21) | copy-start | bytes 6148
  26.3 21.8 %copy-start.15 = (f32[8]{0:T(128)S(1)}, f32[8]{0:T(128)}, u32[]{:S(2)}) copy-start(f32[8]{0:T(128)} %param.20) | copy-start | bytes 100
  26.3 21.8 %copy-start.16 = (f32[8]{0:T(128)S(1)}, f32[8]{0:T(128)}, u32[]{:S(2)}) copy-start(f32[8]{0:T(128)} %param.19) | copy-start | bytes 100
  26.3 22.8 %copy-start.18 = (s32[16]{0:T(128)S(1)}, s32[16]{0:T(128)}, u32[]{:S(2)}) copy-start(s32[16]{0:T(128)} %param.25) | copy-start | bytes 196
  40.3 40.0 %collective-permute-start = (bf16[2048,512]{1,0:T(8,128)(2,1)}, bf16[2048,512]{1,0:T(8,128)(2,1)}, u32[]{:S(2)}, u32[]{:S(2)}) collective-permute-start(bf16[2048,512]{1,0:T(8,128)(2,1)} %param.14), channel_id=1, source_target_pairs={{0,1},{1,0},{2,3},{3,2},{4,5},{5,4},{6,7},{7,6},{8,9},{9,8},{10,11... | collective-permute-start | bytes 6291464 | tf_op jit(solution)/shard_map/ppermute | solution.py:402
  40.3 39.9 %all-to-all-start = ((bf16[4,4,256,128]{3,2,1,0:T(8,128)(2,1)}), bf16[4,4,256,128]{3,2,1,0:T(8,128)(2,1)S(1)}, u32[]{:S(2)}, u32[]{:S(2)}) async-start(bf16[4,4,256,128]{3,2,1,0:T(8,128)(2,1)} %bitcast.30), calls=%async_computation | async-start | bytes 2097152 | tf_op jit(solution)/shard_map/all_to_all | solution.py:405
  45.5 34.8 %collective-permute-start.3 = (bf16[2,2,256,512]{3,2,1,0:T(8,128)(2,1)}, bf16[2,2,256,512]{3,2,1,0:T(8,128)(2,1)}, u32[]{:S(2)}, u32[]{:S(2)}) collective-permute-start(bf16[2,2,256,512]{3,2,1,0:T(8,128)(2,1)} %collective-permute-done.2.refs_3_), channel_id=1, source_target_pairs={{0,1},{1,0},{2,3},{3,2},{4,5},{5,4},{6,7},{7,6},{8,9},{9,8},{10,11... | collective-permute-start | bytes 3145736 | tf_op jit(solution)/shard_map/ppermute | solution.py:402
  45.7 52.0 %collective-permute-start.5 = (bf16[2,2,256,512]{3,2,1,0:T(8,128)(2,1)}, bf16[2,2,256,512]{3,2,1,0:T(8,128)(2,1)}, u32[]{:S(2)}, u32[]{:S(2)}) collective-permute-start(bf16[2,2,256,512]{3,2,1,0:T(8,128)(2,1)} %get-tuple-element.62), channel_id=1, source_target_pairs={{0,2},{1,3},{2,0},{3,1},{4,6},{5,7},{6,4},{7,5},{8,10},{9,11},{10,... | collective-permute-start | bytes 3145736 | tf_op jit(solution)/shard_map/ppermute | solution.py:402
  47.2 50.6 %collective-permute-start.4 = (bf16[512,2048]{1,0:T(8,128)(2,1)}, bf16[512,2048]{1,0:T(8,128)(2,1)}, u32[]{:S(2)}, u32[]{:S(2)}) collective-permute-start(bf16[512,2048]{1,0:T(8,128)(2,1)} %refs_4_.3), channel_id=1, source_target_pairs={{0,1},{1,0},{2,3},{3,2},{4,5},{5,4},{6,7},{7,6},{8,9},{9,8},{10,11... | collective-permute-start | bytes 6291464 | tf_op jit(solution)/shard_map/ppermute | solution.py:402
  80.3 1.0 copy-start.1
  97.7 2.9 %collective-permute-start.6 = (bf16[2,2,256,512]{3,2,1,0:T(8,128)(2,1)}, bf16[2,2,256,512]{3,2,1,0:T(8,128)(2,1)S(1)}, u32[]{:S(2)}, u32[]{:S(2)}) collective-permute-start(bf16[2,2,256,512]{3,2,1,0:T(8,128)(2,1)} %collective-permute-done.5.refs_3_), channel_id=1, source_target_pairs={{0,1},{1,0},{2,3},{3,2},{4,5},{5,4},{6,7},{7,6},{8,9},{9,8},{10,11... | collective-permute-start | bytes 3145736 | tf_op jit(solution)/shard_map/ppermute | solution.py:402
  100.7 1.0 copy-start.3
  117.9 5.8 %copy-start.20 = (bf16[256,512]{1,0:T(8,128)(2,1)S(1)}, bf16[256,512]{1,0:T(8,128)(2,1)}, u32[]{:S(2)}) copy-start(bf16[256,512]{1,0:T(8,128)(2,1)} %get-tuple-element.57) | copy-start | bytes 786436
  118.0 18.3 %collective-permute-start.10 = (bf16[512,2048]{1,0:T(8,128)(2,1)}, bf16[512,2048]{1,0:T(8,128)(2,1)}, u32[]{:S(2)}, u32[]{:S(2)}) collective-permute-start(bf16[512,2048]{1,0:T(8,128)(2,1)} %all-gather.2.cloned.1.call-done.refs_6_), channel_id=1, source_target_pairs={{0,1},{1,0},{2,3},{3,2},{4,5},{5,4},{6,7},{7,6},{8,9},{9,8},{10,11... | collective-permute-start | bytes 6291464 | tf_op jit(solution)/shard_map/ppermute | solution.py:402
  118.2 36.0 %all-to-all-start.1 = ((bf16[4,4,256,128]{3,2,1,0:T(8,128)(2,1)}), bf16[4,4,256,128]{3,2,1,0:T(8,128)(2,1)S(1)}, u32[]{:S(2)}, u32[]{:S(2)}) async-start(bf16[4,4,256,128]{3,2,1,0:T(8,128)(2,1)} %bitcast.29), calls=%async_computation.1 | async-start | bytes 2097152 | tf_op jit(solution)/shard_map/all_to_all | solution.py:405
  121.7 2.6 %collective-permute-start.11 = (bf16[256,512]{1,0:T(8,128)(2,1)}, bf16[256,512]{1,0:T(8,128)(2,1)S(1)}, u32[]{:S(2)}, u32[]{:S(2)}) collective-permute-start(bf16[256,512]{1,0:T(8,128)(2,1)} %get-tuple-element.55), channel_id=1, source_target_pairs={{0,1},{1,0},{2,3},{3,2},{4,5},{5,4},{6,7},{7,6},{8,9},{9,8},{10,11... | collective-permute-start | bytes 786440 | tf_op jit(solution)/shard_map/ppermute | solution.py:402
  122.1 9.4 %collective-permute-start.12 = (bf16[256,512]{1,0:T(8,128)(2,1)}, bf16[256,512]{1,0:T(8,128)(2,1)S(1)}, u32[]{:S(2)}, u32[]{:S(2)}) collective-permute-start(bf16[256,512]{1,0:T(8,128)(2,1)} %get-tuple-element.56), channel_id=1, source_target_pairs={{0,2},{1,3},{2,0},{3,1},{4,6},{5,7},{6,4},{7,5},{8,10},{9,11},{10,... | collective-permute-start | bytes 786440 | tf_op jit(solution)/shard_map/ppermute | solution.py:402
  123.8 12.5 %collective-permute-start.13 = (bf16[256,512]{1,0:T(8,128)(2,1)S(1)}, bf16[256,512]{1,0:T(8,128)(2,1)S(1)}, u32[]{:S(2)}, u32[]{:S(2)}) collective-permute-start(bf16[256,512]{1,0:T(8,128)(2,1)S(1)} %copy-done.20), channel_id=1, source_target_pairs={{0,3},{1,2},{2,1},{3,0},{4,7},{5,6},{6,5},{7,4},{8,11},{9,10},{10,... | collective-permute-start | bytes 786440 | tf_op jit(solution)/shard_map/ppermute | solution.py:402
  123.8 19.9 %collective-permute-start.7 = (bf16[256,512]{1,0:T(8,128)(2,1)}, bf16[256,512]{1,0:T(8,128)(2,1)S(1)}, u32[]{:S(2)}, u32[]{:S(2)}) collective-permute-start(bf16[256,512]{1,0:T(8,128)(2,1)} %get-tuple-element.49), channel_id=1, source_target_pairs={{0,1},{1,0},{2,3},{3,2},{4,5},{5,4},{6,7},{7,6},{8,9},{9,8},{10,11... | collective-permute-start | bytes 786440 | tf_op jit(solution)/shard_map/ppermute | solution.py:402
  124.3 12.0 %copy-start.5 = (bf16[256,512]{1,0:T(8,128)(2,1)}, bf16[256,512]{1,0:T(8,128)(2,1)S(1)}, u32[]{:S(2)}) copy-start(bf16[256,512]{1,0:T(8,128)(2,1)S(1)} %collective-permute-done.11.refs_1_) | copy-start | bytes 786436
  124.3 19.4 %collective-permute-start.8 = (bf16[256,512]{1,0:T(8,128)(2,1)}, bf16[256,512]{1,0:T(8,128)(2,1)S(1)}, u32[]{:S(2)}, u32[]{:S(2)}) collective-permute-start(bf16[256,512]{1,0:T(8,128)(2,1)} %get-tuple-element.50), channel_id=1, source_target_pairs={{0,2},{1,3},{2,0},{3,1},{4,6},{5,7},{6,4},{7,5},{8,10},{9,11},{10,... | collective-permute-start | bytes 786440 | tf_op jit(solution)/shard_map/ppermute | solution.py:402
  131.5 4.8 %copy-start.6 = (bf16[256,512]{1,0:T(8,128)(2,1)}, bf16[256,512]{1,0:T(8,128)(2,1)S(1)}, u32[]{:S(2)}) copy-start(bf16[256,512]{1,0:T(8,128)(2,1)S(1)} %collective-permute-done.12.refs_2_) | copy-start | bytes 786436
  131.5 15.3 %collective-permute-start.9 = (bf16[256,512]{1,0:T(8,128)(2,1)}, bf16[256,512]{1,0:T(8,128)(2,1)S(1)}, u32[]{:S(2)}, u32[]{:S(2)}) collective-permute-start(bf16[256,512]{1,0:T(8,128)(2,1)} %get-tuple-element.51), channel_id=1, source_target_pairs={{0,3},{1,2},{2,1},{3,0},{4,7},{5,6},{6,5},{7,4},{8,11},{9,10},{10,... | collective-permute-start | bytes 786440 | tf_op jit(solution)/shard_map/ppermute | solution.py:402
  136.3 0.7 copy-start.7
  143.6 3.2 %copy-start.9 = (bf16[256,512]{1,0:T(8,128)(2,1)}, bf16[256,512]{1,0:T(8,128)(2,1)S(1)}, u32[]{:S(2)}) copy-start(bf16[256,512]{1,0:T(8,128)(2,1)S(1)} %collective-permute-done.7.refs_1_) | copy-start | bytes 786436
  143.6 3.2 %copy-start.10 = (bf16[256,512]{1,0:T(8,128)(2,1)}, bf16[256,512]{1,0:T(8,128)(2,1)S(1)}, u32[]{:S(2)}) copy-start(bf16[256,512]{1,0:T(8,128)(2,1)S(1)} %collective-permute-done.8.refs_2_) | copy-start | bytes 786436
  146.8 0.7 copy-start.11
  154.2 1.0 copy-start.2
Sparse Core Ops, SparseCore 0:
  40.4 64.6 all-gather.1

commit v11 on v10

--- a/solution.py
+++ b/solution.py
@@ -453,9 +453,8 @@
         + new_column // 128 % 2
     )
     turn = jnp.asarray(old_column[None, :] == np.arange(width)[:, None], BF)
-    x_weight, z_weight, bc_weight, packed = lax.optimization_barrier(
-        (x_weight, z_weight, bc_weight, packed)
-    )
+    bc_weight, inbound = lax.optimization_barrier((bc_weight, inbound))
+    x_weight, z_weight, packed = lax.optimization_barrier((x_weight, z_weight, packed))
     xw = jnp.dot(x_weight, turn, preferred_element_type=F32).astype(BF)
     zw = jnp.dot(z_weight, turn, preferred_element_type=F32).astype(BF)
     order = turn[:256, :256]
@@ -465,8 +464,9 @@
     gain = norm_gain.reshape(heads // 4, 4, 32, 2).transpose(0, 3, 1, 2).reshape(1, width)
     small = jnp.stack([dt_bias, decay_rate], axis=1)
 
-    across[0], xw, zw, bw = lax.optimization_barrier((across[0], xw, zw, bw))
-    ow_part, across[0] = lax.optimization_barrier((ow_part, across[0]))
+    across[0], xw, zw, bw, inbound, ow_part = lax.optimization_barrier(
+        (across[0], xw, zw, bw, inbound, ow_part)
+    )
     ow_across = lax.all_gather(ow_part, ("groups", "dp"), axis=0, tiled=True)
     ow_sibling = exchange(out_weight, 1)
 

time: 167 us -> 150 us (0.90)
  waiting for transfers between devices: 59.6 us -> 40.8 us
  other arithmetic: 3.2 us -> 5.46 us
    all_to_all x2, waiting for transfers between devices: 30.5 us -> 17.4 us  [trade(): lax.all_to_all(value.reshape((shard_count, capacity) + row_shape), 'dp',...]
    ppermute x14, waiting for transfers between devices: 29 us -> 22 us  [exchange(): return lax.ppermute(value, 'mp', pairs)]
    unnamed x45 -> x43, local copies, waits for them, and re-layouts: 4.67 us -> 4.42 us
  transfers between devices with their start and end apart: 17 -> 17, of which waited for: 6 -> 9; matrix products, arithmetic and copies ran while one was open for 9% -> 12% of each run, Pallas kernels for 30% -> 34%
where the time goes in v11:
time: 150 us; the launch traced here: 149 us
  Pallas kernels  54.5 us (36%)
  waiting for transfers between devices  40.8 us (27%)
  starting transfers between devices  17.3 us (12%)
  between operations  14.2 us (9%)
  local copies, waits for them, and re-layouts  10.2 us (7%)
  matrix products  6.4 us (4%)
  other arithmetic  5.46 us (4%)
    pallas_call x2, Pallas kernels, layer_call(): pl.pallas_call(lambda *refs: layer_kernel(heads, span, pairs, half, *refs...  32.9 us
    ppermute x14, waiting for transfers between devices, exchange(): return lax.ppermute(value, 'mp', pairs)  22 us
    all_to_all x2, waiting for transfers between devices, trade(): lax.all_to_all(value.reshape((shard_count, capacity) + row_shape), 'dp',...  17.4 us
    pallas_call x2, Pallas kernels, out_call(): pl.pallas_call(kernel, grid=(columns // block,), out_shape=jax.ShapeDtype...  13.4 us
    ppermute x14, starting transfers between devices, exchange(): return lax.ppermute(value, 'mp', pairs)  8.86 us
    all_to_all x2, starting transfers between devices, trade(): lax.all_to_all(value.reshape((shard_count, capacity) + row_shape), 'dp',...  8.4 us
    unnamed x43, local copies, waits for them, and re-layouts  4.42 us
    pallas_call x1, Pallas kernels, gather_states(): pl.pallas_call(kernel, grid=(lines // 64,), out_shape=jax.ShapeDtypeStruc...  4.08 us
  transfers between devices with their start and end apart: 17, of which 9 were waited for; matrix products, arithmetic and copies ran while one was open for 12% of the time, Pallas kernels for 34%

profile of v11, /device:TPU:0, one launch (start us, length us, event | category | flops | bytes accessed | tf_op | source)
XLA Modules:
  0.0 148.8 jit_solution(8304884876103400083)
XLA Ops:
  7.2 0.0 copy-start
  7.2 1.1 constant_dynamic-slice_fusion
  8.3 3.0 %collective-permute-start.2 = (bf16[64,2048]{1,0:T(8,128)(2,1)S(1)}, bf16[64,2048]{1,0:T(8,128)(2,1)S(1)}, u32[]{:S(2)}, u32[]{:S(2)}) collective-permute-start(bf16[64,2048]{1,0:T(8,128)(2,1)S(1)} %constant_dynamic-slice_fusion), channel_id=1, source_target_pairs={{0,2},{1,3},{2,0},{3,1},{4,6},{5,7},{6,4},{7,5},{8,10},{9,11},{10,... | collective-permute-start | bytes 786440 | tf_op jit(solution)/shard_map/ppermute | solution.py:402
  11.3 0.8 select_reduce_fusion.1
  12.2 0.2 convert_reduce_fusion
  12.4 0.6 select_reduce_fusion.source
  13.0 3.0 %slice_bitcast_fusion = (bf16[2,2,256,512]{3,2,1,0:T(8,128)(2,1)}, bf16[2,2,256,512]{3,2,1,0:T(8,128)(2,1)}) fusion(bf16[2,2,2,256,512]{4,3,2,1,0:T(8,128)(2,1)} %bitcast.26), kind=kLoop, calls=%fused_computation.2 | loop fusion | bytes 4194304 | tf_op jit(solution)/shard_map/squeeze | solution.py:438
  16.0 4.0 %pack_states.1 = bf16[16,256,128]{2,1,0:T(8,128)(2,1)} custom-call(s32[16]{0:T(128)} %select_reduce_fusion.source, bf16[16,32768]{1,0:T(8,128)(2,1)} %store.1, bf16[256,256]{1,0:T(8,128)(2,1)} %constant.61.clone.swap), custom_call_target="tpu_custom_call" | custom-call | flops 1 | bytes 1 | tf_op jit(solution)/shard_map/pack_states/pallas_call | solution.py:39
  20.1 0.0 collective-permute-done.2
  20.1 4.9 %all-to-all-start = ((bf16[4,4,256,128]{3,2,1,0:T(8,128)(2,1)}), bf16[4,4,256,128]{3,2,1,0:T(8,128)(2,1)S(1)}, u32[]{:S(2)}, u32[]{:S(2)}) async-start(bf16[4,4,256,128]{3,2,1,0:T(8,128)(2,1)} %bitcast.31), calls=%async_computation | async-start | bytes 2097152 | tf_op jit(solution)/shard_map/all_to_all | solution.py:405
  24.9 0.5 collective-permute-start.1
  25.5 1.0 copy.37
  26.5 0.1 pad.4.clone
  26.6 3.8 %convolution_convert_fusion.refs_7_ = bf16[2048,512]{1,0:T(8,128)(2,1)} fusion(bf16[2048,512]{1,0:T(8,128)(2,1)S(1)} %copy-done, bf16[512,512]{1,0:T(8,128)(2,1)} %constant.62.clone), kind=kOutput, calls=%fused_computation | convolution fusion | flops 1074790400 | bytes 4718592 | tf_op jit(solution)/shard_map/dot_general | solution.py:459
  30.4 2.6 %convolution_convert_fusion.1.refs_6_ = bf16[2048,512]{1,0:T(8,128)(2,1)} fusion(bf16[2048,512]{1,0:T(8,128)(2,1)S(1)} %copy-done.18, bf16[512,512]{1,0:T(8,128)(2,1)S(1)} %copy-done.20), kind=kOutput, calls=%fused_computation.1 | convolution fusion | flops 1074790400 | bytes 4718592 | tf_op jit(solution)/shard_map/dot_general | solution.py:458
  33.0 0.0 copy-start.17
  33.0 17.4 %all-to-all-done = bf16[4,4,256,128]{3,2,1,0:T(8,128)(2,1)S(1)} async-done(((bf16[4,4,256,128]{3,2,1,0:T(8,128)(2,1)}), bf16[4,4,256,128]{3,2,1,0:T(8,128)(2,1)S(1)}, u32[]{:S(2)}, u32[]{:S(2)}) %all-to-all-start) | async-done | bytes 1048608 | tf_op jit(solution)/shard_map/all_to_all | solution.py:405
  50.4 2.8 %maximum_maximum_fusion.refs_5_ = bf16[2048,256]{1,0:T(8,128)(2,1)} fusion(bf16[2048,8]{1,0:T(8,128)(2,1)} %copy.37, bf16[2048,128]{1,0:T(8,128)(2,1)} %param.17, bf16[256]{0:T(256)(128)(2,1)S(1)} %pad.4.clone), kind=kLoop, calls=%fused_computation.4 | loop fusion | flops 3145728 | bytes 1606144 | tf_op jit(solution)/shard_map/concatenate | solution.py:461
  53.2 0.0 collective-permute-done.1.refs_3_
  53.2 0.0 all-gather.2.cloned.1.call-update
  53.3 0.1 collective-permute-start
  53.3 0.5 collective-permute-start.3
  53.8 0.5 collective-permute-start.5
  54.4 0.0 collective-permute-start.4
  54.4 0.1 reshape.85
  54.5 0.1 copy.38
  54.6 0.7 reshape.86.refs_9_
  55.4 0.7 copy.39.refs_8_
  56.0 0.1 and_select_fusion.2
  56.1 0.2 convert_reduce_fusion.1
  56.3 0.7 pad_add_fusion.refs_0_
  57.0 0.8 collective-permute-done
  57.8 1.5 %collective-permute-done.3.refs_4_ = bf16[2,2,256,512]{3,2,1,0:T(8,128)(2,1)} collective-permute-done((bf16[2,2,256,512]{3,2,1,0:T(8,128)(2,1)}, bf16[2,2,256,512]{3,2,1,0:T(8,128)(2,1)}, u32[]{:S(2)}, u32[]{:S(2)}) %collective-permute-start.3) | collective-permute-done | bytes 1048608 | tf_op jit(solution)/shard_map/ppermute | solution.py:402
  59.3 16.6 %layer.2 = (bf16[256,512]{1,0:T(8,128)(2,1)}, bf16[256,512]{1,0:T(8,128)(2,1)}, bf16[256,512]{1,0:T(8,128)(2,1)}, bf16[256,512]{1,0:T(8,128)(2,1)}, bf16[16,256,128]{2,1,0:T(8,128)(2,1)}) custom-call(s32[33]{0:T(128)} %pad_add_fusion.refs_0_, bf16[2,2,2,256,512]{4,3,2,1,0:T(8,128)(2,1)} %bitcast.27, bf16[2,2,2,256,512]{4,3,2,1,0:T(8,128)(2,1)} %bitcast.2.refs_2_, ...), custom_call_target="tpu_custom_call" | custom-call | flops 1 | bytes 1 | tf_op jit(solution)/shard_map/layer/pallas_call | solution.py:300
  75.9 3.4 %collective-permute-done.5.refs_3_ = bf16[2,2,256,512]{3,2,1,0:T(8,128)(2,1)} collective-permute-done((bf16[2,2,256,512]{3,2,1,0:T(8,128)(2,1)}, bf16[2,2,256,512]{3,2,1,0:T(8,128)(2,1)}, u32[]{:S(2)}, u32[]{:S(2)}) %collective-permute-start.5) | collective-permute-done | bytes 1048608 | tf_op jit(solution)/shard_map/ppermute | solution.py:402
  79.3 0.0 collective-permute-start.6
  79.3 0.0 collective-permute-done.4.refs_5_
  79.3 2.9 %collective-permute-done.6.refs_4_ = bf16[2,2,256,512]{3,2,1,0:T(8,128)(2,1)S(1)} collective-permute-done((bf16[2,2,256,512]{3,2,1,0:T(8,128)(2,1)}, bf16[2,2,256,512]{3,2,1,0:T(8,128)(2,1)S(1)}, u32[]{:S(2)}, u32[]{:S(2)}) %collective-permute-start.6) | collective-permute-done | bytes 1048608 | tf_op jit(solution)/shard_map/ppermute | solution.py:402
  82.2 1.0 copy-done.3
  83.1 16.4 %layer.3 = (bf16[256,512]{1,0:T(8,128)(2,1)}, bf16[256,512]{1,0:T(8,128)(2,1)}, bf16[256,512]{1,0:T(8,128)(2,1)}, bf16[256,512]{1,0:T(8,128)(2,1)}, bf16[16,256,128]{2,1,0:T(8,128)(2,1)}) custom-call(s32[33]{0:T(128)} %pad_add_fusion.refs_0_, bf16[2,2,2,256,512]{4,3,2,1,0:T(8,128)(2,1)} %bitcast.28, ...), custom_call_target="tpu_custom_call", output_to_operand_aliasing={{4}: (15, {})} | custom-call | flops 1 | bytes 1 | tf_op jit(solution)/shard_map/layer/pallas_call | solution.py:300
  99.5 1.4 all-gather.2.cloned.1.call-done.refs_6_
  100.9 0.0 collective-permute-start.10
  100.9 3.5 %all-to-all-start.1 = ((bf16[4,4,256,128]{3,2,1,0:T(8,128)(2,1)}), bf16[4,4,256,128]{3,2,1,0:T(8,128)(2,1)S(1)}, u32[]{:S(2)}, u32[]{:S(2)}) async-start(bf16[4,4,256,128]{3,2,1,0:T(8,128)(2,1)} %bitcast.29), calls=%async_computation.1 | async-start | bytes 2097152 | tf_op jit(solution)/shard_map/all_to_all | solution.py:405
  104.4 0.6 collective-permute-start.11
  105.0 1.5 collective-permute-start.12
  106.5 0.0 collective-permute-start.13
  106.5 0.7 collective-permute-start.7
  107.1 0.0 collective-permute-done.11.refs_1_
  107.1 1.5 collective-permute-start.8
  108.6 5.7 %collective-permute-done.12.refs_2_ = bf16[256,512]{1,0:T(8,128)(2,1)S(1)} collective-permute-done((bf16[256,512]{1,0:T(8,128)(2,1)}, bf16[256,512]{1,0:T(8,128)(2,1)S(1)}, u32[]{:S(2)}, u32[]{:S(2)}) %collective-permute-start.12) | collective-permute-done | bytes 262176 | tf_op jit(solution)/shard_map/ppermute | solution.py:402
  114.3 0.0 collective-permute-start.9
  114.3 4.6 %collective-permute-done.13.refs_3_ = bf16[256,512]{1,0:T(8,128)(2,1)S(1)} collective-permute-done((bf16[256,512]{1,0:T(8,128)(2,1)S(1)}, bf16[256,512]{1,0:T(8,128)(2,1)S(1)}, u32[]{:S(2)}, u32[]{:S(2)}) %collective-permute-start.13) | collective-permute-done | bytes 262176 | tf_op jit(solution)/shard_map/ppermute | solution.py:402
  119.0 0.0 collective-permute-done.10.refs_7_
  119.0 0.7 copy-done.6
  119.7 6.7 %project_out.2.refs_8_ = bf16[512,2048]{1,0:T(8,128)(2,1)} custom-call(bf16[256,512]{1,0:T(8,128)(2,1)} %get-tuple-element.56.refs_0_, bf16[256,512]{1,0:T(8,128)(2,1)} %copy-done.4, bf16[256,512]{1,0:T(8,128)(2,1)} %copy-done.5, bf16[256,512]{1,0:T(8,128)(2,1)} %copy-done.6, bf16[512,2048]{1,0:T(8,128)(2,1)} %refs_4_.3, ...), custom_call_target="tpu_custom_call" | custom-call | flops 1 | bytes 1 | tf_op jit(solution)/shard_map/project_out/pallas_call | solution.py:350
  126.4 0.0 collective-permute-done.7.refs_1_
  126.4 0.0 copy-start.8
  126.4 0.0 collective-permute-done.8.refs_2_
  126.4 3.1 %collective-permute-done.9.refs_3_ = bf16[256,512]{1,0:T(8,128)(2,1)S(1)} collective-permute-done((bf16[256,512]{1,0:T(8,128)(2,1)}, bf16[256,512]{1,0:T(8,128)(2,1)S(1)}, u32[]{:S(2)}, u32[]{:S(2)}) %collective-permute-start.9) | collective-permute-done | bytes 262176 | tf_op jit(solution)/shard_map/ppermute | solution.py:402
  129.5 0.7 copy-done.10
  130.1 6.7 %project_out.3 = bf16[512,2048]{1,0:T(8,128)(2,1)} custom-call(bf16[256,512]{1,0:T(8,128)(2,1)} %get-tuple-element.50.refs_0_, bf16[256,512]{1,0:T(8,128)(2,1)} %copy-done.8, bf16[256,512]{1,0:T(8,128)(2,1)} %copy-done.9, bf16[256,512]{1,0:T(8,128)(2,1)} %copy-done.10, bf16[512,2048]{1,0:T(8,128)(2,1)} %refs_4_.3, ...), custom_call_target="tpu_custom_call", output_to_operand_aliasing={{}: (8, {})} | custom-call | flops 1 | bytes 1 | tf_op jit(solution)/shard_map/project_out/pallas_call | solution.py:350
  136.9 0.0 all-to-all-done.1
  136.9 1.0 copy-done.2
  137.9 4.1 %gather_states.1 = bf16[16,32768]{1,0:T(8,128)(2,1)} custom-call(s32[16]{0:T(128)} %copy-done.13, bf16[16,256,128]{2,1,0:T(8,128)(2,1)} %bitcast.30, bf16[256,256]{1,0:T(8,128)(2,1)} %constant.61.clone.swap), custom_call_target="tpu_custom_call" | custom-call | flops 1 | bytes 1 | tf_op jit(solution)/shard_map/gather_states/pallas_call | solution.py:75
  (43 shorter events, 0.1 us)
Async XLA Ops:
  7.2 19.4 %copy-start = (bf16[2048,512]{1,0:T(8,128)(2,1)S(1)}, bf16[2048,512]{1,0:T(8,128)(2,1)}, u32[]{:S(2)}) copy-start(bf16[2048,512]{1,0:T(8,128)(2,1)} %param.16) | copy-start | bytes 6291460
  8.3 11.7 %collective-permute-start.2 = (bf16[64,2048]{1,0:T(8,128)(2,1)S(1)}, bf16[64,2048]{1,0:T(8,128)(2,1)S(1)}, u32[]{:S(2)}, u32[]{:S(2)}) collective-permute-start(bf16[64,2048]{1,0:T(8,128)(2,1)S(1)} %constant_dynamic-slice_fusion), channel_id=1, source_target_pairs={{0,2},{1,3},{2,0},{3,1},{4,6},{5,7},{6,4},{7,5},{8,10},{9,11},{10,... | collective-permute-start | bytes 786440 | tf_op jit(solution)/shard_map/ppermute | solution.py:402
  12.4 3.6 %copy-start.13 = (s32[16]{0:T(128)}, s32[16]{0:T(128)S(1)}, u32[]{:S(2)}) copy-start(s32[16]{0:T(128)S(1)} %multiply_add_fusion.index) | copy-start | bytes 196
  16.0 9.5 %copy-start.11 = (bf16[2048,8]{0,1:T(8,128)(2,1)S(1)}, bf16[2048,8]{0,1:T(8,128)(2,1)}, u32[]{:S(2)}) copy-start(bf16[2048,8]{0,1:T(8,128)(2,1)} %param.18) | copy-start | bytes 98308
  20.1 10.4 %copy-start.7 = (bf16[64,2048]{1,0:T(8,128)(2,1)}, bf16[64,2048]{1,0:T(8,128)(2,1)S(1)}, u32[]{:S(2)}) copy-start(bf16[64,2048]{1,0:T(8,128)(2,1)S(1)} %collective-permute-done.2) | copy-start | bytes 786436
  20.1 30.3 %all-to-all-start = ((bf16[4,4,256,128]{3,2,1,0:T(8,128)(2,1)}), bf16[4,4,256,128]{3,2,1,0:T(8,128)(2,1)S(1)}, u32[]{:S(2)}, u32[]{:S(2)}) async-start(bf16[4,4,256,128]{3,2,1,0:T(8,128)(2,1)} %bitcast.31), calls=%async_computation | async-start | bytes 2097152 | tf_op jit(solution)/shard_map/all_to_all | solution.py:405
  24.9 75.9 %all-gather.2.cloned.1.call-start = ((), (), s32[]{:S(2)}) async-start(), calls=%async_computation.2 | async-start | bytes 2359296 | tf_op jit(solution)/shard_map/all_gather | solution.py:470
  24.9 28.3 %collective-permute-start.1 = (bf16[2,2,256,512]{3,2,1,0:T(8,128)(2,1)}, bf16[2,2,256,512]{3,2,1,0:T(8,128)(2,1)}, u32[]{:S(2)}, u32[]{:S(2)}) collective-permute-start(bf16[2,2,256,512]{3,2,1,0:T(8,128)(2,1)} %get-tuple-element.65), channel_id=1, source_target_pairs={{0,2},{1,3},{2,0},{3,1},{4,6},{5,7},{6,4},{7,5},{8,10},{9,11},{10,... | collective-permute-start | bytes 3145736 | tf_op jit(solution)/shard_map/ppermute | solution.py:402
  26.6 3.8 %copy-start.18 = (bf16[2048,512]{1,0:T(8,128)(2,1)S(1)}, bf16[2048,512]{1,0:T(8,128)(2,1)}, u32[]{:S(2)}) copy-start(bf16[2048,512]{1,0:T(8,128)(2,1)} %param.15) | copy-start | bytes 6291460
  26.6 3.8 %copy-start.20 = (bf16[512,512]{1,0:T(8,128)(2,1)S(1)}, bf16[512,512]{1,0:T(8,128)(2,1)}, u32[]{:S(2)}) copy-start(bf16[512,512]{1,0:T(8,128)(2,1)} %constant.62.clone) | copy-start | bytes 1572868
  33.0 21.4 %copy-start.12 = (f32[512]{0:T(512)S(1)}, f32[512]{0:T(512)}, u32[]{:S(2)}) copy-start(f32[512]{0:T(512)} %param.21) | copy-start | bytes 6148
  33.0 22.3 %copy-start.14 = (f32[8]{0:T(128)S(1)}, f32[8]{0:T(128)}, u32[]{:S(2)}) copy-start(f32[8]{0:T(128)} %param.20) | copy-start | bytes 100
  33.0 22.3 %copy-start.15 = (f32[8]{0:T(128)S(1)}, f32[8]{0:T(128)}, u32[]{:S(2)}) copy-start(f32[8]{0:T(128)} %param.19) | copy-start | bytes 100
  33.0 23.0 %copy-start.16 = (s32[64]{0:T(128)S(1)}, s32[64]{0:T(128)}, u32[]{:S(2)}) copy-start(s32[64]{0:T(128)} %param.24) | copy-start | bytes 772
  33.0 23.3 %copy-start.17 = (s32[16]{0:T(128)S(1)}, s32[16]{0:T(128)}, u32[]{:S(2)}) copy-start(s32[16]{0:T(128)} %param.25) | copy-start | bytes 196
  50.4 8.9 %copy-start.1 = (bf16[4,4,256,128]{3,2,1,0:T(8,128)(2,1)}, bf16[4,4,256,128]{3,2,1,0:T(8,128)(2,1)S(1)}, u32[]{:S(2)}) copy-start(bf16[4,4,256,128]{3,2,1,0:T(8,128)(2,1)S(1)} %all-to-all-done) | copy-start | bytes 3145732
  53.3 4.6 %collective-permute-start = (bf16[2048,512]{1,0:T(8,128)(2,1)}, bf16[2048,512]{1,0:T(8,128)(2,1)}, u32[]{:S(2)}, u32[]{:S(2)}) collective-permute-start(bf16[2048,512]{1,0:T(8,128)(2,1)} %param.14), channel_id=1, source_target_pairs={{0,1},{1,0},{2,3},{3,2},{4,5},{5,4},{6,7},{7,6},{8,9},{9,8},{10,11... | collective-permute-start | bytes 6291464 | tf_op jit(solution)/shard_map/ppermute | solution.py:402
  53.3 6.0 %collective-permute-start.3 = (bf16[2,2,256,512]{3,2,1,0:T(8,128)(2,1)}, bf16[2,2,256,512]{3,2,1,0:T(8,128)(2,1)}, u32[]{:S(2)}, u32[]{:S(2)}) collective-permute-start(bf16[2,2,256,512]{3,2,1,0:T(8,128)(2,1)} %collective-permute-done.1.refs_3_), channel_id=1, source_target_pairs={{0,1},{1,0},{2,3},{3,2},{4,5},{5,4},{6,7},{7,6},{8,9},{9,8},{10,11... | collective-permute-start | bytes 3145736 | tf_op jit(solution)/shard_map/ppermute | solution.py:402
  53.8 25.5 %collective-permute-start.5 = (bf16[2,2,256,512]{3,2,1,0:T(8,128)(2,1)}, bf16[2,2,256,512]{3,2,1,0:T(8,128)(2,1)}, u32[]{:S(2)}, u32[]{:S(2)}) collective-permute-start(bf16[2,2,256,512]{3,2,1,0:T(8,128)(2,1)} %get-tuple-element.64), channel_id=1, source_target_pairs={{0,2},{1,3},{2,0},{3,1},{4,6},{5,7},{6,4},{7,5},{8,10},{9,11},{10,... | collective-permute-start | bytes 3145736 | tf_op jit(solution)/shard_map/ppermute | solution.py:402
  54.4 24.9 %collective-permute-start.4 = (bf16[512,2048]{1,0:T(8,128)(2,1)}, bf16[512,2048]{1,0:T(8,128)(2,1)}, u32[]{:S(2)}, u32[]{:S(2)}) collective-permute-start(bf16[512,2048]{1,0:T(8,128)(2,1)} %refs_4_.3), channel_id=1, source_target_pairs={{0,1},{1,0},{2,3},{3,2},{4,5},{5,4},{6,7},{7,6},{8,9},{9,8},{10,11... | collective-permute-start | bytes 6291464 | tf_op jit(solution)/shard_map/ppermute | solution.py:402
  79.3 2.9 %collective-permute-start.6 = (bf16[2,2,256,512]{3,2,1,0:T(8,128)(2,1)}, bf16[2,2,256,512]{3,2,1,0:T(8,128)(2,1)S(1)}, u32[]{:S(2)}, u32[]{:S(2)}) collective-permute-start(bf16[2,2,256,512]{3,2,1,0:T(8,128)(2,1)} %collective-permute-done.5.refs_3_), channel_id=1, source_target_pairs={{0,1},{1,0},{2,3},{3,2},{4,5},{5,4},{6,7},{7,6},{8,9},{9,8},{10,11... | collective-permute-start | bytes 3145736 | tf_op jit(solution)/shard_map/ppermute | solution.py:402
  82.2 1.0 copy-start.3
  99.5 7.0 %copy-start.19 = (bf16[256,512]{1,0:T(8,128)(2,1)S(1)}, bf16[256,512]{1,0:T(8,128)(2,1)}, u32[]{:S(2)}) copy-start(bf16[256,512]{1,0:T(8,128)(2,1)} %get-tuple-element.59) | copy-start | bytes 786436
  100.9 18.1 %collective-permute-start.10 = (bf16[512,2048]{1,0:T(8,128)(2,1)}, bf16[512,2048]{1,0:T(8,128)(2,1)}, u32[]{:S(2)}, u32[]{:S(2)}) collective-permute-start(bf16[512,2048]{1,0:T(8,128)(2,1)} %all-gather.2.cloned.1.call-done.refs_6_), channel_id=1, source_target_pairs={{0,1},{1,0},{2,3},{3,2},{4,5},{5,4},{6,7},{7,6},{8,9},{9,8},{10,11... | collective-permute-start | bytes 6291464 | tf_op jit(solution)/shard_map/ppermute | solution.py:402
  100.9 36.0 %all-to-all-start.1 = ((bf16[4,4,256,128]{3,2,1,0:T(8,128)(2,1)}), bf16[4,4,256,128]{3,2,1,0:T(8,128)(2,1)S(1)}, u32[]{:S(2)}, u32[]{:S(2)}) async-start(bf16[4,4,256,128]{3,2,1,0:T(8,128)(2,1)} %bitcast.29), calls=%async_computation.1 | async-start | bytes 2097152 | tf_op jit(solution)/shard_map/all_to_all | solution.py:405
  104.4 2.7 %collective-permute-start.11 = (bf16[256,512]{1,0:T(8,128)(2,1)}, bf16[256,512]{1,0:T(8,128)(2,1)S(1)}, u32[]{:S(2)}, u32[]{:S(2)}) collective-permute-start(bf16[256,512]{1,0:T(8,128)(2,1)} %get-tuple-element.57), channel_id=1, source_target_pairs={{0,1},{1,0},{2,3},{3,2},{4,5},{5,4},{6,7},{7,6},{8,9},{9,8},{10,11... | collective-permute-start | bytes 786440 | tf_op jit(solution)/shard_map/ppermute | solution.py:402
  105.0 9.4 %collective-permute-start.12 = (bf16[256,512]{1,0:T(8,128)(2,1)}, bf16[256,512]{1,0:T(8,128)(2,1)S(1)}, u32[]{:S(2)}, u32[]{:S(2)}) collective-permute-start(bf16[256,512]{1,0:T(8,128)(2,1)} %get-tuple-element.58), channel_id=1, source_target_pairs={{0,2},{1,3},{2,0},{3,1},{4,6},{5,7},{6,4},{7,5},{8,10},{9,11},{10,... | collective-permute-start | bytes 786440 | tf_op jit(solution)/shard_map/ppermute | solution.py:402
  106.5 12.5 %collective-permute-start.13 = (bf16[256,512]{1,0:T(8,128)(2,1)S(1)}, bf16[256,512]{1,0:T(8,128)(2,1)S(1)}, u32[]{:S(2)}, u32[]{:S(2)}) collective-permute-start(bf16[256,512]{1,0:T(8,128)(2,1)S(1)} %copy-done.19), channel_id=1, source_target_pairs={{0,3},{1,2},{2,1},{3,0},{4,7},{5,6},{6,5},{7,4},{8,11},{9,10},{10,... | collective-permute-start | bytes 786440 | tf_op jit(solution)/shard_map/ppermute | solution.py:402
  106.5 19.9 %collective-permute-start.7 = (bf16[256,512]{1,0:T(8,128)(2,1)}, bf16[256,512]{1,0:T(8,128)(2,1)S(1)}, u32[]{:S(2)}, u32[]{:S(2)}) collective-permute-start(bf16[256,512]{1,0:T(8,128)(2,1)} %get-tuple-element.51), channel_id=1, source_target_pairs={{0,1},{1,0},{2,3},{3,2},{4,5},{5,4},{6,7},{7,6},{8,9},{9,8},{10,11... | collective-permute-start | bytes 786440 | tf_op jit(solution)/shard_map/ppermute | solution.py:402
  107.1 11.9 %copy-start.4 = (bf16[256,512]{1,0:T(8,128)(2,1)}, bf16[256,512]{1,0:T(8,128)(2,1)S(1)}, u32[]{:S(2)}) copy-start(bf16[256,512]{1,0:T(8,128)(2,1)S(1)} %collective-permute-done.11.refs_1_) | copy-start | bytes 786436
  107.1 19.3 %collective-permute-start.8 = (bf16[256,512]{1,0:T(8,128)(2,1)}, bf16[256,512]{1,0:T(8,128)(2,1)S(1)}, u32[]{:S(2)}, u32[]{:S(2)}) collective-permute-start(bf16[256,512]{1,0:T(8,128)(2,1)} %get-tuple-element.52), channel_id=1, source_target_pairs={{0,2},{1,3},{2,0},{3,1},{4,6},{5,7},{6,4},{7,5},{8,10},{9,11},{10,... | collective-permute-start | bytes 786440 | tf_op jit(solution)/shard_map/ppermute | solution.py:402
  114.3 4.6 %copy-start.5 = (bf16[256,512]{1,0:T(8,128)(2,1)}, bf16[256,512]{1,0:T(8,128)(2,1)S(1)}, u32[]{:S(2)}) copy-start(bf16[256,512]{1,0:T(8,128)(2,1)S(1)} %collective-permute-done.12.refs_2_) | copy-start | bytes 786436
  114.3 15.1 %collective-permute-start.9 = (bf16[256,512]{1,0:T(8,128)(2,1)}, bf16[256,512]{1,0:T(8,128)(2,1)S(1)}, u32[]{:S(2)}, u32[]{:S(2)}) collective-permute-start(bf16[256,512]{1,0:T(8,128)(2,1)} %get-tuple-element.53), channel_id=1, source_target_pairs={{0,3},{1,2},{2,1},{3,0},{4,7},{5,6},{6,5},{7,4},{8,11},{9,10},{10,... | collective-permute-start | bytes 786440 | tf_op jit(solution)/shard_map/ppermute | solution.py:402
  119.0 0.7 copy-start.6
  126.4 3.1 %copy-start.8 = (bf16[256,512]{1,0:T(8,128)(2,1)}, bf16[256,512]{1,0:T(8,128)(2,1)S(1)}, u32[]{:S(2)}) copy-start(bf16[256,512]{1,0:T(8,128)(2,1)S(1)} %collective-permute-done.7.refs_1_) | copy-start | bytes 786436
  126.4 3.1 %copy-start.9 = (bf16[256,512]{1,0:T(8,128)(2,1)}, bf16[256,512]{1,0:T(8,128)(2,1)S(1)}, u32[]{:S(2)}) copy-start(bf16[256,512]{1,0:T(8,128)(2,1)S(1)} %collective-permute-done.8.refs_2_) | copy-start | bytes 786436
  129.4 0.7 copy-start.10
  136.9 1.0 copy-start.2
Sparse Core Ops, SparseCore 0:
  53.4 47.4 all-gather.1
